TPU v7x, 512 devices: a whole 4x8x8 slice. The times are simulated.
512 devices in a mesh: node: 32 (over z, y_hi, core), dp: 4 (over x), tensor: 4 (over y_lo).
Axes of the slice: x: 4, y: 8 (y_hi: 2, y_lo: 4; y = y_hi * 4 + y_lo), z: 8, core: 2. Of those that a mesh axis runs over, the one named last changes fastest.
Arguments:
- hidden: bfloat16 [65536, 1024], P(('node', 'dp'), 'tensor'), may hold values from -6 to 6
- cotangent: bfloat16 [65536, 8192], P(('node', 'dp'), 'tensor'), may hold values from -0.032958984 to 0.032958984
- feedback: bfloat16 [32, 1024, 8192], P('node', 'dp', 'tensor'), may hold values from -1.5 to 1.5
- chosen: int32 [32, 4, 4, 64], P('node', 'dp', 'tensor'), may hold values from 0 to 127, all different within a row
- momentum: float32 [4, 4, 128, 64, 64], P('dp', 'tensor', 'node'), may hold values from -0.75 to 0.75
Outputs:
- feedback_new: bfloat16 [32, 1024, 8192], P('node', 'dp', 'tensor')
- momentum_new: float32 [4, 4, 128, 64, 64], P('dp', 'tensor', 'node')
- step: bfloat16 [1024, 8192], P('dp', 'tensor')
Inputs may be any that keep to these rules, and one draw needn't show every extreme that they name: `chosen`: each device's list names 64 distinct blocks of its shard. Block b of a shard is owned by node b // (128 / 32).
All inputs are finite; a program needn't handle non-finite values.
Results may differ from a plain program's by a relative error of at most 0.014.
Values may be sent and summed in bfloat16 or wider, within the bound.
No kernel may reach another device: no remote copies, remote signals or barrier semaphores. Data moves between devices by JAX's collectives and lax.ppermute only.
A program may use at most 64 MiB of HBM per device.

v0:
```python
import jax
import jax.numpy as jnp
from jax import lax
from jax.sharding import PartitionSpec as P

BLK = 64


decay_rate = 0.9


def local(hidden, cotangent, feedback, chosen, momentum):
    rows = feedback.shape[1]
    cols = feedback.shape[2]
    rows_blk = rows // BLK
    cols_blk = cols // BLK
    count_blk = rows_blk * cols_blk
    whole = lax.all_gather(hidden, "tensor", axis=1, tiled=True)
    grad = lax.psum_scatter(
        lax.dot_general(
            whole, cotangent, (((0,), (0,)), ((), ())), preferred_element_type=jnp.float32
        ).astype(jnp.bfloat16),
        "dp",
        scatter_dimension=0,
        tiled=True,
    ).astype(jnp.float32)
    acc = feedback[0].astype(jnp.float32) + grad
    acc_blocks = (
        acc.reshape(rows_blk, BLK, cols_blk, BLK).transpose(0, 2, 1, 3).reshape(count_blk, BLK, BLK)
    )
    picks = chosen.reshape(-1)
    mask = jnp.any(picks[:, None] == jnp.arange(count_blk, dtype=jnp.int32)[None, :], axis=0)
    kept = jnp.where(mask[:, None, None], jnp.float32(0.0), acc_blocks)
    feedback_new = (
        kept.reshape(rows_blk, cols_blk, BLK, BLK).transpose(0, 2, 1, 3).reshape(1, rows, cols)
    )
    feedback_new = feedback_new.astype(jnp.bfloat16)
    nodes = lax.axis_size("node")
    owned = momentum.shape[2]
    masked = jnp.where(mask[:, None, None], acc_blocks, jnp.float32(0.0))
    total = lax.psum(masked, "node")
    every_moment = lax.all_gather(momentum, "node", axis=2, tiled=True)
    mean = total / nodes
    moment_all = decay_rate * every_moment[0, 0] + mean
    step_blocks = (mean + decay_rate * moment_all).astype(jnp.bfloat16)
    first = lax.axis_index("node") * owned
    momentum_new = lax.dynamic_slice_in_dim(moment_all, first, owned, 0)[None, None]
    step = (
        step_blocks.reshape(rows_blk, cols_blk, BLK, BLK).transpose(0, 2, 1, 3).reshape(rows, cols)
    )
    return (feedback_new, momentum_new, step)


def solution(mesh):
    placed = (
        P(("node", "dp"), "tensor"),
        P(("node", "dp"), "tensor"),
        P("node", "dp", "tensor"),
        P("node", "dp", "tensor", None),
        P("dp", "tensor", "node", None, None),
    )
    return jax.shard_map(
        local,
        mesh=mesh,
        in_specs=placed,
        out_specs=(
            P("node", "dp", "tensor"),
            P("dp", "tensor", "node", None, None),
            P("dp", "tensor"),
        ),
        check_vma=False,
    )
```

profile of v0, /device:TPU:1, one launch (start us, length us, event | category | flops | bytes accessed | tf_op | source)
XLA Modules:
  0.0 571.7 jit_solution(3463190609089632281)
XLA Ops:
  8.0 0.0 copy-start
  8.0 0.0 all-gather.3.cloned.1.call-start
  8.1 0.7 all-gather.3.cloned.1.call-update
  8.7 0.0 reduce-scatter.2.cloned.1.call-start
  8.8 44.4 %all-gather.3.cloned.1.call-done = bf16[512,1024]{1,0:T(8,128)(2,1)} async-done(((bf16[512,256]{1,0:T(8,128)(2,1)}), bf16[512,1024]{1,0:T(8,128)(2,1)}) %all-gather.3.cloned.1.call-update) | async-done | bytes 1048592 | tf_op jit(solution)/shard_map/all_gather | solution.py:18
  53.2 0.0 copy-done
  53.2 5.6 convolution_convert_fusion
  58.8 0.0 copy-start.1
  58.8 0.0 reduce-scatter.2.cloned.1.call-update
  58.8 0.0 all-gather.5.cloned.1.call-start
  58.9 0.5 all-gather.5.cloned.1.call-update
  59.4 0.2 all-reduce.2.cloned.1.call-start
  59.6 0.0 copy-done.1
  59.6 0.1 fusion.1
  59.7 0.1 broadcast_in_dim.34
  59.8 0.3 broadcast_in_dim.35
  60.2 2.5 broadcast_in_dim.36
  62.6 48.8 %reduce-scatter.2.cloned.1.call-done = bf16[256,2048]{1,0:T(8,128)(2,1)} async-done(((bf16[1024,2048]{1,0:T(8,128)(2,1)}), bf16[256,2048]{1,0:T(8,128)(2,1)}) %reduce-scatter.2.cloned.1.call-update) | async-done | bytes 1048592 | tf_op jit(solution)/shard_map/reduce_scatter | solution.py:19
  111.4 3.9 convert_add_fusion
  115.3 4.9 reshape.37
  120.2 4.6 copy.14
  124.8 2.3 bitcast_select_fusion
  127.2 0.0 all-reduce.2.cloned.1.call-update
  127.2 44.1 %all-gather.5.cloned.1.call-done = f32[1,1,128,64,64]{4,3,1,0,2:T(8,128)} async-done(((f32[1,1,4,64,64]{4,3,1,0,2:T(8,128)}), f32[1,1,128,64,64]{4,3,1,0,2:T(8,128)}) %all-gather.5.cloned.1.call-update) | async-done | bytes 2097168 | tf_op jit(solution)/shard_map/all_gather | solution.py:42
  171.3 377.4 %all-reduce.2.cloned.1.call-done = f32[128,64,64]{2,1,0:T(8,128)} async-done(((f32[128,64,64]{2,1,0:T(8,128)}), f32[128,64,64]{2,1,0:T(8,128)}) %all-reduce.2.cloned.1.call-update) | async-done | bytes 2097168 | tf_op jit(solution)/shard_map/psum | solution.py:41
  548.7 7.1 %add_convert_fusion = (bf16[128,64,64]{2,1,0:T(8,128)(2,1)S(1)}, f32[128,64,64]{2,1,0:T(8,128)}) fusion(f32[128,64,64]{2,1,0:T(8,128)} %all-reduce.2.cloned.1.call-done, f32[1,1,128,64,64]{4,3,1,0,2:T(8,128)} %all-gather.5.cloned.1.call-done), kind=kLoop, calls=%fused_computation.2 | loop fusion | flops 3145728 | bytes 7340032 | tf_op jit(solution)/shard_map/convert_element_type | solution.py:45
  555.8 2.7 copy.15
  558.5 4.2 reshape.40
  562.7 1.6 dynamic-slice_bitcast_fusion
Async XLA Ops:
  8.0 45.2 %copy-start = (bf16[512,2048]{1,0:T(8,128)(2,1)S(1)}, bf16[512,2048]{1,0:T(8,128)(2,1)}, u32[]{:S(2)}) copy-start(bf16[512,2048]{1,0:T(8,128)(2,1)} %param.6) | copy-start | bytes 6291460
  8.0 45.2 %all-gather.3.cloned.1.call-start = ((), (), s32[]{:S(2)}) async-start(), calls=%async_computation.1 | async-start | bytes 1310720 | tf_op jit(solution)/shard_map/all_gather | solution.py:18
  8.7 102.7 %reduce-scatter.2.cloned.1.call-start = ((), (), s32[]{:S(2)}) async-start(), calls=%async_computation.2 | async-start | bytes 5242880 | tf_op jit(solution)/shard_map/reduce_scatter | solution.py:19
  58.8 0.8 copy-start.1
  58.8 112.5 %all-gather.5.cloned.1.call-start = ((), (), s32[]{:S(2)}) async-start(), calls=%async_computation.3 | async-start | bytes 4325376 | tf_op jit(solution)/shard_map/all_gather | solution.py:42
  59.4 489.3 %all-reduce.2.cloned.1.call-start = ((), (), s32[]{:S(2)}) async-start(), calls=%async_computation.4 | async-start | bytes 8388608 | tf_op jit(solution)/shard_map/psum | solution.py:41
Sparse Core Ops, SparseCore 0:
  10.9 42.2 all-gather.2
  58.9 52.4 reduce-scatter.1
Sparse Core Ops, SparseCore 1:
  63.2 108.1 all-gather.4
  174.4 374.3 all-reduce.1
where the time goes:
time: 583 us; the launch traced here: 572 us
  waiting for transfers between devices  516 us (89%)
  local copies, waits for them, and re-layouts  20.9 us (4%)
  between operations  15.5 us (3%)
  other arithmetic  13.4 us (2%)
    psum x1, waiting for transfers between devices, local(): total = lax.psum(masked, 'node')  377 us
    reduce_scatter x1, waiting for transfers between devices, local(): lax.psum_scatter(lax.dot_general(whole, cotangent, (((0,), (0,)), ((), ()...  48.8 us
    all_gather x1, waiting for transfers between devices, local(): whole = lax.all_gather(hidden, 'tensor', axis=1, tiled=True)  44.4 us
    all_gather x1, waiting for transfers between devices, local(): every_moment = lax.all_gather(momentum, 'node', axis=2, tiled=True)  44.1 us
  transfers between devices with their start and end apart: 4, of which 4 were waited for; matrix products, arithmetic and copies ran while one was open for 3% of the time, Pallas kernels for 0%

commit v1 on v0

v1 whole, which is shorter than its diff:
```python
import jax
import jax.numpy as jnp
from jax import lax
from jax.sharding import Mesh, PartitionSpec as P

BLK = 64
DECAY = 0.9
F32, BF16 = jnp.float32, jnp.bfloat16
NODE = ("z", "yh", "c")
SHAPE = (8, 2, 2, 4, 4)


def swap(value, axis, flip, size):
    return lax.ppermute(value, axis, [(i, i ^ flip) for i in range(size)])


def sum_over_dp(hidden, cotangent):
    d, t = lax.axis_index("dp"), lax.axis_index("t")
    whole = [hidden]
    for shift in (1, 2, 3):
        whole.append(lax.ppermute(hidden, "t", [(i, (i + shift) % 4) for i in range(4)]))
    whole = jnp.stack(whole)
    half = cotangent.shape[1] // 2

    def part(flip, cols):
        rows = lax.dynamic_index_in_dim(whole, (t - (d ^ flip)) % 4, 0, keepdims=False)
        return lax.dot_general(
            rows, cols, (((0,), (0,)), ((), ())), preferred_element_type=F32
        ).astype(BF16)

    a, b = cotangent[:, :half], cotangent[:, half:]
    own_a, own_b = part(0, a), part(0, b)
    a1, a2, a3 = part(1, a), part(2, a), part(3, a)
    b1, b2, b3 = part(1, b), part(2, b), part(3, b)
    got_a = swap(jnp.stack([a1, a2]), "dp", 1, 4)
    got_b = swap(jnp.stack([b3, b2]), "dp", 3, 4)
    next_a = swap((a3.astype(F32) + got_a[1].astype(F32)).astype(BF16), "dp", 3, 4)
    next_b = swap((b1.astype(F32) + got_b[1].astype(F32)).astype(BF16), "dp", 1, 4)
    sum_a = own_a.astype(F32) + got_a[0].astype(F32) + next_a.astype(F32)
    sum_b = own_b.astype(F32) + got_b[0].astype(F32) + next_b.astype(F32)
    return jnp.concatenate([sum_a, sum_b], axis=1)


def local(hidden, cotangent, feedback, chosen, momentum):
    rows, cols = feedback.shape[1:]
    rows_blk, cols_blk = rows // BLK, cols // BLK
    nodes = 32
    c, yh = lax.axis_index("c"), lax.axis_index("yh")
    grad = sum_over_dp(hidden, cotangent)
    acc = feedback[0].astype(F32) + grad
    picks = chosen.reshape(-1)
    mask = jnp.any(
        picks[:, None] == jnp.arange(rows_blk * cols_blk, dtype=jnp.int32)[None, :], axis=0
    ).reshape(rows_blk, cols_blk)
    wide = jnp.repeat(mask, BLK, axis=1)
    wide = jnp.broadcast_to(wide[:, None, :], (rows_blk, BLK, cols)).reshape(rows, cols)
    feedback_new = jnp.where(wide, 0.0, acc).astype(BF16)[None]
    sent = jnp.where(wide, acc, 0.0)
    sent = sent.reshape(rows, 4, 2, 256)
    mine = lax.dynamic_index_in_dim(sent, c, 2, keepdims=False)
    other = lax.dynamic_index_in_dim(sent, 1 - c, 2, keepdims=False).astype(BF16)
    pair = (mine + swap(other, "c", 1, 2).astype(F32)).astype(BF16)
    pair = pair.reshape(4, BLK, 2, 2, 256).transpose(0, 2, 1, 3, 4).reshape(8, BLK, 512)
    got = lax.all_to_all(pair, "z", 0, 0, tiled=True)
    summed = jnp.sum(got.astype(F32), axis=0).reshape(BLK, 2, 256)
    keep = lax.dynamic_index_in_dim(summed, yh, 1, keepdims=False)
    give = lax.dynamic_index_in_dim(summed, 1 - yh, 1, keepdims=False)
    total = keep + swap(give, "yh", 1, 2)
    mean = total.reshape(BLK, 4, BLK).transpose(1, 0, 2) / nodes
    momentum_new = DECAY * momentum[0, 0] + mean
    step = (mean + DECAY * momentum_new).astype(BF16)
    step = step.transpose(1, 0, 2).reshape(BLK, 256)
    peer = swap(step, "yh", 1, 2)
    both = jnp.where(yh == 0, jnp.concatenate([step, peer], 1), jnp.concatenate([peer, step], 1))
    every = lax.all_gather(both, "z", axis=0)
    far = swap(every, "c", 1, 2)
    first, second = jnp.where(c == 0, every, far), jnp.where(c == 0, far, every)
    out = jnp.stack([first.reshape(4, 2, BLK, 2, 256), second.reshape(4, 2, BLK, 2, 256)], axis=4)
    out = out.transpose(0, 2, 1, 3, 4, 5).reshape(rows, cols)
    return feedback_new, momentum_new[None, None], out


def solution(mesh):
    fine = Mesh(mesh.devices.reshape(SHAPE), (*NODE, "dp", "t"))
    tokens = P((*NODE, "dp"), "t")
    return jax.shard_map(
        local,
        mesh=fine,
        in_specs=(
            tokens,
            tokens,
            P(NODE, "dp", "t"),
            P(NODE, "dp", "t", None),
            P("dp", "t", NODE, None, None),
        ),
        out_specs=(P(NODE, "dp", "t"), P("dp", "t", NODE, None, None), P("dp", "t")),
        check_vma=False,
    )
```

time: 583 us -> 187 us (0.32); the launches traced: 572 us -> 185 us
  waiting for transfers between devices: 516 us -> 62.9 us
  starting transfers between devices: 0.34 us -> 59.7 us
  blocking collectives: 0 us -> 20.1 us
  between operations: 15.5 us -> 1.11 us
    psum x1 -> x0, waiting for transfers between devices: 377 us -> none  [local(): total = lax.psum(masked, 'node')]
    all_gather x2 -> x0, waiting for transfers between devices: 88.5 us -> none  [the longest x1 44.4 us: local(): whole = lax.all_gather(hidden, 'tensor', axis=1, tiled=True)]
    ppermute x0 -> x11, starting transfers between devices: none -> 49.6 us  [the longest x8 39.3 us: swap(): return lax.ppermute(value, axis, [(i, i ^ flip) for i in range(size)])]
    reduce_scatter x1 -> x0, waiting for transfers between devices: 48.8 us -> none  [local(): lax.psum_scatter(lax.dot_general(whole, cotangent, (((0,), (0,)), ((), ()...]
    ppermute x0 -> x11, waiting for transfers between devices: none -> 44.8 us  [the longest x8 27.3 us: swap(): return lax.ppermute(value, axis, [(i, i ^ flip) for i in range(size)])]
    all_gather x0 -> x1, blocking collectives: none -> 20.1 us  [local(): every = lax.all_gather(both, 'z', axis=0)]
    all_to_all x0 -> x1, waiting for transfers between devices: none -> 18 us  [local(): got = lax.all_to_all(pair, 'z', 0, 0, tiled=True)]
    all_to_all x0 -> x1, starting transfers between devices: none -> 10 us  [local(): got = lax.all_to_all(pair, 'z', 0, 0, tiled=True)]
  transfers between devices with their start and end apart: 4 -> 12, of which waited for: 4 -> 7; matrix products, arithmetic and copies ran while one was open for 3% -> 10% of each run, Pallas kernels for 0% -> 0%
where the time goes in v1:
time: 187 us; the launch traced here: 185 us
  waiting for transfers between devices  62.9 us (34%)
  starting transfers between devices  59.7 us (32%)
  local copies, waits for them, and re-layouts  21.1 us (11%)
  blocking collectives  20.1 us (11%)
  other arithmetic  12 us (6%)
  matrix products  8.36 us (4%)
    ppermute x8, starting transfers between devices, swap(): return lax.ppermute(value, axis, [(i, i ^ flip) for i in range(size)])  39.3 us
    ppermute x8, waiting for transfers between devices, swap(): return lax.ppermute(value, axis, [(i, i ^ flip) for i in range(size)])  27.3 us
    all_gather x1, blocking collectives, local(): every = lax.all_gather(both, 'z', axis=0)  20.1 us
    all_to_all x1, waiting for transfers between devices, local(): got = lax.all_to_all(pair, 'z', 0, 0, tiled=True)  18 us
    ppermute x3, waiting for transfers between devices, sum_over_dp(): lax.ppermute(hidden, 't', [(i, (i + shift) % 4) for i in range(4)])  17.5 us
    ppermute x3, starting transfers between devices, sum_over_dp(): lax.ppermute(hidden, 't', [(i, (i + shift) % 4) for i in range(4)])  10.3 us
    all_to_all x1, starting transfers between devices, local(): got = lax.all_to_all(pair, 'z', 0, 0, tiled=True)  10 us
    dot_general x8, matrix products, part(): lax.dot_general(rows, cols, (((0,), (0,)), ((), ())), preferred_element_t...  8.36 us
  transfers between devices with their start and end apart: 12, of which 7 were waited for; matrix products, arithmetic and copies ran while one was open for 10% of the time, Pallas kernels for 0%

profile of v1, /device:TPU:1, one launch (start us, length us, event | category | flops | bytes accessed | tf_op | source)
XLA Modules:
  0.0 185.2 jit_solution(9077578426775105842)
XLA Ops:
  0.6 6.1 %collective-permute-start.2 = (bf16[512,256]{1,0:T(8,128)(2,1)}, bf16[512,256]{1,0:T(8,128)(2,1)S(1)}, u32[]{:S(2)}, u32[]{:S(2)}) collective-permute-start(bf16[512,256]{1,0:T(8,128)(2,1)} %param.5), channel_id=1, source_target_pairs={{0,3},{1,0},{2,1},{3,2},{4,7},{5,4},{6,5},{7,6},{8,11},{9,8},{10,9... | collective-permute-start | bytes 786440 | tf_op jit(solution)/shard_map/ppermute | solution.py:21
  6.7 1.9 %collective-permute-start.1 = (bf16[512,256]{1,0:T(8,128)(2,1)}, bf16[512,256]{1,0:T(8,128)(2,1)S(1)}, u32[]{:S(2)}, u32[]{:S(2)}) collective-permute-start(bf16[512,256]{1,0:T(8,128)(2,1)} %param.5), channel_id=1, source_target_pairs={{0,2},{1,3},{2,0},{3,1},{4,6},{5,7},{6,4},{7,5},{8,10},{9,11},{10,... | collective-permute-start | bytes 786440 | tf_op jit(solution)/shard_map/ppermute | solution.py:21
  8.6 2.3 %collective-permute-start = (bf16[512,256]{1,0:T(8,128)(2,1)}, bf16[512,256]{1,0:T(8,128)(2,1)S(1)}, u32[]{:S(2)}, u32[]{:S(2)}) collective-permute-start(bf16[512,256]{1,0:T(8,128)(2,1)} %param.5), channel_id=1, source_target_pairs={{0,1},{1,2},{2,3},{3,0},{4,5},{5,6},{6,7},{7,4},{8,9},{9,10},{10,1... | collective-permute-start | bytes 786440 | tf_op jit(solution)/shard_map/ppermute | solution.py:21
  11.1 17.5 %collective-permute-done.1 = bf16[512,256]{1,0:T(8,128)(2,1)S(1)} collective-permute-done((bf16[512,256]{1,0:T(8,128)(2,1)}, bf16[512,256]{1,0:T(8,128)(2,1)S(1)}, u32[]{:S(2)}, u32[]{:S(2)}) %collective-permute-start.1) | collective-permute-done | bytes 262176 | tf_op jit(solution)/shard_map/ppermute | solution.py:21
  31.2 5.1 %collective-permute-start.5 = (bf16[2,256,1024]{2,1,0:T(8,128)(2,1)S(1)}, bf16[2,256,1024]{2,1,0:T(8,128)(2,1)S(1)}, u32[]{:S(2)}, u32[]{:S(2)}) collective-permute-start(bf16[2,256,1024]{2,1,0:T(8,128)(2,1)S(1)} %pad_maximum_fusion.2), channel_id=1, source_target_pairs={{0,12},{4,8},{8,4},{12,0},{1,13},{5,9},{9,5},{13,1},{2,14},{6,10},... | collective-permute-start | bytes 3145736 | tf_op jit(solution)/shard_map/ppermute | solution.py:14
  36.9 1.9 %collective-permute-start.3 = (bf16[2,256,1024]{2,1,0:T(8,128)(2,1)S(1)}, bf16[2,256,1024]{2,1,0:T(8,128)(2,1)S(1)}, u32[]{:S(2)}, u32[]{:S(2)}) collective-permute-start(bf16[2,256,1024]{2,1,0:T(8,128)(2,1)S(1)} %pad_maximum_fusion.1), channel_id=1, source_target_pairs={{0,4},{4,0},{8,12},{12,8},{1,5},{5,1},{9,13},{13,9},{2,6},{6,2},{1... | collective-permute-start | bytes 3145736 | tf_op jit(solution)/shard_map/ppermute | solution.py:14
  38.9 19.6 %collective-permute-done.5 = bf16[2,256,1024]{2,1,0:T(8,128)(2,1)S(1)} collective-permute-done((bf16[2,256,1024]{2,1,0:T(8,128)(2,1)S(1)}, bf16[2,256,1024]{2,1,0:T(8,128)(2,1)S(1)}, u32[]{:S(2)}, u32[]{:S(2)}) %collective-permute-start.5) | collective-permute-done | bytes 1048608 | tf_op jit(solution)/shard_map/ppermute | solution.py:14
  59.8 2.5 %collective-permute-start.6 = (bf16[256,1024]{1,0:T(8,128)(2,1)}, bf16[256,1024]{1,0:T(8,128)(2,1)S(1)}, u32[]{:S(2)}, u32[]{:S(2)}) collective-permute-start(bf16[256,1024]{1,0:T(8,128)(2,1)} %fusion.11), channel_id=1, source_target_pairs={{0,4},{4,0},{8,12},{12,8},{1,5},{5,1},{9,13},{13,9},{2,6},{6,2},{1... | collective-permute-start | bytes 1572872 | tf_op jit(solution)/shard_map/ppermute | solution.py:14
  62.4 1.3 fusion.13
  63.7 4.3 %collective-permute-start.4 = (bf16[256,1024]{1,0:T(8,128)(2,1)}, bf16[256,1024]{1,0:T(8,128)(2,1)}, u32[]{:S(2)}, u32[]{:S(2)}) collective-permute-start(bf16[256,1024]{1,0:T(8,128)(2,1)} %fusion.13), channel_id=1, source_target_pairs={{0,12},{4,8},{8,4},{12,0},{1,13},{5,9},{9,5},{13,1},{2,14},{6,10},... | collective-permute-start | bytes 1572872 | tf_op jit(solution)/shard_map/ppermute | solution.py:14
  68.6 2.5 %reshape.114 = pred[256,4,2,256]{3,2,1,0:T(4,128)(4,1)} reshape(pred[4,64,2048]{2,1,0:T(8,128)(4,1)S(1)} %broadcast_in_dim.25) | data formatting | bytes 1048576 | tf_op jit(solution)/shard_map/reshape | solution.py:56
  71.1 3.1 %reshape.124 = f32[256,4,2,256]{3,2,1,0:T(2,128)} reshape(bf16[1,256,2048]{2,1,0:T(8,128)(2,1)S(1)} %copy-done.1) | data formatting | bytes 3145728 | tf_op jit(solution)/shard_map/convert_element_type | solution.py:50
  74.2 1.8 fusion.12
  76.1 1.9 %concatenate.43 = f32[256,2,2,256]{3,2,1,0:T(2,128)} reshape(f32[256,1024]{1,0:T(8,128)S(1)} %fusion.12) | data formatting | bytes 2097152 | tf_op jit(solution)/shard_map/concatenate | solution.py:41
  78.4 2.1 %fusion.14 = f32[256,1024]{1,0:T(8,128)S(1)} fusion(bf16[256,1024]{1,0:T(8,128)(2,1)} %collective-permute-done.4, bf16[512,2048]{1,0:T(8,128)(2,1)} %param.6, bf16[2,256,1024]{2,1,0:T(8,128)(2,1)} %copy-done.4, bf16[4,512,256]{2,1,0:T(8,128)(2,1)} %copy-done.2, s32[]{:T(128)S(6)} %select_n.96), kind=kOutput, calls=%fused_computation.32 | convolution fusion | flops 270008320 | bytes 3407876 | tf_op jit(solution)/shard_map/dot_general | solution.py:27
  80.5 1.9 %concatenate.42 = f32[256,2,2,256]{3,2,1,0:T(2,128)} reshape(f32[256,1024]{1,0:T(8,128)S(1)} %fusion.14) | data formatting | bytes 2097152 | tf_op jit(solution)/shard_map/concatenate | solution.py:41
  82.4 3.9 %fusion.2 = f32[256,4,2,256]{3,2,1,0:T(2,128)S(1)} fusion(pred[256,4,2,256]{3,2,1,0:T(4,128)(4,1)} %reshape.114, f32[256,4,2,256]{3,2,1,0:T(2,128)} %reshape.124, f32[256,2,2,256]{3,2,1,0:T(2,128)} %concatenate.43, f32[256,2,2,256]{3,2,1,0:T(2,128)} %concatenate.42), kind=kLoop, calls=%fused_computation.4 | loop fusion | flops 1572864 | bytes 6815744 | tf_op jit(solution)/shard_map/jit(_where)/select_n | solution.py:58
  86.3 1.3 copy-done
  88.7 5.1 %collective-permute-start.7 = (bf16[256,4,256]{2,0,1:T(8,128)(2,1)S(1)}, bf16[256,4,256]{2,0,1:T(8,128)(2,1)}, u32[]{:S(2)}, u32[]{:S(2)}) collective-permute-start(bf16[256,4,256]{2,0,1:T(8,128)(2,1)S(1)} %bitcast.107), channel_id=1, source_target_pairs={{0,16},{16,0},{1,17},{17,1},{2,18},{18,2},{3,19},{19,3},{4,20},{20... | collective-permute-start | bytes 1572872 | tf_op jit(solution)/shard_map/ppermute | solution.py:14
  93.8 2.5 %constant_dynamic-slice_fusion.2 = f32[256,4,1,256]{3,2,1,0:T(1,128)S(1)} fusion(f32[256,4,2,256]{3,2,1,0:T(2,128)} %copy-done, s32[]{:T(128)S(6)} %select_n.105), kind=kLoop, calls=%fused_computation.88 | loop fusion | bytes 2097156 | tf_op jit(solution)/shard_map/jit(dynamic_index_in_dim)/dynamic_slice | solution.py:60
  99.2 10.0 %all-to-all-start = ((bf16[8,64,512]{2,1,0:T(8,128)(2,1)}), bf16[8,64,512]{2,1,0:T(8,128)(2,1)S(1)}, u32[]{:S(2)}, u32[]{:S(2)}) async-start(bf16[8,64,512]{2,1,0:T(8,128)(2,1)} %reshape.116), calls=%async_computation | async-start | bytes 1048576 | tf_op jit(solution)/shard_map/all_to_all | solution.py:64
  109.3 18.0 %all-to-all-done = bf16[8,64,512]{2,1,0:T(8,128)(2,1)S(1)} async-done(((bf16[8,64,512]{2,1,0:T(8,128)(2,1)}), bf16[8,64,512]{2,1,0:T(8,128)(2,1)S(1)}, u32[]{:S(2)}, u32[]{:S(2)}) %all-to-all-start) | async-done | bytes 524320 | tf_op jit(solution)/shard_map/all_to_all | solution.py:64
  127.6 5.1 %collective-permute-start.8 = (f32[64,256]{1,0:T(8,128)S(1)}, f32[64,256]{1,0:T(8,128)S(1)}, u32[]{:S(2)}, u32[]{:S(2)}) collective-permute-start(f32[64,256]{1,0:T(8,128)S(1)} %bitcast.112), channel_id=1, source_target_pairs={{0,32},{32,0},{1,33},{33,1},{2,34},{34,2},{3,35},{35,3},{4,36},{36... | collective-permute-start | bytes 196616 | tf_op jit(solution)/shard_map/ppermute | solution.py:14
  132.8 3.7 %collective-permute-done.8 = f32[64,256]{1,0:T(8,128)S(1)} collective-permute-done((f32[64,256]{1,0:T(8,128)S(1)}, f32[64,256]{1,0:T(8,128)S(1)}, u32[]{:S(2)}, u32[]{:S(2)}) %collective-permute-start.8) | collective-permute-done | bytes 65568 | tf_op jit(solution)/shard_map/ppermute | solution.py:14
  136.9 5.1 %collective-permute-start.9 = (bf16[64,256]{1,0:T(8,128)(2,1)S(1)}, bf16[64,256]{1,0:T(8,128)(2,1)S(1)}, u32[]{:S(2)}, u32[]{:S(2)}) collective-permute-start(bf16[64,256]{1,0:T(8,128)(2,1)S(1)} %reshape.118), channel_id=1, source_target_pairs={{0,32},{32,0},{1,33},{33,1},{2,34},{34,2},{3,35},{35,3},{4,36},{36... | collective-permute-start | bytes 98312 | tf_op jit(solution)/shard_map/ppermute | solution.py:14
  142.2 3.3 %collective-permute-done.9 = bf16[64,256]{1,0:T(8,128)(2,1)S(1)} collective-permute-done((bf16[64,256]{1,0:T(8,128)(2,1)S(1)}, bf16[64,256]{1,0:T(8,128)(2,1)S(1)}, u32[]{:S(2)}, u32[]{:S(2)}) %collective-permute-start.9) | collective-permute-done | bytes 32800 | tf_op jit(solution)/shard_map/ppermute | solution.py:14
  145.5 20.1 %all_gather.4 = bf16[8,64,512]{2,1,0:T(8,128)(2,1)S(1)} all-gather(bf16[1,64,512]{2,1,0:T(8,128)(2,1)S(1)} %maximum_select_fusion), channel_id=1, replica_groups=mesh['z'=8,'yh'=2,'c'=2,'dp'=4,'t'=4] {'z'}, dimensions={0}, use_global_device_ids=true | all-gather | bytes 589824 | tf_op jit(solution)/shard_map/all_gather | solution.py:75
  165.5 10.2 %collective-permute-start.10 = (bf16[8,64,512]{2,1,0:T(8,128)(2,1)S(1)}, bf16[8,64,512]{2,1,0:T(8,128)(2,1)}, u32[]{:S(2)}, u32[]{:S(2)}) collective-permute-start(bf16[8,64,512]{2,1,0:T(8,128)(2,1)S(1)} %all_gather.4), channel_id=1, source_target_pairs={{0,16},{16,0},{1,17},{17,1},{2,18},{18,2},{3,19},{19,3},{4,20},{20... | collective-permute-start | bytes 1572872 | tf_op jit(solution)/shard_map/ppermute | solution.py:14
  175.8 2.7 %fusion.1 = bf16[1,256,2048]{2,1,0:T(8,128)(2,1)} fusion(f32[1,256,1024]{2,1,0:T(8,128)S(1)} %bitcast.102, f32[1,256,1024]{2,1,0:T(8,128)S(1)} %bitcast.103, bf16[1,256,2048]{2,1,0:T(8,128)(2,1)} %param.7, pred[1,256,2048]{2,1,0:T(8,128)(4,1)S(1)} %bitcast.104), kind=kLoop, calls=%fused_computation.2 | loop fusion | flops 2621440 | bytes 4718592 | tf_op jit(solution)/shard_map/convert_element_type | solution.py:57
  180.5 1.5 maximum_bitcast_fusion
  181.9 1.6 copy.28
  183.6 1.6 reshape.119
  (55 shorter events, 12.5 us)
Async XLA Ops:
  0.6 10.4 %collective-permute-start.2 = (bf16[512,256]{1,0:T(8,128)(2,1)}, bf16[512,256]{1,0:T(8,128)(2,1)S(1)}, u32[]{:S(2)}, u32[]{:S(2)}) collective-permute-start(bf16[512,256]{1,0:T(8,128)(2,1)} %param.5), channel_id=1, source_target_pairs={{0,3},{1,0},{2,1},{3,2},{4,7},{5,4},{6,5},{7,6},{8,11},{9,8},{10,9... | collective-permute-start | bytes 786440 | tf_op jit(solution)/shard_map/ppermute | solution.py:21
  6.7 21.9 %collective-permute-start.1 = (bf16[512,256]{1,0:T(8,128)(2,1)}, bf16[512,256]{1,0:T(8,128)(2,1)S(1)}, u32[]{:S(2)}, u32[]{:S(2)}) collective-permute-start(bf16[512,256]{1,0:T(8,128)(2,1)} %param.5), channel_id=1, source_target_pairs={{0,2},{1,3},{2,0},{3,1},{4,6},{5,7},{6,4},{7,5},{8,10},{9,11},{10,... | collective-permute-start | bytes 786440 | tf_op jit(solution)/shard_map/ppermute | solution.py:21
  8.6 20.0 %collective-permute-start = (bf16[512,256]{1,0:T(8,128)(2,1)}, bf16[512,256]{1,0:T(8,128)(2,1)S(1)}, u32[]{:S(2)}, u32[]{:S(2)}) collective-permute-start(bf16[512,256]{1,0:T(8,128)(2,1)} %param.5), channel_id=1, source_target_pairs={{0,1},{1,2},{2,3},{3,0},{4,5},{5,6},{6,7},{7,4},{8,9},{9,10},{10,1... | collective-permute-start | bytes 786440 | tf_op jit(solution)/shard_map/ppermute | solution.py:21
  11.1 18.6 %copy-start.3 = (bf16[512,2048]{1,0:T(8,128)(2,1)S(1)}, bf16[512,2048]{1,0:T(8,128)(2,1)}, u32[]{:S(2)}) copy-start(bf16[512,2048]{1,0:T(8,128)(2,1)} %param.6) | copy-start | bytes 6291460
  29.7 44.5 %copy-start.2 = (bf16[4,512,256]{2,1,0:T(8,128)(2,1)}, bf16[4,512,256]{2,1,0:T(8,128)(2,1)S(1)}, u32[]{:S(2)}) copy-start(bf16[4,512,256]{2,1,0:T(8,128)(2,1)S(1)} %pad_maximum_fusion) | copy-start | bytes 3145732
  31.2 27.3 %collective-permute-start.5 = (bf16[2,256,1024]{2,1,0:T(8,128)(2,1)S(1)}, bf16[2,256,1024]{2,1,0:T(8,128)(2,1)S(1)}, u32[]{:S(2)}, u32[]{:S(2)}) collective-permute-start(bf16[2,256,1024]{2,1,0:T(8,128)(2,1)S(1)} %pad_maximum_fusion.2), channel_id=1, source_target_pairs={{0,12},{4,8},{8,4},{12,0},{1,13},{5,9},{9,5},{13,1},{2,14},{6,10},... | collective-permute-start | bytes 3145736 | tf_op jit(solution)/shard_map/ppermute | solution.py:14
  36.9 25.4 %collective-permute-start.3 = (bf16[2,256,1024]{2,1,0:T(8,128)(2,1)S(1)}, bf16[2,256,1024]{2,1,0:T(8,128)(2,1)S(1)}, u32[]{:S(2)}, u32[]{:S(2)}) collective-permute-start(bf16[2,256,1024]{2,1,0:T(8,128)(2,1)S(1)} %pad_maximum_fusion.1), channel_id=1, source_target_pairs={{0,4},{4,0},{8,12},{12,8},{1,5},{5,1},{9,13},{13,9},{2,6},{6,2},{1... | collective-permute-start | bytes 3145736 | tf_op jit(solution)/shard_map/ppermute | solution.py:14
  58.5 5.2 %copy-start.5 = (bf16[2,256,1024]{2,1,0:T(8,128)(2,1)}, bf16[2,256,1024]{2,1,0:T(8,128)(2,1)S(1)}, u32[]{:S(2)}) copy-start(bf16[2,256,1024]{2,1,0:T(8,128)(2,1)S(1)} %collective-permute-done.5) | copy-start | bytes 3145732
  59.8 8.2 %copy-start.7 = (s32[1,1,1,64]{3,2,1,0:T(1,128)S(1)}, s32[1,1,1,64]{3,2,1,0:T(1,128)}, u32[]{:S(2)}) copy-start(s32[1,1,1,64]{3,2,1,0:T(1,128)} %param.8) | copy-start | bytes 772
  59.8 11.3 %copy-start.1 = (bf16[1,256,2048]{2,1,0:T(8,128)(2,1)S(1)}, bf16[1,256,2048]{2,1,0:T(8,128)(2,1)}, u32[]{:S(2)}) copy-start(bf16[1,256,2048]{2,1,0:T(8,128)(2,1)} %param.7) | copy-start | bytes 3145732
  59.8 14.4 %collective-permute-start.6 = (bf16[256,1024]{1,0:T(8,128)(2,1)}, bf16[256,1024]{1,0:T(8,128)(2,1)S(1)}, u32[]{:S(2)}, u32[]{:S(2)}) collective-permute-start(bf16[256,1024]{1,0:T(8,128)(2,1)} %fusion.11), channel_id=1, source_target_pairs={{0,4},{4,0},{8,12},{12,8},{1,5},{5,1},{9,13},{13,9},{2,6},{6,2},{1... | collective-permute-start | bytes 1572872 | tf_op jit(solution)/shard_map/ppermute | solution.py:14
  62.4 1.3 copy-start.4
  63.7 14.8 %collective-permute-start.4 = (bf16[256,1024]{1,0:T(8,128)(2,1)}, bf16[256,1024]{1,0:T(8,128)(2,1)}, u32[]{:S(2)}, u32[]{:S(2)}) collective-permute-start(bf16[256,1024]{1,0:T(8,128)(2,1)} %fusion.13), channel_id=1, source_target_pairs={{0,12},{4,8},{8,4},{12,0},{1,13},{5,9},{9,5},{13,1},{2,14},{6,10},... | collective-permute-start | bytes 1572872 | tf_op jit(solution)/shard_map/ppermute | solution.py:14
  86.3 1.3 copy-start
  88.7 7.6 %collective-permute-start.7 = (bf16[256,4,256]{2,0,1:T(8,128)(2,1)S(1)}, bf16[256,4,256]{2,0,1:T(8,128)(2,1)}, u32[]{:S(2)}, u32[]{:S(2)}) collective-permute-start(bf16[256,4,256]{2,0,1:T(8,128)(2,1)S(1)} %bitcast.107), channel_id=1, source_target_pairs={{0,16},{16,0},{1,17},{17,1},{2,18},{18,2},{3,19},{19,3},{4,20},{20... | collective-permute-start | bytes 1572872 | tf_op jit(solution)/shard_map/ppermute | solution.py:14
  97.5 35.2 %copy-start.6 = (f32[1,1,4,64,64]{4,3,2,1,0:T(8,128)S(1)}, f32[1,1,4,64,64]{4,3,2,1,0:T(8,128)}, u32[]{:S(2)}) copy-start(f32[1,1,4,64,64]{4,3,2,1,0:T(8,128)} %param.9) | copy-start | bytes 196612
  99.2 28.1 %all-to-all-start = ((bf16[8,64,512]{2,1,0:T(8,128)(2,1)}), bf16[8,64,512]{2,1,0:T(8,128)(2,1)S(1)}, u32[]{:S(2)}, u32[]{:S(2)}) async-start(bf16[8,64,512]{2,1,0:T(8,128)(2,1)} %reshape.116), calls=%async_computation | async-start | bytes 1048576 | tf_op jit(solution)/shard_map/all_to_all | solution.py:64
  127.6 8.9 %collective-permute-start.8 = (f32[64,256]{1,0:T(8,128)S(1)}, f32[64,256]{1,0:T(8,128)S(1)}, u32[]{:S(2)}, u32[]{:S(2)}) collective-permute-start(f32[64,256]{1,0:T(8,128)S(1)} %bitcast.112), channel_id=1, source_target_pairs={{0,32},{32,0},{1,33},{33,1},{2,34},{34,2},{3,35},{35,3},{4,36},{36... | collective-permute-start | bytes 196616 | tf_op jit(solution)/shard_map/ppermute | solution.py:14
  136.9 8.6 %collective-permute-start.9 = (bf16[64,256]{1,0:T(8,128)(2,1)S(1)}, bf16[64,256]{1,0:T(8,128)(2,1)S(1)}, u32[]{:S(2)}, u32[]{:S(2)}) collective-permute-start(bf16[64,256]{1,0:T(8,128)(2,1)S(1)} %reshape.118), channel_id=1, source_target_pairs={{0,32},{32,0},{1,33},{33,1},{2,34},{34,2},{3,35},{35,3},{4,36},{36... | collective-permute-start | bytes 98312 | tf_op jit(solution)/shard_map/ppermute | solution.py:14
  165.5 13.5 %collective-permute-start.10 = (bf16[8,64,512]{2,1,0:T(8,128)(2,1)S(1)}, bf16[8,64,512]{2,1,0:T(8,128)(2,1)}, u32[]{:S(2)}, u32[]{:S(2)}) collective-permute-start(bf16[8,64,512]{2,1,0:T(8,128)(2,1)S(1)} %all_gather.4), channel_id=1, source_target_pairs={{0,16},{16,0},{1,17},{17,1},{2,18},{18,2},{3,19},{19,3},{4,20},{20... | collective-permute-start | bytes 1572872 | tf_op jit(solution)/shard_map/ppermute | solution.py:14

commit v2 on v1

v2 whole, which is shorter than its diff:
```python
import jax
import jax.numpy as jnp
from jax import lax
from jax.experimental import pallas as pl
from jax.experimental.pallas import tpu as pltpu
from jax.sharding import Mesh, PartitionSpec as P

BLK = 64
DECAY = 0.9
NODES = 32
F32, BF16 = jnp.float32, jnp.bfloat16
NODE = ("z", "yh", "c")
SHAPE = (8, 2, 2, 4, 4)
VMEM_LIMIT = 32 * 1024 * 1024


def swap(value, axis, flip, size):
    return lax.ppermute(value, axis, [(i, i ^ flip) for i in range(size)])


def kernel_call(body, grid, ins, outs, out_shape, cost):
    return pl.pallas_call(
        body,
        grid=grid,
        in_specs=ins,
        out_specs=outs,
        out_shape=out_shape,
        compiler_params=pltpu.CompilerParams(vmem_limit_bytes=VMEM_LIMIT),
        cost_estimate=pl.CostEstimate(flops=cost, bytes_accessed=cost, transcendentals=0),
    )


SMEM = pl.BlockSpec(memory_space=pltpu.SMEM)


def feedback_kernel(
    c_ref, mask_ref, fb_ref, own_ref, got_a, got_b, next_a, next_b, new_ref, mine_ref, other_ref
):
    first = c_ref[0] == 0
    for h, got, nxt in ((0, got_a, next_a), (1, got_b, next_b)):
        for yh in range(2):
            sent = []
            for c in range(2):
                near = slice(yh * 512 + c * 256, yh * 512 + c * 256 + 256)
                far = slice(h * 1024 + near.start, h * 1024 + near.stop)
                acc = (
                    own_ref[:, far].astype(F32)
                    + got[0, :, near].astype(F32)
                    + nxt[:, near].astype(F32)
                )
                acc = fb_ref[:, far].astype(F32) + acc
                chosen = jnp.broadcast_to(mask_ref[0, :, far], acc.shape) > 0.5
                new_ref[:, far] = jnp.where(chosen, 0.0, acc).astype(BF16)
                sent.append(jnp.where(chosen, acc, 0.0))
            place = slice(yh * 256, yh * 256 + 256)
            mine_ref[h, :, place] = jnp.where(first, sent[0], sent[1])
            other_ref[h, :, place] = jnp.where(first, sent[1], sent[0]).astype(BF16)


def error_feedback(c, mask, feedback, own, got_a, got_b, next_a, next_b):
    rows, cols = feedback.shape
    groups = rows // BLK
    wide = pl.BlockSpec((BLK, cols), lambda i: (i, 0))
    half = pl.BlockSpec((BLK, cols // 2), lambda i: (i, 0))
    slab = pl.BlockSpec((2, BLK, 512), lambda i: (i, 0, 0))
    line = pl.BlockSpec((1, 1, cols), lambda i: (i, 0, 0))
    got = pl.BlockSpec((1, BLK, cols // 2), lambda i: (0, i, 0))
    return kernel_call(
        feedback_kernel,
        (groups,),
        [SMEM, line, wide, wide, got, got, half, half],
        [wide, slab, slab],
        [
            jax.ShapeDtypeStruct((rows, cols), BF16),
            jax.ShapeDtypeStruct((2 * groups, BLK, 512), F32),
            jax.ShapeDtypeStruct((2 * groups, BLK, 512), BF16),
        ],
        8 * rows * cols,
    )(c, mask, feedback, own, got_a, got_b, next_a, next_b)


def owner_kernel(yh_ref, mine_ref, peer_ref, moment_ref, new_ref, step_ref):
    mean = (mine_ref[...] + peer_ref[...]) * (1.0 / NODES)
    moment = DECAY * moment_ref[...] + mean
    step = (mean + DECAY * moment).astype(BF16)
    for z in range(8):
        step_ref[z] = step
    own = jnp.where(yh_ref[0] == 0, moment[:, :256], moment[:, 256:])
    for b in range(4):
        new_ref[b] = own[:, b * BLK : (b + 1) * BLK]


def owner_update(yh, mine, peer, moment):
    whole = pl.BlockSpec(memory_space=pltpu.VMEM)
    return kernel_call(
        owner_kernel,
        (),
        [SMEM, whole, whole, whole],
        [whole, whole],
        [
            jax.ShapeDtypeStruct((4, BLK, BLK), F32),
            jax.ShapeDtypeStruct((8, BLK, 512), BF16),
        ],
        8 * BLK * 512,
    )(yh, mine, peer, moment)


def assemble_kernel(c_ref, mine_ref, other_ref, out_ref):
    first = c_ref[0] == 0
    for h in range(2):
        for yh in range(2):
            place = slice(yh * 256, yh * 256 + 256)
            mine, other = mine_ref[h, :, place], other_ref[h, :, place]
            at = h * 1024 + yh * 512
            out_ref[:, at : at + 256] = jnp.where(first, mine, other)
            out_ref[:, at + 256 : at + 512] = jnp.where(first, other, mine)


def assemble(c, mine, other, rows, cols):
    slab = pl.BlockSpec((2, BLK, 512), lambda i: (i, 0, 0))
    return kernel_call(
        assemble_kernel,
        (rows // BLK,),
        [SMEM, slab, slab],
        pl.BlockSpec((BLK, cols), lambda i: (i, 0)),
        jax.ShapeDtypeStruct((rows, cols), BF16),
        4 * rows * cols,
    )(c, mine, other)


def partial_sums(hidden, cotangent, early):
    d, t = lax.axis_index("dp"), lax.axis_index("t")
    whole = [hidden]
    for shift in (1, 2, 3):
        whole.append(lax.ppermute(hidden, "t", [(i, (i + shift) % 4) for i in range(4)]))
    *whole, early = lax.optimization_barrier((*whole, early))
    whole = jnp.stack(whole)

    def part(flip, cols):
        rows = lax.dynamic_index_in_dim(whole, (t - (d ^ flip)) % 4, 0, keepdims=False)
        return lax.dot_general(
            rows, cols, (((0,), (0,)), ((), ())), preferred_element_type=F32
        ).astype(BF16)

    half = cotangent.shape[1] // 2
    a, b = cotangent[:, :half], cotangent[:, half:]
    a1, a2, a3 = part(1, a), part(2, a), part(3, a)
    b1, b2, b3 = part(1, b), part(2, b), part(3, b)
    own = part(0, cotangent)
    got_a = swap(jnp.stack([a1, a2]), "dp", 1, 4)
    got_b = swap(jnp.stack([b3, b2]), "dp", 3, 4)
    next_a = swap((a3.astype(F32) + got_a[1].astype(F32)).astype(BF16), "dp", 3, 4)
    next_b = swap((b1.astype(F32) + got_b[1].astype(F32)).astype(BF16), "dp", 1, 4)
    return early, own, got_a, got_b, next_a, next_b


def as_matrix(blocks):
    return blocks.transpose(1, 0, 2).reshape(BLK, -1)


def local(hidden, cotangent, feedback, chosen, momentum):
    rows, cols = feedback.shape[1:]
    rows_blk, cols_blk = rows // BLK, cols // BLK
    c, yh = lax.axis_index("c"), lax.axis_index("yh")
    at_c, at_yh = c.astype(jnp.int32).reshape(1), yh.astype(jnp.int32).reshape(1)
    block_of = (
        jnp.arange(rows_blk, dtype=jnp.int32)[:, None] * cols_blk
        + jnp.arange(cols, dtype=jnp.int32)[None, :] // BLK
    )
    mask = jnp.any(chosen.reshape(-1, 1, 1) == block_of[None], axis=0).astype(F32)
    moment = as_matrix(momentum[0, 0])
    far_moment = swap(moment, "yh", 1, 2)
    far_moment, *parts = partial_sums(hidden, cotangent, far_moment)
    moment = jnp.where(
        yh == 0, jnp.concatenate([moment, far_moment], 1), jnp.concatenate([far_moment, moment], 1)
    )
    feedback_new, mine, other = error_feedback(at_c, mask[:, None], feedback[0], *parts)
    pair = (mine + swap(other, "c", 1, 2).astype(F32)).astype(BF16)
    got = lax.all_to_all(pair, "z", 0, 0, tiled=True)
    near = jnp.sum(got.astype(F32), axis=0)
    momentum_new, copies = owner_update(at_yh, near, swap(near, "yh", 1, 2), moment)
    every = lax.all_to_all(copies, "z", 0, 0, tiled=True)
    step = assemble(at_c, every, swap(every, "c", 1, 2), rows, cols)
    return feedback_new[None], momentum_new[None, None], step


def solution(mesh):
    fine = Mesh(mesh.devices.reshape(SHAPE), (*NODE, "dp", "t"))
    tokens = P((*NODE, "dp"), "t")
    return jax.shard_map(
        local,
        mesh=fine,
        in_specs=(
            tokens,
            tokens,
            P(NODE, "dp", "t"),
            P(NODE, "dp", "t", None),
            P("dp", "t", NODE, None, None),
        ),
        out_specs=(P(NODE, "dp", "t"), P("dp", "t", NODE, None, None), P("dp", "t")),
        check_vma=False,
    )
```

time: 187 us -> 155 us (0.83)
  the two profiles are of different devices: /device:TPU:1 before, /device:TPU:17 now
where the time goes in v2:
time: 155 us
  waiting for transfers between devices  51.6 us (33%)
  blocking collectives  43.1 us (28%)
  starting transfers between devices  42.8 us (28%)
  matrix products  6.85 us (4%)
  Pallas kernels  6.01 us (4%)
  other arithmetic  1.97 us (1%)
    ppermute x8, waiting for transfers between devices, swap(): return lax.ppermute(value, axis, [(i, i ^ flip) for i in range(size)])  49 us
    ppermute x8, starting transfers between devices, swap(): return lax.ppermute(value, axis, [(i, i ^ flip) for i in range(size)])  34.4 us
    all_to_all x1, blocking collectives, local(): got = lax.all_to_all(pair, 'z', 0, 0, tiled=True)  26.5 us
    all_to_all x1, blocking collectives, local(): every = lax.all_to_all(copies, 'z', 0, 0, tiled=True)  16.6 us
    ppermute x3, starting transfers between devices, partial_sums(): lax.ppermute(hidden, 't', [(i, (i + shift) % 4) for i in range(4)])  8.35 us
    dot_general x7, matrix products, part(): lax.dot_general(rows, cols, (((0,), (0,)), ((), ())), preferred_element_t...  6.85 us
    pallas_call x1, Pallas kernels, error_feedback(): kernel_call(feedback_kernel, (groups,), [SMEM, line, wide, wide, got, got...  3.71 us
  transfers between devices with their start and end apart: 11, of which 8 were waited for; matrix products, arithmetic and copies ran while one was open for 5% of the time, Pallas kernels for 0%

profile of v2, /device:TPU:17, one launch (start us, length us, event | category | flops | bytes accessed | tf_op | source)
XLA Modules:
  0.0 154.5 jit_solution(4194358498743468536)
XLA Ops:
  0.6 2.1 %collective-permute-start.1 = (bf16[512,256]{1,0:T(8,128)(2,1)}, bf16[512,256]{1,0:T(8,128)(2,1)S(1)}, u32[]{:S(2)}, u32[]{:S(2)}) collective-permute-start(bf16[512,256]{1,0:T(8,128)(2,1)} %param.5), channel_id=1, source_target_pairs={{0,2},{1,3},{2,0},{3,1},{4,6},{5,7},{6,4},{7,5},{8,10},{9,11},{10,... | collective-permute-start | bytes 786440 | tf_op jit(solution)/shard_map/ppermute | solution.py:135
  2.7 3.3 %collective-permute-start = (bf16[512,256]{1,0:T(8,128)(2,1)}, bf16[512,256]{1,0:T(8,128)(2,1)S(1)}, u32[]{:S(2)}, u32[]{:S(2)}) collective-permute-start(bf16[512,256]{1,0:T(8,128)(2,1)} %param.5), channel_id=1, source_target_pairs={{0,1},{1,2},{2,3},{3,0},{4,5},{5,6},{6,7},{7,4},{8,9},{9,10},{10,1... | collective-permute-start | bytes 786440 | tf_op jit(solution)/shard_map/ppermute | solution.py:135
  6.0 3.0 %collective-permute-start.2 = (bf16[512,256]{1,0:T(8,128)(2,1)}, bf16[512,256]{1,0:T(8,128)(2,1)S(1)}, u32[]{:S(2)}, u32[]{:S(2)}) collective-permute-start(bf16[512,256]{1,0:T(8,128)(2,1)} %param.5), channel_id=1, source_target_pairs={{0,3},{1,0},{2,1},{3,2},{4,7},{5,4},{6,5},{7,6},{8,11},{9,8},{10,9... | collective-permute-start | bytes 786440 | tf_op jit(solution)/shard_map/ppermute | solution.py:135
  9.0 1.0 copy.9
  10.2 6.5 %collective-permute-start.3 = (f32[64,256]{1,0:T(8,128)S(1)}, f32[64,256]{1,0:T(8,128)S(1)}, u32[]{:S(2)}, u32[]{:S(2)}) collective-permute-start(f32[64,256]{1,0:T(8,128)S(1)} %reshape.100), channel_id=1, source_target_pairs={{0,32},{32,0},{1,33},{33,1},{2,34},{34,2},{3,35},{35,3},{4,36},{36... | collective-permute-start | bytes 196616 | tf_op jit(solution)/shard_map/ppermute | solution.py:18
  16.7 12.3 %collective-permute-done.3 = f32[64,256]{1,0:T(8,128)S(1)} collective-permute-done((f32[64,256]{1,0:T(8,128)S(1)}, f32[64,256]{1,0:T(8,128)S(1)}, u32[]{:S(2)}, u32[]{:S(2)}) %collective-permute-start.3) | collective-permute-done | bytes 65568 | tf_op jit(solution)/shard_map/ppermute | solution.py:18
  29.1 2.7 %collective-permute-done = bf16[512,256]{1,0:T(8,128)(2,1)S(1)} collective-permute-done((bf16[512,256]{1,0:T(8,128)(2,1)}, bf16[512,256]{1,0:T(8,128)(2,1)S(1)}, u32[]{:S(2)}, u32[]{:S(2)}) %collective-permute-start) | collective-permute-done | bytes 262176 | tf_op jit(solution)/shard_map/ppermute | solution.py:135
  31.7 1.1 pad_maximum_fusion
  32.8 0.5 fusion.5
  33.8 0.5 fusion.2
  34.4 3.3 %collective-permute-start.4 = (bf16[2,256,1024]{2,1,0:T(8,128)(2,1)S(1)}, bf16[2,256,1024]{2,1,0:T(8,128)(2,1)S(1)}, u32[]{:S(2)}, u32[]{:S(2)}) collective-permute-start(bf16[2,256,1024]{2,1,0:T(8,128)(2,1)S(1)} %pad_maximum_fusion.1), channel_id=1, source_target_pairs={{0,4},{4,0},{8,12},{12,8},{1,5},{5,1},{9,13},{13,9},{2,6},{6,2},{1... | collective-permute-start | bytes 3145736 | tf_op jit(solution)/shard_map/ppermute | solution.py:18
  37.6 0.5 fusion.4
  38.2 3.7 %collective-permute-start.5 = (bf16[2,256,1024]{2,1,0:T(8,128)(2,1)S(1)}, bf16[2,256,1024]{2,1,0:T(8,128)(2,1)S(1)}, u32[]{:S(2)}, u32[]{:S(2)}) collective-permute-start(bf16[2,256,1024]{2,1,0:T(8,128)(2,1)S(1)} %pad_maximum_fusion.2), channel_id=1, source_target_pairs={{0,12},{4,8},{8,4},{12,0},{1,13},{5,9},{9,5},{13,1},{2,14},{6,10},... | collective-permute-start | bytes 3145736 | tf_op jit(solution)/shard_map/ppermute | solution.py:18
  42.0 18.7 %collective-permute-done.4.got_a = bf16[2,256,1024]{2,1,0:T(8,128)(2,1)S(1)} collective-permute-done((bf16[2,256,1024]{2,1,0:T(8,128)(2,1)S(1)}, bf16[2,256,1024]{2,1,0:T(8,128)(2,1)S(1)}, u32[]{:S(2)}, u32[]{:S(2)}) %collective-permute-start.4) | collective-permute-done | bytes 1048608 | tf_op jit(solution)/shard_map/ppermute | solution.py:18
  60.6 1.3 fusion.7
  61.9 4.5 %collective-permute-start.6 = (bf16[256,1024]{1,0:T(8,128)(2,1)}, bf16[256,1024]{1,0:T(8,128)(2,1)}, u32[]{:S(2)}, u32[]{:S(2)}) collective-permute-start(bf16[256,1024]{1,0:T(8,128)(2,1)} %fusion.7), channel_id=1, source_target_pairs={{0,12},{4,8},{8,4},{12,0},{1,13},{5,9},{9,5},{13,1},{2,14},{6,10},... | collective-permute-start | bytes 1572872 | tf_op jit(solution)/shard_map/ppermute | solution.py:18
  66.5 1.3 fusion.6
  67.8 2.0 %collective-permute-start.7 = (bf16[256,1024]{1,0:T(8,128)(2,1)}, bf16[256,1024]{1,0:T(8,128)(2,1)}, u32[]{:S(2)}, u32[]{:S(2)}) collective-permute-start(bf16[256,1024]{1,0:T(8,128)(2,1)} %fusion.6), channel_id=1, source_target_pairs={{0,4},{4,0},{8,12},{12,8},{1,5},{5,1},{9,13},{13,9},{2,6},{6,2},{1... | collective-permute-start | bytes 1572872 | tf_op jit(solution)/shard_map/ppermute | solution.py:18
  70.3 2.4 %convolution_convert_fusion.own_ref = bf16[256,2048]{1,0:T(8,128)(2,1)S(1)} fusion(bf16[512,2048]{1,0:T(8,128)(2,1)} %param.6, bf16[4,512,256]{2,1,0:T(8,128)(2,1)} %copy-done.3, s32[]{:T(128)S(6)} %select_n.61), kind=kOutput, calls=%fused_computation | convolution fusion | flops 537395200 | bytes 3407876 | tf_op jit(solution)/shard_map/dot_general | solution.py:141
  72.7 4.8 %collective-permute-done.6.next_a = bf16[256,1024]{1,0:T(8,128)(2,1)} collective-permute-done((bf16[256,1024]{1,0:T(8,128)(2,1)}, bf16[256,1024]{1,0:T(8,128)(2,1)}, u32[]{:S(2)}, u32[]{:S(2)}) %collective-permute-start.6) | collective-permute-done | bytes 524320 | tf_op jit(solution)/shard_map/ppermute | solution.py:18
  77.5 4.4 %collective-permute-done.7.next_b = bf16[256,1024]{1,0:T(8,128)(2,1)} collective-permute-done((bf16[256,1024]{1,0:T(8,128)(2,1)}, bf16[256,1024]{1,0:T(8,128)(2,1)}, u32[]{:S(2)}, u32[]{:S(2)}) %collective-permute-start.7) | collective-permute-done | bytes 524320 | tf_op jit(solution)/shard_map/ppermute | solution.py:18
  81.9 3.7 %shard_map.76 = (bf16[256,2048]{1,0:T(8,128)(2,1)}, f32[8,64,512]{2,1,0:T(8,128)S(1)}, bf16[8,64,512]{2,1,0:T(8,128)(2,1)S(1)}) custom-call(s32[1]{0:T(128)} %bitcast.c_ref, f32[4,1,2048]{2,1,0:T(1,128)S(1)} %reshape.102.mask_ref, bf16[256,2048]{1,0:T(8,128)(2,1)S(1)} %bitcast.54, bf16[256,2048]{1,0:T(8,128)(2,1)S(1)} %convolution_convert_fusion.own_ref, ...), custom_call_target="tpu_custom_call" | custom-call | flops 4194304 | bytes 4194304 | tf_op jit(solution)/shard_map/pallas_call | solution.py:68
  85.6 4.4 %collective-permute-start.8 = (bf16[8,64,512]{2,1,0:T(8,128)(2,1)S(1)}, bf16[8,64,512]{2,1,0:T(8,128)(2,1)S(1)}, u32[]{:S(2)}, u32[]{:S(2)}) collective-permute-start(bf16[8,64,512]{2,1,0:T(8,128)(2,1)S(1)} %get-tuple-element.19), channel_id=1, source_target_pairs={{0,16},{16,0},{1,17},{17,1},{2,18},{18,2},{3,19},{19,3},{4,20},{20... | collective-permute-start | bytes 1572872 | tf_op jit(solution)/shard_map/ppermute | solution.py:18
  90.1 1.5 collective-permute-done.8
  91.7 26.5 %all_to_all.10 = bf16[8,64,512]{2,1,0:T(8,128)(2,1)S(1)} all-to-all(bf16[8,64,512]{2,1,0:T(8,128)(2,1)S(1)} %add_convert_fusion), channel_id=1, replica_groups=mesh['z'=8,'yh'=2,'c'=2,'dp'=4,'t'=4] {'z'}, dimensions={0} | all-to-all | bytes 1048576 | tf_op jit(solution)/shard_map/all_to_all | solution.py:179
  118.3 3.8 %collective-permute-start.9 = (f32[64,512]{1,0:T(8,128)S(1)}, f32[64,512]{1,0:T(8,128)S(1)}, u32[]{:S(2)}, u32[]{:S(2)}) collective-permute-start(f32[64,512]{1,0:T(8,128)S(1)} %convert_reduce_fusion.mine_ref), channel_id=1, source_target_pairs={{0,32},{32,0},{1,33},{33,1},{2,34},{34,2},{3,35},{35,3},{4,36},{36... | collective-permute-start | bytes 393224 | tf_op jit(solution)/shard_map/ppermute | solution.py:18
  122.2 5.7 %collective-permute-done.9.peer_ref = f32[64,512]{1,0:T(8,128)S(1)} collective-permute-done((f32[64,512]{1,0:T(8,128)S(1)}, f32[64,512]{1,0:T(8,128)S(1)}, u32[]{:S(2)}, u32[]{:S(2)}) %collective-permute-start.9) | collective-permute-done | bytes 131104 | tf_op jit(solution)/shard_map/ppermute | solution.py:18
  127.9 0.8 shard_map.77
  128.7 16.6 %all_to_all.11.mine_ref = bf16[8,64,512]{2,1,0:T(8,128)(2,1)S(1)} all-to-all(bf16[8,64,512]{2,1,0:T(8,128)(2,1)S(1)} %get-tuple-element.22), channel_id=1, replica_groups=mesh['z'=8,'yh'=2,'c'=2,'dp'=4,'t'=4] {'z'}, dimensions={0} | all-to-all | bytes 1048576 | tf_op jit(solution)/shard_map/all_to_all | solution.py:182
  145.3 6.1 %collective-permute-start.10 = (bf16[8,64,512]{2,1,0:T(8,128)(2,1)S(1)}, bf16[8,64,512]{2,1,0:T(8,128)(2,1)S(1)}, u32[]{:S(2)}, u32[]{:S(2)}) collective-permute-start(bf16[8,64,512]{2,1,0:T(8,128)(2,1)S(1)} %all_to_all.11.mine_ref), channel_id=1, source_target_pairs={{0,16},{16,0},{1,17},{17,1},{2,18},{18,2},{3,19},{19,3},{4,20},{20... | collective-permute-start | bytes 1572872 | tf_op jit(solution)/shard_map/ppermute | solution.py:18
  151.4 1.5 collective-permute-done.10.other_ref
  153.0 1.5 shard_map.78
  (26 shorter events, 1.5 us)
Async XLA Ops:
  0.6 32.2 %copy-start.1 = (bf16[512,2048]{1,0:T(8,128)(2,1)S(1)}, bf16[512,2048]{1,0:T(8,128)(2,1)}, u32[]{:S(2)}) copy-start(bf16[512,2048]{1,0:T(8,128)(2,1)} %param.6) | copy-start | bytes 6291460
  0.6 28.4 %collective-permute-start.1 = (bf16[512,256]{1,0:T(8,128)(2,1)}, bf16[512,256]{1,0:T(8,128)(2,1)S(1)}, u32[]{:S(2)}, u32[]{:S(2)}) collective-permute-start(bf16[512,256]{1,0:T(8,128)(2,1)} %param.5), channel_id=1, source_target_pairs={{0,2},{1,3},{2,0},{3,1},{4,6},{5,7},{6,4},{7,5},{8,10},{9,11},{10,... | collective-permute-start | bytes 786440 | tf_op jit(solution)/shard_map/ppermute | solution.py:135
  2.7 29.0 %collective-permute-start = (bf16[512,256]{1,0:T(8,128)(2,1)}, bf16[512,256]{1,0:T(8,128)(2,1)S(1)}, u32[]{:S(2)}, u32[]{:S(2)}) collective-permute-start(bf16[512,256]{1,0:T(8,128)(2,1)} %param.5), channel_id=1, source_target_pairs={{0,1},{1,2},{2,3},{3,0},{4,5},{5,6},{6,7},{7,4},{8,9},{9,10},{10,1... | collective-permute-start | bytes 786440 | tf_op jit(solution)/shard_map/ppermute | solution.py:135
  6.0 25.8 %collective-permute-start.2 = (bf16[512,256]{1,0:T(8,128)(2,1)}, bf16[512,256]{1,0:T(8,128)(2,1)S(1)}, u32[]{:S(2)}, u32[]{:S(2)}) collective-permute-start(bf16[512,256]{1,0:T(8,128)(2,1)} %param.5), channel_id=1, source_target_pairs={{0,3},{1,0},{2,1},{3,2},{4,7},{5,4},{6,5},{7,6},{8,11},{9,8},{10,9... | collective-permute-start | bytes 786440 | tf_op jit(solution)/shard_map/ppermute | solution.py:135
  10.2 18.9 %collective-permute-start.3 = (f32[64,256]{1,0:T(8,128)S(1)}, f32[64,256]{1,0:T(8,128)S(1)}, u32[]{:S(2)}, u32[]{:S(2)}) collective-permute-start(f32[64,256]{1,0:T(8,128)S(1)} %reshape.100), channel_id=1, source_target_pairs={{0,32},{32,0},{1,33},{33,1},{2,34},{34,2},{3,35},{35,3},{4,36},{36... | collective-permute-start | bytes 196616 | tf_op jit(solution)/shard_map/ppermute | solution.py:18
  32.8 33.6 %copy-start.3 = (bf16[4,512,256]{2,1,0:T(8,128)(2,1)}, bf16[4,512,256]{2,1,0:T(8,128)(2,1)S(1)}, u32[]{:S(2)}) copy-start(bf16[4,512,256]{2,1,0:T(8,128)(2,1)S(1)} %pad_maximum_fusion) | copy-start | bytes 3145732
  34.4 26.3 %copy-start.2 = (bf16[512,2048]{1,0:T(8,128)(2,1)S(1)}, bf16[512,2048]{1,0:T(8,128)(2,1)}, u32[]{:S(2)}) copy-start(bf16[512,2048]{1,0:T(8,128)(2,1)} %param.6) | copy-start | bytes 6291460
  34.4 26.3 %collective-permute-start.4 = (bf16[2,256,1024]{2,1,0:T(8,128)(2,1)S(1)}, bf16[2,256,1024]{2,1,0:T(8,128)(2,1)S(1)}, u32[]{:S(2)}, u32[]{:S(2)}) collective-permute-start(bf16[2,256,1024]{2,1,0:T(8,128)(2,1)S(1)} %pad_maximum_fusion.1), channel_id=1, source_target_pairs={{0,4},{4,0},{8,12},{12,8},{1,5},{5,1},{9,13},{13,9},{2,6},{6,2},{1... | collective-permute-start | bytes 3145736 | tf_op jit(solution)/shard_map/ppermute | solution.py:18
  38.2 28.2 %collective-permute-start.5 = (bf16[2,256,1024]{2,1,0:T(8,128)(2,1)S(1)}, bf16[2,256,1024]{2,1,0:T(8,128)(2,1)S(1)}, u32[]{:S(2)}, u32[]{:S(2)}) collective-permute-start(bf16[2,256,1024]{2,1,0:T(8,128)(2,1)S(1)} %pad_maximum_fusion.2), channel_id=1, source_target_pairs={{0,12},{4,8},{8,4},{12,0},{1,13},{5,9},{9,5},{13,1},{2,14},{6,10},... | collective-permute-start | bytes 3145736 | tf_op jit(solution)/shard_map/ppermute | solution.py:18
  61.9 8.0 %copy-start.4 = (s32[1,1,1,64]{3,2,1,0:T(1,128)S(1)}, s32[1,1,1,64]{3,2,1,0:T(1,128)}, u32[]{:S(2)}) copy-start(s32[1,1,1,64]{3,2,1,0:T(1,128)} %param.8) | copy-start | bytes 772
  61.9 15.6 %collective-permute-start.6 = (bf16[256,1024]{1,0:T(8,128)(2,1)}, bf16[256,1024]{1,0:T(8,128)(2,1)}, u32[]{:S(2)}, u32[]{:S(2)}) collective-permute-start(bf16[256,1024]{1,0:T(8,128)(2,1)} %fusion.7), channel_id=1, source_target_pairs={{0,12},{4,8},{8,4},{12,0},{1,13},{5,9},{9,5},{13,1},{2,14},{6,10},... | collective-permute-start | bytes 1572872 | tf_op jit(solution)/shard_map/ppermute | solution.py:18
  67.8 14.1 %copy-start = (bf16[1,256,2048]{2,1,0:T(8,128)(2,1)S(1)}, bf16[1,256,2048]{2,1,0:T(8,128)(2,1)}, u32[]{:S(2)}) copy-start(bf16[1,256,2048]{2,1,0:T(8,128)(2,1)} %param.7) | copy-start | bytes 3145732
  67.8 14.1 %collective-permute-start.7 = (bf16[256,1024]{1,0:T(8,128)(2,1)}, bf16[256,1024]{1,0:T(8,128)(2,1)}, u32[]{:S(2)}, u32[]{:S(2)}) collective-permute-start(bf16[256,1024]{1,0:T(8,128)(2,1)} %fusion.6), channel_id=1, source_target_pairs={{0,4},{4,0},{8,12},{12,8},{1,5},{5,1},{9,13},{13,9},{2,6},{6,2},{1... | collective-permute-start | bytes 1572872 | tf_op jit(solution)/shard_map/ppermute | solution.py:18
  85.6 5.9 %collective-permute-start.8 = (bf16[8,64,512]{2,1,0:T(8,128)(2,1)S(1)}, bf16[8,64,512]{2,1,0:T(8,128)(2,1)S(1)}, u32[]{:S(2)}, u32[]{:S(2)}) collective-permute-start(bf16[8,64,512]{2,1,0:T(8,128)(2,1)S(1)} %get-tuple-element.19), channel_id=1, source_target_pairs={{0,16},{16,0},{1,17},{17,1},{2,18},{18,2},{3,19},{19,3},{4,20},{20... | collective-permute-start | bytes 1572872 | tf_op jit(solution)/shard_map/ppermute | solution.py:18
  118.3 9.6 %collective-permute-start.9 = (f32[64,512]{1,0:T(8,128)S(1)}, f32[64,512]{1,0:T(8,128)S(1)}, u32[]{:S(2)}, u32[]{:S(2)}) collective-permute-start(f32[64,512]{1,0:T(8,128)S(1)} %convert_reduce_fusion.mine_ref), channel_id=1, source_target_pairs={{0,32},{32,0},{1,33},{33,1},{2,34},{34,2},{3,35},{35,3},{4,36},{36... | collective-permute-start | bytes 393224 | tf_op jit(solution)/shard_map/ppermute | solution.py:18
  145.3 7.7 %collective-permute-start.10 = (bf16[8,64,512]{2,1,0:T(8,128)(2,1)S(1)}, bf16[8,64,512]{2,1,0:T(8,128)(2,1)S(1)}, u32[]{:S(2)}, u32[]{:S(2)}) collective-permute-start(bf16[8,64,512]{2,1,0:T(8,128)(2,1)S(1)} %all_to_all.11.mine_ref), channel_id=1, source_target_pairs={{0,16},{16,0},{1,17},{17,1},{2,18},{18,2},{3,19},{19,3},{4,20},{20... | collective-permute-start | bytes 1572872 | tf_op jit(solution)/shard_map/ppermute | solution.py:18

commit v3 on v2

--- a/solution.py
+++ b/solution.py
@@ -7,6 +7,7 @@
 
 BLK = 64
 DECAY = 0.9
+CHUNKS = 2
 NODES = 32
 F32, BF16 = jnp.float32, jnp.bfloat16
 NODE = ("z", "yh", "c")
@@ -34,7 +35,7 @@
 
 
 def feedback_kernel(
-    c_ref, mask_ref, fb_ref, own_ref, got_a, got_b, next_a, next_b, new_ref, mine_ref, other_ref
+    c_ref, mask_ref, fb_ref, own_ref, got_a, got_b, next_a, next_b, _, new_ref, mine_ref, other_ref
 ):
     first = c_ref[0] == 0
     for h, got, nxt in ((0, got_a, next_a), (1, got_b, next_b)):
@@ -57,30 +58,34 @@
             other_ref[h, :, place] = jnp.where(first, sent[1], sent[0]).astype(BF16)
 
 
-def error_feedback(c, mask, feedback, own, got_a, got_b, next_a, next_b):
-    rows, cols = feedback.shape
-    groups = rows // BLK
+def error_feedback(chunk, c, mask, feedback, own, got_a, got_b, next_a, next_b, new):
+    cols = feedback.shape[1]
+    groups = own.shape[0] // BLK
+    base = chunk * groups
+    line = pl.BlockSpec((1, 1, cols), lambda i: (base + i, 0, 0))
+    state = pl.BlockSpec((BLK, cols), lambda i: (base + i, 0))
     wide = pl.BlockSpec((BLK, cols), lambda i: (i, 0))
     half = pl.BlockSpec((BLK, cols // 2), lambda i: (i, 0))
     slab = pl.BlockSpec((2, BLK, 512), lambda i: (i, 0, 0))
-    line = pl.BlockSpec((1, 1, cols), lambda i: (i, 0, 0))
     got = pl.BlockSpec((1, BLK, cols // 2), lambda i: (0, i, 0))
-    return kernel_call(
+    return pl.pallas_call(
         feedback_kernel,
-        (groups,),
-        [SMEM, line, wide, wide, got, got, half, half],
-        [wide, slab, slab],
-        [
-            jax.ShapeDtypeStruct((rows, cols), BF16),
+        grid=(groups,),
+        in_specs=[SMEM, line, state, wide, got, got, half, half, pl.BlockSpec(memory_space=pl.ANY)],
+        out_specs=[state, slab, slab],
+        out_shape=[
+            jax.ShapeDtypeStruct(feedback.shape, BF16),
             jax.ShapeDtypeStruct((2 * groups, BLK, 512), F32),
             jax.ShapeDtypeStruct((2 * groups, BLK, 512), BF16),
         ],
-        8 * rows * cols,
-    )(c, mask, feedback, own, got_a, got_b, next_a, next_b)
+        input_output_aliases={8: 0},
+        compiler_params=pltpu.CompilerParams(vmem_limit_bytes=VMEM_LIMIT),
+        cost_estimate=pl.CostEstimate(flops=1 << 22, bytes_accessed=1 << 22, transcendentals=0),
+    )(c, mask, feedback, own, got_a, got_b, next_a, next_b, new)
 
 
 def owner_kernel(yh_ref, mine_ref, peer_ref, moment_ref, new_ref, step_ref):
-    mean = (mine_ref[...] + peer_ref[...]) * (1.0 / NODES)
+    mean = (mine_ref[...].astype(F32) + peer_ref[...].astype(F32)) * (1.0 / NODES)
     moment = DECAY * moment_ref[...] + mean
     step = (mean + DECAY * moment).astype(BF16)
     for z in range(8):
@@ -128,30 +133,29 @@
     )(c, mine, other)
 
 
-def partial_sums(hidden, cotangent, early):
+def ring_shift(value, shift):
+    return lax.ppermute(value, "t", [(i, (i + shift) % 4) for i in range(4)])
+
+
+def products(shards, cotangent):
     d, t = lax.axis_index("dp"), lax.axis_index("t")
-    whole = [hidden]
-    for shift in (1, 2, 3):
-        whole.append(lax.ppermute(hidden, "t", [(i, (i + shift) % 4) for i in range(4)]))
-    *whole, early = lax.optimization_barrier((*whole, early))
-    whole = jnp.stack(whole)
+    shards = jnp.stack(shards)
+    half = cotangent.shape[1] // 2
 
     def part(flip, cols):
-        rows = lax.dynamic_index_in_dim(whole, (t - (d ^ flip)) % 4, 0, keepdims=False)
+        rows = lax.dynamic_index_in_dim(shards, (t - (d ^ flip)) % 4, 0, keepdims=False)
         return lax.dot_general(
             rows, cols, (((0,), (0,)), ((), ())), preferred_element_type=F32
         ).astype(BF16)
 
-    half = cotangent.shape[1] // 2
     a, b = cotangent[:, :half], cotangent[:, half:]
-    a1, a2, a3 = part(1, a), part(2, a), part(3, a)
-    b1, b2, b3 = part(1, b), part(2, b), part(3, b)
-    own = part(0, cotangent)
-    got_a = swap(jnp.stack([a1, a2]), "dp", 1, 4)
-    got_b = swap(jnp.stack([b3, b2]), "dp", 3, 4)
-    next_a = swap((a3.astype(F32) + got_a[1].astype(F32)).astype(BF16), "dp", 3, 4)
-    next_b = swap((b1.astype(F32) + got_b[1].astype(F32)).astype(BF16), "dp", 1, 4)
-    return early, own, got_a, got_b, next_a, next_b
+    send_a = jnp.stack([part(1, a), part(2, a)])
+    send_b = jnp.stack([part(3, b), part(2, b)])
+    return send_a, send_b, part(3, a), part(1, b), part(0, cotangent)
+
+
+def plus(kept, got):
+    return (kept.astype(F32) + got[1].astype(F32)).astype(BF16)
 
 
 def as_matrix(blocks):
@@ -168,16 +172,36 @@
         + jnp.arange(cols, dtype=jnp.int32)[None, :] // BLK
     )
     mask = jnp.any(chosen.reshape(-1, 1, 1) == block_of[None], axis=0).astype(F32)
+    width = hidden.shape[1] // CHUNKS
+    shards = []
+    for r in range(CHUNKS):
+        piece = hidden[:, r * width : (r + 1) * width]
+        shards.append([piece] + [ring_shift(piece, k) for k in (1, 2, 3)])
     moment = as_matrix(momentum[0, 0])
     far_moment = swap(moment, "yh", 1, 2)
-    far_moment, *parts = partial_sums(hidden, cotangent, far_moment)
+    work = [products(shards[0], cotangent)]
+    *held, far_moment = lax.optimization_barrier((*shards[1], far_moment, work[0][0], work[0][1]))[:5]
+    work.append(products(held, cotangent))
     moment = jnp.where(
         yh == 0, jnp.concatenate([moment, far_moment], 1), jnp.concatenate([far_moment, moment], 1)
     )
-    feedback_new, mine, other = error_feedback(at_c, mask[:, None], feedback[0], *parts)
-    pair = (mine + swap(other, "c", 1, 2).astype(F32)).astype(BF16)
-    got = lax.all_to_all(pair, "z", 0, 0, tiled=True)
-    near = jnp.sum(got.astype(F32), axis=0)
+    got = [(swap(w[0], "dp", 1, 4), swap(w[1], "dp", 3, 4)) for w in work]
+    feedback_new = jnp.zeros((rows, cols), BF16)
+    own = [w[4] for w in work]
+    got_a, mask, feedback_new, *own = lax.optimization_barrier((got[0][0], mask, feedback_new, *own))
+    got[0] = (got_a, got[0][1])
+    after = [
+        (swap(plus(w[2], g[0]), "dp", 3, 4), swap(plus(w[3], g[1]), "dp", 1, 4))
+        for w, g in zip(work, got)
+    ]
+    pairs = []
+    for r in range(CHUNKS):
+        feedback_new, mine, other = error_feedback(
+            r, at_c, mask[:, None], feedback[0], own[r], *got[r], *after[r], feedback_new
+        )
+        pairs.append((mine + swap(other, "c", 1, 2).astype(F32)).astype(BF16))
+    across = lax.all_to_all(jnp.concatenate(pairs), "z", 0, 0, tiled=True)
+    near = jnp.sum(across.astype(F32), axis=0).astype(BF16)
     momentum_new, copies = owner_update(at_yh, near, swap(near, "yh", 1, 2), moment)
     every = lax.all_to_all(copies, "z", 0, 0, tiled=True)
     step = assemble(at_c, every, swap(every, "c", 1, 2), rows, cols)

time: 155 us -> 154 us (level)
  the two profiles are of different devices: /device:TPU:17 before, /device:TPU:1 now
where the time goes in v3:
time: 154 us; the launch traced here: 152 us
  starting transfers between devices  84.2 us (55%)
  waiting for transfers between devices  26.3 us (17%)
  blocking collectives  16.9 us (11%)
  matrix products  7.85 us (5%)
  Pallas kernels  6.49 us (4%)
  local copies, waits for them, and re-layouts  5.02 us (3%)
  other arithmetic  4.4 us (3%)
    ppermute x13, starting transfers between devices, swap(): return lax.ppermute(value, axis, [(i, i ^ flip) for i in range(size)])  54.4 us
    ppermute x6, starting transfers between devices, ring_shift(): return lax.ppermute(value, 't', [(i, (i + shift) % 4) for i in range(4)])  20.2 us
    all_to_all x1, waiting for transfers between devices, local(): across = lax.all_to_all(jnp.concatenate(pairs), 'z', 0, 0, tiled=True)  18 us
    all_to_all x1, blocking collectives, local(): every = lax.all_to_all(copies, 'z', 0, 0, tiled=True)  16.9 us
    all_to_all x1, starting transfers between devices, local(): across = lax.all_to_all(jnp.concatenate(pairs), 'z', 0, 0, tiled=True)  9.5 us
    ppermute x13, waiting for transfers between devices, swap(): return lax.ppermute(value, axis, [(i, i ^ flip) for i in range(size)])  8.35 us
    dot_general x14, matrix products, part(): lax.dot_general(rows, cols, (((0,), (0,)), ((), ())), preferred_element_t...  7.85 us
    pallas_call x2, Pallas kernels, error_feedback(): pl.pallas_call(feedback_kernel, grid=(groups,), in_specs=[SMEM, line, sta...  4.17 us
  transfers between devices with their start and end apart: 20, of which 5 were waited for; matrix products, arithmetic and copies ran while one was open for 9% of the time, Pallas kernels for 3%

profile of v3, /device:TPU:1, one launch (start us, length us, event | category | flops | bytes accessed | tf_op | source)
XLA Modules:
  0.0 152.3 jit_solution(2276790058998730552)
XLA Ops:
  0.6 1.2 fusion.84
  1.8 4.0 %collective-permute-start = (bf16[512,128]{1,0:T(8,128)(2,1)S(1)}, bf16[512,128]{1,0:T(8,128)(2,1)S(1)}, u32[]{:S(2)}, u32[]{:S(2)}) collective-permute-start(bf16[512,128]{1,0:T(8,128)(2,1)S(1)} %get-tuple-element.41), channel_id=1, source_target_pairs={{0,1},{1,2},{2,3},{3,0},{4,5},{5,6},{6,7},{7,4},{8,9},{9,10},{10,1... | collective-permute-start | bytes 393224 | tf_op jit(solution)/shard_map/ppermute | solution.py:137
  5.8 4.2 %collective-permute-start.1 = (bf16[512,128]{1,0:T(8,128)(2,1)S(1)}, bf16[512,128]{1,0:T(8,128)(2,1)S(1)}, u32[]{:S(2)}, u32[]{:S(2)}) collective-permute-start(bf16[512,128]{1,0:T(8,128)(2,1)S(1)} %get-tuple-element.41), channel_id=1, source_target_pairs={{0,2},{1,3},{2,0},{3,1},{4,6},{5,7},{6,4},{7,5},{8,10},{9,11},{10,... | collective-permute-start | bytes 393224 | tf_op jit(solution)/shard_map/ppermute | solution.py:137
  10.1 3.0 %collective-permute-start.2 = (bf16[512,128]{1,0:T(8,128)(2,1)S(1)}, bf16[512,128]{1,0:T(8,128)(2,1)S(1)}, u32[]{:S(2)}, u32[]{:S(2)}) collective-permute-start(bf16[512,128]{1,0:T(8,128)(2,1)S(1)} %get-tuple-element.41), channel_id=1, source_target_pairs={{0,3},{1,0},{2,1},{3,2},{4,7},{5,4},{6,5},{7,6},{8,11},{9,8},{10,9... | collective-permute-start | bytes 393224 | tf_op jit(solution)/shard_map/ppermute | solution.py:137
  13.1 2.3 %collective-permute-start.4 = (bf16[512,128]{1,0:T(8,128)(2,1)S(1)}, bf16[512,128]{1,0:T(8,128)(2,1)}, u32[]{:S(2)}, u32[]{:S(2)}) collective-permute-start(bf16[512,128]{1,0:T(8,128)(2,1)S(1)} %get-tuple-element.21), channel_id=1, source_target_pairs={{0,1},{1,2},{2,3},{3,0},{4,5},{5,6},{6,7},{7,4},{8,9},{9,10},{10,1... | collective-permute-start | bytes 393224 | tf_op jit(solution)/shard_map/ppermute | solution.py:137
  15.4 2.0 %collective-permute-start.5 = (bf16[512,128]{1,0:T(8,128)(2,1)S(1)}, bf16[512,128]{1,0:T(8,128)(2,1)}, u32[]{:S(2)}, u32[]{:S(2)}) collective-permute-start(bf16[512,128]{1,0:T(8,128)(2,1)S(1)} %get-tuple-element.21), channel_id=1, source_target_pairs={{0,2},{1,3},{2,0},{3,1},{4,6},{5,7},{6,4},{7,5},{8,10},{9,11},{10,... | collective-permute-start | bytes 393224 | tf_op jit(solution)/shard_map/ppermute | solution.py:137
  19.7 4.7 %collective-permute-start.6 = (bf16[512,128]{1,0:T(8,128)(2,1)S(1)}, bf16[512,128]{1,0:T(8,128)(2,1)S(1)}, u32[]{:S(2)}, u32[]{:S(2)}) collective-permute-start(bf16[512,128]{1,0:T(8,128)(2,1)S(1)} %get-tuple-element.21), channel_id=1, source_target_pairs={{0,3},{1,0},{2,1},{3,2},{4,7},{5,4},{6,5},{7,6},{8,11},{9,8},{10,9... | collective-permute-start | bytes 393224 | tf_op jit(solution)/shard_map/ppermute | solution.py:137
  24.5 6.6 %collective-permute-start.7 = (f32[64,256]{1,0:T(8,128)S(1)}, f32[64,256]{1,0:T(8,128)}, u32[]{:S(2)}, u32[]{:S(2)}) collective-permute-start(f32[64,256]{1,0:T(8,128)S(1)} %reshape.95), channel_id=1, source_target_pairs={{0,32},{32,0},{1,33},{33,1},{2,34},{34,2},{3,35},{35,3},{4,36},{36... | collective-permute-start | bytes 196616 | tf_op jit(solution)/shard_map/ppermute | solution.py:19
  32.6 3.1 %collective-permute-start.3 = (bf16[2,128,1024]{2,1,0:T(8,128)(2,1)S(1)}, bf16[2,128,1024]{2,1,0:T(8,128)(2,1)S(1)}, u32[]{:S(2)}, u32[]{:S(2)}) collective-permute-start(bf16[2,128,1024]{2,1,0:T(8,128)(2,1)S(1)} %pad_maximum_fusion.1), channel_id=1, source_target_pairs={{0,4},{4,0},{8,12},{12,8},{1,5},{5,1},{9,13},{13,9},{2,6},{6,2},{1... | collective-permute-start | bytes 1572872 | tf_op jit(solution)/shard_map/ppermute | solution.py:19
  35.8 3.7 %collective-permute-start.12 = (bf16[2,128,1024]{2,1,0:T(8,128)(2,1)S(1)}, bf16[2,128,1024]{2,1,0:T(8,128)(2,1)S(1)}, u32[]{:S(2)}, u32[]{:S(2)}) collective-permute-start(bf16[2,128,1024]{2,1,0:T(8,128)(2,1)S(1)} %pad_maximum_fusion.2), channel_id=1, source_target_pairs={{0,12},{4,8},{8,4},{12,0},{1,13},{5,9},{9,5},{13,1},{2,14},{6,10},... | collective-permute-start | bytes 1572872 | tf_op jit(solution)/shard_map/ppermute | solution.py:19
  42.0 2.9 %collective-permute-start.9 = (bf16[2,128,1024]{2,1,0:T(8,128)(2,1)S(1)}, bf16[2,128,1024]{2,1,0:T(8,128)(2,1)S(1)}, u32[]{:S(2)}, u32[]{:S(2)}) collective-permute-start(bf16[2,128,1024]{2,1,0:T(8,128)(2,1)S(1)} %pad_maximum_fusion.5), channel_id=1, source_target_pairs={{0,12},{4,8},{8,4},{12,0},{1,13},{5,9},{9,5},{13,1},{2,14},{6,10},... | collective-permute-start | bytes 1572872 | tf_op jit(solution)/shard_map/ppermute | solution.py:19
  45.0 1.9 %collective-permute-start.8 = (bf16[2,128,1024]{2,1,0:T(8,128)(2,1)S(1)}, bf16[2,128,1024]{2,1,0:T(8,128)(2,1)S(1)}, u32[]{:S(2)}, u32[]{:S(2)}) collective-permute-start(bf16[2,128,1024]{2,1,0:T(8,128)(2,1)S(1)} %pad_maximum_fusion.4), channel_id=1, source_target_pairs={{0,4},{4,0},{8,12},{12,8},{1,5},{5,1},{9,13},{13,9},{2,6},{6,2},{1... | collective-permute-start | bytes 1572872 | tf_op jit(solution)/shard_map/ppermute | solution.py:19
  49.0 3.7 %collective-permute-start.13 = (bf16[128,1024]{1,0:T(8,128)(2,1)}, bf16[128,1024]{1,0:T(8,128)(2,1)}, u32[]{:S(2)}, u32[]{:S(2)}) collective-permute-start(bf16[128,1024]{1,0:T(8,128)(2,1)} %fusion.4), channel_id=1, source_target_pairs={{0,12},{4,8},{8,4},{12,0},{1,13},{5,9},{9,5},{13,1},{2,14},{6,10},... | collective-permute-start | bytes 786440 | tf_op jit(solution)/shard_map/ppermute | solution.py:19
  53.8 2.9 %collective-permute-start.14 = (bf16[128,1024]{1,0:T(8,128)(2,1)}, bf16[128,1024]{1,0:T(8,128)(2,1)}, u32[]{:S(2)}, u32[]{:S(2)}) collective-permute-start(bf16[128,1024]{1,0:T(8,128)(2,1)} %fusion.14), channel_id=1, source_target_pairs={{0,4},{4,0},{8,12},{12,8},{1,5},{5,1},{9,13},{13,9},{2,6},{6,2},{1... | collective-permute-start | bytes 786440 | tf_op jit(solution)/shard_map/ppermute | solution.py:19
  56.7 2.6 %collective-permute-done.9.got_b = bf16[2,128,1024]{2,1,0:T(8,128)(2,1)S(1)} collective-permute-done((bf16[2,128,1024]{2,1,0:T(8,128)(2,1)S(1)}, bf16[2,128,1024]{2,1,0:T(8,128)(2,1)S(1)}, u32[]{:S(2)}, u32[]{:S(2)}) %collective-permute-start.9) | collective-permute-done | bytes 524320 | tf_op jit(solution)/shard_map/ppermute | solution.py:19
  61.1 3.1 %collective-permute-start.11 = (bf16[128,1024]{1,0:T(8,128)(2,1)}, bf16[128,1024]{1,0:T(8,128)(2,1)S(1)}, u32[]{:S(2)}, u32[]{:S(2)}) collective-permute-start(bf16[128,1024]{1,0:T(8,128)(2,1)} %fusion.15), channel_id=1, source_target_pairs={{0,4},{4,0},{8,12},{12,8},{1,5},{5,1},{9,13},{13,9},{2,6},{6,2},{1... | collective-permute-start | bytes 786440 | tf_op jit(solution)/shard_map/ppermute | solution.py:19
  64.1 1.1 fusion.16
  66.0 3.7 %collective-permute-start.10 = (bf16[128,1024]{1,0:T(8,128)(2,1)}, bf16[128,1024]{1,0:T(8,128)(2,1)}, u32[]{:S(2)}, u32[]{:S(2)}) collective-permute-start(bf16[128,1024]{1,0:T(8,128)(2,1)} %fusion.16), channel_id=1, source_target_pairs={{0,12},{4,8},{8,4},{12,0},{1,13},{5,9},{9,5},{13,1},{2,14},{6,10},... | collective-permute-start | bytes 786440 | tf_op jit(solution)/shard_map/ppermute | solution.py:19
  69.7 1.1 broadcast_in_dim.16._
  70.8 2.2 %shard_map.76 = (bf16[256,2048]{1,0:T(8,128)(2,1)}, f32[4,64,512]{2,1,0:T(8,128)S(1)}, bf16[4,64,512]{2,1,0:T(8,128)(2,1)S(1)}) custom-call(s32[1]{0:T(128)} %bitcast.c_ref, f32[4,1,2048]{2,1,0:T(1,128)S(1)} %broadcast_in_dim.17.mask_ref, bf16[256,2048]{1,0:T(8,128)(2,1)S(1)} %bitcast.94, ...), custom_call_target="tpu_custom_call", output_to_operand_aliasing={{0}: (8, {})} | custom-call | flops 4194304 | bytes 4194304 | tf_op jit(solution)/shard_map/pallas_call | solution.py:71
  73.0 9.1 %collective-permute-start.15 = (bf16[4,64,512]{2,1,0:T(8,128)(2,1)S(1)}, bf16[4,64,512]{2,1,0:T(8,128)(2,1)S(1)}, u32[]{:S(2)}, u32[]{:S(2)}) collective-permute-start(bf16[4,64,512]{2,1,0:T(8,128)(2,1)S(1)} %get-tuple-element.33), channel_id=1, source_target_pairs={{0,16},{16,0},{1,17},{17,1},{2,18},{18,2},{3,19},{19,3},{4,20},{20... | collective-permute-start | bytes 786440 | tf_op jit(solution)/shard_map/ppermute | solution.py:19
  82.2 2.0 %shard_map.77 = (bf16[256,2048]{1,0:T(8,128)(2,1)}, f32[4,64,512]{2,1,0:T(8,128)S(1)}, bf16[4,64,512]{2,1,0:T(8,128)(2,1)S(1)}) custom-call(s32[1]{0:T(128)} %bitcast.c_ref, f32[4,1,2048]{2,1,0:T(1,128)S(1)} %broadcast_in_dim.17.mask_ref, bf16[256,2048]{1,0:T(8,128)(2,1)S(1)} %bitcast.95, ...), custom_call_target="tpu_custom_call", output_to_operand_aliasing={{0}: (8, {})} | custom-call | flops 4194304 | bytes 4194304 | tf_op jit(solution)/shard_map/pallas_call | solution.py:71
  84.2 2.9 %collective-permute-start.16 = (bf16[4,64,512]{2,1,0:T(8,128)(2,1)S(1)}, bf16[4,64,512]{2,1,0:T(8,128)(2,1)S(1)}, u32[]{:S(2)}, u32[]{:S(2)}) collective-permute-start(bf16[4,64,512]{2,1,0:T(8,128)(2,1)S(1)} %get-tuple-element.35), channel_id=1, source_target_pairs={{0,16},{16,0},{1,17},{17,1},{2,18},{18,2},{3,19},{19,3},{4,20},{20... | collective-permute-start | bytes 786440 | tf_op jit(solution)/shard_map/ppermute | solution.py:19
  87.2 1.0 collective-permute-done.16
  89.2 9.5 %all-to-all-start = ((bf16[8,64,512]{2,1,0:T(8,128)(2,1)}), bf16[8,64,512]{2,1,0:T(8,128)(2,1)S(1)}, u32[]{:S(2)}, u32[]{:S(2)}) async-start(bf16[8,64,512]{2,1,0:T(8,128)(2,1)} %pad_maximum_fusion.6), calls=%async_computation | async-start | bytes 1048576 | tf_op jit(solution)/shard_map/all_to_all | solution.py:203
  98.7 18.0 %all-to-all-done = bf16[8,64,512]{2,1,0:T(8,128)(2,1)S(1)} async-done(((bf16[8,64,512]{2,1,0:T(8,128)(2,1)}), bf16[8,64,512]{2,1,0:T(8,128)(2,1)S(1)}, u32[]{:S(2)}, u32[]{:S(2)}) %all-to-all-start) | async-done | bytes 524320 | tf_op jit(solution)/shard_map/all_to_all | solution.py:203
  116.7 4.9 %collective-permute-start.17 = (bf16[64,512]{1,0:T(8,128)(2,1)S(1)}, bf16[64,512]{1,0:T(8,128)(2,1)S(1)}, u32[]{:S(2)}, u32[]{:S(2)}) collective-permute-start(bf16[64,512]{1,0:T(8,128)(2,1)S(1)} %reduce_sum.12.mine_ref), channel_id=1, source_target_pairs={{0,32},{32,0},{1,33},{33,1},{2,34},{34,2},{3,35},{35,3},{4,36},{36... | collective-permute-start | bytes 196616 | tf_op jit(solution)/shard_map/ppermute | solution.py:19
  122.6 3.2 %collective-permute-done.17.peer_ref = bf16[64,512]{1,0:T(8,128)(2,1)S(1)} collective-permute-done((bf16[64,512]{1,0:T(8,128)(2,1)S(1)}, bf16[64,512]{1,0:T(8,128)(2,1)S(1)}, u32[]{:S(2)}, u32[]{:S(2)}) %collective-permute-start.17) | collective-permute-done | bytes 65568 | tf_op jit(solution)/shard_map/ppermute | solution.py:19
  126.5 16.9 %all_to_all.10.mine_ref = bf16[8,64,512]{2,1,0:T(8,128)(2,1)S(1)} all-to-all(bf16[8,64,512]{2,1,0:T(8,128)(2,1)S(1)} %get-tuple-element.38), channel_id=1, replica_groups=mesh['z'=8,'yh'=2,'c'=2,'dp'=4,'t'=4] {'z'}, dimensions={0} | all-to-all | bytes 1048576 | tf_op jit(solution)/shard_map/all_to_all | solution.py:206
  143.4 5.9 %collective-permute-start.18 = (bf16[8,64,512]{2,1,0:T(8,128)(2,1)S(1)}, bf16[8,64,512]{2,1,0:T(8,128)(2,1)S(1)}, u32[]{:S(2)}, u32[]{:S(2)}) collective-permute-start(bf16[8,64,512]{2,1,0:T(8,128)(2,1)S(1)} %all_to_all.10.mine_ref), channel_id=1, source_target_pairs={{0,16},{16,0},{1,17},{17,1},{2,18},{18,2},{3,19},{19,3},{4,20},{20... | collective-permute-start | bytes 1572872 | tf_op jit(solution)/shard_map/ppermute | solution.py:19
  149.3 1.5 collective-permute-done.18.other_ref
  150.8 1.5 %shard_map.79 = bf16[256,2048]{1,0:T(8,128)(2,1)} custom-call(s32[1]{0:T(128)} %bitcast.c_ref, bf16[8,64,512]{2,1,0:T(8,128)(2,1)S(1)} %all_to_all.10.mine_ref, bf16[8,64,512]{2,1,0:T(8,128)(2,1)S(1)} %collective-permute-done.18.other_ref), custom_call_target="tpu_custom_call" | custom-call | flops 2097152 | bytes 2097152 | tf_op jit(solution)/shard_map/pallas_call | solution.py:126
  (62 shorter events, 14.8 us)
Async XLA Ops:
  0.6 30.5 %copy-start.5 = (bf16[512,2048]{1,0:T(8,128)(2,1)S(1)}, bf16[512,2048]{1,0:T(8,128)(2,1)}, u32[]{:S(2)}) copy-start(bf16[512,2048]{1,0:T(8,128)(2,1)} %param.6) | copy-start | bytes 6291460
  1.8 17.9 %collective-permute-start = (bf16[512,128]{1,0:T(8,128)(2,1)S(1)}, bf16[512,128]{1,0:T(8,128)(2,1)S(1)}, u32[]{:S(2)}, u32[]{:S(2)}) collective-permute-start(bf16[512,128]{1,0:T(8,128)(2,1)S(1)} %get-tuple-element.41), channel_id=1, source_target_pairs={{0,1},{1,2},{2,3},{3,0},{4,5},{5,6},{6,7},{7,4},{8,9},{9,10},{10,1... | collective-permute-start | bytes 393224 | tf_op jit(solution)/shard_map/ppermute | solution.py:137
  5.8 18.6 %collective-permute-start.1 = (bf16[512,128]{1,0:T(8,128)(2,1)S(1)}, bf16[512,128]{1,0:T(8,128)(2,1)S(1)}, u32[]{:S(2)}, u32[]{:S(2)}) collective-permute-start(bf16[512,128]{1,0:T(8,128)(2,1)S(1)} %get-tuple-element.41), channel_id=1, source_target_pairs={{0,2},{1,3},{2,0},{3,1},{4,6},{5,7},{6,4},{7,5},{8,10},{9,11},{10,... | collective-permute-start | bytes 393224 | tf_op jit(solution)/shard_map/ppermute | solution.py:137
  10.1 21.0 %collective-permute-start.2 = (bf16[512,128]{1,0:T(8,128)(2,1)S(1)}, bf16[512,128]{1,0:T(8,128)(2,1)S(1)}, u32[]{:S(2)}, u32[]{:S(2)}) collective-permute-start(bf16[512,128]{1,0:T(8,128)(2,1)S(1)} %get-tuple-element.41), channel_id=1, source_target_pairs={{0,3},{1,0},{2,1},{3,2},{4,7},{5,4},{6,5},{7,6},{8,11},{9,8},{10,9... | collective-permute-start | bytes 393224 | tf_op jit(solution)/shard_map/ppermute | solution.py:137
  13.1 26.5 %collective-permute-start.4 = (bf16[512,128]{1,0:T(8,128)(2,1)S(1)}, bf16[512,128]{1,0:T(8,128)(2,1)}, u32[]{:S(2)}, u32[]{:S(2)}) collective-permute-start(bf16[512,128]{1,0:T(8,128)(2,1)S(1)} %get-tuple-element.21), channel_id=1, source_target_pairs={{0,1},{1,2},{2,3},{3,0},{4,5},{5,6},{6,7},{7,4},{8,9},{9,10},{10,1... | collective-permute-start | bytes 393224 | tf_op jit(solution)/shard_map/ppermute | solution.py:137
  15.4 24.2 %collective-permute-start.5 = (bf16[512,128]{1,0:T(8,128)(2,1)S(1)}, bf16[512,128]{1,0:T(8,128)(2,1)}, u32[]{:S(2)}, u32[]{:S(2)}) collective-permute-start(bf16[512,128]{1,0:T(8,128)(2,1)S(1)} %get-tuple-element.21), channel_id=1, source_target_pairs={{0,2},{1,3},{2,0},{3,1},{4,6},{5,7},{6,4},{7,5},{8,10},{9,11},{10,... | collective-permute-start | bytes 393224 | tf_op jit(solution)/shard_map/ppermute | solution.py:137
  19.7 19.8 %collective-permute-start.6 = (bf16[512,128]{1,0:T(8,128)(2,1)S(1)}, bf16[512,128]{1,0:T(8,128)(2,1)S(1)}, u32[]{:S(2)}, u32[]{:S(2)}) collective-permute-start(bf16[512,128]{1,0:T(8,128)(2,1)S(1)} %get-tuple-element.21), channel_id=1, source_target_pairs={{0,3},{1,0},{2,1},{3,2},{4,7},{5,4},{6,5},{7,6},{8,11},{9,8},{10,9... | collective-permute-start | bytes 393224 | tf_op jit(solution)/shard_map/ppermute | solution.py:137
  24.5 11.3 %collective-permute-start.7 = (f32[64,256]{1,0:T(8,128)S(1)}, f32[64,256]{1,0:T(8,128)}, u32[]{:S(2)}, u32[]{:S(2)}) collective-permute-start(f32[64,256]{1,0:T(8,128)S(1)} %reshape.95), channel_id=1, source_target_pairs={{0,32},{32,0},{1,33},{33,1},{2,34},{34,2},{3,35},{35,3},{4,36},{36... | collective-permute-start | bytes 196616 | tf_op jit(solution)/shard_map/ppermute | solution.py:19
  32.6 15.3 %collective-permute-start.3 = (bf16[2,128,1024]{2,1,0:T(8,128)(2,1)S(1)}, bf16[2,128,1024]{2,1,0:T(8,128)(2,1)S(1)}, u32[]{:S(2)}, u32[]{:S(2)}) collective-permute-start(bf16[2,128,1024]{2,1,0:T(8,128)(2,1)S(1)} %pad_maximum_fusion.1), channel_id=1, source_target_pairs={{0,4},{4,0},{8,12},{12,8},{1,5},{5,1},{9,13},{13,9},{2,6},{6,2},{1... | collective-permute-start | bytes 1572872 | tf_op jit(solution)/shard_map/ppermute | solution.py:19
  35.8 16.9 %collective-permute-start.12 = (bf16[2,128,1024]{2,1,0:T(8,128)(2,1)S(1)}, bf16[2,128,1024]{2,1,0:T(8,128)(2,1)S(1)}, u32[]{:S(2)}, u32[]{:S(2)}) collective-permute-start(bf16[2,128,1024]{2,1,0:T(8,128)(2,1)S(1)} %pad_maximum_fusion.2), channel_id=1, source_target_pairs={{0,12},{4,8},{8,4},{12,0},{1,13},{5,9},{9,5},{13,1},{2,14},{6,10},... | collective-permute-start | bytes 1572872 | tf_op jit(solution)/shard_map/ppermute | solution.py:19
  41.6 5.3 %copy-start.6 = (bf16[512,2048]{1,0:T(8,128)(2,1)S(1)}, bf16[512,2048]{1,0:T(8,128)(2,1)}, u32[]{:S(2)}) copy-start(bf16[512,2048]{1,0:T(8,128)(2,1)} %param.6) | copy-start | bytes 6291460
  42.0 17.2 %collective-permute-start.9 = (bf16[2,128,1024]{2,1,0:T(8,128)(2,1)S(1)}, bf16[2,128,1024]{2,1,0:T(8,128)(2,1)S(1)}, u32[]{:S(2)}, u32[]{:S(2)}) collective-permute-start(bf16[2,128,1024]{2,1,0:T(8,128)(2,1)S(1)} %pad_maximum_fusion.5), channel_id=1, source_target_pairs={{0,12},{4,8},{8,4},{12,0},{1,13},{5,9},{9,5},{13,1},{2,14},{6,10},... | collective-permute-start | bytes 1572872 | tf_op jit(solution)/shard_map/ppermute | solution.py:19
  45.0 19.1 %collective-permute-start.8 = (bf16[2,128,1024]{2,1,0:T(8,128)(2,1)S(1)}, bf16[2,128,1024]{2,1,0:T(8,128)(2,1)S(1)}, u32[]{:S(2)}, u32[]{:S(2)}) collective-permute-start(bf16[2,128,1024]{2,1,0:T(8,128)(2,1)S(1)} %pad_maximum_fusion.4), channel_id=1, source_target_pairs={{0,4},{4,0},{8,12},{12,8},{1,5},{5,1},{9,13},{13,9},{2,6},{6,2},{1... | collective-permute-start | bytes 1572872 | tf_op jit(solution)/shard_map/ppermute | solution.py:19
  49.0 20.7 %collective-permute-start.13 = (bf16[128,1024]{1,0:T(8,128)(2,1)}, bf16[128,1024]{1,0:T(8,128)(2,1)}, u32[]{:S(2)}, u32[]{:S(2)}) collective-permute-start(bf16[128,1024]{1,0:T(8,128)(2,1)} %fusion.4), channel_id=1, source_target_pairs={{0,12},{4,8},{8,4},{12,0},{1,13},{5,9},{9,5},{13,1},{2,14},{6,10},... | collective-permute-start | bytes 786440 | tf_op jit(solution)/shard_map/ppermute | solution.py:19
  53.8 17.1 %copy-start = (bf16[1,256,2048]{2,1,0:T(8,128)(2,1)S(1)}, bf16[1,256,2048]{2,1,0:T(8,128)(2,1)}, u32[]{:S(2)}) copy-start(bf16[1,256,2048]{2,1,0:T(8,128)(2,1)} %param.7) | copy-start | bytes 3145732
  53.8 16.0 %collective-permute-start.14 = (bf16[128,1024]{1,0:T(8,128)(2,1)}, bf16[128,1024]{1,0:T(8,128)(2,1)}, u32[]{:S(2)}, u32[]{:S(2)}) collective-permute-start(bf16[128,1024]{1,0:T(8,128)(2,1)} %fusion.14), channel_id=1, source_target_pairs={{0,4},{4,0},{8,12},{12,8},{1,5},{5,1},{9,13},{13,9},{2,6},{6,2},{1... | collective-permute-start | bytes 786440 | tf_op jit(solution)/shard_map/ppermute | solution.py:19
  60.3 0.8 copy-start.1
  61.1 21.1 %collective-permute-start.11 = (bf16[128,1024]{1,0:T(8,128)(2,1)}, bf16[128,1024]{1,0:T(8,128)(2,1)S(1)}, u32[]{:S(2)}, u32[]{:S(2)}) collective-permute-start(bf16[128,1024]{1,0:T(8,128)(2,1)} %fusion.15), channel_id=1, source_target_pairs={{0,4},{4,0},{8,12},{12,8},{1,5},{5,1},{9,13},{13,9},{2,6},{6,2},{1... | collective-permute-start | bytes 786440 | tf_op jit(solution)/shard_map/ppermute | solution.py:19
  65.2 0.8 copy-start.3
  66.0 16.1 %collective-permute-start.10 = (bf16[128,1024]{1,0:T(8,128)(2,1)}, bf16[128,1024]{1,0:T(8,128)(2,1)}, u32[]{:S(2)}, u32[]{:S(2)}) collective-permute-start(bf16[128,1024]{1,0:T(8,128)(2,1)} %fusion.16), channel_id=1, source_target_pairs={{0,12},{4,8},{8,4},{12,0},{1,13},{5,9},{9,5},{13,1},{2,14},{6,10},... | collective-permute-start | bytes 786440 | tf_op jit(solution)/shard_map/ppermute | solution.py:19
  70.8 11.3 %copy-start.2 = (bf16[2,128,1024]{2,1,0:T(8,128)(2,1)S(1)}, bf16[2,128,1024]{2,1,0:T(8,128)(2,1)}, u32[]{:S(2)}) copy-start(bf16[2,128,1024]{2,1,0:T(8,128)(2,1)} %copy-done.1) | copy-start | bytes 1572868
  70.8 11.3 %copy-start.4 = (bf16[2,128,1024]{2,1,0:T(8,128)(2,1)S(1)}, bf16[2,128,1024]{2,1,0:T(8,128)(2,1)}, u32[]{:S(2)}) copy-start(bf16[2,128,1024]{2,1,0:T(8,128)(2,1)} %copy-done.3) | copy-start | bytes 1572868
  73.0 14.2 %collective-permute-start.15 = (bf16[4,64,512]{2,1,0:T(8,128)(2,1)S(1)}, bf16[4,64,512]{2,1,0:T(8,128)(2,1)S(1)}, u32[]{:S(2)}, u32[]{:S(2)}) collective-permute-start(bf16[4,64,512]{2,1,0:T(8,128)(2,1)S(1)} %get-tuple-element.33), channel_id=1, source_target_pairs={{0,16},{16,0},{1,17},{17,1},{2,18},{18,2},{3,19},{19,3},{4,20},{20... | collective-permute-start | bytes 786440 | tf_op jit(solution)/shard_map/ppermute | solution.py:19
  84.2 4.1 %collective-permute-start.16 = (bf16[4,64,512]{2,1,0:T(8,128)(2,1)S(1)}, bf16[4,64,512]{2,1,0:T(8,128)(2,1)S(1)}, u32[]{:S(2)}, u32[]{:S(2)}) collective-permute-start(bf16[4,64,512]{2,1,0:T(8,128)(2,1)S(1)} %get-tuple-element.35), channel_id=1, source_target_pairs={{0,16},{16,0},{1,17},{17,1},{2,18},{18,2},{3,19},{19,3},{4,20},{20... | collective-permute-start | bytes 786440 | tf_op jit(solution)/shard_map/ppermute | solution.py:19
  89.2 27.5 %all-to-all-start = ((bf16[8,64,512]{2,1,0:T(8,128)(2,1)}), bf16[8,64,512]{2,1,0:T(8,128)(2,1)S(1)}, u32[]{:S(2)}, u32[]{:S(2)}) async-start(bf16[8,64,512]{2,1,0:T(8,128)(2,1)} %pad_maximum_fusion.6), calls=%async_computation | async-start | bytes 1048576 | tf_op jit(solution)/shard_map/all_to_all | solution.py:203
  116.7 9.0 %collective-permute-start.17 = (bf16[64,512]{1,0:T(8,128)(2,1)S(1)}, bf16[64,512]{1,0:T(8,128)(2,1)S(1)}, u32[]{:S(2)}, u32[]{:S(2)}) collective-permute-start(bf16[64,512]{1,0:T(8,128)(2,1)S(1)} %reduce_sum.12.mine_ref), channel_id=1, source_target_pairs={{0,32},{32,0},{1,33},{33,1},{2,34},{34,2},{3,35},{35,3},{4,36},{36... | collective-permute-start | bytes 196616 | tf_op jit(solution)/shard_map/ppermute | solution.py:19
  143.4 7.4 %collective-permute-start.18 = (bf16[8,64,512]{2,1,0:T(8,128)(2,1)S(1)}, bf16[8,64,512]{2,1,0:T(8,128)(2,1)S(1)}, u32[]{:S(2)}, u32[]{:S(2)}) collective-permute-start(bf16[8,64,512]{2,1,0:T(8,128)(2,1)S(1)} %all_to_all.10.mine_ref), channel_id=1, source_target_pairs={{0,16},{16,0},{1,17},{17,1},{2,18},{18,2},{3,19},{19,3},{4,20},{20... | collective-permute-start | bytes 1572872 | tf_op jit(solution)/shard_map/ppermute | solution.py:19

commit v4 on v2

--- a/solution.py
+++ b/solution.py
@@ -45,7 +45,7 @@
                 far = slice(h * 1024 + near.start, h * 1024 + near.stop)
                 acc = (
                     own_ref[:, far].astype(F32)
-                    + got[0, :, near].astype(F32)
+                    + got[:, near].astype(F32)
                     + nxt[:, near].astype(F32)
                 )
                 acc = fb_ref[:, far].astype(F32) + acc
@@ -64,11 +64,10 @@
     half = pl.BlockSpec((BLK, cols // 2), lambda i: (i, 0))
     slab = pl.BlockSpec((2, BLK, 512), lambda i: (i, 0, 0))
     line = pl.BlockSpec((1, 1, cols), lambda i: (i, 0, 0))
-    got = pl.BlockSpec((1, BLK, cols // 2), lambda i: (0, i, 0))
     return kernel_call(
         feedback_kernel,
         (groups,),
-        [SMEM, line, wide, wide, got, got, half, half],
+        [SMEM, line, wide, wide, half, half, half, half],
         [wide, slab, slab],
         [
             jax.ShapeDtypeStruct((rows, cols), BF16),
@@ -128,30 +127,30 @@
     )(c, mine, other)
 
 
-def partial_sums(hidden, cotangent, early):
-    d, t = lax.axis_index("dp"), lax.axis_index("t")
-    whole = [hidden]
-    for shift in (1, 2, 3):
-        whole.append(lax.ppermute(hidden, "t", [(i, (i + shift) % 4) for i in range(4)]))
-    *whole, early = lax.optimization_barrier((*whole, early))
-    whole = jnp.stack(whole)
+def partial_sums(hidden, cotangent, mask, early):
+    d = lax.axis_index("dp")
+    copies = jnp.broadcast_to(hidden[None], (4, *hidden.shape))
+    whole = lax.all_to_all(copies, "t", 0, 0, tiled=True)
 
     def part(flip, cols):
-        rows = lax.dynamic_index_in_dim(whole, (t - (d ^ flip)) % 4, 0, keepdims=False)
+        rows = lax.dynamic_index_in_dim(whole, d ^ flip, 0, keepdims=False)
         return lax.dot_general(
             rows, cols, (((0,), (0,)), ((), ())), preferred_element_type=F32
         ).astype(BF16)
 
+    def plus(kept, got):
+        return (kept.astype(F32) + got.astype(F32)).astype(BF16)
+
     half = cotangent.shape[1] // 2
     a, b = cotangent[:, :half], cotangent[:, half:]
-    a1, a2, a3 = part(1, a), part(2, a), part(3, a)
-    b1, b2, b3 = part(1, b), part(2, b), part(3, b)
-    own = part(0, cotangent)
-    got_a = swap(jnp.stack([a1, a2]), "dp", 1, 4)
-    got_b = swap(jnp.stack([b3, b2]), "dp", 3, 4)
-    next_a = swap((a3.astype(F32) + got_a[1].astype(F32)).astype(BF16), "dp", 3, 4)
-    next_b = swap((b1.astype(F32) + got_b[1].astype(F32)).astype(BF16), "dp", 1, 4)
-    return early, own, got_a, got_b, next_a, next_b
+    far_a, far_b = swap(part(2, a), "dp", 1, 4), swap(part(2, b), "dp", 3, 4)
+    got_a, got_b = swap(part(1, a), "dp", 1, 4), swap(part(3, b), "dp", 3, 4)
+    kept_a, kept_b, own = part(3, a), part(1, b), part(0, cotangent)
+    far_a, kept_a, kept_b, own, mask = lax.optimization_barrier((far_a, kept_a, kept_b, own, mask))
+    next_a = swap(plus(kept_a, far_a), "dp", 3, 4)
+    next_b = swap(plus(kept_b, far_b), "dp", 1, 4)
+    got_a, got_b, early = lax.optimization_barrier((got_a, got_b, early))
+    return early, mask, own, got_a, got_b, next_a, next_b
 
 
 def as_matrix(blocks):
@@ -170,11 +169,11 @@
     mask = jnp.any(chosen.reshape(-1, 1, 1) == block_of[None], axis=0).astype(F32)
     moment = as_matrix(momentum[0, 0])
     far_moment = swap(moment, "yh", 1, 2)
-    far_moment, *parts = partial_sums(hidden, cotangent, far_moment)
+    far_moment, mask, *parts = partial_sums(hidden, cotangent, mask[:, None], far_moment)
     moment = jnp.where(
         yh == 0, jnp.concatenate([moment, far_moment], 1), jnp.concatenate([far_moment, moment], 1)
     )
-    feedback_new, mine, other = error_feedback(at_c, mask[:, None], feedback[0], *parts)
+    feedback_new, mine, other = error_feedback(at_c, mask, feedback[0], *parts)
     pair = (mine + swap(other, "c", 1, 2).astype(F32)).astype(BF16)
     got = lax.all_to_all(pair, "z", 0, 0, tiled=True)
     near = jnp.sum(got.astype(F32), axis=0)

time: 155 us -> 156 us (level)
  the two profiles are of different devices: /device:TPU:17 before, /device:TPU:1 now
where the time goes in v4:
time: 156 us; the launch traced here: 155 us
  starting transfers between devices  52.4 us (34%)
  waiting for transfers between devices  42.4 us (27%)
  blocking collectives  41.3 us (26%)
  matrix products  6.08 us (4%)
  Pallas kernels  6.01 us (4%)
  local copies, waits for them, and re-layouts  3.39 us (2%)
  other arithmetic  2.68 us (2%)
    ppermute x10, starting transfers between devices, swap(): return lax.ppermute(value, axis, [(i, i ^ flip) for i in range(size)])  47 us
    all_to_all x1, blocking collectives, local(): got = lax.all_to_all(pair, 'z', 0, 0, tiled=True)  26.5 us
    all_to_all x1, waiting for transfers between devices, partial_sums(): whole = lax.all_to_all(copies, 't', 0, 0, tiled=True)  23.1 us
    ppermute x10, waiting for transfers between devices, swap(): return lax.ppermute(value, axis, [(i, i ^ flip) for i in range(size)])  19.3 us
    all_to_all x1, blocking collectives, local(): every = lax.all_to_all(copies, 'z', 0, 0, tiled=True)  14.8 us
    dot_general x7, matrix products, part(): lax.dot_general(rows, cols, (((0,), (0,)), ((), ())), preferred_element_t...  6.08 us
    all_to_all x1, starting transfers between devices, partial_sums(): whole = lax.all_to_all(copies, 't', 0, 0, tiled=True)  5.42 us
    pallas_call x1, Pallas kernels, error_feedback(): kernel_call(feedback_kernel, (groups,), [SMEM, line, wide, wide, half, ha...  3.71 us
  transfers between devices with their start and end apart: 11, of which 9 were waited for; matrix products, arithmetic and copies ran while one was open for 5% of the time, Pallas kernels for 0%

profile of v4, /device:TPU:1, one launch (start us, length us, event | category | flops | bytes accessed | tf_op | source)
XLA Modules:
  0.0 155.3 jit_solution(5426838785503507198)
XLA Ops:
  0.7 2.1 %broadcast_in_dim.6 = bf16[4,512,256]{2,1,0:T(8,128)(2,1)} broadcast(bf16[512,256]{1,0:T(8,128)(2,1)} %param.5), dimensions={1,2} | broadcast | bytes 1310720 | tf_op jit(solution)/shard_map/broadcast_in_dim | solution.py:132
  2.8 5.4 %all-to-all-start = ((bf16[4,512,256]{2,1,0:T(8,128)(2,1)}), bf16[4,512,256]{2,1,0:T(8,128)(2,1)S(1)}, u32[]{:S(2)}, u32[]{:S(2)}) async-start(bf16[4,512,256]{2,1,0:T(8,128)(2,1)} %broadcast_in_dim.6), calls=%async_computation | async-start | bytes 2097152 | tf_op jit(solution)/shard_map/all_to_all | solution.py:133
  8.7 23.1 %all-to-all-done = bf16[4,512,256]{2,1,0:T(8,128)(2,1)S(1)} async-done(((bf16[4,512,256]{2,1,0:T(8,128)(2,1)}), bf16[4,512,256]{2,1,0:T(8,128)(2,1)S(1)}, u32[]{:S(2)}, u32[]{:S(2)}) %all-to-all-start) | async-done | bytes 1048608 | tf_op jit(solution)/shard_map/all_to_all | solution.py:133
  31.8 1.0 copy-done.3
  32.8 1.3 convolution_convert_fusion.3
  34.1 4.8 %collective-permute-start.1 = (bf16[256,1024]{1,0:T(8,128)(2,1)}, bf16[256,1024]{1,0:T(8,128)(2,1)S(1)}, u32[]{:S(2)}, u32[]{:S(2)}) collective-permute-start(bf16[256,1024]{1,0:T(8,128)(2,1)} %convolution_convert_fusion.3), channel_id=1, source_target_pairs={{0,4},{4,0},{8,12},{12,8},{1,5},{5,1},{9,13},{13,9},{2,6},{6,2},{1... | collective-permute-start | bytes 1572872 | tf_op jit(solution)/shard_map/ppermute | solution.py:18
  38.9 2.2 %convolution_convert_fusion.2 = bf16[256,1024]{1,0:T(8,128)(2,1)} fusion(bf16[512,2048]{1,0:T(8,128)(2,1)S(1)} %copy-done.1, bf16[4,512,256]{2,1,0:T(8,128)(2,1)} %copy-done.3, s32[]{:T(128)S(6)} %select_n.35), kind=kOutput, calls=%fused_computation.3 | convolution fusion | flops 268697600 | bytes 1835012 | tf_op jit(solution)/shard_map/dot_general | solution.py:137
  41.1 3.8 %collective-permute-start.2 = (bf16[256,1024]{1,0:T(8,128)(2,1)}, bf16[256,1024]{1,0:T(8,128)(2,1)S(1)}, u32[]{:S(2)}, u32[]{:S(2)}) collective-permute-start(bf16[256,1024]{1,0:T(8,128)(2,1)} %convolution_convert_fusion.2), channel_id=1, source_target_pairs={{0,12},{4,8},{8,4},{12,0},{1,13},{5,9},{9,5},{13,1},{2,14},{6,10},... | collective-permute-start | bytes 1572872 | tf_op jit(solution)/shard_map/ppermute | solution.py:18
  45.0 0.5 convolution_convert_fusion.6
  45.5 2.2 %collective-permute-start = (bf16[256,1024]{1,0:T(8,128)(2,1)S(1)}, bf16[256,1024]{1,0:T(8,128)(2,1)S(1)}, u32[]{:S(2)}, u32[]{:S(2)}) collective-permute-start(bf16[256,1024]{1,0:T(8,128)(2,1)S(1)} %convolution_convert_fusion.6), channel_id=1, source_target_pairs={{0,4},{4,0},{8,12},{12,8},{1,5},{5,1},{9,13},{13,9},{2,6},{6,2},{1... | collective-permute-start | bytes 1572872 | tf_op jit(solution)/shard_map/ppermute | solution.py:18
  48.2 2.5 %collective-permute-start.5 = (bf16[256,1024]{1,0:T(8,128)(2,1)S(1)}, bf16[256,1024]{1,0:T(8,128)(2,1)S(1)}, u32[]{:S(2)}, u32[]{:S(2)}) collective-permute-start(bf16[256,1024]{1,0:T(8,128)(2,1)S(1)} %convolution_convert_fusion.1), channel_id=1, source_target_pairs={{0,12},{4,8},{8,4},{12,0},{1,13},{5,9},{9,5},{13,1},{2,14},{6,10},... | collective-permute-start | bytes 1572872 | tf_op jit(solution)/shard_map/ppermute | solution.py:18
  50.7 0.7 convolution_convert_fusion.own_ref
  51.5 0.5 convolution_convert_fusion.5
  52.4 8.9 %collective-permute-done = bf16[256,1024]{1,0:T(8,128)(2,1)S(1)} collective-permute-done((bf16[256,1024]{1,0:T(8,128)(2,1)S(1)}, bf16[256,1024]{1,0:T(8,128)(2,1)S(1)}, u32[]{:S(2)}, u32[]{:S(2)}) %collective-permute-start) | collective-permute-done | bytes 524320 | tf_op jit(solution)/shard_map/ppermute | solution.py:18
  61.4 1.0 add_convert_fusion.2
  62.4 4.1 %collective-permute-start.4 = (bf16[256,1024]{1,0:T(8,128)(2,1)}, bf16[256,1024]{1,0:T(8,128)(2,1)}, u32[]{:S(2)}, u32[]{:S(2)}) collective-permute-start(bf16[256,1024]{1,0:T(8,128)(2,1)} %add_convert_fusion.2), channel_id=1, source_target_pairs={{0,12},{4,8},{8,4},{12,0},{1,13},{5,9},{9,5},{13,1},{2,14},{6,10},... | collective-permute-start | bytes 1572872 | tf_op jit(solution)/shard_map/ppermute | solution.py:18
  66.5 1.0 collective-permute-done.5
  67.5 1.0 add_convert_fusion.1
  68.5 1.9 %collective-permute-start.6 = (bf16[256,1024]{1,0:T(8,128)(2,1)}, bf16[256,1024]{1,0:T(8,128)(2,1)}, u32[]{:S(2)}, u32[]{:S(2)}) collective-permute-start(bf16[256,1024]{1,0:T(8,128)(2,1)} %add_convert_fusion.1), channel_id=1, source_target_pairs={{0,4},{4,0},{8,12},{12,8},{1,5},{5,1},{9,13},{13,9},{2,6},{6,2},{1... | collective-permute-start | bytes 1572872 | tf_op jit(solution)/shard_map/ppermute | solution.py:18
  70.7 6.4 %collective-permute-start.3 = (f32[64,256]{1,0:T(8,128)S(1)}, f32[64,256]{1,0:T(8,128)S(1)}, u32[]{:S(2)}, u32[]{:S(2)}) collective-permute-start(f32[64,256]{1,0:T(8,128)S(1)} %reshape.97), channel_id=1, source_target_pairs={{0,32},{32,0},{1,33},{33,1},{2,34},{34,2},{3,35},{35,3},{4,36},{36... | collective-permute-start | bytes 196616 | tf_op jit(solution)/shard_map/ppermute | solution.py:18
  77.1 2.5 %collective-permute-done.3 = f32[64,256]{1,0:T(8,128)S(1)} collective-permute-done((f32[64,256]{1,0:T(8,128)S(1)}, f32[64,256]{1,0:T(8,128)S(1)}, u32[]{:S(2)}, u32[]{:S(2)}) %collective-permute-start.3) | collective-permute-done | bytes 65568 | tf_op jit(solution)/shard_map/ppermute | solution.py:18
  80.2 3.7 %shard_map.76 = (bf16[256,2048]{1,0:T(8,128)(2,1)}, f32[8,64,512]{2,1,0:T(8,128)S(1)}, bf16[8,64,512]{2,1,0:T(8,128)(2,1)S(1)}) custom-call(s32[1]{0:T(128)} %bitcast.c_ref, f32[4,1,2048]{2,1,0:T(1,128)S(1)} %reshape.99.mask_ref, bf16[256,2048]{1,0:T(8,128)(2,1)S(1)} %bitcast.28, bf16[256,2048]{1,0:T(8,128)(2,1)S(1)} %convolution_convert_fusion.own_ref, ...), custom_call_target="tpu_custom_call" | custom-call | flops 4194304 | bytes 4194304 | tf_op jit(solution)/shard_map/pallas_call | solution.py:67
  83.9 6.8 %collective-permute-start.7 = (bf16[8,64,512]{2,1,0:T(8,128)(2,1)S(1)}, bf16[8,64,512]{2,1,0:T(8,128)(2,1)S(1)}, u32[]{:S(2)}, u32[]{:S(2)}) collective-permute-start(bf16[8,64,512]{2,1,0:T(8,128)(2,1)S(1)} %get-tuple-element.25), channel_id=1, source_target_pairs={{0,16},{16,0},{1,17},{17,1},{2,18},{18,2},{3,19},{19,3},{4,20},{20... | collective-permute-start | bytes 1572872 | tf_op jit(solution)/shard_map/ppermute | solution.py:18
  90.7 1.5 collective-permute-done.7
  92.4 26.5 %all_to_all.15 = bf16[8,64,512]{2,1,0:T(8,128)(2,1)S(1)} all-to-all(bf16[8,64,512]{2,1,0:T(8,128)(2,1)S(1)} %add_convert_fusion), channel_id=1, replica_groups=mesh['z'=8,'yh'=2,'c'=2,'dp'=4,'t'=4] {'z'}, dimensions={0} | all-to-all | bytes 1048576 | tf_op jit(solution)/shard_map/all_to_all | solution.py:178
  119.0 6.4 %collective-permute-start.8 = (f32[64,512]{1,0:T(8,128)S(1)}, f32[64,512]{1,0:T(8,128)S(1)}, u32[]{:S(2)}, u32[]{:S(2)}) collective-permute-start(f32[64,512]{1,0:T(8,128)S(1)} %convert_reduce_fusion.mine_ref), channel_id=1, source_target_pairs={{0,32},{32,0},{1,33},{33,1},{2,34},{34,2},{3,35},{35,3},{4,36},{36... | collective-permute-start | bytes 393224 | tf_op jit(solution)/shard_map/ppermute | solution.py:18
  125.4 3.3 %collective-permute-done.8.peer_ref = f32[64,512]{1,0:T(8,128)S(1)} collective-permute-done((f32[64,512]{1,0:T(8,128)S(1)}, f32[64,512]{1,0:T(8,128)S(1)}, u32[]{:S(2)}, u32[]{:S(2)}) %collective-permute-start.8) | collective-permute-done | bytes 131104 | tf_op jit(solution)/shard_map/ppermute | solution.py:18
  128.7 0.8 shard_map.77
  129.5 14.8 %all_to_all.16.mine_ref = bf16[8,64,512]{2,1,0:T(8,128)(2,1)S(1)} all-to-all(bf16[8,64,512]{2,1,0:T(8,128)(2,1)S(1)} %get-tuple-element.28), channel_id=1, replica_groups=mesh['z'=8,'yh'=2,'c'=2,'dp'=4,'t'=4] {'z'}, dimensions={0} | all-to-all | bytes 1048576 | tf_op jit(solution)/shard_map/all_to_all | solution.py:181
  144.3 7.9 %collective-permute-start.9 = (bf16[8,64,512]{2,1,0:T(8,128)(2,1)S(1)}, bf16[8,64,512]{2,1,0:T(8,128)(2,1)S(1)}, u32[]{:S(2)}, u32[]{:S(2)}) collective-permute-start(bf16[8,64,512]{2,1,0:T(8,128)(2,1)S(1)} %all_to_all.16.mine_ref), channel_id=1, source_target_pairs={{0,16},{16,0},{1,17},{17,1},{2,18},{18,2},{3,19},{19,3},{4,20},{20... | collective-permute-start | bytes 1572872 | tf_op jit(solution)/shard_map/ppermute | solution.py:18
  152.2 1.5 collective-permute-done.9.other_ref
  153.7 1.5 shard_map.78
  (30 shorter events, 2.5 us)
Async XLA Ops:
  0.6 7.7 %copy-start.6 = (s32[1,1,1,64]{3,2,1,0:T(1,128)S(1)}, s32[1,1,1,64]{3,2,1,0:T(1,128)}, u32[]{:S(2)}) copy-start(s32[1,1,1,64]{3,2,1,0:T(1,128)} %param.8) | copy-start | bytes 772
  0.6 32.2 %copy-start.1 = (bf16[512,2048]{1,0:T(8,128)(2,1)S(1)}, bf16[512,2048]{1,0:T(8,128)(2,1)}, u32[]{:S(2)}) copy-start(bf16[512,2048]{1,0:T(8,128)(2,1)} %param.6) | copy-start | bytes 6291460
  2.8 29.0 %all-to-all-start = ((bf16[4,512,256]{2,1,0:T(8,128)(2,1)}), bf16[4,512,256]{2,1,0:T(8,128)(2,1)S(1)}, u32[]{:S(2)}, u32[]{:S(2)}) async-start(bf16[4,512,256]{2,1,0:T(8,128)(2,1)} %broadcast_in_dim.6), calls=%async_computation | async-start | bytes 2097152 | tf_op jit(solution)/shard_map/all_to_all | solution.py:133
  31.8 1.0 copy-start.3
  34.1 10.9 %copy-start.4 = (bf16[4,512,256]{2,1,0:T(8,128)(2,1)S(1)}, bf16[4,512,256]{2,1,0:T(8,128)(2,1)}, u32[]{:S(2)}) copy-start(bf16[4,512,256]{2,1,0:T(8,128)(2,1)} %copy-done.3) | copy-start | bytes 3145732
  34.1 45.5 %collective-permute-start.1 = (bf16[256,1024]{1,0:T(8,128)(2,1)}, bf16[256,1024]{1,0:T(8,128)(2,1)S(1)}, u32[]{:S(2)}, u32[]{:S(2)}) collective-permute-start(bf16[256,1024]{1,0:T(8,128)(2,1)} %convolution_convert_fusion.3), channel_id=1, source_target_pairs={{0,4},{4,0},{8,12},{12,8},{1,5},{5,1},{9,13},{13,9},{2,6},{6,2},{1... | collective-permute-start | bytes 1572872 | tf_op jit(solution)/shard_map/ppermute | solution.py:18
  41.1 9.6 %copy-start.2 = (bf16[512,2048]{1,0:T(8,128)(2,1)S(1)}, bf16[512,2048]{1,0:T(8,128)(2,1)}, u32[]{:S(2)}) copy-start(bf16[512,2048]{1,0:T(8,128)(2,1)} %param.6) | copy-start | bytes 6291460
  41.1 38.4 %collective-permute-start.2 = (bf16[256,1024]{1,0:T(8,128)(2,1)}, bf16[256,1024]{1,0:T(8,128)(2,1)S(1)}, u32[]{:S(2)}, u32[]{:S(2)}) collective-permute-start(bf16[256,1024]{1,0:T(8,128)(2,1)} %convolution_convert_fusion.2), channel_id=1, source_target_pairs={{0,12},{4,8},{8,4},{12,0},{1,13},{5,9},{9,5},{13,1},{2,14},{6,10},... | collective-permute-start | bytes 1572872 | tf_op jit(solution)/shard_map/ppermute | solution.py:18
  45.5 15.9 %collective-permute-start = (bf16[256,1024]{1,0:T(8,128)(2,1)S(1)}, bf16[256,1024]{1,0:T(8,128)(2,1)S(1)}, u32[]{:S(2)}, u32[]{:S(2)}) collective-permute-start(bf16[256,1024]{1,0:T(8,128)(2,1)S(1)} %convolution_convert_fusion.6), channel_id=1, source_target_pairs={{0,4},{4,0},{8,12},{12,8},{1,5},{5,1},{9,13},{13,9},{2,6},{6,2},{1... | collective-permute-start | bytes 1572872 | tf_op jit(solution)/shard_map/ppermute | solution.py:18
  48.2 19.3 %collective-permute-start.5 = (bf16[256,1024]{1,0:T(8,128)(2,1)S(1)}, bf16[256,1024]{1,0:T(8,128)(2,1)S(1)}, u32[]{:S(2)}, u32[]{:S(2)}) collective-permute-start(bf16[256,1024]{1,0:T(8,128)(2,1)S(1)} %convolution_convert_fusion.1), channel_id=1, source_target_pairs={{0,12},{4,8},{8,4},{12,0},{1,13},{5,9},{9,5},{13,1},{2,14},{6,10},... | collective-permute-start | bytes 1572872 | tf_op jit(solution)/shard_map/ppermute | solution.py:18
  52.4 18.0 %copy-start.5 = (f32[1,1,4,64,64]{4,3,2,1,0:T(8,128)S(1)}, f32[1,1,4,64,64]{4,3,2,1,0:T(8,128)}, u32[]{:S(2)}) copy-start(f32[1,1,4,64,64]{4,3,2,1,0:T(8,128)} %param.9) | copy-start | bytes 196612
  52.4 27.7 %copy-start = (bf16[1,256,2048]{2,1,0:T(8,128)(2,1)S(1)}, bf16[1,256,2048]{2,1,0:T(8,128)(2,1)}, u32[]{:S(2)}) copy-start(bf16[1,256,2048]{2,1,0:T(8,128)(2,1)} %param.7) | copy-start | bytes 3145732
  62.4 17.4 %collective-permute-start.4 = (bf16[256,1024]{1,0:T(8,128)(2,1)}, bf16[256,1024]{1,0:T(8,128)(2,1)}, u32[]{:S(2)}, u32[]{:S(2)}) collective-permute-start(bf16[256,1024]{1,0:T(8,128)(2,1)} %add_convert_fusion.2), channel_id=1, source_target_pairs={{0,12},{4,8},{8,4},{12,0},{1,13},{5,9},{9,5},{13,1},{2,14},{6,10},... | collective-permute-start | bytes 1572872 | tf_op jit(solution)/shard_map/ppermute | solution.py:18
  68.5 11.7 %collective-permute-start.6 = (bf16[256,1024]{1,0:T(8,128)(2,1)}, bf16[256,1024]{1,0:T(8,128)(2,1)}, u32[]{:S(2)}, u32[]{:S(2)}) collective-permute-start(bf16[256,1024]{1,0:T(8,128)(2,1)} %add_convert_fusion.1), channel_id=1, source_target_pairs={{0,4},{4,0},{8,12},{12,8},{1,5},{5,1},{9,13},{13,9},{2,6},{6,2},{1... | collective-permute-start | bytes 1572872 | tf_op jit(solution)/shard_map/ppermute | solution.py:18
  70.7 8.9 %collective-permute-start.3 = (f32[64,256]{1,0:T(8,128)S(1)}, f32[64,256]{1,0:T(8,128)S(1)}, u32[]{:S(2)}, u32[]{:S(2)}) collective-permute-start(f32[64,256]{1,0:T(8,128)S(1)} %reshape.97), channel_id=1, source_target_pairs={{0,32},{32,0},{1,33},{33,1},{2,34},{34,2},{3,35},{35,3},{4,36},{36... | collective-permute-start | bytes 196616 | tf_op jit(solution)/shard_map/ppermute | solution.py:18
  83.9 8.3 %collective-permute-start.7 = (bf16[8,64,512]{2,1,0:T(8,128)(2,1)S(1)}, bf16[8,64,512]{2,1,0:T(8,128)(2,1)S(1)}, u32[]{:S(2)}, u32[]{:S(2)}) collective-permute-start(bf16[8,64,512]{2,1,0:T(8,128)(2,1)S(1)} %get-tuple-element.25), channel_id=1, source_target_pairs={{0,16},{16,0},{1,17},{17,1},{2,18},{18,2},{3,19},{19,3},{4,20},{20... | collective-permute-start | bytes 1572872 | tf_op jit(solution)/shard_map/ppermute | solution.py:18
  119.0 9.7 %collective-permute-start.8 = (f32[64,512]{1,0:T(8,128)S(1)}, f32[64,512]{1,0:T(8,128)S(1)}, u32[]{:S(2)}, u32[]{:S(2)}) collective-permute-start(f32[64,512]{1,0:T(8,128)S(1)} %convert_reduce_fusion.mine_ref), channel_id=1, source_target_pairs={{0,32},{32,0},{1,33},{33,1},{2,34},{34,2},{3,35},{35,3},{4,36},{36... | collective-permute-start | bytes 393224 | tf_op jit(solution)/shard_map/ppermute | solution.py:18
  144.3 9.5 %collective-permute-start.9 = (bf16[8,64,512]{2,1,0:T(8,128)(2,1)S(1)}, bf16[8,64,512]{2,1,0:T(8,128)(2,1)S(1)}, u32[]{:S(2)}, u32[]{:S(2)}) collective-permute-start(bf16[8,64,512]{2,1,0:T(8,128)(2,1)S(1)} %all_to_all.16.mine_ref), channel_id=1, source_target_pairs={{0,16},{16,0},{1,17},{17,1},{2,18},{18,2},{3,19},{19,3},{4,20},{20... | collective-permute-start | bytes 1572872 | tf_op jit(solution)/shard_map/ppermute | solution.py:18

commit v5 on v4

--- a/solution.py
+++ b/solution.py
@@ -128,12 +128,15 @@
 
 
 def partial_sums(hidden, cotangent, mask, early):
-    d = lax.axis_index("dp")
-    copies = jnp.broadcast_to(hidden[None], (4, *hidden.shape))
-    whole = lax.all_to_all(copies, "t", 0, 0, tiled=True)
-
-    def part(flip, cols):
-        rows = lax.dynamic_index_in_dim(whole, d ^ flip, 0, keepdims=False)
+    d, t = lax.axis_index("dp"), lax.axis_index("t")
+    far = swap(hidden, "t", 2, 4)
+    near = swap(hidden, "t", 1, 4)
+    whole = lax.optimization_barrier((hidden, near, far, swap(far, "t", 1, 4), early))
+    early = whole[4]
+    whole = jnp.stack(whole[:4])
+
+    def part(flip, cols, shards=whole):
+        rows = lax.dynamic_index_in_dim(shards, t ^ d ^ flip, 0, keepdims=False)
         return lax.dot_general(
             rows, cols, (((0,), (0,)), ((), ())), preferred_element_type=F32
         ).astype(BF16)
@@ -143,13 +146,14 @@
 
     half = cotangent.shape[1] // 2
     a, b = cotangent[:, :half], cotangent[:, half:]
-    far_a, far_b = swap(part(2, a), "dp", 1, 4), swap(part(2, b), "dp", 3, 4)
-    got_a, got_b = swap(part(1, a), "dp", 1, 4), swap(part(3, b), "dp", 3, 4)
-    kept_a, kept_b, own = part(3, a), part(1, b), part(0, cotangent)
+    give_a, give_b = part(2, a), part(2, b)
+    far_a, far_b = swap(give_a, "dp", 1, 4), swap(give_b, "dp", 3, 4)
+    later, give_a, give_b = lax.optimization_barrier((whole, give_a, give_b))
+    got_a, got_b = swap(part(1, a, later), "dp", 1, 4), swap(part(3, b, later), "dp", 3, 4)
+    kept_a, kept_b, own = part(3, a, later), part(1, b, later), part(0, cotangent, later)
     far_a, kept_a, kept_b, own, mask = lax.optimization_barrier((far_a, kept_a, kept_b, own, mask))
     next_a = swap(plus(kept_a, far_a), "dp", 3, 4)
     next_b = swap(plus(kept_b, far_b), "dp", 1, 4)
-    got_a, got_b, early = lax.optimization_barrier((got_a, got_b, early))
     return early, mask, own, got_a, got_b, next_a, next_b
 
 

time: 156 us -> 147 us (0.942)
  the two profiles are of different devices: /device:TPU:1 before, /device:TPU:17 now
where the time goes in v5:
time: 147 us; the launch traced here: 146 us
  starting transfers between devices  50.3 us (34%)
  blocking collectives  44.7 us (30%)
  waiting for transfers between devices  33.5 us (23%)
  Pallas kernels  6.02 us (4%)
  matrix products  5.14 us (3%)
  other arithmetic  4.42 us (3%)
    ppermute x13, starting transfers between devices, swap(): return lax.ppermute(value, axis, [(i, i ^ flip) for i in range(size)])  50.3 us
    ppermute x13, waiting for transfers between devices, swap(): return lax.ppermute(value, axis, [(i, i ^ flip) for i in range(size)])  33.5 us
    all_to_all x1, blocking collectives, local(): got = lax.all_to_all(pair, 'z', 0, 0, tiled=True)  26.5 us
    all_to_all x1, blocking collectives, local(): every = lax.all_to_all(copies, 'z', 0, 0, tiled=True)  18.1 us
    dot_general x7, matrix products, part(): lax.dot_general(rows, cols, (((0,), (0,)), ((), ())), preferred_element_t...  5.14 us
    pallas_call x1, Pallas kernels, error_feedback(): kernel_call(feedback_kernel, (groups,), [SMEM, line, wide, wide, half, ha...  3.72 us
  transfers between devices with their start and end apart: 13, of which 8 were waited for; matrix products, arithmetic and copies ran while one was open for 6% of the time, Pallas kernels for 0%

profile of v5, /device:TPU:17, one launch (start us, length us, event | category | flops | bytes accessed | tf_op | source)
XLA Modules:
  0.0 146.2 jit_solution(9690307129683817183)
XLA Ops:
  0.6 2.1 %collective-permute-start.1 = (bf16[512,256]{1,0:T(8,128)(2,1)}, bf16[512,256]{1,0:T(8,128)(2,1)S(1)}, u32[]{:S(2)}, u32[]{:S(2)}) collective-permute-start(bf16[512,256]{1,0:T(8,128)(2,1)} %param.5), channel_id=1, source_target_pairs={{0,2},{1,3},{2,0},{3,1},{4,6},{5,7},{6,4},{7,5},{8,10},{9,11},{10,... | collective-permute-start | bytes 786440 | tf_op jit(solution)/shard_map/ppermute | solution.py:18
  2.7 3.3 %collective-permute-start = (bf16[512,256]{1,0:T(8,128)(2,1)}, bf16[512,256]{1,0:T(8,128)(2,1)S(1)}, u32[]{:S(2)}, u32[]{:S(2)}) collective-permute-start(bf16[512,256]{1,0:T(8,128)(2,1)} %param.5), channel_id=1, source_target_pairs={{0,1},{1,0},{2,3},{3,2},{4,5},{5,4},{6,7},{7,6},{8,9},{9,8},{10,11... | collective-permute-start | bytes 786440 | tf_op jit(solution)/shard_map/ppermute | solution.py:18
  6.0 1.0 copy.9
  7.1 6.5 %collective-permute-start.3 = (f32[64,256]{1,0:T(8,128)S(1)}, f32[64,256]{1,0:T(8,128)S(1)}, u32[]{:S(2)}, u32[]{:S(2)}) collective-permute-start(f32[64,256]{1,0:T(8,128)S(1)} %reshape.96), channel_id=1, source_target_pairs={{0,32},{32,0},{1,33},{33,1},{2,34},{34,2},{3,35},{35,3},{4,36},{36... | collective-permute-start | bytes 196616 | tf_op jit(solution)/shard_map/ppermute | solution.py:18
  13.7 7.8 %collective-permute-start.2 = (bf16[512,256]{1,0:T(8,128)(2,1)S(1)}, bf16[512,256]{1,0:T(8,128)(2,1)S(1)}, u32[]{:S(2)}, u32[]{:S(2)}) collective-permute-start(bf16[512,256]{1,0:T(8,128)(2,1)S(1)} %collective-permute-done.1), channel_id=1, source_target_pairs={{0,1},{1,0},{2,3},{3,2},{4,5},{5,4},{6,7},{7,6},{8,9},{9,8},{10,11... | collective-permute-start | bytes 786440 | tf_op jit(solution)/shard_map/ppermute | solution.py:18
  21.6 1.0 compare_reduce_fusion
  23.4 5.2 %collective-permute-done.2 = bf16[512,256]{1,0:T(8,128)(2,1)S(1)} collective-permute-done((bf16[512,256]{1,0:T(8,128)(2,1)S(1)}, bf16[512,256]{1,0:T(8,128)(2,1)S(1)}, u32[]{:S(2)}, u32[]{:S(2)}) %collective-permute-start.2) | collective-permute-done | bytes 262176 | tf_op jit(solution)/shard_map/ppermute | solution.py:18
  28.6 1.1 pad_maximum_fusion
  30.6 3.6 %collective-permute-start.4 = (bf16[256,1024]{1,0:T(8,128)(2,1)S(1)}, bf16[256,1024]{1,0:T(8,128)(2,1)S(1)}, u32[]{:S(2)}, u32[]{:S(2)}) collective-permute-start(bf16[256,1024]{1,0:T(8,128)(2,1)S(1)} %convolution_convert_fusion.6), channel_id=1, source_target_pairs={{0,4},{4,0},{8,12},{12,8},{1,5},{5,1},{9,13},{13,9},{2,6},{6,2},{1... | collective-permute-start | bytes 1572872 | tf_op jit(solution)/shard_map/ppermute | solution.py:18
  34.3 3.7 %collective-permute-start.8 = (bf16[256,1024]{1,0:T(8,128)(2,1)S(1)}, bf16[256,1024]{1,0:T(8,128)(2,1)S(1)}, u32[]{:S(2)}, u32[]{:S(2)}) collective-permute-start(bf16[256,1024]{1,0:T(8,128)(2,1)S(1)} %convolution_convert_fusion.5), channel_id=1, source_target_pairs={{0,12},{4,8},{8,4},{12,0},{1,13},{5,9},{9,5},{13,1},{2,14},{6,10},... | collective-permute-start | bytes 1572872 | tf_op jit(solution)/shard_map/ppermute | solution.py:18
  38.0 1.3 convolution_convert_fusion.1
  39.3 1.3 convolution_convert_fusion.2
  41.3 2.2 %collective-permute-start.5 = (bf16[256,1024]{1,0:T(8,128)(2,1)}, bf16[256,1024]{1,0:T(8,128)(2,1)S(1)}, u32[]{:S(2)}, u32[]{:S(2)}) collective-permute-start(bf16[256,1024]{1,0:T(8,128)(2,1)} %convolution_convert_fusion.2), channel_id=1, source_target_pairs={{0,4},{4,0},{8,12},{12,8},{1,5},{5,1},{9,13},{13,9},{2,6},{6,2},{1... | collective-permute-start | bytes 1572872 | tf_op jit(solution)/shard_map/ppermute | solution.py:18
  43.5 2.5 %collective-permute-start.6 = (bf16[256,1024]{1,0:T(8,128)(2,1)}, bf16[256,1024]{1,0:T(8,128)(2,1)S(1)}, u32[]{:S(2)}, u32[]{:S(2)}) collective-permute-start(bf16[256,1024]{1,0:T(8,128)(2,1)} %convolution_convert_fusion.1), channel_id=1, source_target_pairs={{0,12},{4,8},{8,4},{12,0},{1,13},{5,9},{9,5},{13,1},{2,14},{6,10},... | collective-permute-start | bytes 1572872 | tf_op jit(solution)/shard_map/ppermute | solution.py:18
  47.0 1.0 add_convert_fusion.2
  48.0 4.0 %collective-permute-start.7 = (bf16[256,1024]{1,0:T(8,128)(2,1)}, bf16[256,1024]{1,0:T(8,128)(2,1)}, u32[]{:S(2)}, u32[]{:S(2)}) collective-permute-start(bf16[256,1024]{1,0:T(8,128)(2,1)} %add_convert_fusion.2), channel_id=1, source_target_pairs={{0,12},{4,8},{8,4},{12,0},{1,13},{5,9},{9,5},{13,1},{2,14},{6,10},... | collective-permute-start | bytes 1572872 | tf_op jit(solution)/shard_map/ppermute | solution.py:18
  52.0 1.0 add_convert_fusion.1
  53.0 1.9 %collective-permute-start.9 = (bf16[256,1024]{1,0:T(8,128)(2,1)}, bf16[256,1024]{1,0:T(8,128)(2,1)}, u32[]{:S(2)}, u32[]{:S(2)}) collective-permute-start(bf16[256,1024]{1,0:T(8,128)(2,1)} %add_convert_fusion.1), channel_id=1, source_target_pairs={{0,4},{4,0},{8,12},{12,8},{1,5},{5,1},{9,13},{13,9},{2,6},{6,2},{1... | collective-permute-start | bytes 1572872 | tf_op jit(solution)/shard_map/ppermute | solution.py:18
  54.9 1.9 %collective-permute-done.5.got_a = bf16[256,1024]{1,0:T(8,128)(2,1)S(1)} collective-permute-done((bf16[256,1024]{1,0:T(8,128)(2,1)}, bf16[256,1024]{1,0:T(8,128)(2,1)S(1)}, u32[]{:S(2)}, u32[]{:S(2)}) %collective-permute-start.5) | collective-permute-done | bytes 524320 | tf_op jit(solution)/shard_map/ppermute | solution.py:18
  56.8 4.2 %collective-permute-done.6.got_b = bf16[256,1024]{1,0:T(8,128)(2,1)S(1)} collective-permute-done((bf16[256,1024]{1,0:T(8,128)(2,1)}, bf16[256,1024]{1,0:T(8,128)(2,1)S(1)}, u32[]{:S(2)}, u32[]{:S(2)}) %collective-permute-start.6) | collective-permute-done | bytes 524320 | tf_op jit(solution)/shard_map/ppermute | solution.py:18
  61.0 11.3 %collective-permute-done.7.next_a = bf16[256,1024]{1,0:T(8,128)(2,1)} collective-permute-done((bf16[256,1024]{1,0:T(8,128)(2,1)}, bf16[256,1024]{1,0:T(8,128)(2,1)}, u32[]{:S(2)}, u32[]{:S(2)}) %collective-permute-start.7) | collective-permute-done | bytes 524320 | tf_op jit(solution)/shard_map/ppermute | solution.py:18
  72.3 3.7 %shard_map.76 = (bf16[256,2048]{1,0:T(8,128)(2,1)}, f32[8,64,512]{2,1,0:T(8,128)S(1)}, bf16[8,64,512]{2,1,0:T(8,128)(2,1)S(1)}) custom-call(s32[1]{0:T(128)} %bitcast.c_ref, f32[4,1,2048]{2,1,0:T(1,128)S(1)} %reshape.98.mask_ref, bf16[256,2048]{1,0:T(8,128)(2,1)S(1)} %bitcast.32, bf16[256,2048]{1,0:T(8,128)(2,1)S(1)} %convolution_convert_fusion.own_ref, ...), custom_call_target="tpu_custom_call" | custom-call | flops 4194304 | bytes 4194304 | tf_op jit(solution)/shard_map/pallas_call | solution.py:67
  76.1 3.8 %collective-permute-start.10 = (bf16[8,64,512]{2,1,0:T(8,128)(2,1)S(1)}, bf16[8,64,512]{2,1,0:T(8,128)(2,1)S(1)}, u32[]{:S(2)}, u32[]{:S(2)}) collective-permute-start(bf16[8,64,512]{2,1,0:T(8,128)(2,1)S(1)} %get-tuple-element.31), channel_id=1, source_target_pairs={{0,16},{16,0},{1,17},{17,1},{2,18},{18,2},{3,19},{19,3},{4,20},{20... | collective-permute-start | bytes 1572872 | tf_op jit(solution)/shard_map/ppermute | solution.py:18
  79.9 1.5 %collective-permute-done.10 = bf16[8,64,512]{2,1,0:T(8,128)(2,1)S(1)} collective-permute-done((bf16[8,64,512]{2,1,0:T(8,128)(2,1)S(1)}, bf16[8,64,512]{2,1,0:T(8,128)(2,1)S(1)}, u32[]{:S(2)}, u32[]{:S(2)}) %collective-permute-start.10) | collective-permute-done | bytes 524320 | tf_op jit(solution)/shard_map/ppermute | solution.py:18
  81.6 26.5 %all_to_all.10 = bf16[8,64,512]{2,1,0:T(8,128)(2,1)S(1)} all-to-all(bf16[8,64,512]{2,1,0:T(8,128)(2,1)S(1)} %add_convert_fusion), channel_id=1, replica_groups=mesh['z'=8,'yh'=2,'c'=2,'dp'=4,'t'=4] {'z'}, dimensions={0} | all-to-all | bytes 1048576 | tf_op jit(solution)/shard_map/all_to_all | solution.py:182
  108.2 3.3 %collective-permute-start.11 = (f32[64,512]{1,0:T(8,128)S(1)}, f32[64,512]{1,0:T(8,128)S(1)}, u32[]{:S(2)}, u32[]{:S(2)}) collective-permute-start(f32[64,512]{1,0:T(8,128)S(1)} %convert_reduce_fusion.mine_ref), channel_id=1, source_target_pairs={{0,32},{32,0},{1,33},{33,1},{2,34},{34,2},{3,35},{35,3},{4,36},{36... | collective-permute-start | bytes 393224 | tf_op jit(solution)/shard_map/ppermute | solution.py:18
  111.5 7.2 %collective-permute-done.11.peer_ref = f32[64,512]{1,0:T(8,128)S(1)} collective-permute-done((f32[64,512]{1,0:T(8,128)S(1)}, f32[64,512]{1,0:T(8,128)S(1)}, u32[]{:S(2)}, u32[]{:S(2)}) %collective-permute-start.11) | collective-permute-done | bytes 131104 | tf_op jit(solution)/shard_map/ppermute | solution.py:18
  118.6 0.8 shard_map.77
  119.4 18.1 %all_to_all.11.mine_ref = bf16[8,64,512]{2,1,0:T(8,128)(2,1)S(1)} all-to-all(bf16[8,64,512]{2,1,0:T(8,128)(2,1)S(1)} %get-tuple-element.34), channel_id=1, replica_groups=mesh['z'=8,'yh'=2,'c'=2,'dp'=4,'t'=4] {'z'}, dimensions={0} | all-to-all | bytes 1048576 | tf_op jit(solution)/shard_map/all_to_all | solution.py:185
  137.6 5.6 %collective-permute-start.12 = (bf16[8,64,512]{2,1,0:T(8,128)(2,1)S(1)}, bf16[8,64,512]{2,1,0:T(8,128)(2,1)S(1)}, u32[]{:S(2)}, u32[]{:S(2)}) collective-permute-start(bf16[8,64,512]{2,1,0:T(8,128)(2,1)S(1)} %all_to_all.11.mine_ref), channel_id=1, source_target_pairs={{0,16},{16,0},{1,17},{17,1},{2,18},{18,2},{3,19},{19,3},{4,20},{20... | collective-permute-start | bytes 1572872 | tf_op jit(solution)/shard_map/ppermute | solution.py:18
  143.1 1.5 %collective-permute-done.12.other_ref = bf16[8,64,512]{2,1,0:T(8,128)(2,1)S(1)} collective-permute-done((bf16[8,64,512]{2,1,0:T(8,128)(2,1)S(1)}, bf16[8,64,512]{2,1,0:T(8,128)(2,1)S(1)}, u32[]{:S(2)}, u32[]{:S(2)}) %collective-permute-start.12) | collective-permute-done | bytes 524320 | tf_op jit(solution)/shard_map/ppermute | solution.py:18
  144.7 1.5 %shard_map.78 = bf16[256,2048]{1,0:T(8,128)(2,1)} custom-call(s32[1]{0:T(128)} %bitcast.c_ref, bf16[8,64,512]{2,1,0:T(8,128)(2,1)S(1)} %all_to_all.11.mine_ref, bf16[8,64,512]{2,1,0:T(8,128)(2,1)S(1)} %collective-permute-done.12.other_ref), custom_call_target="tpu_custom_call" | custom-call | flops 2097152 | bytes 2097152 | tf_op jit(solution)/shard_map/pallas_call | solution.py:120
  (26 shorter events, 3.9 us)
Async XLA Ops:
  0.6 29.1 %copy-start.1 = (bf16[512,2048]{1,0:T(8,128)(2,1)S(1)}, bf16[512,2048]{1,0:T(8,128)(2,1)}, u32[]{:S(2)}) copy-start(bf16[512,2048]{1,0:T(8,128)(2,1)} %param.6) | copy-start | bytes 6291460
  0.6 13.0 %collective-permute-start.1 = (bf16[512,256]{1,0:T(8,128)(2,1)}, bf16[512,256]{1,0:T(8,128)(2,1)S(1)}, u32[]{:S(2)}, u32[]{:S(2)}) collective-permute-start(bf16[512,256]{1,0:T(8,128)(2,1)} %param.5), channel_id=1, source_target_pairs={{0,2},{1,3},{2,0},{3,1},{4,6},{5,7},{6,4},{7,5},{8,10},{9,11},{10,... | collective-permute-start | bytes 786440 | tf_op jit(solution)/shard_map/ppermute | solution.py:18
  2.7 20.7 %collective-permute-start = (bf16[512,256]{1,0:T(8,128)(2,1)}, bf16[512,256]{1,0:T(8,128)(2,1)S(1)}, u32[]{:S(2)}, u32[]{:S(2)}) collective-permute-start(bf16[512,256]{1,0:T(8,128)(2,1)} %param.5), channel_id=1, source_target_pairs={{0,1},{1,0},{2,3},{3,2},{4,5},{5,4},{6,7},{7,6},{8,9},{9,8},{10,11... | collective-permute-start | bytes 786440 | tf_op jit(solution)/shard_map/ppermute | solution.py:18
  7.1 16.3 %collective-permute-start.3 = (f32[64,256]{1,0:T(8,128)S(1)}, f32[64,256]{1,0:T(8,128)S(1)}, u32[]{:S(2)}, u32[]{:S(2)}) collective-permute-start(f32[64,256]{1,0:T(8,128)S(1)} %reshape.96), channel_id=1, source_target_pairs={{0,32},{32,0},{1,33},{33,1},{2,34},{34,2},{3,35},{35,3},{4,36},{36... | collective-permute-start | bytes 196616 | tf_op jit(solution)/shard_map/ppermute | solution.py:18
  13.7 14.9 %collective-permute-start.2 = (bf16[512,256]{1,0:T(8,128)(2,1)S(1)}, bf16[512,256]{1,0:T(8,128)(2,1)S(1)}, u32[]{:S(2)}, u32[]{:S(2)}) collective-permute-start(bf16[512,256]{1,0:T(8,128)(2,1)S(1)} %collective-permute-done.1), channel_id=1, source_target_pairs={{0,1},{1,0},{2,3},{3,2},{4,5},{5,4},{6,7},{7,6},{8,9},{9,8},{10,11... | collective-permute-start | bytes 786440 | tf_op jit(solution)/shard_map/ppermute | solution.py:18
  30.6 16.4 %collective-permute-start.4 = (bf16[256,1024]{1,0:T(8,128)(2,1)S(1)}, bf16[256,1024]{1,0:T(8,128)(2,1)S(1)}, u32[]{:S(2)}, u32[]{:S(2)}) collective-permute-start(bf16[256,1024]{1,0:T(8,128)(2,1)S(1)} %convolution_convert_fusion.6), channel_id=1, source_target_pairs={{0,4},{4,0},{8,12},{12,8},{1,5},{5,1},{9,13},{13,9},{2,6},{6,2},{1... | collective-permute-start | bytes 1572872 | tf_op jit(solution)/shard_map/ppermute | solution.py:18
  34.3 17.7 %collective-permute-start.8 = (bf16[256,1024]{1,0:T(8,128)(2,1)S(1)}, bf16[256,1024]{1,0:T(8,128)(2,1)S(1)}, u32[]{:S(2)}, u32[]{:S(2)}) collective-permute-start(bf16[256,1024]{1,0:T(8,128)(2,1)S(1)} %convolution_convert_fusion.5), channel_id=1, source_target_pairs={{0,12},{4,8},{8,4},{12,0},{1,13},{5,9},{9,5},{13,1},{2,14},{6,10},... | collective-permute-start | bytes 1572872 | tf_op jit(solution)/shard_map/ppermute | solution.py:18
  40.5 5.5 %copy-start.2 = (bf16[512,2048]{1,0:T(8,128)(2,1)S(1)}, bf16[512,2048]{1,0:T(8,128)(2,1)}, u32[]{:S(2)}) copy-start(bf16[512,2048]{1,0:T(8,128)(2,1)} %param.6) | copy-start | bytes 6291460
  41.3 15.5 %collective-permute-start.5 = (bf16[256,1024]{1,0:T(8,128)(2,1)}, bf16[256,1024]{1,0:T(8,128)(2,1)S(1)}, u32[]{:S(2)}, u32[]{:S(2)}) collective-permute-start(bf16[256,1024]{1,0:T(8,128)(2,1)} %convolution_convert_fusion.2), channel_id=1, source_target_pairs={{0,4},{4,0},{8,12},{12,8},{1,5},{5,1},{9,13},{13,9},{2,6},{6,2},{1... | collective-permute-start | bytes 1572872 | tf_op jit(solution)/shard_map/ppermute | solution.py:18
  43.5 17.5 %collective-permute-start.6 = (bf16[256,1024]{1,0:T(8,128)(2,1)}, bf16[256,1024]{1,0:T(8,128)(2,1)S(1)}, u32[]{:S(2)}, u32[]{:S(2)}) collective-permute-start(bf16[256,1024]{1,0:T(8,128)(2,1)} %convolution_convert_fusion.1), channel_id=1, source_target_pairs={{0,12},{4,8},{8,4},{12,0},{1,13},{5,9},{9,5},{13,1},{2,14},{6,10},... | collective-permute-start | bytes 1572872 | tf_op jit(solution)/shard_map/ppermute | solution.py:18
  47.0 25.4 %copy-start = (bf16[1,256,2048]{2,1,0:T(8,128)(2,1)S(1)}, bf16[1,256,2048]{2,1,0:T(8,128)(2,1)}, u32[]{:S(2)}) copy-start(bf16[1,256,2048]{2,1,0:T(8,128)(2,1)} %param.7) | copy-start | bytes 3145732
  48.0 24.3 %collective-permute-start.7 = (bf16[256,1024]{1,0:T(8,128)(2,1)}, bf16[256,1024]{1,0:T(8,128)(2,1)}, u32[]{:S(2)}, u32[]{:S(2)}) collective-permute-start(bf16[256,1024]{1,0:T(8,128)(2,1)} %add_convert_fusion.2), channel_id=1, source_target_pairs={{0,12},{4,8},{8,4},{12,0},{1,13},{5,9},{9,5},{13,1},{2,14},{6,10},... | collective-permute-start | bytes 1572872 | tf_op jit(solution)/shard_map/ppermute | solution.py:18
  53.0 19.4 %collective-permute-start.9 = (bf16[256,1024]{1,0:T(8,128)(2,1)}, bf16[256,1024]{1,0:T(8,128)(2,1)}, u32[]{:S(2)}, u32[]{:S(2)}) collective-permute-start(bf16[256,1024]{1,0:T(8,128)(2,1)} %add_convert_fusion.1), channel_id=1, source_target_pairs={{0,4},{4,0},{8,12},{12,8},{1,5},{5,1},{9,13},{13,9},{2,6},{6,2},{1... | collective-permute-start | bytes 1572872 | tf_op jit(solution)/shard_map/ppermute | solution.py:18
  76.1 5.4 %collective-permute-start.10 = (bf16[8,64,512]{2,1,0:T(8,128)(2,1)S(1)}, bf16[8,64,512]{2,1,0:T(8,128)(2,1)S(1)}, u32[]{:S(2)}, u32[]{:S(2)}) collective-permute-start(bf16[8,64,512]{2,1,0:T(8,128)(2,1)S(1)} %get-tuple-element.31), channel_id=1, source_target_pairs={{0,16},{16,0},{1,17},{17,1},{2,18},{18,2},{3,19},{19,3},{4,20},{20... | collective-permute-start | bytes 1572872 | tf_op jit(solution)/shard_map/ppermute | solution.py:18
  108.2 10.5 %collective-permute-start.11 = (f32[64,512]{1,0:T(8,128)S(1)}, f32[64,512]{1,0:T(8,128)S(1)}, u32[]{:S(2)}, u32[]{:S(2)}) collective-permute-start(f32[64,512]{1,0:T(8,128)S(1)} %convert_reduce_fusion.mine_ref), channel_id=1, source_target_pairs={{0,32},{32,0},{1,33},{33,1},{2,34},{34,2},{3,35},{35,3},{4,36},{36... | collective-permute-start | bytes 393224 | tf_op jit(solution)/shard_map/ppermute | solution.py:18
  137.6 7.1 %collective-permute-start.12 = (bf16[8,64,512]{2,1,0:T(8,128)(2,1)S(1)}, bf16[8,64,512]{2,1,0:T(8,128)(2,1)S(1)}, u32[]{:S(2)}, u32[]{:S(2)}) collective-permute-start(bf16[8,64,512]{2,1,0:T(8,128)(2,1)S(1)} %all_to_all.11.mine_ref), channel_id=1, source_target_pairs={{0,16},{16,0},{1,17},{17,1},{2,18},{18,2},{3,19},{19,3},{4,20},{20... | collective-permute-start | bytes 1572872 | tf_op jit(solution)/shard_map/ppermute | solution.py:18

commit v6 on v5

v6 whole, which is shorter than its diff:
```python
import functools

import jax
import jax.numpy as jnp
from jax import lax
from jax.experimental import pallas as pl
from jax.experimental.pallas import tpu as pltpu
from jax.sharding import Mesh, PartitionSpec as P

BLK = 64
LANES = 128
DECAY = 0.9
NODES = 32
F32, BF16 = jnp.float32, jnp.bfloat16
NODE = ("z", "yh", "c")
SHAPE = (8, 2, 2, 4, 4)
VMEM_LIMIT = 32 * 1024 * 1024


def swap(value, axis, flip, size):
    return lax.ppermute(value, axis, [(i, i ^ flip) for i in range(size)])


def kernel_call(body, grid, ins, outs, out_shape, cost):
    return pl.pallas_call(
        body,
        grid=grid,
        in_specs=ins,
        out_specs=outs,
        out_shape=out_shape,
        compiler_params=pltpu.CompilerParams(vmem_limit_bytes=VMEM_LIMIT),
        cost_estimate=pl.CostEstimate(flops=cost, bytes_accessed=cost, transcendentals=0),
    )


SMEM = pl.BlockSpec(memory_space=pltpu.SMEM)


def place_of(block):
    row, col = block // 32, block % 32
    rows = pl.ds(pl.multiple_of(row * BLK, BLK), BLK)
    return rows, pl.ds(pl.multiple_of(col // 2 * LANES, LANES), LANES), col % 2


def lane_halves():
    return lax.broadcasted_iota(jnp.int32, (BLK, LANES), 1) // BLK


def pack_kernel(picks, base, pieces, list_ref, *refs):
    mats, outs = refs[: len(picks)], refs[len(picks) :]
    upper = lane_halves() == 1
    span = 64 // 2 // pieces
    for n, k in enumerate(picks):
        for p in range(pieces):
            out_ref = outs[n * pieces + p]

            def tile(q, carry, k=k, n=n, p=p, out_ref=out_ref):
                slot = base + 2 * (p * span + q)
                sides = []
                for side in range(2):
                    rows, cols, half = place_of(list_ref[k, slot + side])
                    block = mats[n][rows, cols].astype(F32)
                    sides.append(pltpu.roll(block, (half + side) % 2 * BLK, 1))
                at = pl.ds(pl.multiple_of(q * LANES, LANES), LANES)
                out_ref[:, at] = jnp.where(upper, sides[1], sides[0]).astype(BF16)
                return carry

            lax.fori_loop(0, span, tile, 0, unroll=4)


def pack(lists, mats, picks, base, pieces):
    whole = pl.BlockSpec(memory_space=pltpu.VMEM)
    count = len(picks) * pieces
    return kernel_call(
        functools.partial(pack_kernel, picks, base, pieces),
        (),
        [SMEM] + [whole] * len(picks),
        [whole] * count,
        [jax.ShapeDtypeStruct((BLK, 64 * BLK // pieces), BF16)] * count,
        1 << 20,
    )(lists, *mats)


def unpack(list_ref, base, pieces, grad_ref):
    halves = lane_halves()
    span = 64 // 2 // len(pieces)
    for p, terms in enumerate(pieces):

        def tile(q, carry, p=p, terms=terms):
            at = pl.ds(pl.multiple_of(q * LANES, LANES), LANES)
            value = terms[0][:, at].astype(F32)
            for term in terms[1:]:
                value = value + term[:, at].astype(F32)
            for side in range(2):
                rows, cols, half = place_of(list_ref[0, base + 2 * (p * span + q) + side])
                moved = pltpu.roll(value, (half + side) % 2 * BLK, 1)
                grad_ref[rows, cols] = jnp.where(halves == half, moved, grad_ref[rows, cols])
            return carry

        lax.fori_loop(0, span, tile, 0, unroll=2)


def chosen_kernel(
    list_ref, c_ref, mask_ref, fb_ref, own_ref, got_a, got_b, next_a, next_b, mine_ref, other_ref, grad_ref
):
    row = pl.program_id(0)

    @pl.when(row == 0)
    def _():
        unpack(list_ref, 0, ((got_a, next_a), (got_b, next_b)), grad_ref)

    first = c_ref[0] == 0
    rows = pl.ds(pl.multiple_of(row * BLK, BLK), BLK)
    for h in range(2):
        for yh in range(2):
            sent = []
            for c in range(2):
                at = h * 1024 + yh * 512 + c * 256
                at = slice(at, at + 256)
                acc = own_ref[:, at].astype(F32) + grad_ref[rows, at]
                acc = fb_ref[:, at].astype(F32) + acc
                chosen = jnp.broadcast_to(mask_ref[0, :, at], acc.shape) > 0.5
                sent.append(jnp.where(chosen, acc, 0.0))
            place = slice(yh * 256, yh * 256 + 256)
            mine_ref[h, :, place] = jnp.where(first, sent[0], sent[1])
            other_ref[h, :, place] = jnp.where(first, sent[1], sent[0]).astype(BF16)


def residual_kernel(list_ref, mask_ref, fb_ref, own_ref, got_1, got_2, got_3, new_ref, grad_ref):
    row = pl.program_id(0)

    @pl.when(row == 0)
    def _():
        unpack(list_ref, 64, ((got_1, got_2, got_3),), grad_ref)

    rows = pl.ds(pl.multiple_of(row * BLK, BLK), BLK)
    for at in range(0, fb_ref.shape[1], 256):
        at = slice(at, at + 256)
        acc = own_ref[:, at].astype(F32) + grad_ref[rows, at]
        acc = fb_ref[:, at].astype(F32) + acc
        chosen = jnp.broadcast_to(mask_ref[0, :, at], acc.shape) > 0.5
        new_ref[:, at] = jnp.where(chosen, 0.0, acc).astype(BF16)


def state_call(body, scalars, mask, feedback, own, received, outs, out_shape):
    rows, cols = feedback.shape
    wide = pl.BlockSpec((BLK, cols), lambda i: (i, 0))
    line = pl.BlockSpec((1, 1, cols), lambda i: (i, 0, 0))
    packed = [pl.BlockSpec(r.shape, lambda i: (0, 0)) for r in received]
    return pl.pallas_call(
        body,
        grid=(rows // BLK,),
        in_specs=[SMEM] * len(scalars) + [line, wide, wide] + packed,
        out_specs=outs,
        out_shape=out_shape,
        scratch_shapes=[pltpu.VMEM((rows, cols), F32)],
        compiler_params=pltpu.CompilerParams(vmem_limit_bytes=VMEM_LIMIT),
        cost_estimate=pl.CostEstimate(flops=1 << 22, bytes_accessed=1 << 22, transcendentals=0),
    )(*scalars, mask, feedback, own, *received)


def chosen_sums(lists, c, mask, feedback, own, *received):
    slab = pl.BlockSpec((2, BLK, 512), lambda i: (i, 0, 0))
    shape = (8, BLK, 512)
    return state_call(
        chosen_kernel, (lists, c), mask, feedback, own, received, [slab, slab],
        [jax.ShapeDtypeStruct(shape, F32), jax.ShapeDtypeStruct(shape, BF16)],
    )


def residual(lists, mask, feedback, own, *received):
    rows, cols = feedback.shape
    return state_call(
        residual_kernel, (lists,), mask, feedback, own, received,
        pl.BlockSpec((BLK, cols), lambda i: (i, 0)), jax.ShapeDtypeStruct((rows, cols), BF16),
    )


def owner_kernel(yh_ref, mine_ref, peer_ref, moment_ref, new_ref, step_ref):
    mean = (mine_ref[...] + peer_ref[...]) * (1.0 / NODES)
    moment = DECAY * moment_ref[...] + mean
    step = (mean + DECAY * moment).astype(BF16)
    for z in range(8):
        step_ref[z] = step
    own = jnp.where(yh_ref[0] == 0, moment[:, :256], moment[:, 256:])
    for b in range(4):
        new_ref[b] = own[:, b * BLK : (b + 1) * BLK]


def owner_update(yh, mine, peer, moment):
    whole = pl.BlockSpec(memory_space=pltpu.VMEM)
    return kernel_call(
        owner_kernel,
        (),
        [SMEM, whole, whole, whole],
        [whole, whole],
        [
            jax.ShapeDtypeStruct((4, BLK, BLK), F32),
            jax.ShapeDtypeStruct((8, BLK, 512), BF16),
        ],
        8 * BLK * 512,
    )(yh, mine, peer, moment)


def assemble_kernel(c_ref, mine_ref, other_ref, out_ref):
    first = c_ref[0] == 0
    for h in range(2):
        for yh in range(2):
            place = slice(yh * 256, yh * 256 + 256)
            mine, other = mine_ref[h, :, place], other_ref[h, :, place]
            at = h * 1024 + yh * 512
            out_ref[:, at : at + 256] = jnp.where(first, mine, other)
            out_ref[:, at + 256 : at + 512] = jnp.where(first, other, mine)


def assemble(c, mine, other, rows, cols):
    slab = pl.BlockSpec((2, BLK, 512), lambda i: (i, 0, 0))
    return kernel_call(
        assemble_kernel,
        (rows // BLK,),
        [SMEM, slab, slab],
        pl.BlockSpec((BLK, cols), lambda i: (i, 0)),
        jax.ShapeDtypeStruct((rows, cols), BF16),
        4 * rows * cols,
    )(c, mine, other)


def block_lists(chosen, count):
    near = swap(chosen, "dp", 1, 4)
    across = swap(jnp.stack([chosen, near]), "dp", 3, 4)
    lists = jnp.stack([chosen, near, across[1], across[0]])
    blocks = jnp.arange(count, dtype=jnp.int32)
    left = jnp.all(lists[:, :, None] != blocks, axis=1)
    before = blocks[:, None] < blocks[None, :]
    rank = jnp.sum(jnp.where(left[:, :, None] & before, 1, 0), axis=1)
    slots = jnp.arange(count // 2, dtype=jnp.int32)
    hit = left[:, None, :] & (rank[:, None, :] == slots[None, :, None])
    others = jnp.sum(jnp.where(hit, blocks, 0), axis=2)
    return jnp.concatenate([lists, others], axis=1)


def gather_hidden(hidden):
    far = swap(hidden, "t", 2, 4)
    near = swap(hidden, "t", 1, 4)
    return hidden, near, far, swap(far, "t", 1, 4)


def plus(kept, got):
    return (kept.astype(F32) + got.astype(F32)).astype(BF16)


def as_matrix(blocks):
    return blocks.transpose(1, 0, 2).reshape(BLK, -1)


def local(hidden, cotangent, feedback, chosen, momentum):
    rows, cols = feedback.shape[1:]
    rows_blk, cols_blk = rows // BLK, cols // BLK
    c, yh = lax.axis_index("c"), lax.axis_index("yh")
    at_c, at_yh = c.astype(jnp.int32).reshape(1), yh.astype(jnp.int32).reshape(1)
    block_of = (
        jnp.arange(rows_blk, dtype=jnp.int32)[:, None] * cols_blk
        + jnp.arange(cols, dtype=jnp.int32)[None, :] // BLK
    )
    mask = jnp.any(chosen.reshape(-1, 1, 1) == block_of[None], axis=0).astype(F32)
    moment = as_matrix(momentum[0, 0])
    far_moment = swap(moment, "yh", 1, 2)
    mask = mask[:, None]
    lists = block_lists(chosen.reshape(-1), rows_blk * cols_blk)
    *shards, far_moment, lists = lax.optimization_barrier(
        (*gather_hidden(hidden), far_moment, lists)
    )
    shards = jnp.stack(shards)
    moment = jnp.where(
        yh == 0, jnp.concatenate([moment, far_moment], 1), jnp.concatenate([far_moment, moment], 1)
    )
    d, t = lax.axis_index("dp"), lax.axis_index("t")

    def product(flip, shards):
        part = lax.dynamic_index_in_dim(shards, t ^ d ^ flip, 0, keepdims=False)
        return lax.dot_general(
            part, cotangent, (((0,), (0,)), ((), ())), preferred_element_type=F32
        ).astype(BF16)

    far_rows = product(2, shards)
    give_a, give_b = pack(lists, (far_rows,), (2,), 0, 2)
    far_a, far_b = swap(give_a, "dp", 1, 4), swap(give_b, "dp", 3, 4)
    shards, give_a, give_b = lax.optimization_barrier((shards, give_a, give_b))
    near_rows, side_rows = product(1, shards), product(3, shards)
    near_a, near_b, side_a, side_b = pack(lists, (near_rows, side_rows), (1, 3), 0, 2)
    got_a, got_b = swap(near_a, "dp", 1, 4), swap(side_b, "dp", 3, 4)
    own = product(0, shards)
    far_a, near_b, side_a, own, mask = lax.optimization_barrier((far_a, near_b, side_a, own, mask))
    next_a = swap(plus(side_a, far_a), "dp", 3, 4)
    next_b = swap(plus(near_b, far_b), "dp", 1, 4)
    mine, other = chosen_sums(
        lists, at_c, mask, feedback[0], own, got_a, got_b, next_a, next_b
    )
    pair = (mine + swap(other, "c", 1, 2).astype(F32)).astype(BF16)
    near_rows, far_rows, side_rows, _ = lax.optimization_barrier(
        (near_rows, far_rows, side_rows, pair)
    )
    left = pack(lists, (near_rows, far_rows, side_rows), (1, 2, 3), 64, 1)
    left = [swap(part, "dp", flip, 4) for flip, part in zip((1, 2, 3), left)]
    got = lax.all_to_all(pair, "z", 0, 0, tiled=True)
    near = jnp.sum(got.astype(F32), axis=0)
    momentum_new, copies = owner_update(at_yh, near, swap(near, "yh", 1, 2), moment)
    every = lax.all_to_all(copies, "z", 0, 0, tiled=True)
    *left, _ = lax.optimization_barrier((*left, copies))
    feedback_new = residual(lists, mask, feedback[0], own, *left)
    step = assemble(at_c, every, swap(every, "c", 1, 2), rows, cols)
    return feedback_new[None], momentum_new[None, None], step


def solution(mesh):
    fine = Mesh(mesh.devices.reshape(SHAPE), (*NODE, "dp", "t"))
    tokens = P((*NODE, "dp"), "t")
    return jax.shard_map(
        local,
        mesh=fine,
        in_specs=(
            tokens,
            tokens,
            P(NODE, "dp", "t"),
            P(NODE, "dp", "t", None),
            P("dp", "t", NODE, None, None),
        ),
        out_specs=(P(NODE, "dp", "t"), P("dp", "t", NODE, None, None), P("dp", "t")),
        check_vma=False,
    )
```

time: 147 us -> 182 us (1.24)
  the two profiles are of different devices: /device:TPU:17 before, /device:TPU:1 now
where the time goes in v6:
time: 182 us; the launch traced here: 180 us
  starting transfers between devices  71.8 us (39%)
  waiting for transfers between devices  35.2 us (19%)
  Pallas kernels  26.5 us (15%)
  blocking collectives  26.5 us (15%)
  local copies, waits for them, and re-layouts  8.12 us (4%)
  other arithmetic  7.39 us (4%)
  matrix products  2.95 us (2%)
    ppermute x18, starting transfers between devices, swap(): return lax.ppermute(value, axis, [(i, i ^ flip) for i in range(size)])  67.6 us
    ppermute x18, waiting for transfers between devices, swap(): return lax.ppermute(value, axis, [(i, i ^ flip) for i in range(size)])  35.2 us
    all_to_all x1, blocking collectives, local(): got = lax.all_to_all(pair, 'z', 0, 0, tiled=True)  26.5 us
    pallas_call x3, Pallas kernels, pack(): kernel_call(functools.partial(pack_kernel, picks, base, pieces), (), [SME...  13.1 us
    pallas_call x2, Pallas kernels, state_call(): pl.pallas_call(body, grid=(rows // BLK,), in_specs=[SMEM] * len(scalars)...  9.35 us
    unnamed x22, local copies, waits for them, and re-layouts  6.96 us
    all_to_all x1, starting transfers between devices, local(): every = lax.all_to_all(copies, 'z', 0, 0, tiled=True)  4.15 us
  transfers between devices with their start and end apart: 19, of which 8 were waited for; matrix products, arithmetic and copies ran while one was open for 5% of the time, Pallas kernels for 9%

profile of v6, /device:TPU:1, one launch (start us, length us, event | category | flops | bytes accessed | tf_op | source)
XLA Modules:
  0.0 179.5 jit_solution(18349981916474162532)
XLA Ops:
  0.6 4.2 %collective-permute-start = (bf16[512,256]{1,0:T(8,128)(2,1)}, bf16[512,256]{1,0:T(8,128)(2,1)S(1)}, u32[]{:S(2)}, u32[]{:S(2)}) collective-permute-start(bf16[512,256]{1,0:T(8,128)(2,1)} %param.5), channel_id=1, source_target_pairs={{0,1},{1,0},{2,3},{3,2},{4,5},{5,4},{6,7},{7,6},{8,9},{9,8},{10,11... | collective-permute-start | bytes 786440 | tf_op jit(solution)/shard_map/ppermute | solution.py:21
  4.8 4.2 %collective-permute-start.1 = (bf16[512,256]{1,0:T(8,128)(2,1)}, bf16[512,256]{1,0:T(8,128)(2,1)S(1)}, u32[]{:S(2)}, u32[]{:S(2)}) collective-permute-start(bf16[512,256]{1,0:T(8,128)(2,1)} %param.5), channel_id=1, source_target_pairs={{0,2},{1,3},{2,0},{3,1},{4,6},{5,7},{6,4},{7,5},{8,10},{9,11},{10,... | collective-permute-start | bytes 786440 | tf_op jit(solution)/shard_map/ppermute | solution.py:21
  9.0 3.1 %collective-permute-start.4 = (s32[64]{0:T(128)}, s32[64]{0:T(128)S(1)}, u32[]{:S(2)}, u32[]{:S(2)}) collective-permute-start(s32[64]{0:T(128)} %bitcast.39), channel_id=1, source_target_pairs={{0,4},{4,0},{8,12},{12,8},{1,5},{5,1},{9,13},{13,9},{2,6},{6,2},{1... | collective-permute-start | bytes 776 | tf_op jit(solution)/shard_map/ppermute | solution.py:21
  13.3 4.7 %collective-permute-start.3 = (f32[64,256]{1,0:T(8,128)S(1)}, f32[64,256]{1,0:T(8,128)S(1)}, u32[]{:S(2)}, u32[]{:S(2)}) collective-permute-start(f32[64,256]{1,0:T(8,128)S(1)} %reshape.114), channel_id=1, source_target_pairs={{0,32},{32,0},{1,33},{33,1},{2,34},{34,2},{3,35},{35,3},{4,36},{36... | collective-permute-start | bytes 196616 | tf_op jit(solution)/shard_map/ppermute | solution.py:21
  19.9 3.7 %collective-permute-start.5 = (s32[2,64]{1,0:T(2,128)S(1)}, s32[2,64]{1,0:T(2,128)S(1)}, u32[]{:S(2)}, u32[]{:S(2)}) collective-permute-start(s32[2,64]{1,0:T(2,128)S(1)} %pad_add_fusion.2), channel_id=1, source_target_pairs={{0,12},{4,8},{8,4},{12,0},{1,13},{5,9},{9,5},{13,1},{2,14},{6,10},... | collective-permute-start | bytes 1544 | tf_op jit(solution)/shard_map/ppermute | solution.py:21
  23.7 1.7 collective-permute-done.5
  26.2 3.3 %collective-permute-start.2 = (bf16[512,256]{1,0:T(8,128)(2,1)S(1)}, bf16[512,256]{1,0:T(8,128)(2,1)S(1)}, u32[]{:S(2)}, u32[]{:S(2)}) collective-permute-start(bf16[512,256]{1,0:T(8,128)(2,1)S(1)} %collective-permute-done.1), channel_id=1, source_target_pairs={{0,1},{1,0},{2,3},{3,2},{4,5},{5,4},{6,7},{7,6},{8,9},{9,8},{10,11... | collective-permute-start | bytes 786440 | tf_op jit(solution)/shard_map/ppermute | solution.py:21
  30.5 2.8 %collective-permute-done.2 = bf16[512,256]{1,0:T(8,128)(2,1)S(1)} collective-permute-done((bf16[512,256]{1,0:T(8,128)(2,1)S(1)}, bf16[512,256]{1,0:T(8,128)(2,1)S(1)}, u32[]{:S(2)}, u32[]{:S(2)}) %collective-permute-start.2) | collective-permute-done | bytes 262176 | tf_op jit(solution)/shard_map/ppermute | solution.py:21
  35.2 2.2 %shard_map.76 = (bf16[64,2048]{1,0:T(8,128)(2,1)S(1)}, bf16[64,2048]{1,0:T(8,128)(2,1)S(1)}) custom-call(s32[4,128]{1,0:T(4,128)S(1)} %pad_add_fusion.1.list_ref, bf16[256,2048]{1,0:T(8,128)(2,1)S(1)} %convolution_convert_fusion.3.refs_0_.refs_1_), custom_call_target="tpu_custom_call" | custom-call | flops 1048576 | bytes 1048576 | tf_op jit(solution)/shard_map/pallas_call | solution.py:74
  37.3 1.9 %collective-permute-start.6 = (bf16[64,2048]{1,0:T(8,128)(2,1)S(1)}, bf16[64,2048]{1,0:T(8,128)(2,1)S(1)}, u32[]{:S(2)}, u32[]{:S(2)}) collective-permute-start(bf16[64,2048]{1,0:T(8,128)(2,1)S(1)} %get-tuple-element.39), channel_id=1, source_target_pairs={{0,4},{4,0},{8,12},{12,8},{1,5},{5,1},{9,13},{13,9},{2,6},{6,2},{1... | collective-permute-start | bytes 786440 | tf_op jit(solution)/shard_map/ppermute | solution.py:21
  39.3 3.7 %collective-permute-start.10 = (bf16[64,2048]{1,0:T(8,128)(2,1)S(1)}, bf16[64,2048]{1,0:T(8,128)(2,1)S(1)}, u32[]{:S(2)}, u32[]{:S(2)}) collective-permute-start(bf16[64,2048]{1,0:T(8,128)(2,1)S(1)} %get-tuple-element.40), channel_id=1, source_target_pairs={{0,12},{4,8},{8,4},{12,0},{1,13},{5,9},{9,5},{13,1},{2,14},{6,10},... | collective-permute-start | bytes 786440 | tf_op jit(solution)/shard_map/ppermute | solution.py:21
  44.5 4.5 %shard_map.77 = (bf16[64,2048]{1,0:T(8,128)(2,1)}, bf16[64,2048]{1,0:T(8,128)(2,1)S(1)}, bf16[64,2048]{1,0:T(8,128)(2,1)S(1)}, bf16[64,2048]{1,0:T(8,128)(2,1)}) custom-call(s32[4,128]{1,0:T(4,128)S(1)} %pad_add_fusion.1.list_ref, bf16[256,2048]{1,0:T(8,128)(2,1)S(1)} %convolution_convert_fusion.2.refs_0_, ...), custom_call_target="tpu_custom_call" | custom-call | flops 1048576 | bytes 1048576 | tf_op jit(solution)/shard_map/pallas_call | solution.py:74
  49.0 2.7 %collective-permute-start.7 = (bf16[64,2048]{1,0:T(8,128)(2,1)}, bf16[64,2048]{1,0:T(8,128)(2,1)}, u32[]{:S(2)}, u32[]{:S(2)}) collective-permute-start(bf16[64,2048]{1,0:T(8,128)(2,1)} %get-tuple-element.46), channel_id=1, source_target_pairs={{0,4},{4,0},{8,12},{12,8},{1,5},{5,1},{9,13},{13,9},{2,6},{6,2},{1... | collective-permute-start | bytes 786440 | tf_op jit(solution)/shard_map/ppermute | solution.py:21
  51.8 2.8 %collective-permute-start.8 = (bf16[64,2048]{1,0:T(8,128)(2,1)}, bf16[64,2048]{1,0:T(8,128)(2,1)}, u32[]{:S(2)}, u32[]{:S(2)}) collective-permute-start(bf16[64,2048]{1,0:T(8,128)(2,1)} %get-tuple-element.47), channel_id=1, source_target_pairs={{0,12},{4,8},{8,4},{12,0},{1,13},{5,9},{9,5},{13,1},{2,14},{6,10},... | collective-permute-start | bytes 786440 | tf_op jit(solution)/shard_map/ppermute | solution.py:21
  56.1 3.7 %collective-permute-start.9 = (bf16[64,2048]{1,0:T(8,128)(2,1)}, bf16[64,2048]{1,0:T(8,128)(2,1)}, u32[]{:S(2)}, u32[]{:S(2)}) collective-permute-start(bf16[64,2048]{1,0:T(8,128)(2,1)} %add_convert_fusion.2), channel_id=1, source_target_pairs={{0,12},{4,8},{8,4},{12,0},{1,13},{5,9},{9,5},{13,1},{2,14},{6,10},... | collective-permute-start | bytes 786440 | tf_op jit(solution)/shard_map/ppermute | solution.py:21
  60.6 1.9 %collective-permute-start.11 = (bf16[64,2048]{1,0:T(8,128)(2,1)}, bf16[64,2048]{1,0:T(8,128)(2,1)}, u32[]{:S(2)}, u32[]{:S(2)}) collective-permute-start(bf16[64,2048]{1,0:T(8,128)(2,1)} %add_convert_fusion.1), channel_id=1, source_target_pairs={{0,4},{4,0},{8,12},{12,8},{1,5},{5,1},{9,13},{13,9},{2,6},{6,2},{1... | collective-permute-start | bytes 786440 | tf_op jit(solution)/shard_map/ppermute | solution.py:21
  62.5 4.2 %collective-permute-done.9.next_a = bf16[64,2048]{1,0:T(8,128)(2,1)} collective-permute-done((bf16[64,2048]{1,0:T(8,128)(2,1)}, bf16[64,2048]{1,0:T(8,128)(2,1)}, u32[]{:S(2)}, u32[]{:S(2)}) %collective-permute-start.9) | collective-permute-done | bytes 262176 | tf_op jit(solution)/shard_map/ppermute | solution.py:21
  69.5 4.0 %shard_map.78 = (f32[8,64,512]{2,1,0:T(8,128)S(1)}, bf16[8,64,512]{2,1,0:T(8,128)(2,1)S(1)}) custom-call(s32[4,128]{1,0:T(4,128)S(1)} %pad_add_fusion.1.list_ref, s32[1]{0:T(128)} %bitcast.14.c_ref, f32[4,1,2048]{2,1,0:T(1,128)S(1)} %reshape.118.mask_ref, bf16[256,2048]{1,0:T(8,128)(2,1)S(1)} %bitcast.31, ...), custom_call_target="tpu_custom_call" | custom-call | flops 4194304 | bytes 4194304 | tf_op jit(solution)/shard_map/pallas_call | solution.py:150
  73.6 8.3 %collective-permute-start.12 = (bf16[8,64,512]{2,1,0:T(8,128)(2,1)S(1)}, bf16[8,64,512]{2,1,0:T(8,128)(2,1)S(1)}, u32[]{:S(2)}, u32[]{:S(2)}) collective-permute-start(bf16[8,64,512]{2,1,0:T(8,128)(2,1)S(1)} %get-tuple-element.52), channel_id=1, source_target_pairs={{0,16},{16,0},{1,17},{17,1},{2,18},{18,2},{3,19},{19,3},{4,20},{20... | collective-permute-start | bytes 1572872 | tf_op jit(solution)/shard_map/ppermute | solution.py:21
  83.5 26.5 %all_to_all.10 = bf16[8,64,512]{2,1,0:T(8,128)(2,1)S(1)} all-to-all(bf16[8,64,512]{2,1,0:T(8,128)(2,1)S(1)} %add_convert_fusion), channel_id=1, replica_groups=mesh['z'=8,'yh'=2,'c'=2,'dp'=4,'t'=4] {'z'}, dimensions={0} | all-to-all | bytes 1048576 | tf_op jit(solution)/shard_map/all_to_all | solution.py:305
  110.1 4.4 %collective-permute-start.16 = (f32[64,512]{1,0:T(8,128)S(1)}, f32[64,512]{1,0:T(8,128)S(1)}, u32[]{:S(2)}, u32[]{:S(2)}) collective-permute-start(f32[64,512]{1,0:T(8,128)S(1)} %convert_reduce_fusion.mine_ref), channel_id=1, source_target_pairs={{0,32},{32,0},{1,33},{33,1},{2,34},{34,2},{3,35},{35,3},{4,36},{36... | collective-permute-start | bytes 393224 | tf_op jit(solution)/shard_map/ppermute | solution.py:21
  115.5 6.6 %collective-permute-done.16.peer_ref = f32[64,512]{1,0:T(8,128)S(1)} collective-permute-done((f32[64,512]{1,0:T(8,128)S(1)}, f32[64,512]{1,0:T(8,128)S(1)}, u32[]{:S(2)}, u32[]{:S(2)}) %collective-permute-start.16) | collective-permute-done | bytes 131104 | tf_op jit(solution)/shard_map/ppermute | solution.py:21
  123.6 4.1 %all-to-all-start.1 = ((bf16[8,64,512]{2,1,0:T(8,128)(2,1)}), bf16[8,64,512]{2,1,0:T(8,128)(2,1)}, u32[]{:S(2)}, u32[]{:S(2)}) async-start(bf16[8,64,512]{2,1,0:T(8,128)(2,1)} %copy-done.9), calls=%async_computation.1 | async-start | bytes 1048576 | tf_op jit(solution)/shard_map/all_to_all | solution.py:308
  131.5 6.4 %shard_map.79 = (bf16[64,4096]{1,0:T(8,128)(2,1)}, bf16[64,4096]{1,0:T(8,128)(2,1)}, bf16[64,4096]{1,0:T(8,128)(2,1)}) custom-call(s32[4,128]{1,0:T(4,128)S(1)} %pad_add_fusion.1.list_ref, bf16[256,2048]{1,0:T(8,128)(2,1)S(1)} %copy-done.6, bf16[256,2048]{1,0:T(8,128)(2,1)S(1)} %copy-done.2, bf16[256,2048]{1,0:T(8,128)(2,1)S(1)} %copy-done.4), custom_call_target="tpu_custom_call" | custom-call | flops 1048576 | bytes 1048576 | tf_op jit(solution)/shard_map/pallas_call | solution.py:74
  137.9 1.9 %collective-permute-start.13 = (bf16[64,4096]{1,0:T(8,128)(2,1)}, bf16[64,4096]{1,0:T(8,128)(2,1)}, u32[]{:S(2)}, u32[]{:S(2)}) collective-permute-start(bf16[64,4096]{1,0:T(8,128)(2,1)} %get-tuple-element.56), channel_id=1, source_target_pairs={{0,4},{4,0},{8,12},{12,8},{1,5},{5,1},{9,13},{13,9},{2,6},{6,2},{1... | collective-permute-start | bytes 1572872 | tf_op jit(solution)/shard_map/ppermute | solution.py:21
  139.8 3.9 %collective-permute-start.14 = (bf16[64,4096]{1,0:T(8,128)(2,1)}, bf16[64,4096]{1,0:T(8,128)(2,1)}, u32[]{:S(2)}, u32[]{:S(2)}) collective-permute-start(bf16[64,4096]{1,0:T(8,128)(2,1)} %get-tuple-element.57), channel_id=1, source_target_pairs={{0,8},{4,12},{8,0},{12,4},{1,9},{5,13},{9,1},{13,5},{2,10},{6,14},... | collective-permute-start | bytes 1572872 | tf_op jit(solution)/shard_map/ppermute | solution.py:21
  143.8 3.7 %collective-permute-start.15 = (bf16[64,4096]{1,0:T(8,128)(2,1)}, bf16[64,4096]{1,0:T(8,128)(2,1)}, u32[]{:S(2)}, u32[]{:S(2)}) collective-permute-start(bf16[64,4096]{1,0:T(8,128)(2,1)} %get-tuple-element.58), channel_id=1, source_target_pairs={{0,12},{4,8},{8,4},{12,0},{1,13},{5,9},{9,5},{13,1},{2,14},{6,10},... | collective-permute-start | bytes 1572872 | tf_op jit(solution)/shard_map/ppermute | solution.py:21
  147.5 5.3 %collective-permute-start.17 = (bf16[8,64,512]{2,1,0:T(8,128)(2,1)}, bf16[8,64,512]{2,1,0:T(8,128)(2,1)S(1)}, u32[]{:S(2)}, u32[]{:S(2)}) collective-permute-start(bf16[8,64,512]{2,1,0:T(8,128)(2,1)} %all-to-all-done.1.mine_ref), channel_id=1, source_target_pairs={{0,16},{16,0},{1,17},{17,1},{2,18},{18,2},{3,19},{19,3},{4,20},{20... | collective-permute-start | bytes 1572872 | tf_op jit(solution)/shard_map/ppermute | solution.py:21
  152.9 10.0 %collective-permute-done.14.got_2 = bf16[64,4096]{1,0:T(8,128)(2,1)} collective-permute-done((bf16[64,4096]{1,0:T(8,128)(2,1)}, bf16[64,4096]{1,0:T(8,128)(2,1)}, u32[]{:S(2)}, u32[]{:S(2)}) %collective-permute-start.14) | collective-permute-done | bytes 524320 | tf_op jit(solution)/shard_map/ppermute | solution.py:21
  162.8 6.9 %collective-permute-done.15.got_3 = bf16[64,4096]{1,0:T(8,128)(2,1)} collective-permute-done((bf16[64,4096]{1,0:T(8,128)(2,1)}, bf16[64,4096]{1,0:T(8,128)(2,1)}, u32[]{:S(2)}, u32[]{:S(2)}) %collective-permute-start.15) | collective-permute-done | bytes 524320 | tf_op jit(solution)/shard_map/ppermute | solution.py:21
  170.9 5.3 %shard_map.81 = bf16[256,2048]{1,0:T(8,128)(2,1)} custom-call(s32[4,128]{1,0:T(4,128)S(1)} %pad_add_fusion.1.list_ref, f32[4,1,2048]{2,1,0:T(1,128)S(1)} %reshape.118.mask_ref, bf16[256,2048]{1,0:T(8,128)(2,1)S(1)} %bitcast.32, bf16[256,2048]{1,0:T(8,128)(2,1)S(1)} %convolution_convert_fusion.own_ref, bf16[64,4096]{1,0:T(8,128)(2,1)} %collective-permute-done.13.got_1, ...), custom_call_target="tpu_custom_call" | custom-call | flops 4194304 | bytes 4194304 | tf_op jit(solution)/shard_map/pallas_call | solution.py:150
  176.3 3.3 %shard_map.82 = bf16[256,2048]{1,0:T(8,128)(2,1)} custom-call(s32[1]{0:T(128)} %bitcast.14.c_ref, bf16[8,64,512]{2,1,0:T(8,128)(2,1)} %all-to-all-done.1.mine_ref, bf16[8,64,512]{2,1,0:T(8,128)(2,1)S(1)} %collective-permute-done.17.other_ref), custom_call_target="tpu_custom_call" | custom-call | flops 2097152 | bytes 2097152 | tf_op jit(solution)/shard_map/pallas_call | solution.py:218
  (62 shorter events, 22.3 us)
Async XLA Ops:
  0.6 33.8 %copy-start = (bf16[512,2048]{1,0:T(8,128)(2,1)S(1)}, bf16[512,2048]{1,0:T(8,128)(2,1)}, u32[]{:S(2)}) copy-start(bf16[512,2048]{1,0:T(8,128)(2,1)} %param.6) | copy-start | bytes 6291460
  0.6 29.9 %collective-permute-start = (bf16[512,256]{1,0:T(8,128)(2,1)}, bf16[512,256]{1,0:T(8,128)(2,1)S(1)}, u32[]{:S(2)}, u32[]{:S(2)}) collective-permute-start(bf16[512,256]{1,0:T(8,128)(2,1)} %param.5), channel_id=1, source_target_pairs={{0,1},{1,0},{2,3},{3,2},{4,5},{5,4},{6,7},{7,6},{8,9},{9,8},{10,11... | collective-permute-start | bytes 786440 | tf_op jit(solution)/shard_map/ppermute | solution.py:21
  4.8 21.4 %collective-permute-start.1 = (bf16[512,256]{1,0:T(8,128)(2,1)}, bf16[512,256]{1,0:T(8,128)(2,1)S(1)}, u32[]{:S(2)}, u32[]{:S(2)}) collective-permute-start(bf16[512,256]{1,0:T(8,128)(2,1)} %param.5), channel_id=1, source_target_pairs={{0,2},{1,3},{2,0},{3,1},{4,6},{5,7},{6,4},{7,5},{8,10},{9,11},{10,... | collective-permute-start | bytes 786440 | tf_op jit(solution)/shard_map/ppermute | solution.py:21
  9.0 10.2 %collective-permute-start.4 = (s32[64]{0:T(128)}, s32[64]{0:T(128)S(1)}, u32[]{:S(2)}, u32[]{:S(2)}) collective-permute-start(s32[64]{0:T(128)} %bitcast.39), channel_id=1, source_target_pairs={{0,4},{4,0},{8,12},{12,8},{1,5},{5,1},{9,13},{13,9},{2,6},{6,2},{1... | collective-permute-start | bytes 776 | tf_op jit(solution)/shard_map/ppermute | solution.py:21
  13.3 17.2 %collective-permute-start.3 = (f32[64,256]{1,0:T(8,128)S(1)}, f32[64,256]{1,0:T(8,128)S(1)}, u32[]{:S(2)}, u32[]{:S(2)}) collective-permute-start(f32[64,256]{1,0:T(8,128)S(1)} %reshape.114), channel_id=1, source_target_pairs={{0,32},{32,0},{1,33},{33,1},{2,34},{34,2},{3,35},{35,3},{4,36},{36... | collective-permute-start | bytes 196616 | tf_op jit(solution)/shard_map/ppermute | solution.py:21
  19.9 5.5 %collective-permute-start.5 = (s32[2,64]{1,0:T(2,128)S(1)}, s32[2,64]{1,0:T(2,128)S(1)}, u32[]{:S(2)}, u32[]{:S(2)}) collective-permute-start(s32[2,64]{1,0:T(2,128)S(1)} %pad_add_fusion.2), channel_id=1, source_target_pairs={{0,12},{4,8},{8,4},{12,0},{1,13},{5,9},{9,5},{13,1},{2,14},{6,10},... | collective-permute-start | bytes 1544 | tf_op jit(solution)/shard_map/ppermute | solution.py:21
  26.2 7.1 %collective-permute-start.2 = (bf16[512,256]{1,0:T(8,128)(2,1)S(1)}, bf16[512,256]{1,0:T(8,128)(2,1)S(1)}, u32[]{:S(2)}, u32[]{:S(2)}) collective-permute-start(bf16[512,256]{1,0:T(8,128)(2,1)S(1)} %collective-permute-done.1), channel_id=1, source_target_pairs={{0,1},{1,0},{2,3},{3,2},{4,5},{5,4},{6,7},{7,6},{8,9},{9,8},{10,11... | collective-permute-start | bytes 786440 | tf_op jit(solution)/shard_map/ppermute | solution.py:21
  30.5 4.6 %copy-start.10 = (f32[64,256]{1,0:T(8,128)}, f32[64,256]{1,0:T(8,128)S(1)}, u32[]{:S(2)}) copy-start(f32[64,256]{1,0:T(8,128)S(1)} %collective-permute-done.3) | copy-start | bytes 196612
  35.2 8.6 %copy-start.1 = (bf16[256,2048]{1,0:T(8,128)(2,1)}, bf16[256,2048]{1,0:T(8,128)(2,1)S(1)}, u32[]{:S(2)}) copy-start(bf16[256,2048]{1,0:T(8,128)(2,1)S(1)} %convolution_convert_fusion.3.refs_0_.refs_1_) | copy-start | bytes 3145732
  37.3 18.0 %collective-permute-start.6 = (bf16[64,2048]{1,0:T(8,128)(2,1)S(1)}, bf16[64,2048]{1,0:T(8,128)(2,1)S(1)}, u32[]{:S(2)}, u32[]{:S(2)}) collective-permute-start(bf16[64,2048]{1,0:T(8,128)(2,1)S(1)} %get-tuple-element.39), channel_id=1, source_target_pairs={{0,4},{4,0},{8,12},{12,8},{1,5},{5,1},{9,13},{13,9},{2,6},{6,2},{1... | collective-permute-start | bytes 786440 | tf_op jit(solution)/shard_map/ppermute | solution.py:21
  39.3 20.6 %collective-permute-start.10 = (bf16[64,2048]{1,0:T(8,128)(2,1)S(1)}, bf16[64,2048]{1,0:T(8,128)(2,1)S(1)}, u32[]{:S(2)}, u32[]{:S(2)}) collective-permute-start(bf16[64,2048]{1,0:T(8,128)(2,1)S(1)} %get-tuple-element.40), channel_id=1, source_target_pairs={{0,12},{4,8},{8,4},{12,0},{1,13},{5,9},{9,5},{13,1},{2,14},{6,10},... | collective-permute-start | bytes 786440 | tf_op jit(solution)/shard_map/ppermute | solution.py:21
  43.7 5.3 %copy-start.3 = (bf16[256,2048]{1,0:T(8,128)(2,1)}, bf16[256,2048]{1,0:T(8,128)(2,1)S(1)}, u32[]{:S(2)}) copy-start(bf16[256,2048]{1,0:T(8,128)(2,1)S(1)} %convolution_convert_fusion.1.refs_1_.refs_2_) | copy-start | bytes 3145732
  44.5 10.8 %copy-start.5 = (bf16[256,2048]{1,0:T(8,128)(2,1)}, bf16[256,2048]{1,0:T(8,128)(2,1)S(1)}, u32[]{:S(2)}) copy-start(bf16[256,2048]{1,0:T(8,128)(2,1)S(1)} %convolution_convert_fusion.2.refs_0_) | copy-start | bytes 3145732
  49.0 13.5 %collective-permute-start.7 = (bf16[64,2048]{1,0:T(8,128)(2,1)}, bf16[64,2048]{1,0:T(8,128)(2,1)}, u32[]{:S(2)}, u32[]{:S(2)}) collective-permute-start(bf16[64,2048]{1,0:T(8,128)(2,1)} %get-tuple-element.46), channel_id=1, source_target_pairs={{0,4},{4,0},{8,12},{12,8},{1,5},{5,1},{9,13},{13,9},{2,6},{6,2},{1... | collective-permute-start | bytes 786440 | tf_op jit(solution)/shard_map/ppermute | solution.py:21
  51.8 10.8 %collective-permute-start.8 = (bf16[64,2048]{1,0:T(8,128)(2,1)}, bf16[64,2048]{1,0:T(8,128)(2,1)}, u32[]{:S(2)}, u32[]{:S(2)}) collective-permute-start(bf16[64,2048]{1,0:T(8,128)(2,1)} %get-tuple-element.47), channel_id=1, source_target_pairs={{0,12},{4,8},{8,4},{12,0},{1,13},{5,9},{9,5},{13,1},{2,14},{6,10},... | collective-permute-start | bytes 786440 | tf_op jit(solution)/shard_map/ppermute | solution.py:21
  56.1 10.6 %collective-permute-start.9 = (bf16[64,2048]{1,0:T(8,128)(2,1)}, bf16[64,2048]{1,0:T(8,128)(2,1)}, u32[]{:S(2)}, u32[]{:S(2)}) collective-permute-start(bf16[64,2048]{1,0:T(8,128)(2,1)} %add_convert_fusion.2), channel_id=1, source_target_pairs={{0,12},{4,8},{8,4},{12,0},{1,13},{5,9},{9,5},{13,1},{2,14},{6,10},... | collective-permute-start | bytes 786440 | tf_op jit(solution)/shard_map/ppermute | solution.py:21
  60.6 7.7 %collective-permute-start.11 = (bf16[64,2048]{1,0:T(8,128)(2,1)}, bf16[64,2048]{1,0:T(8,128)(2,1)}, u32[]{:S(2)}, u32[]{:S(2)}) collective-permute-start(bf16[64,2048]{1,0:T(8,128)(2,1)} %add_convert_fusion.1), channel_id=1, source_target_pairs={{0,4},{4,0},{8,12},{12,8},{1,5},{5,1},{9,13},{13,9},{2,6},{6,2},{1... | collective-permute-start | bytes 786440 | tf_op jit(solution)/shard_map/ppermute | solution.py:21
  68.3 1.2 copy-start.7
  73.6 9.8 %collective-permute-start.12 = (bf16[8,64,512]{2,1,0:T(8,128)(2,1)S(1)}, bf16[8,64,512]{2,1,0:T(8,128)(2,1)S(1)}, u32[]{:S(2)}, u32[]{:S(2)}) collective-permute-start(bf16[8,64,512]{2,1,0:T(8,128)(2,1)S(1)} %get-tuple-element.52), channel_id=1, source_target_pairs={{0,16},{16,0},{1,17},{17,1},{2,18},{18,2},{3,19},{19,3},{4,20},{20... | collective-permute-start | bytes 1572872 | tf_op jit(solution)/shard_map/ppermute | solution.py:21
  110.1 11.9 %collective-permute-start.16 = (f32[64,512]{1,0:T(8,128)S(1)}, f32[64,512]{1,0:T(8,128)S(1)}, u32[]{:S(2)}, u32[]{:S(2)}) collective-permute-start(f32[64,512]{1,0:T(8,128)S(1)} %convert_reduce_fusion.mine_ref), channel_id=1, source_target_pairs={{0,32},{32,0},{1,33},{33,1},{2,34},{34,2},{3,35},{35,3},{4,36},{36... | collective-permute-start | bytes 393224 | tf_op jit(solution)/shard_map/ppermute | solution.py:21
  122.8 0.8 copy-start.9
  123.6 23.9 %all-to-all-start.1 = ((bf16[8,64,512]{2,1,0:T(8,128)(2,1)}), bf16[8,64,512]{2,1,0:T(8,128)(2,1)}, u32[]{:S(2)}, u32[]{:S(2)}) async-start(bf16[8,64,512]{2,1,0:T(8,128)(2,1)} %copy-done.9), calls=%async_computation.1 | async-start | bytes 1048576 | tf_op jit(solution)/shard_map/all_to_all | solution.py:308
  127.8 1.2 copy-start.2
  129.0 1.2 copy-start.4
  130.2 1.2 copy-start.6
  137.9 14.9 %collective-permute-start.13 = (bf16[64,4096]{1,0:T(8,128)(2,1)}, bf16[64,4096]{1,0:T(8,128)(2,1)}, u32[]{:S(2)}, u32[]{:S(2)}) collective-permute-start(bf16[64,4096]{1,0:T(8,128)(2,1)} %get-tuple-element.56), channel_id=1, source_target_pairs={{0,4},{4,0},{8,12},{12,8},{1,5},{5,1},{9,13},{13,9},{2,6},{6,2},{1... | collective-permute-start | bytes 1572872 | tf_op jit(solution)/shard_map/ppermute | solution.py:21
  139.8 23.0 %collective-permute-start.14 = (bf16[64,4096]{1,0:T(8,128)(2,1)}, bf16[64,4096]{1,0:T(8,128)(2,1)}, u32[]{:S(2)}, u32[]{:S(2)}) collective-permute-start(bf16[64,4096]{1,0:T(8,128)(2,1)} %get-tuple-element.57), channel_id=1, source_target_pairs={{0,8},{4,12},{8,0},{12,4},{1,9},{5,13},{9,1},{13,5},{2,10},{6,14},... | collective-permute-start | bytes 1572872 | tf_op jit(solution)/shard_map/ppermute | solution.py:21
  143.8 25.9 %collective-permute-start.15 = (bf16[64,4096]{1,0:T(8,128)(2,1)}, bf16[64,4096]{1,0:T(8,128)(2,1)}, u32[]{:S(2)}, u32[]{:S(2)}) collective-permute-start(bf16[64,4096]{1,0:T(8,128)(2,1)} %get-tuple-element.58), channel_id=1, source_target_pairs={{0,12},{4,8},{8,4},{12,0},{1,13},{5,9},{9,5},{13,1},{2,14},{6,10},... | collective-permute-start | bytes 1572872 | tf_op jit(solution)/shard_map/ppermute | solution.py:21
  147.5 28.7 %collective-permute-start.17 = (bf16[8,64,512]{2,1,0:T(8,128)(2,1)}, bf16[8,64,512]{2,1,0:T(8,128)(2,1)S(1)}, u32[]{:S(2)}, u32[]{:S(2)}) collective-permute-start(bf16[8,64,512]{2,1,0:T(8,128)(2,1)} %all-to-all-done.1.mine_ref), channel_id=1, source_target_pairs={{0,16},{16,0},{1,17},{17,1},{2,18},{18,2},{3,19},{19,3},{4,20},{20... | collective-permute-start | bytes 1572872 | tf_op jit(solution)/shard_map/ppermute | solution.py:21
  169.7 1.2 copy-start.8

commit v7 on v6

--- a/solution.py
+++ b/solution.py
@@ -9,6 +9,7 @@
 
 BLK = 64
 LANES = 128
+HALF = 64
 DECAY = 0.9
 NODES = 32
 F32, BF16 = jnp.float32, jnp.bfloat16
@@ -46,68 +47,60 @@
     return lax.broadcasted_iota(jnp.int32, (BLK, LANES), 1) // BLK
 
 
-def pack_kernel(picks, base, pieces, list_ref, *refs):
-    mats, outs = refs[: len(picks)], refs[len(picks) :]
+def pack_kernel(k, base, list_ref, mat_ref, out_ref):
     upper = lane_halves() == 1
-    span = 64 // 2 // pieces
-    for n, k in enumerate(picks):
-        for p in range(pieces):
-            out_ref = outs[n * pieces + p]
-
-            def tile(q, carry, k=k, n=n, p=p, out_ref=out_ref):
-                slot = base + 2 * (p * span + q)
-                sides = []
-                for side in range(2):
-                    rows, cols, half = place_of(list_ref[k, slot + side])
-                    block = mats[n][rows, cols].astype(F32)
-                    sides.append(pltpu.roll(block, (half + side) % 2 * BLK, 1))
-                at = pl.ds(pl.multiple_of(q * LANES, LANES), LANES)
-                out_ref[:, at] = jnp.where(upper, sides[1], sides[0]).astype(BF16)
-                return carry
-
-            lax.fori_loop(0, span, tile, 0, unroll=4)
-
-
-def pack(lists, mats, picks, base, pieces):
+
+    def tile(q, carry):
+        sides = []
+        for side in range(2):
+            rows, cols, half = place_of(list_ref[k, base + 2 * q + side])
+            block = mat_ref[rows, cols]
+            sides.append(jnp.where(half == side, block, pltpu.roll(block, BLK, 1)))
+        at = pl.ds(pl.multiple_of(q * LANES, LANES), LANES)
+        out_ref[:, at] = jnp.where(upper, sides[1], sides[0])
+        return carry
+
+    lax.fori_loop(0, HALF // 2, tile, 0, unroll=True)
+
+
+def pack(lists, mat, k, base):
     whole = pl.BlockSpec(memory_space=pltpu.VMEM)
-    count = len(picks) * pieces
     return kernel_call(
-        functools.partial(pack_kernel, picks, base, pieces),
+        functools.partial(pack_kernel, k, base),
         (),
-        [SMEM] + [whole] * len(picks),
-        [whole] * count,
-        [jax.ShapeDtypeStruct((BLK, 64 * BLK // pieces), BF16)] * count,
+        [SMEM, whole],
+        whole,
+        jax.ShapeDtypeStruct((BLK, HALF * BLK), BF16),
         1 << 20,
-    )(lists, *mats)
-
-
-def unpack(list_ref, base, pieces, grad_ref):
+    )(lists, mat)
+
+
+def unpack(list_ref, base, terms, grad_ref):
     halves = lane_halves()
-    span = 64 // 2 // len(pieces)
-    for p, terms in enumerate(pieces):
-
-        def tile(q, carry, p=p, terms=terms):
-            at = pl.ds(pl.multiple_of(q * LANES, LANES), LANES)
-            value = terms[0][:, at].astype(F32)
-            for term in terms[1:]:
-                value = value + term[:, at].astype(F32)
-            for side in range(2):
-                rows, cols, half = place_of(list_ref[0, base + 2 * (p * span + q) + side])
-                moved = pltpu.roll(value, (half + side) % 2 * BLK, 1)
-                grad_ref[rows, cols] = jnp.where(halves == half, moved, grad_ref[rows, cols])
-            return carry
-
-        lax.fori_loop(0, span, tile, 0, unroll=2)
+
+    def tile(q, carry):
+        at = pl.ds(pl.multiple_of(q * LANES, LANES), LANES)
+        value = terms[0][:, at].astype(F32)
+        for term in terms[1:]:
+            value = value + term[:, at].astype(F32)
+        turned = pltpu.roll(value, BLK, 1)
+        for side in range(2):
+            rows, cols, half = place_of(list_ref[0, base + 2 * q + side])
+            moved = jnp.where(half == side, value, turned)
+            grad_ref[rows, cols] = jnp.where(halves == half, moved, grad_ref[rows, cols])
+        return carry
+
+    lax.fori_loop(0, HALF // 2, tile, 0, unroll=True)
 
 
 def chosen_kernel(
-    list_ref, c_ref, mask_ref, fb_ref, own_ref, got_a, got_b, next_a, next_b, mine_ref, other_ref, grad_ref
+    list_ref, c_ref, mask_ref, fb_ref, own_ref, got_1, got_2, got_3, mine_ref, other_ref, grad_ref
 ):
     row = pl.program_id(0)
 
     @pl.when(row == 0)
     def _():
-        unpack(list_ref, 0, ((got_a, next_a), (got_b, next_b)), grad_ref)
+        unpack(list_ref, 0, (got_1, got_2, got_3), grad_ref)
 
     first = c_ref[0] == 0
     rows = pl.ds(pl.multiple_of(row * BLK, BLK), BLK)
@@ -131,7 +124,7 @@
 
     @pl.when(row == 0)
     def _():
-        unpack(list_ref, 64, ((got_1, got_2, got_3),), grad_ref)
+        unpack(list_ref, HALF, (got_1, got_2, got_3), grad_ref)
 
     rows = pl.ds(pl.multiple_of(row * BLK, BLK), BLK)
     for at in range(0, fb_ref.shape[1], 256):
@@ -245,10 +238,6 @@
     return hidden, near, far, swap(far, "t", 1, 4)
 
 
-def plus(kept, got):
-    return (kept.astype(F32) + got.astype(F32)).astype(BF16)
-
-
 def as_matrix(blocks):
     return blocks.transpose(1, 0, 2).reshape(BLK, -1)
 
@@ -264,16 +253,10 @@
     )
     mask = jnp.any(chosen.reshape(-1, 1, 1) == block_of[None], axis=0).astype(F32)
     moment = as_matrix(momentum[0, 0])
-    far_moment = swap(moment, "yh", 1, 2)
     mask = mask[:, None]
     lists = block_lists(chosen.reshape(-1), rows_blk * cols_blk)
-    *shards, far_moment, lists = lax.optimization_barrier(
-        (*gather_hidden(hidden), far_moment, lists)
-    )
+    *shards, lists = lax.optimization_barrier((*gather_hidden(hidden), lists))
     shards = jnp.stack(shards)
-    moment = jnp.where(
-        yh == 0, jnp.concatenate([moment, far_moment], 1), jnp.concatenate([far_moment, moment], 1)
-    )
     d, t = lax.axis_index("dp"), lax.axis_index("t")
 
     def product(flip, shards):
@@ -282,29 +265,32 @@
             part, cotangent, (((0,), (0,)), ((), ())), preferred_element_type=F32
         ).astype(BF16)
 
-    far_rows = product(2, shards)
-    give_a, give_b = pack(lists, (far_rows,), (2,), 0, 2)
-    far_a, far_b = swap(give_a, "dp", 1, 4), swap(give_b, "dp", 3, 4)
-    shards, give_a, give_b = lax.optimization_barrier((shards, give_a, give_b))
-    near_rows, side_rows = product(1, shards), product(3, shards)
-    near_a, near_b, side_a, side_b = pack(lists, (near_rows, side_rows), (1, 3), 0, 2)
-    got_a, got_b = swap(near_a, "dp", 1, 4), swap(side_b, "dp", 3, 4)
+    parts, got = {}, {}
+    for k in (2, 1, 3):
+        parts[k] = product(k, shards)
+        given = pack(lists, parts[k], k, 0)
+        got[k] = swap(given, "dp", k, 4)
+        shards, given = lax.optimization_barrier((shards, given))
+    moment, given = lax.optimization_barrier((moment, given))
+    far_moment = swap(moment, "yh", 1, 2)
     own = product(0, shards)
-    far_a, near_b, side_a, own, mask = lax.optimization_barrier((far_a, near_b, side_a, own, mask))
-    next_a = swap(plus(side_a, far_a), "dp", 3, 4)
-    next_b = swap(plus(near_b, far_b), "dp", 1, 4)
-    mine, other = chosen_sums(
-        lists, at_c, mask, feedback[0], own, got_a, got_b, next_a, next_b
-    )
+    left = [pack(lists, parts[k], k, HALF) for k in (1, 2, 3)]
+    got = [got[k] for k in (1, 2, 3)]
+    *got, far_moment, own, left_1, left_2, left_3 = lax.optimization_barrier(
+        (*got, far_moment, own, *left)
+    )
+    mine, other = chosen_sums(lists, at_c, mask, feedback[0], own, *got)
     pair = (mine + swap(other, "c", 1, 2).astype(F32)).astype(BF16)
-    near_rows, far_rows, side_rows, _ = lax.optimization_barrier(
-        (near_rows, far_rows, side_rows, pair)
-    )
-    left = pack(lists, (near_rows, far_rows, side_rows), (1, 2, 3), 64, 1)
-    left = [swap(part, "dp", flip, 4) for flip, part in zip((1, 2, 3), left)]
-    got = lax.all_to_all(pair, "z", 0, 0, tiled=True)
-    near = jnp.sum(got.astype(F32), axis=0)
-    momentum_new, copies = owner_update(at_yh, near, swap(near, "yh", 1, 2), moment)
+    pair, *left = lax.optimization_barrier((pair, left_1, left_2, left_3))
+    left = [swap(part, "dp", k, 4) for k, part in zip((1, 2, 3), left)]
+    across = lax.all_to_all(pair, "z", 0, 0, tiled=True)
+    near = jnp.sum(across.astype(F32), axis=0)
+    far = swap(near, "yh", 1, 2)
+    far, *left = lax.optimization_barrier((far, *left))
+    moment = jnp.where(
+        yh == 0, jnp.concatenate([moment, far_moment], 1), jnp.concatenate([far_moment, moment], 1)
+    )
+    momentum_new, copies = owner_update(at_yh, near, far, moment)
     every = lax.all_to_all(copies, "z", 0, 0, tiled=True)
     *left, _ = lax.optimization_barrier((*left, copies))
     feedback_new = residual(lists, mask, feedback[0], own, *left)

time: 182 us -> 155 us (0.85)
  waiting for transfers between devices: 35.2 us -> 25.8 us
  blocking collectives: 26.5 us -> 20.5 us
  Pallas kernels: 26.5 us -> 20.8 us
  starting transfers between devices: 71.8 us -> 68.5 us
  local copies, waits for them, and re-layouts: 8.12 us -> 6.15 us
    ppermute x18 -> x15, waiting for transfers between devices: 35.2 us -> 17.3 us  [swap(): return lax.ppermute(value, axis, [(i, i ^ flip) for i in range(size)])]
    ppermute x18 -> x15, starting transfers between devices: 67.6 us -> 58.5 us  [swap(): return lax.ppermute(value, axis, [(i, i ^ flip) for i in range(size)])]
    all_to_all x1, waiting for transfers between devices: 0.01 us -> 8.46 us  [local(): across = lax.all_to_all(pair, 'z', 0, 0, tiled=True)]
    all_to_all x1, blocking collectives: 26.5 us -> 20.5 us  [local(): every = lax.all_to_all(copies, 'z', 0, 0, tiled=True)]
    all_to_all x1, starting transfers between devices: 4.15 us -> 10 us  [local(): across = lax.all_to_all(pair, 'z', 0, 0, tiled=True)]
    pallas_call x2, Pallas kernels: 9.35 us -> 6.93 us  [state_call(): pl.pallas_call(body, grid=(rows // BLK,), in_specs=[SMEM] * len(scalars)...]
    unnamed x22 -> x30, local copies, waits for them, and re-layouts: 6.96 us -> 5 us
    pallas_call x3 -> x6, Pallas kernels: 13.1 us -> 11.6 us  [pack(): kernel_call(functools.partial(pack_kernel, k, base), (), [SMEM, whole], w...]
  transfers between devices with their start and end apart: 19 -> 16, of which waited for: 8 -> 7; matrix products, arithmetic and copies ran while one was open for 5% -> 7% of each run, Pallas kernels for 9% -> 10%
where the time goes in v7:
time: 155 us; the launch traced here: 154 us
  starting transfers between devices  68.5 us (44%)
  waiting for transfers between devices  25.8 us (17%)
  Pallas kernels  20.8 us (13%)
  blocking collectives  20.5 us (13%)
  other arithmetic  7.09 us (5%)
  local copies, waits for them, and re-layouts  6.15 us (4%)
  matrix products  3.97 us (3%)
    ppermute x15, starting transfers between devices, swap(): return lax.ppermute(value, axis, [(i, i ^ flip) for i in range(size)])  58.5 us
    all_to_all x1, blocking collectives, local(): every = lax.all_to_all(copies, 'z', 0, 0, tiled=True)  20.5 us
    ppermute x15, waiting for transfers between devices, swap(): return lax.ppermute(value, axis, [(i, i ^ flip) for i in range(size)])  17.3 us
    pallas_call x6, Pallas kernels, pack(): kernel_call(functools.partial(pack_kernel, k, base), (), [SMEM, whole], w...  11.6 us
    all_to_all x1, starting transfers between devices, local(): across = lax.all_to_all(pair, 'z', 0, 0, tiled=True)  10 us
    all_to_all x1, waiting for transfers between devices, local(): across = lax.all_to_all(pair, 'z', 0, 0, tiled=True)  8.46 us
    pallas_call x2, Pallas kernels, state_call(): pl.pallas_call(body, grid=(rows // BLK,), in_specs=[SMEM] * len(scalars)...  6.93 us
    unnamed x30, local copies, waits for them, and re-layouts  5 us
  transfers between devices with their start and end apart: 16, of which 7 were waited for; matrix products, arithmetic and copies ran while one was open for 7% of the time, Pallas kernels for 10%

profile of v7, /device:TPU:1, one launch (start us, length us, event | category | flops | bytes accessed | tf_op | source)
XLA Modules:
  0.0 153.9 jit_solution(13990526657526724075)
XLA Ops:
  0.6 4.2 %collective-permute-start = (bf16[512,256]{1,0:T(8,128)(2,1)}, bf16[512,256]{1,0:T(8,128)(2,1)S(1)}, u32[]{:S(2)}, u32[]{:S(2)}) collective-permute-start(bf16[512,256]{1,0:T(8,128)(2,1)} %param.5), channel_id=1, source_target_pairs={{0,1},{1,0},{2,3},{3,2},{4,5},{5,4},{6,7},{7,6},{8,9},{9,8},{10,11... | collective-permute-start | bytes 786440 | tf_op jit(solution)/shard_map/ppermute | solution.py:22
  4.8 4.2 %collective-permute-start.1 = (bf16[512,256]{1,0:T(8,128)(2,1)}, bf16[512,256]{1,0:T(8,128)(2,1)S(1)}, u32[]{:S(2)}, u32[]{:S(2)}) collective-permute-start(bf16[512,256]{1,0:T(8,128)(2,1)} %param.5), channel_id=1, source_target_pairs={{0,2},{1,3},{2,0},{3,1},{4,6},{5,7},{6,4},{7,5},{8,10},{9,11},{10,... | collective-permute-start | bytes 786440 | tf_op jit(solution)/shard_map/ppermute | solution.py:22
  9.0 3.1 %collective-permute-start.3 = (s32[64]{0:T(128)}, s32[64]{0:T(128)S(1)}, u32[]{:S(2)}, u32[]{:S(2)}) collective-permute-start(s32[64]{0:T(128)} %bitcast.39), channel_id=1, source_target_pairs={{0,4},{4,0},{8,12},{12,8},{1,5},{5,1},{9,13},{13,9},{2,6},{6,2},{1... | collective-permute-start | bytes 776 | tf_op jit(solution)/shard_map/ppermute | solution.py:22
  13.3 4.7 %collective-permute-start.8 = (f32[64,256]{1,0:T(8,128)S(1)}, f32[64,256]{1,0:T(8,128)S(1)}, u32[]{:S(2)}, u32[]{:S(2)}) collective-permute-start(f32[64,256]{1,0:T(8,128)S(1)} %reshape.115), channel_id=1, source_target_pairs={{0,32},{32,0},{1,33},{33,1},{2,34},{34,2},{3,35},{35,3},{4,36},{36... | collective-permute-start | bytes 196616 | tf_op jit(solution)/shard_map/ppermute | solution.py:22
  18.8 3.7 %collective-permute-start.4 = (s32[2,64]{1,0:T(2,128)S(1)}, s32[2,64]{1,0:T(2,128)S(1)}, u32[]{:S(2)}, u32[]{:S(2)}) collective-permute-start(s32[2,64]{1,0:T(2,128)S(1)} %pad_add_fusion.2), channel_id=1, source_target_pairs={{0,12},{4,8},{8,4},{12,0},{1,13},{5,9},{9,5},{13,1},{2,14},{6,10},... | collective-permute-start | bytes 1544 | tf_op jit(solution)/shard_map/ppermute | solution.py:22
  22.5 2.0 %collective-permute-done.4 = s32[2,64]{1,0:T(2,128)S(1)} collective-permute-done((s32[2,64]{1,0:T(2,128)S(1)}, s32[2,64]{1,0:T(2,128)S(1)}, u32[]{:S(2)}, u32[]{:S(2)}) %collective-permute-start.4) | collective-permute-done | bytes 544 | tf_op jit(solution)/shard_map/ppermute | solution.py:22
  25.3 3.1 %collective-permute-start.2 = (bf16[512,256]{1,0:T(8,128)(2,1)S(1)}, bf16[512,256]{1,0:T(8,128)(2,1)S(1)}, u32[]{:S(2)}, u32[]{:S(2)}) collective-permute-start(bf16[512,256]{1,0:T(8,128)(2,1)S(1)} %collective-permute-done.1), channel_id=1, source_target_pairs={{0,1},{1,0},{2,3},{3,2},{4,5},{5,4},{6,7},{7,6},{8,9},{9,8},{10,11... | collective-permute-start | bytes 786440 | tf_op jit(solution)/shard_map/ppermute | solution.py:22
  29.4 3.0 %collective-permute-done.2 = bf16[512,256]{1,0:T(8,128)(2,1)S(1)} collective-permute-done((bf16[512,256]{1,0:T(8,128)(2,1)S(1)}, bf16[512,256]{1,0:T(8,128)(2,1)S(1)}, u32[]{:S(2)}, u32[]{:S(2)}) %collective-permute-start.2) | collective-permute-done | bytes 262176 | tf_op jit(solution)/shard_map/ppermute | solution.py:22
  34.3 2.3 %shard_map.76 = bf16[64,4096]{1,0:T(8,128)(2,1)} custom-call(s32[4,128]{1,0:T(4,128)S(1)} %pad_add_fusion.1.list_ref, bf16[256,2048]{1,0:T(8,128)(2,1)S(1)} %convolution_convert_fusion.3.mat_ref), custom_call_target="tpu_custom_call" | custom-call | flops 1048576 | bytes 1048576 | tf_op jit(solution)/shard_map/pallas_call | solution.py:68
  37.6 3.2 %collective-permute-start.6 = (bf16[64,4096]{1,0:T(8,128)(2,1)}, bf16[64,4096]{1,0:T(8,128)(2,1)}, u32[]{:S(2)}, u32[]{:S(2)}) collective-permute-start(bf16[64,4096]{1,0:T(8,128)(2,1)} %shard_map.76), channel_id=1, source_target_pairs={{0,8},{4,12},{8,0},{12,4},{1,9},{5,13},{9,1},{13,5},{2,10},{6,14},... | collective-permute-start | bytes 1572872 | tf_op jit(solution)/shard_map/ppermute | solution.py:22
  41.6 2.3 %shard_map.77 = bf16[64,4096]{1,0:T(8,128)(2,1)} custom-call(s32[4,128]{1,0:T(4,128)S(1)} %pad_add_fusion.1.list_ref, bf16[256,2048]{1,0:T(8,128)(2,1)S(1)} %convolution_convert_fusion.2.mat_ref), custom_call_target="tpu_custom_call" | custom-call | flops 1048576 | bytes 1048576 | tf_op jit(solution)/shard_map/pallas_call | solution.py:68
  44.8 3.1 %collective-permute-start.5 = (bf16[64,4096]{1,0:T(8,128)(2,1)}, bf16[64,4096]{1,0:T(8,128)(2,1)}, u32[]{:S(2)}, u32[]{:S(2)}) collective-permute-start(bf16[64,4096]{1,0:T(8,128)(2,1)} %shard_map.77), channel_id=1, source_target_pairs={{0,4},{4,0},{8,12},{12,8},{1,5},{5,1},{9,13},{13,9},{2,6},{6,2},{1... | collective-permute-start | bytes 1572872 | tf_op jit(solution)/shard_map/ppermute | solution.py:22
  48.7 2.3 %shard_map.78 = bf16[64,4096]{1,0:T(8,128)(2,1)} custom-call(s32[4,128]{1,0:T(4,128)S(1)} %pad_add_fusion.1.list_ref, bf16[256,2048]{1,0:T(8,128)(2,1)S(1)} %convolution_convert_fusion.1.mat_ref), custom_call_target="tpu_custom_call" | custom-call | flops 1048576 | bytes 1048576 | tf_op jit(solution)/shard_map/pallas_call | solution.py:68
  52.0 2.8 %collective-permute-start.7 = (bf16[64,4096]{1,0:T(8,128)(2,1)}, bf16[64,4096]{1,0:T(8,128)(2,1)}, u32[]{:S(2)}, u32[]{:S(2)}) collective-permute-start(bf16[64,4096]{1,0:T(8,128)(2,1)} %shard_map.78), channel_id=1, source_target_pairs={{0,12},{4,8},{8,4},{12,0},{1,13},{5,9},{9,5},{13,1},{2,14},{6,10},... | collective-permute-start | bytes 1572872 | tf_op jit(solution)/shard_map/ppermute | solution.py:22
  55.3 1.8 %convolution_convert_fusion.own_ref = bf16[256,2048]{1,0:T(8,128)(2,1)S(1)} fusion(bf16[512,2048]{1,0:T(8,128)(2,1)S(1)} %copy-done, bf16[4,512,256]{2,1,0:T(8,128)(2,1)} %copy-done.12, s32[]{:T(128)S(6)} %select_n.45), kind=kOutput, calls=%fused_computation | convolution fusion | flops 537395200 | bytes 3407876 | tf_op jit(solution)/shard_map/dot_general | solution.py:264
  58.3 1.6 %shard_map.80 = bf16[64,4096]{1,0:T(8,128)(2,1)S(1)} custom-call(s32[4,128]{1,0:T(4,128)S(1)} %pad_add_fusion.1.list_ref, bf16[256,2048]{1,0:T(8,128)(2,1)S(1)} %copy-done.2), custom_call_target="tpu_custom_call" | custom-call | flops 1048576 | bytes 1048576 | tf_op jit(solution)/shard_map/pallas_call | solution.py:68
  59.8 1.6 %shard_map.79 = bf16[64,4096]{1,0:T(8,128)(2,1)S(1)} custom-call(s32[4,128]{1,0:T(4,128)S(1)} %pad_add_fusion.1.list_ref, bf16[256,2048]{1,0:T(8,128)(2,1)S(1)} %copy-done.4), custom_call_target="tpu_custom_call" | custom-call | flops 1048576 | bytes 1048576 | tf_op jit(solution)/shard_map/pallas_call | solution.py:68
  61.4 1.6 %shard_map.81 = bf16[64,4096]{1,0:T(8,128)(2,1)S(1)} custom-call(s32[4,128]{1,0:T(4,128)S(1)} %pad_add_fusion.1.list_ref, bf16[256,2048]{1,0:T(8,128)(2,1)S(1)} %copy-done.6), custom_call_target="tpu_custom_call" | custom-call | flops 1048576 | bytes 1048576 | tf_op jit(solution)/shard_map/pallas_call | solution.py:68
  63.8 2.1 %collective-permute-done.7.got_3 = bf16[64,4096]{1,0:T(8,128)(2,1)} collective-permute-done((bf16[64,4096]{1,0:T(8,128)(2,1)}, bf16[64,4096]{1,0:T(8,128)(2,1)}, u32[]{:S(2)}, u32[]{:S(2)}) %collective-permute-start.7) | collective-permute-done | bytes 524320 | tf_op jit(solution)/shard_map/ppermute | solution.py:22
  65.9 2.9 %shard_map.82 = (f32[8,64,512]{2,1,0:T(8,128)S(1)}, bf16[8,64,512]{2,1,0:T(8,128)(2,1)S(1)}) custom-call(s32[4,128]{1,0:T(4,128)S(1)} %pad_add_fusion.1.list_ref, s32[1]{0:T(128)} %bitcast.14.c_ref, f32[4,1,2048]{2,1,0:T(1,128)S(1)} %reshape.118.mask_ref, bf16[256,2048]{1,0:T(8,128)(2,1)S(1)} %bitcast.31, ...), custom_call_target="tpu_custom_call" | custom-call | flops 4194304 | bytes 4194304 | tf_op jit(solution)/shard_map/pallas_call | solution.py:143
  68.8 6.5 %collective-permute-start.9 = (bf16[8,64,512]{2,1,0:T(8,128)(2,1)S(1)}, bf16[8,64,512]{2,1,0:T(8,128)(2,1)S(1)}, u32[]{:S(2)}, u32[]{:S(2)}) collective-permute-start(bf16[8,64,512]{2,1,0:T(8,128)(2,1)S(1)} %get-tuple-element.47), channel_id=1, source_target_pairs={{0,16},{16,0},{1,17},{17,1},{2,18},{18,2},{3,19},{19,3},{4,20},{20... | collective-permute-start | bytes 1572872 | tf_op jit(solution)/shard_map/ppermute | solution.py:22
  77.8 10.0 %all-to-all-start = ((bf16[8,64,512]{2,1,0:T(8,128)(2,1)}), bf16[8,64,512]{2,1,0:T(8,128)(2,1)}, u32[]{:S(2)}, u32[]{:S(2)}) async-start(bf16[8,64,512]{2,1,0:T(8,128)(2,1)} %add_convert_fusion), calls=%async_computation | async-start | bytes 1048576 | tf_op jit(solution)/shard_map/all_to_all | solution.py:286
  87.8 1.9 %collective-permute-start.11 = (bf16[64,4096]{1,0:T(8,128)(2,1)}, bf16[64,4096]{1,0:T(8,128)(2,1)}, u32[]{:S(2)}, u32[]{:S(2)}) collective-permute-start(bf16[64,4096]{1,0:T(8,128)(2,1)} %copy-done.11), channel_id=1, source_target_pairs={{0,4},{4,0},{8,12},{12,8},{1,5},{5,1},{9,13},{13,9},{2,6},{6,2},{1... | collective-permute-start | bytes 1572872 | tf_op jit(solution)/shard_map/ppermute | solution.py:22
  89.7 4.4 %collective-permute-start.12 = (bf16[64,4096]{1,0:T(8,128)(2,1)}, bf16[64,4096]{1,0:T(8,128)(2,1)}, u32[]{:S(2)}, u32[]{:S(2)}) collective-permute-start(bf16[64,4096]{1,0:T(8,128)(2,1)} %copy-done.9), channel_id=1, source_target_pairs={{0,8},{4,12},{8,0},{12,4},{1,9},{5,13},{9,1},{13,5},{2,10},{6,14},... | collective-permute-start | bytes 1572872 | tf_op jit(solution)/shard_map/ppermute | solution.py:22
  94.2 3.2 %collective-permute-start.13 = (bf16[64,4096]{1,0:T(8,128)(2,1)}, bf16[64,4096]{1,0:T(8,128)(2,1)}, u32[]{:S(2)}, u32[]{:S(2)}) collective-permute-start(bf16[64,4096]{1,0:T(8,128)(2,1)} %copy-done.10), channel_id=1, source_target_pairs={{0,12},{4,8},{8,4},{12,0},{1,13},{5,9},{9,5},{13,1},{2,14},{6,10},... | collective-permute-start | bytes 1572872 | tf_op jit(solution)/shard_map/ppermute | solution.py:22
  97.4 8.5 %all-to-all-done = bf16[8,64,512]{2,1,0:T(8,128)(2,1)} async-done(((bf16[8,64,512]{2,1,0:T(8,128)(2,1)}), bf16[8,64,512]{2,1,0:T(8,128)(2,1)}, u32[]{:S(2)}, u32[]{:S(2)}) %all-to-all-start) | async-done | bytes 524320 | tf_op jit(solution)/shard_map/all_to_all | solution.py:286
  107.0 4.3 %collective-permute-start.10 = (f32[64,512]{1,0:T(8,128)S(1)}, f32[64,512]{1,0:T(8,128)S(1)}, u32[]{:S(2)}, u32[]{:S(2)}) collective-permute-start(f32[64,512]{1,0:T(8,128)S(1)} %convert_reduce_fusion.mine_ref), channel_id=1, source_target_pairs={{0,32},{32,0},{1,33},{33,1},{2,34},{34,2},{3,35},{35,3},{4,36},{36... | collective-permute-start | bytes 393224 | tf_op jit(solution)/shard_map/ppermute | solution.py:22
  112.3 2.9 %collective-permute-done.12.got_2 = bf16[64,4096]{1,0:T(8,128)(2,1)} collective-permute-done((bf16[64,4096]{1,0:T(8,128)(2,1)}, bf16[64,4096]{1,0:T(8,128)(2,1)}, u32[]{:S(2)}, u32[]{:S(2)}) %collective-permute-start.12) | collective-permute-done | bytes 524320 | tf_op jit(solution)/shard_map/ppermute | solution.py:22
  115.2 5.8 %collective-permute-done.13.got_3 = bf16[64,4096]{1,0:T(8,128)(2,1)} collective-permute-done((bf16[64,4096]{1,0:T(8,128)(2,1)}, bf16[64,4096]{1,0:T(8,128)(2,1)}, u32[]{:S(2)}, u32[]{:S(2)}) %collective-permute-start.13) | collective-permute-done | bytes 524320 | tf_op jit(solution)/shard_map/ppermute | solution.py:22
  121.8 20.5 %all_to_all.10.mine_ref = bf16[8,64,512]{2,1,0:T(8,128)(2,1)S(1)} all-to-all(bf16[8,64,512]{2,1,0:T(8,128)(2,1)S(1)} %get-tuple-element.60), channel_id=1, replica_groups=mesh['z'=8,'yh'=2,'c'=2,'dp'=4,'t'=4] {'z'}, dimensions={0} | all-to-all | bytes 1048576 | tf_op jit(solution)/shard_map/all_to_all | solution.py:294
  142.3 6.0 %collective-permute-start.14 = (bf16[8,64,512]{2,1,0:T(8,128)(2,1)S(1)}, bf16[8,64,512]{2,1,0:T(8,128)(2,1)S(1)}, u32[]{:S(2)}, u32[]{:S(2)}) collective-permute-start(bf16[8,64,512]{2,1,0:T(8,128)(2,1)S(1)} %all_to_all.10.mine_ref), channel_id=1, source_target_pairs={{0,16},{16,0},{1,17},{17,1},{2,18},{18,2},{3,19},{19,3},{4,20},{20... | collective-permute-start | bytes 1572872 | tf_op jit(solution)/shard_map/ppermute | solution.py:22
  148.3 4.1 %shard_map.84 = bf16[256,2048]{1,0:T(8,128)(2,1)} custom-call(s32[4,128]{1,0:T(4,128)S(1)} %pad_add_fusion.1.list_ref, f32[4,1,2048]{2,1,0:T(1,128)S(1)} %reshape.118.mask_ref, bf16[256,2048]{1,0:T(8,128)(2,1)S(1)} %bitcast.32, bf16[256,2048]{1,0:T(8,128)(2,1)S(1)} %convolution_convert_fusion.own_ref, bf16[64,4096]{1,0:T(8,128)(2,1)} %collective-permute-done.11.got_1, ...), custom_call_target="tpu_custom_call" | custom-call | flops 4194304 | bytes 4194304 | tf_op jit(solution)/shard_map/pallas_call | solution.py:143
  (65 shorter events, 19.3 us)
Async XLA Ops:
  0.6 32.9 %copy-start = (bf16[512,2048]{1,0:T(8,128)(2,1)S(1)}, bf16[512,2048]{1,0:T(8,128)(2,1)}, u32[]{:S(2)}) copy-start(bf16[512,2048]{1,0:T(8,128)(2,1)} %param.6) | copy-start | bytes 6291460
  0.6 28.8 %collective-permute-start = (bf16[512,256]{1,0:T(8,128)(2,1)}, bf16[512,256]{1,0:T(8,128)(2,1)S(1)}, u32[]{:S(2)}, u32[]{:S(2)}) collective-permute-start(bf16[512,256]{1,0:T(8,128)(2,1)} %param.5), channel_id=1, source_target_pairs={{0,1},{1,0},{2,3},{3,2},{4,5},{5,4},{6,7},{7,6},{8,9},{9,8},{10,11... | collective-permute-start | bytes 786440 | tf_op jit(solution)/shard_map/ppermute | solution.py:22
  4.8 20.5 %collective-permute-start.1 = (bf16[512,256]{1,0:T(8,128)(2,1)}, bf16[512,256]{1,0:T(8,128)(2,1)S(1)}, u32[]{:S(2)}, u32[]{:S(2)}) collective-permute-start(bf16[512,256]{1,0:T(8,128)(2,1)} %param.5), channel_id=1, source_target_pairs={{0,2},{1,3},{2,0},{3,1},{4,6},{5,7},{6,4},{7,5},{8,10},{9,11},{10,... | collective-permute-start | bytes 786440 | tf_op jit(solution)/shard_map/ppermute | solution.py:22
  9.0 9.1 %collective-permute-start.3 = (s32[64]{0:T(128)}, s32[64]{0:T(128)S(1)}, u32[]{:S(2)}, u32[]{:S(2)}) collective-permute-start(s32[64]{0:T(128)} %bitcast.39), channel_id=1, source_target_pairs={{0,4},{4,0},{8,12},{12,8},{1,5},{5,1},{9,13},{13,9},{2,6},{6,2},{1... | collective-permute-start | bytes 776 | tf_op jit(solution)/shard_map/ppermute | solution.py:22
  13.3 50.5 %collective-permute-start.8 = (f32[64,256]{1,0:T(8,128)S(1)}, f32[64,256]{1,0:T(8,128)S(1)}, u32[]{:S(2)}, u32[]{:S(2)}) collective-permute-start(f32[64,256]{1,0:T(8,128)S(1)} %reshape.115), channel_id=1, source_target_pairs={{0,32},{32,0},{1,33},{33,1},{2,34},{34,2},{3,35},{35,3},{4,36},{36... | collective-permute-start | bytes 196616 | tf_op jit(solution)/shard_map/ppermute | solution.py:22
  18.8 5.7 %collective-permute-start.4 = (s32[2,64]{1,0:T(2,128)S(1)}, s32[2,64]{1,0:T(2,128)S(1)}, u32[]{:S(2)}, u32[]{:S(2)}) collective-permute-start(s32[2,64]{1,0:T(2,128)S(1)} %pad_add_fusion.2), channel_id=1, source_target_pairs={{0,12},{4,8},{8,4},{12,0},{1,13},{5,9},{9,5},{13,1},{2,14},{6,10},... | collective-permute-start | bytes 1544 | tf_op jit(solution)/shard_map/ppermute | solution.py:22
  25.3 7.1 %collective-permute-start.2 = (bf16[512,256]{1,0:T(8,128)(2,1)S(1)}, bf16[512,256]{1,0:T(8,128)(2,1)S(1)}, u32[]{:S(2)}, u32[]{:S(2)}) collective-permute-start(bf16[512,256]{1,0:T(8,128)(2,1)S(1)} %collective-permute-done.1), channel_id=1, source_target_pairs={{0,1},{1,0},{2,3},{3,2},{4,5},{5,4},{6,7},{7,6},{8,9},{9,8},{10,11... | collective-permute-start | bytes 786440 | tf_op jit(solution)/shard_map/ppermute | solution.py:22
  33.5 14.4 %copy-start.12 = (bf16[4,512,256]{2,1,0:T(8,128)(2,1)}, bf16[4,512,256]{2,1,0:T(8,128)(2,1)S(1)}, u32[]{:S(2)}) copy-start(bf16[4,512,256]{2,1,0:T(8,128)(2,1)S(1)} %pad_maximum_fusion) | copy-start | bytes 3145732
  36.6 1.0 copy-start.1
  37.6 26.2 %collective-permute-start.6 = (bf16[64,4096]{1,0:T(8,128)(2,1)}, bf16[64,4096]{1,0:T(8,128)(2,1)}, u32[]{:S(2)}, u32[]{:S(2)}) collective-permute-start(bf16[64,4096]{1,0:T(8,128)(2,1)} %shard_map.76), channel_id=1, source_target_pairs={{0,8},{4,12},{8,0},{12,4},{1,9},{5,13},{9,1},{13,5},{2,10},{6,14},... | collective-permute-start | bytes 1572872 | tf_op jit(solution)/shard_map/ppermute | solution.py:22
  43.9 1.0 copy-start.3
  44.8 10.0 %copy-start.14 = (s32[1,1,1,64]{3,2,1,0:T(1,128)S(1)}, s32[1,1,1,64]{3,2,1,0:T(1,128)}, u32[]{:S(2)}) copy-start(s32[1,1,1,64]{3,2,1,0:T(1,128)} %param.8) | copy-start | bytes 772
  44.8 19.0 %collective-permute-start.5 = (bf16[64,4096]{1,0:T(8,128)(2,1)}, bf16[64,4096]{1,0:T(8,128)(2,1)}, u32[]{:S(2)}, u32[]{:S(2)}) collective-permute-start(bf16[64,4096]{1,0:T(8,128)(2,1)} %shard_map.77), channel_id=1, source_target_pairs={{0,4},{4,0},{8,12},{12,8},{1,5},{5,1},{9,13},{13,9},{2,6},{6,2},{1... | collective-permute-start | bytes 1572872 | tf_op jit(solution)/shard_map/ppermute | solution.py:22
  51.0 1.0 copy-start.5
  52.0 13.9 %collective-permute-start.7 = (bf16[64,4096]{1,0:T(8,128)(2,1)}, bf16[64,4096]{1,0:T(8,128)(2,1)}, u32[]{:S(2)}, u32[]{:S(2)}) collective-permute-start(bf16[64,4096]{1,0:T(8,128)(2,1)} %shard_map.78), channel_id=1, source_target_pairs={{0,12},{4,8},{8,4},{12,0},{1,13},{5,9},{9,5},{13,1},{2,14},{6,10},... | collective-permute-start | bytes 1572872 | tf_op jit(solution)/shard_map/ppermute | solution.py:22
  55.2 4.6 %copy-start.4 = (bf16[256,2048]{1,0:T(8,128)(2,1)S(1)}, bf16[256,2048]{1,0:T(8,128)(2,1)}, u32[]{:S(2)}) copy-start(bf16[256,2048]{1,0:T(8,128)(2,1)} %copy-done.3) | copy-start | bytes 3145732
  57.0 1.2 copy-start.2
  58.3 3.2 %copy-start.6 = (bf16[256,2048]{1,0:T(8,128)(2,1)S(1)}, bf16[256,2048]{1,0:T(8,128)(2,1)}, u32[]{:S(2)}) copy-start(bf16[256,2048]{1,0:T(8,128)(2,1)} %copy-done.5) | copy-start | bytes 3145732
  58.3 7.7 %copy-start.7 = (bf16[1,256,2048]{2,1,0:T(8,128)(2,1)S(1)}, bf16[1,256,2048]{2,1,0:T(8,128)(2,1)}, u32[]{:S(2)}) copy-start(bf16[1,256,2048]{2,1,0:T(8,128)(2,1)} %param.7) | copy-start | bytes 3145732
  59.8 6.1 %copy-start.9 = (bf16[64,4096]{1,0:T(8,128)(2,1)}, bf16[64,4096]{1,0:T(8,128)(2,1)S(1)}, u32[]{:S(2)}) copy-start(bf16[64,4096]{1,0:T(8,128)(2,1)S(1)} %shard_map.80) | copy-start | bytes 1572868
  61.4 4.5 %copy-start.11 = (bf16[64,4096]{1,0:T(8,128)(2,1)}, bf16[64,4096]{1,0:T(8,128)(2,1)S(1)}, u32[]{:S(2)}) copy-start(bf16[64,4096]{1,0:T(8,128)(2,1)S(1)} %shard_map.79) | copy-start | bytes 1572868
  63.0 0.8 copy-start.10
  63.8 14.0 %copy-start.13 = (f32[64,256]{1,0:T(8,128)}, f32[64,256]{1,0:T(8,128)S(1)}, u32[]{:S(2)}) copy-start(f32[64,256]{1,0:T(8,128)S(1)} %collective-permute-done.8) | copy-start | bytes 196612
  68.8 8.0 %collective-permute-start.9 = (bf16[8,64,512]{2,1,0:T(8,128)(2,1)S(1)}, bf16[8,64,512]{2,1,0:T(8,128)(2,1)S(1)}, u32[]{:S(2)}, u32[]{:S(2)}) collective-permute-start(bf16[8,64,512]{2,1,0:T(8,128)(2,1)S(1)} %get-tuple-element.47), channel_id=1, source_target_pairs={{0,16},{16,0},{1,17},{17,1},{2,18},{18,2},{3,19},{19,3},{4,20},{20... | collective-permute-start | bytes 1572872 | tf_op jit(solution)/shard_map/ppermute | solution.py:22
  77.8 28.1 %all-to-all-start = ((bf16[8,64,512]{2,1,0:T(8,128)(2,1)}), bf16[8,64,512]{2,1,0:T(8,128)(2,1)}, u32[]{:S(2)}, u32[]{:S(2)}) async-start(bf16[8,64,512]{2,1,0:T(8,128)(2,1)} %add_convert_fusion), calls=%async_computation | async-start | bytes 1048576 | tf_op jit(solution)/shard_map/all_to_all | solution.py:286
  87.8 24.5 %collective-permute-start.11 = (bf16[64,4096]{1,0:T(8,128)(2,1)}, bf16[64,4096]{1,0:T(8,128)(2,1)}, u32[]{:S(2)}, u32[]{:S(2)}) collective-permute-start(bf16[64,4096]{1,0:T(8,128)(2,1)} %copy-done.11), channel_id=1, source_target_pairs={{0,4},{4,0},{8,12},{12,8},{1,5},{5,1},{9,13},{13,9},{2,6},{6,2},{1... | collective-permute-start | bytes 1572872 | tf_op jit(solution)/shard_map/ppermute | solution.py:22
  89.7 25.4 %collective-permute-start.12 = (bf16[64,4096]{1,0:T(8,128)(2,1)}, bf16[64,4096]{1,0:T(8,128)(2,1)}, u32[]{:S(2)}, u32[]{:S(2)}) collective-permute-start(bf16[64,4096]{1,0:T(8,128)(2,1)} %copy-done.9), channel_id=1, source_target_pairs={{0,8},{4,12},{8,0},{12,4},{1,9},{5,13},{9,1},{13,5},{2,10},{6,14},... | collective-permute-start | bytes 1572872 | tf_op jit(solution)/shard_map/ppermute | solution.py:22
  94.2 26.9 %collective-permute-start.13 = (bf16[64,4096]{1,0:T(8,128)(2,1)}, bf16[64,4096]{1,0:T(8,128)(2,1)}, u32[]{:S(2)}, u32[]{:S(2)}) collective-permute-start(bf16[64,4096]{1,0:T(8,128)(2,1)} %copy-done.10), channel_id=1, source_target_pairs={{0,12},{4,8},{8,4},{12,0},{1,13},{5,9},{9,5},{13,1},{2,14},{6,10},... | collective-permute-start | bytes 1572872 | tf_op jit(solution)/shard_map/ppermute | solution.py:22
  107.0 14.0 %collective-permute-start.10 = (f32[64,512]{1,0:T(8,128)S(1)}, f32[64,512]{1,0:T(8,128)S(1)}, u32[]{:S(2)}, u32[]{:S(2)}) collective-permute-start(f32[64,512]{1,0:T(8,128)S(1)} %convert_reduce_fusion.mine_ref), channel_id=1, source_target_pairs={{0,32},{32,0},{1,33},{33,1},{2,34},{34,2},{3,35},{35,3},{4,36},{36... | collective-permute-start | bytes 393224 | tf_op jit(solution)/shard_map/ppermute | solution.py:22
  111.3 37.0 %copy-start.8 = (bf16[1,256,2048]{2,1,0:T(8,128)(2,1)S(1)}, bf16[1,256,2048]{2,1,0:T(8,128)(2,1)}, u32[]{:S(2)}) copy-start(bf16[1,256,2048]{2,1,0:T(8,128)(2,1)} %param.7) | copy-start | bytes 3145732
  142.3 10.1 %collective-permute-start.14 = (bf16[8,64,512]{2,1,0:T(8,128)(2,1)S(1)}, bf16[8,64,512]{2,1,0:T(8,128)(2,1)S(1)}, u32[]{:S(2)}, u32[]{:S(2)}) collective-permute-start(bf16[8,64,512]{2,1,0:T(8,128)(2,1)S(1)} %all_to_all.10.mine_ref), channel_id=1, source_target_pairs={{0,16},{16,0},{1,17},{17,1},{2,18},{18,2},{3,19},{19,3},{4,20},{20... | collective-permute-start | bytes 1572872 | tf_op jit(solution)/shard_map/ppermute | solution.py:22

commit v8 on v7

--- a/solution.py
+++ b/solution.py
@@ -15,7 +15,7 @@
 F32, BF16 = jnp.float32, jnp.bfloat16
 NODE = ("z", "yh", "c")
 SHAPE = (8, 2, 2, 4, 4)
-VMEM_LIMIT = 32 * 1024 * 1024
+VMEM_LIMIT = 16 * 1024 * 1024
 
 
 def swap(value, axis, flip, size):
@@ -47,42 +47,104 @@
     return lax.broadcasted_iota(jnp.int32, (BLK, LANES), 1) // BLK
 
 
-def pack_kernel(k, base, list_ref, mat_ref, out_ref):
+def product(at_ref, k, shards, cot_ref, left_ref, part_ref):
+    for m, shard in enumerate(shards):
+
+        @pl.when(at_ref[0] ^ k == m)
+        def _(shard=shard):
+            left_ref[...] = shard[...]
+
+    for at in range(0, cot_ref.shape[1], 512):
+        part_ref[:, at : at + 512] = lax.dot_general(
+            left_ref[...],
+            cot_ref[:, at : at + 512],
+            (((0,), (0,)), ((), ())),
+            preferred_element_type=F32,
+        ).astype(BF16)
+
+
+def pack(list_ref, k, base, count, part_ref, out_ref, lead=None):
     upper = lane_halves() == 1
 
     def tile(q, carry):
         sides = []
         for side in range(2):
             rows, cols, half = place_of(list_ref[k, base + 2 * q + side])
-            block = mat_ref[rows, cols]
+            block = part_ref[rows, cols]
             sides.append(jnp.where(half == side, block, pltpu.roll(block, BLK, 1)))
         at = pl.ds(pl.multiple_of(q * LANES, LANES), LANES)
-        out_ref[:, at] = jnp.where(upper, sides[1], sides[0])
+        value = jnp.where(upper, sides[1], sides[0])
+        if lead is None:
+            out_ref[:, at] = value
+        else:
+            out_ref[lead, :, at] = value
         return carry
 
-    lax.fori_loop(0, HALF // 2, tile, 0, unroll=True)
-
-
-def pack(lists, mat, k, base):
+    lax.fori_loop(0, count // 2, tile, 0, unroll=True)
+
+
+def first_kernel(row, list_ref, part_ref, out_ref):
+    pack(list_ref, row, 0, HALF, part_ref, out_ref)
+
+
+def rest_kernel(
+    list_ref, at_ref, s0, s1, s2, s3, cot_ref,
+    give_a, give_b, keep_a, keep_b, own_ref, left_ref, part_ref,
+):
+    shards, half = (s0, s1, s2, s3), HALF // 2
+    low, high = 0, half
+    product(at_ref, 1, shards, cot_ref, left_ref, part_ref)
+    pack(list_ref, 1, low, half, part_ref, give_a, 0)
+    pack(list_ref, 1, high, half, part_ref, keep_b)
+    product(at_ref, 2, shards, cot_ref, left_ref, part_ref)
+    pack(list_ref, 2, low, half, part_ref, give_a, 1)
+    pack(list_ref, 2, high, half, part_ref, give_b, 1)
+    product(at_ref, 3, shards, cot_ref, left_ref, part_ref)
+    pack(list_ref, 3, high, half, part_ref, give_b, 0)
+    pack(list_ref, 3, low, half, part_ref, keep_a)
+    product(at_ref, 0, shards, cot_ref, left_ref, own_ref)
+
+
+def products_call(body, lists, at, shards, cotangent, out_shape):
     whole = pl.BlockSpec(memory_space=pltpu.VMEM)
-    return kernel_call(
-        functools.partial(pack_kernel, k, base),
-        (),
-        [SMEM, whole],
-        whole,
-        jax.ShapeDtypeStruct((BLK, HALF * BLK), BF16),
-        1 << 20,
-    )(lists, mat)
-
-
-def unpack(list_ref, base, terms, grad_ref):
+    depth, width = shards[0].shape
+    cols = cotangent.shape[1]
+    return pl.pallas_call(
+        body,
+        in_specs=[SMEM, SMEM] + [whole] * 5,
+        out_specs=jax.tree.map(lambda _: whole, out_shape),
+        out_shape=out_shape,
+        scratch_shapes=[pltpu.VMEM((depth, width), BF16), pltpu.VMEM((width, cols), BF16)],
+        compiler_params=pltpu.CompilerParams(vmem_limit_bytes=VMEM_LIMIT),
+        cost_estimate=pl.CostEstimate(flops=1 << 20, bytes_accessed=1 << 20, transcendentals=0),
+    )(lists, at, *shards, cotangent)
+
+
+def packed(*lead, blocks=HALF):
+    return jax.ShapeDtypeStruct((*lead, BLK, blocks * BLK), BF16)
+
+
+def chosen_part(row, lists, part):
+    whole = pl.BlockSpec(memory_space=pltpu.VMEM)
+    body = functools.partial(first_kernel, row)
+    return kernel_call(body, (), [SMEM, whole], whole, packed(), 1 << 20)(lists, part)
+
+
+def rest_parts(lists, at, shards, cotangent):
+    half = HALF // 2
+    own = jax.ShapeDtypeStruct((shards[0].shape[1], cotangent.shape[1]), BF16)
+    shapes = [packed(2, blocks=half)] * 2 + [packed(blocks=half)] * 2 + [own]
+    return products_call(rest_kernel, lists, at, shards, cotangent, shapes)
+
+
+def unpack(list_ref, base, count, terms, grad_ref):
     halves = lane_halves()
 
     def tile(q, carry):
         at = pl.ds(pl.multiple_of(q * LANES, LANES), LANES)
-        value = terms[0][:, at].astype(F32)
+        value = terms[0](at).astype(F32)
         for term in terms[1:]:
-            value = value + term[:, at].astype(F32)
+            value = value + term(at).astype(F32)
         turned = pltpu.roll(value, BLK, 1)
         for side in range(2):
             rows, cols, half = place_of(list_ref[0, base + 2 * q + side])
@@ -90,7 +152,7 @@
             grad_ref[rows, cols] = jnp.where(halves == half, moved, grad_ref[rows, cols])
         return carry
 
-    lax.fori_loop(0, HALF // 2, tile, 0, unroll=True)
+    lax.fori_loop(0, count // 2, tile, 0, unroll=True)
 
 
 def chosen_kernel(
@@ -100,7 +162,8 @@
 
     @pl.when(row == 0)
     def _():
-        unpack(list_ref, 0, (got_1, got_2, got_3), grad_ref)
+        terms = [lambda at, ref=ref: ref[:, at] for ref in (got_1, got_2, got_3)]
+        unpack(list_ref, 0, HALF, terms, grad_ref)
 
     first = c_ref[0] == 0
     rows = pl.ds(pl.multiple_of(row * BLK, BLK), BLK)
@@ -119,12 +182,17 @@
             other_ref[h, :, place] = jnp.where(first, sent[1], sent[0]).astype(BF16)
 
 
-def residual_kernel(list_ref, mask_ref, fb_ref, own_ref, got_1, got_2, got_3, new_ref, grad_ref):
+def residual_kernel(
+    list_ref, mask_ref, fb_ref, own_ref, got_a, got_b, next_a, next_b, new_ref, grad_ref
+):
     row = pl.program_id(0)
 
     @pl.when(row == 0)
     def _():
-        unpack(list_ref, HALF, (got_1, got_2, got_3), grad_ref)
+        half = HALF // 2
+        for base, got, nxt in ((0, got_a, next_a), (half, got_b, next_b)):
+            terms = [lambda at, ref=got: ref[0, :, at], lambda at, ref=nxt: ref[:, at]]
+            unpack(list_ref, base, half, terms, grad_ref)
 
     rows = pl.ds(pl.multiple_of(row * BLK, BLK), BLK)
     for at in range(0, fb_ref.shape[1], 256):
@@ -139,11 +207,11 @@
     rows, cols = feedback.shape
     wide = pl.BlockSpec((BLK, cols), lambda i: (i, 0))
     line = pl.BlockSpec((1, 1, cols), lambda i: (i, 0, 0))
-    packed = [pl.BlockSpec(r.shape, lambda i: (0, 0)) for r in received]
+    given = [pl.BlockSpec(r.shape, lambda i, n=r.ndim: (0,) * n) for r in received]
     return pl.pallas_call(
         body,
         grid=(rows // BLK,),
-        in_specs=[SMEM] * len(scalars) + [line, wide, wide] + packed,
+        in_specs=[SMEM] * len(scalars) + [line, wide, wide] + given,
         out_specs=outs,
         out_shape=out_shape,
         scratch_shapes=[pltpu.VMEM((rows, cols), F32)],
@@ -218,24 +286,24 @@
     )(c, mine, other)
 
 
-def block_lists(chosen, count):
-    near = swap(chosen, "dp", 1, 4)
-    across = swap(jnp.stack([chosen, near]), "dp", 3, 4)
-    lists = jnp.stack([chosen, near, across[1], across[0]])
+def others_of(lists, count):
     blocks = jnp.arange(count, dtype=jnp.int32)
     left = jnp.all(lists[:, :, None] != blocks, axis=1)
     before = blocks[:, None] < blocks[None, :]
     rank = jnp.sum(jnp.where(left[:, :, None] & before, 1, 0), axis=1)
     slots = jnp.arange(count // 2, dtype=jnp.int32)
     hit = left[:, None, :] & (rank[:, None, :] == slots[None, :, None])
-    others = jnp.sum(jnp.where(hit, blocks, 0), axis=2)
-    return jnp.concatenate([lists, others], axis=1)
+    return jnp.sum(jnp.where(hit, blocks, 0), axis=2)
 
 
 def gather_hidden(hidden):
     far = swap(hidden, "t", 2, 4)
     near = swap(hidden, "t", 1, 4)
     return hidden, near, far, swap(far, "t", 1, 4)
+
+
+def plus(kept, got):
+    return (kept.astype(F32) + got.astype(F32)).astype(BF16)
 
 
 def as_matrix(blocks):
@@ -254,46 +322,51 @@
     mask = jnp.any(chosen.reshape(-1, 1, 1) == block_of[None], axis=0).astype(F32)
     moment = as_matrix(momentum[0, 0])
     mask = mask[:, None]
-    lists = block_lists(chosen.reshape(-1), rows_blk * cols_blk)
-    *shards, lists = lax.optimization_barrier((*gather_hidden(hidden), lists))
-    shards = jnp.stack(shards)
-    d, t = lax.axis_index("dp"), lax.axis_index("t")
-
-    def product(flip, shards):
-        part = lax.dynamic_index_in_dim(shards, t ^ d ^ flip, 0, keepdims=False)
-        return lax.dot_general(
-            part, cotangent, (((0,), (0,)), ((), ())), preferred_element_type=F32
+    picks = chosen.reshape(1, -1)
+    near_picks = swap(picks, "dp", 1, 4)
+    far_picks = swap(jnp.concatenate([picks, near_picks]), "dp", 3, 4)
+    *shards, near_picks, far_picks = lax.optimization_barrier(
+        (*gather_hidden(hidden), near_picks, far_picks)
+    )
+    at = (lax.axis_index("dp") ^ lax.axis_index("t")).astype(jnp.int32).reshape(1)
+    got = {}
+    for k, row, lists in ((2, 1, far_picks), (1, 0, near_picks), (3, 0, far_picks)):
+        part = lax.dot_general(
+            lax.select_n(at[0] ^ k, *shards),
+            cotangent,
+            (((0,), (0,)), ((), ())),
+            preferred_element_type=F32,
         ).astype(BF16)
-
-    parts, got = {}, {}
-    for k in (2, 1, 3):
-        parts[k] = product(k, shards)
-        given = pack(lists, parts[k], k, 0)
+        given = chosen_part(row, lists, part)
+        if k == 3:
+            *shards, given, moment = lax.optimization_barrier((*shards, given, moment))
+        else:
+            *shards, _ = lax.optimization_barrier((*shards, given))
         got[k] = swap(given, "dp", k, 4)
-        shards, given = lax.optimization_barrier((shards, given))
-    moment, given = lax.optimization_barrier((moment, given))
     far_moment = swap(moment, "yh", 1, 2)
-    own = product(0, shards)
-    left = [pack(lists, parts[k], k, HALF) for k in (1, 2, 3)]
-    got = [got[k] for k in (1, 2, 3)]
-    *got, far_moment, own, left_1, left_2, left_3 = lax.optimization_barrier(
-        (*got, far_moment, own, *left)
-    )
-    mine, other = chosen_sums(lists, at_c, mask, feedback[0], own, *got)
+    others = jnp.concatenate([picks, near_picks, far_picks[1:], far_picks[:1]])
+    others = others_of(others, rows_blk * cols_blk)
+    rest = rest_parts(others, at, shards, cotangent)
+    got_1, got_2, got_3, far_moment, give_a, give_b, keep_a, keep_b, own = (
+        lax.optimization_barrier((got[1], got[2], got[3], far_moment, *rest))
+    )
+    mine, other = chosen_sums(picks, at_c, mask, feedback[0], own, got_1, got_2, got_3)
     pair = (mine + swap(other, "c", 1, 2).astype(F32)).astype(BF16)
-    pair, *left = lax.optimization_barrier((pair, left_1, left_2, left_3))
-    left = [swap(part, "dp", k, 4) for k, part in zip((1, 2, 3), left)]
+    pair, give_a, give_b = lax.optimization_barrier((pair, give_a, give_b))
+    got_a, got_b = swap(give_a, "dp", 1, 4), swap(give_b, "dp", 3, 4)
     across = lax.all_to_all(pair, "z", 0, 0, tiled=True)
     near = jnp.sum(across.astype(F32), axis=0)
     far = swap(near, "yh", 1, 2)
-    far, *left = lax.optimization_barrier((far, *left))
+    far, got_a, got_b = lax.optimization_barrier((far, got_a, got_b))
     moment = jnp.where(
         yh == 0, jnp.concatenate([moment, far_moment], 1), jnp.concatenate([far_moment, moment], 1)
     )
     momentum_new, copies = owner_update(at_yh, near, far, moment)
+    copies, got_a, got_b = lax.optimization_barrier((copies, got_a, got_b))
+    next_a = swap(plus(keep_a, got_a[1]), "dp", 3, 4)
+    next_b = swap(plus(keep_b, got_b[1]), "dp", 1, 4)
     every = lax.all_to_all(copies, "z", 0, 0, tiled=True)
-    *left, _ = lax.optimization_barrier((*left, copies))
-    feedback_new = residual(lists, mask, feedback[0], own, *left)
+    feedback_new = residual(others, mask, feedback[0], own, got_a, got_b, next_a, next_b)
     step = assemble(at_c, every, swap(every, "c", 1, 2), rows, cols)
     return feedback_new[None], momentum_new[None, None], step
 

time: 155 us -> 168 us (1.084)
  the two profiles are of different devices: /device:TPU:1 before, /device:TPU:16 now
where the time goes in v8:
time: 168 us; the launch traced here: 167 us
  starting transfers between devices  68.4 us (41%)
  waiting for transfers between devices  60.8 us (36%)
  Pallas kernels  19.7 us (12%)
  other arithmetic  8.07 us (5%)
  local copies, waits for them, and re-layouts  4.69 us (3%)
  matrix products  3.98 us (2%)
    ppermute x16, starting transfers between devices, swap(): return lax.ppermute(value, axis, [(i, i ^ flip) for i in range(size)])  54.6 us
    ppermute x16, waiting for transfers between devices, swap(): return lax.ppermute(value, axis, [(i, i ^ flip) for i in range(size)])  33.5 us
    all_to_all x1, waiting for transfers between devices, local(): every = lax.all_to_all(copies, 'z', 0, 0, tiled=True)  14.1 us
    all_to_all x1, waiting for transfers between devices, local(): across = lax.all_to_all(pair, 'z', 0, 0, tiled=True)  13.2 us
    all_to_all x1, starting transfers between devices, local(): across = lax.all_to_all(pair, 'z', 0, 0, tiled=True)  10.3 us
    pallas_call x1, Pallas kernels, products_call(): pl.pallas_call(body, in_specs=[SMEM, SMEM] + [whole] * 5, out_specs=jax.t...  6.6 us
    pallas_call x2, Pallas kernels, state_call(): pl.pallas_call(body, grid=(rows // BLK,), in_specs=[SMEM] * len(scalars)...  5.23 us
    pallas_call x3, Pallas kernels, chosen_part(): kernel_call(body, (), [SMEM, whole], whole, packed(), 1 << 20)(lists, part)  4.62 us
  transfers between devices with their start and end apart: 18, of which 8 were waited for; matrix products, arithmetic and copies ran while one was open for 5% of the time, Pallas kernels for 7%

profile of v8, /device:TPU:16, one launch (start us, length us, event | category | flops | bytes accessed | tf_op | source)
XLA Modules:
  0.0 166.7 jit_solution(11227019557416121774)
XLA Ops:
  0.6 7.6 %collective-permute-start.1 = (bf16[512,256]{1,0:T(8,128)(2,1)}, bf16[512,256]{1,0:T(8,128)(2,1)S(1)}, u32[]{:S(2)}, u32[]{:S(2)}) collective-permute-start(bf16[512,256]{1,0:T(8,128)(2,1)} %s0), channel_id=1, source_target_pairs={{0,2},{1,3},{2,0},{3,1},{4,6},{5,7},{6,4},{7,5},{8,10},{9,11},{10,... | collective-permute-start | bytes 786440 | tf_op jit(solution)/shard_map/ppermute | solution.py:22
  8.3 1.9 %collective-permute-start = (bf16[512,256]{1,0:T(8,128)(2,1)}, bf16[512,256]{1,0:T(8,128)(2,1)S(1)}, u32[]{:S(2)}, u32[]{:S(2)}) collective-permute-start(bf16[512,256]{1,0:T(8,128)(2,1)} %s0), channel_id=1, source_target_pairs={{0,1},{1,0},{2,3},{3,2},{4,5},{5,4},{6,7},{7,6},{8,9},{9,8},{10,11... | collective-permute-start | bytes 786440 | tf_op jit(solution)/shard_map/ppermute | solution.py:22
  10.2 1.9 %collective-permute-start.3 = (s32[1,64]{1,0:T(1,128)}, s32[1,64]{1,0:T(1,128)S(1)}, u32[]{:S(2)}, u32[]{:S(2)}) collective-permute-start(s32[1,64]{1,0:T(1,128)} %bitcast.22), channel_id=1, source_target_pairs={{0,4},{4,0},{8,12},{12,8},{1,5},{5,1},{9,13},{13,9},{2,6},{6,2},{1... | collective-permute-start | bytes 776 | tf_op jit(solution)/shard_map/ppermute | solution.py:22
  12.2 2.7 %collective-permute-done.1.s2 = bf16[512,256]{1,0:T(8,128)(2,1)S(1)} collective-permute-done((bf16[512,256]{1,0:T(8,128)(2,1)}, bf16[512,256]{1,0:T(8,128)(2,1)S(1)}, u32[]{:S(2)}, u32[]{:S(2)}) %collective-permute-start.1) | collective-permute-done | bytes 262176 | tf_op jit(solution)/shard_map/ppermute | solution.py:22
  14.9 5.9 %collective-permute-start.2 = (bf16[512,256]{1,0:T(8,128)(2,1)S(1)}, bf16[512,256]{1,0:T(8,128)(2,1)S(1)}, u32[]{:S(2)}, u32[]{:S(2)}) collective-permute-start(bf16[512,256]{1,0:T(8,128)(2,1)S(1)} %collective-permute-done.1.s2), channel_id=1, source_target_pairs={{0,1},{1,0},{2,3},{3,2},{4,5},{5,4},{6,7},{7,6},{8,9},{9,8},{10,11... | collective-permute-start | bytes 786440 | tf_op jit(solution)/shard_map/ppermute | solution.py:22
  22.6 4.6 %collective-permute-start.4 = (s32[2,64]{1,0:T(2,128)S(1)}, s32[2,64]{1,0:T(2,128)S(1)}, u32[]{:S(2)}, u32[]{:S(2)}) collective-permute-start(s32[2,64]{1,0:T(2,128)S(1)} %pad_add_fusion.1), channel_id=1, source_target_pairs={{0,12},{4,8},{8,4},{12,0},{1,13},{5,9},{9,5},{13,1},{2,14},{6,10},... | collective-permute-start | bytes 1544 | tf_op jit(solution)/shard_map/ppermute | solution.py:22
  29.2 2.4 %convolution_convert_fusion.2.part_ref = bf16[256,2048]{1,0:T(8,128)(2,1)S(1)} fusion(bf16[512,2048]{1,0:T(8,128)(2,1)} %cot_ref.1, bf16[512,256]{1,0:T(8,128)(2,1)S(1)} %collective-permute-done.1.s2, bf16[512,256]{1,0:T(8,128)(2,1)S(1)} %collective-permute-done.2.s3, bf16[512,256]{1,0:T(8,128)(2,1)} %s0, bf16[512,256]{1,0:T(8,128)(2,1)S(1)} %collective-permute-done.s1, ...), kind=kOutput, calls=%fused_computation.2 | convolution fusion | flops 537788416 | bytes 4194307 | tf_op jit(solution)/shard_map/dot_general | solution.py:334
  31.7 1.5 shard_map.76
  35.6 2.0 %collective-permute-start.5 = (bf16[64,4096]{1,0:T(8,128)(2,1)S(1)}, bf16[64,4096]{1,0:T(8,128)(2,1)S(1)}, u32[]{:S(2)}, u32[]{:S(2)}) collective-permute-start(bf16[64,4096]{1,0:T(8,128)(2,1)S(1)} %shard_map.77), channel_id=1, source_target_pairs={{0,4},{4,0},{8,12},{12,8},{1,5},{5,1},{9,13},{13,9},{2,6},{6,2},{1... | collective-permute-start | bytes 1572872 | tf_op jit(solution)/shard_map/ppermute | solution.py:22
  37.6 5.8 %collective-permute-start.6 = (bf16[64,4096]{1,0:T(8,128)(2,1)S(1)}, bf16[64,4096]{1,0:T(8,128)(2,1)S(1)}, u32[]{:S(2)}, u32[]{:S(2)}) collective-permute-start(bf16[64,4096]{1,0:T(8,128)(2,1)S(1)} %shard_map.76), channel_id=1, source_target_pairs={{0,8},{4,12},{8,0},{12,4},{1,9},{5,13},{9,1},{13,5},{2,10},{6,14},... | collective-permute-start | bytes 1572872 | tf_op jit(solution)/shard_map/ppermute | solution.py:22
  45.8 2.5 %collective-permute-start.7 = (bf16[64,4096]{1,0:T(8,128)(2,1)S(1)}, bf16[64,4096]{1,0:T(8,128)(2,1)S(1)}, u32[]{:S(2)}, u32[]{:S(2)}) collective-permute-start(bf16[64,4096]{1,0:T(8,128)(2,1)S(1)} %shard_map.78), channel_id=1, source_target_pairs={{0,12},{4,8},{8,4},{12,0},{1,13},{5,9},{9,5},{13,1},{2,14},{6,10},... | collective-permute-start | bytes 1572872 | tf_op jit(solution)/shard_map/ppermute | solution.py:22
  48.4 5.1 %collective-permute-start.8 = (f32[64,256]{1,0:T(8,128)S(1)}, f32[64,256]{1,0:T(8,128)S(1)}, u32[]{:S(2)}, u32[]{:S(2)}) collective-permute-start(f32[64,256]{1,0:T(8,128)S(1)} %reshape.122), channel_id=1, source_target_pairs={{0,32},{32,0},{1,33},{33,1},{2,34},{34,2},{3,35},{35,3},{4,36},{36... | collective-permute-start | bytes 196616 | tf_op jit(solution)/shard_map/ppermute | solution.py:22
  53.9 6.6 %shard_map.79 = (bf16[2,64,2048]{2,1,0:T(8,128)(2,1)}, bf16[2,64,2048]{2,1,0:T(8,128)(2,1)S(1)}, bf16[64,2048]{1,0:T(8,128)(2,1)S(1)}, bf16[64,2048]{1,0:T(8,128)(2,1)S(1)}, bf16[256,2048]{1,0:T(8,128)(2,1)S(1)}) custom-call(s32[4,64]{1,0:T(4,128)S(1)} %select_reduce_fusion.1.list_ref, s32[1]{0:T(128)} %bitcast.5.at_ref, bf16[512,256]{1,0:T(8,128)(2,1)S(1)} %copy-done.1, ...), custom_call_target="tpu_custom_call" | custom-call | flops 1048576 | bytes 1048576 | tf_op jit(solution)/shard_map/pallas_call | solution.py:112
  60.6 11.3 %collective-permute-done.7.got_3 = bf16[64,4096]{1,0:T(8,128)(2,1)S(1)} collective-permute-done((bf16[64,4096]{1,0:T(8,128)(2,1)S(1)}, bf16[64,4096]{1,0:T(8,128)(2,1)S(1)}, u32[]{:S(2)}, u32[]{:S(2)}) %collective-permute-start.7) | collective-permute-done | bytes 524320 | tf_op jit(solution)/shard_map/ppermute | solution.py:22
  71.9 2.0 %shard_map.80 = (f32[8,64,512]{2,1,0:T(8,128)S(1)}, bf16[8,64,512]{2,1,0:T(8,128)(2,1)S(1)}) custom-call(s32[1,64]{1,0:T(1,128)S(1)} %bitcast.26, s32[1]{0:T(128)} %bitcast.7.c_ref, f32[4,1,2048]{2,1,0:T(1,128)S(1)} %reshape.126.mask_ref, bf16[256,2048]{1,0:T(8,128)(2,1)S(1)} %bitcast.20, bf16[256,2048]{1,0:T(8,128)(2,1)S(1)} %get-tuple-element.75.own_ref, ...), custom_call_target="tpu_custom_call" | custom-call | flops 4194304 | bytes 4194304 | tf_op jit(solution)/shard_map/pallas_call | solution.py:211
  74.0 1.9 %collective-permute-start.9 = (bf16[8,64,512]{2,1,0:T(8,128)(2,1)S(1)}, bf16[8,64,512]{2,1,0:T(8,128)(2,1)S(1)}, u32[]{:S(2)}, u32[]{:S(2)}) collective-permute-start(bf16[8,64,512]{2,1,0:T(8,128)(2,1)S(1)} %get-tuple-element.80), channel_id=1, source_target_pairs={{0,16},{16,0},{1,17},{17,1},{2,18},{18,2},{3,19},{19,3},{4,20},{20... | collective-permute-start | bytes 1572872 | tf_op jit(solution)/shard_map/ppermute | solution.py:22
  75.9 1.9 %collective-permute-done.9 = bf16[8,64,512]{2,1,0:T(8,128)(2,1)S(1)} collective-permute-done((bf16[8,64,512]{2,1,0:T(8,128)(2,1)S(1)}, bf16[8,64,512]{2,1,0:T(8,128)(2,1)S(1)}, u32[]{:S(2)}, u32[]{:S(2)}) %collective-permute-start.9) | collective-permute-done | bytes 524320 | tf_op jit(solution)/shard_map/ppermute | solution.py:22
  78.8 10.3 %all-to-all-start = ((bf16[8,64,512]{2,1,0:T(8,128)(2,1)}), bf16[8,64,512]{2,1,0:T(8,128)(2,1)}, u32[]{:S(2)}, u32[]{:S(2)}) async-start(bf16[8,64,512]{2,1,0:T(8,128)(2,1)} %add_convert_fusion), calls=%async_computation | async-start | bytes 1048576 | tf_op jit(solution)/shard_map/all_to_all | solution.py:357
  89.1 1.9 %collective-permute-start.11 = (bf16[2,64,2048]{2,1,0:T(8,128)(2,1)}, bf16[2,64,2048]{2,1,0:T(8,128)(2,1)S(1)}, u32[]{:S(2)}, u32[]{:S(2)}) collective-permute-start(bf16[2,64,2048]{2,1,0:T(8,128)(2,1)} %get-tuple-element.84), channel_id=1, source_target_pairs={{0,4},{4,0},{8,12},{12,8},{1,5},{5,1},{9,13},{13,9},{2,6},{6,2},{1... | collective-permute-start | bytes 1572872 | tf_op jit(solution)/shard_map/ppermute | solution.py:22
  91.0 2.8 %collective-permute-start.12 = (bf16[2,64,2048]{2,1,0:T(8,128)(2,1)}, bf16[2,64,2048]{2,1,0:T(8,128)(2,1)S(1)}, u32[]{:S(2)}, u32[]{:S(2)}) collective-permute-start(bf16[2,64,2048]{2,1,0:T(8,128)(2,1)} %copy-done.11), channel_id=1, source_target_pairs={{0,12},{4,8},{8,4},{12,0},{1,13},{5,9},{9,5},{13,1},{2,14},{6,10},... | collective-permute-start | bytes 1572872 | tf_op jit(solution)/shard_map/ppermute | solution.py:22
  93.8 13.2 %all-to-all-done = bf16[8,64,512]{2,1,0:T(8,128)(2,1)} async-done(((bf16[8,64,512]{2,1,0:T(8,128)(2,1)}), bf16[8,64,512]{2,1,0:T(8,128)(2,1)}, u32[]{:S(2)}, u32[]{:S(2)}) %all-to-all-start) | async-done | bytes 524320 | tf_op jit(solution)/shard_map/all_to_all | solution.py:357
  108.1 3.9 %collective-permute-start.10 = (f32[64,512]{1,0:T(8,128)S(1)}, f32[64,512]{1,0:T(8,128)}, u32[]{:S(2)}, u32[]{:S(2)}) collective-permute-start(f32[64,512]{1,0:T(8,128)S(1)} %convert_reduce_fusion.mine_ref), channel_id=1, source_target_pairs={{0,32},{32,0},{1,33},{33,1},{2,34},{34,2},{3,35},{35,3},{4,36},{36... | collective-permute-start | bytes 393224 | tf_op jit(solution)/shard_map/ppermute | solution.py:22
  113.0 8.4 %collective-permute-done.10.peer_ref = f32[64,512]{1,0:T(8,128)} collective-permute-done((f32[64,512]{1,0:T(8,128)S(1)}, f32[64,512]{1,0:T(8,128)}, u32[]{:S(2)}, u32[]{:S(2)}) %collective-permute-start.10) | collective-permute-done | bytes 131104 | tf_op jit(solution)/shard_map/ppermute | solution.py:22
  121.4 1.7 shard_map.81
  123.9 3.5 %all-to-all-start.1 = ((bf16[8,64,512]{2,1,0:T(8,128)(2,1)}), bf16[8,64,512]{2,1,0:T(8,128)(2,1)S(1)}, u32[]{:S(2)}, u32[]{:S(2)}) async-start(bf16[8,64,512]{2,1,0:T(8,128)(2,1)} %copy-done.5), calls=%async_computation.1 | async-start | bytes 1048576 | tf_op jit(solution)/shard_map/all_to_all | solution.py:368
  127.4 1.8 %fusion = bf16[64,2048]{1,0:T(8,128)(2,1)} fusion(bf16[64,2048]{1,0:T(8,128)(2,1)} %copy-done.7, bf16[2,64,2048]{2,1,0:T(8,128)(2,1)} %copy-done.3), kind=kLoop, calls=%fused_computation.7 | loop fusion | flops 524288 | bytes 786432 | tf_op jit(solution)/shard_map/convert_element_type | solution.py:306
  129.2 1.9 %collective-permute-start.14 = (bf16[64,2048]{1,0:T(8,128)(2,1)}, bf16[64,2048]{1,0:T(8,128)(2,1)S(1)}, u32[]{:S(2)}, u32[]{:S(2)}) collective-permute-start(bf16[64,2048]{1,0:T(8,128)(2,1)} %fusion), channel_id=1, source_target_pairs={{0,4},{4,0},{8,12},{12,8},{1,5},{5,1},{9,13},{13,9},{2,6},{6,2},{1... | collective-permute-start | bytes 786440 | tf_op jit(solution)/shard_map/ppermute | solution.py:22
  131.1 14.1 %all-to-all-done.1.mine_ref = bf16[8,64,512]{2,1,0:T(8,128)(2,1)S(1)} async-done(((bf16[8,64,512]{2,1,0:T(8,128)(2,1)}), bf16[8,64,512]{2,1,0:T(8,128)(2,1)S(1)}, u32[]{:S(2)}, u32[]{:S(2)}) %all-to-all-start.1) | async-done | bytes 524320 | tf_op jit(solution)/shard_map/all_to_all | solution.py:368
  145.2 1.9 %collective-permute-start.15 = (bf16[8,64,512]{2,1,0:T(8,128)(2,1)S(1)}, bf16[8,64,512]{2,1,0:T(8,128)(2,1)S(1)}, u32[]{:S(2)}, u32[]{:S(2)}) collective-permute-start(bf16[8,64,512]{2,1,0:T(8,128)(2,1)S(1)} %all-to-all-done.1.mine_ref), channel_id=1, source_target_pairs={{0,16},{16,0},{1,17},{17,1},{2,18},{18,2},{3,19},{19,3},{4,20},{20... | collective-permute-start | bytes 1572872 | tf_op jit(solution)/shard_map/ppermute | solution.py:22
  148.1 2.7 %collective-permute-start.13 = (bf16[64,2048]{1,0:T(8,128)(2,1)S(1)}, bf16[64,2048]{1,0:T(8,128)(2,1)S(1)}, u32[]{:S(2)}, u32[]{:S(2)}) collective-permute-start(bf16[64,2048]{1,0:T(8,128)(2,1)S(1)} %fusion.1), channel_id=1, source_target_pairs={{0,12},{4,8},{8,4},{12,0},{1,13},{5,9},{9,5},{13,1},{2,14},{6,10},... | collective-permute-start | bytes 786440 | tf_op jit(solution)/shard_map/ppermute | solution.py:22
  151.6 8.4 %collective-permute-done.13.next_a = bf16[64,2048]{1,0:T(8,128)(2,1)S(1)} collective-permute-done((bf16[64,2048]{1,0:T(8,128)(2,1)S(1)}, bf16[64,2048]{1,0:T(8,128)(2,1)S(1)}, u32[]{:S(2)}, u32[]{:S(2)}) %collective-permute-start.13) | collective-permute-done | bytes 262176 | tf_op jit(solution)/shard_map/ppermute | solution.py:22
  161.9 3.2 %shard_map.82 = bf16[256,2048]{1,0:T(8,128)(2,1)} custom-call(s32[4,64]{1,0:T(4,128)S(1)} %select_reduce_fusion.1.list_ref, f32[4,1,2048]{2,1,0:T(1,128)S(1)} %reshape.126.mask_ref, bf16[256,2048]{1,0:T(8,128)(2,1)S(1)} %bitcast.21, bf16[256,2048]{1,0:T(8,128)(2,1)S(1)} %get-tuple-element.75.own_ref, bf16[2,64,2048]{2,1,0:T(8,128)(2,1)S(1)} %collective-permute-done.11.got_a, ...), custom_call_target="tpu_custom_call" | custom-call | flops 4194304 | bytes 4194304 | tf_op jit(solution)/shard_map/pallas_call | solution.py:211
  (61 shorter events, 18.0 us)
Async XLA Ops:
  0.6 14.3 %collective-permute-start.1 = (bf16[512,256]{1,0:T(8,128)(2,1)}, bf16[512,256]{1,0:T(8,128)(2,1)S(1)}, u32[]{:S(2)}, u32[]{:S(2)}) collective-permute-start(bf16[512,256]{1,0:T(8,128)(2,1)} %s0), channel_id=1, source_target_pairs={{0,2},{1,3},{2,0},{3,1},{4,6},{5,7},{6,4},{7,5},{8,10},{9,11},{10,... | collective-permute-start | bytes 786440 | tf_op jit(solution)/shard_map/ppermute | solution.py:22
  8.3 21.0 %collective-permute-start = (bf16[512,256]{1,0:T(8,128)(2,1)}, bf16[512,256]{1,0:T(8,128)(2,1)S(1)}, u32[]{:S(2)}, u32[]{:S(2)}) collective-permute-start(bf16[512,256]{1,0:T(8,128)(2,1)} %s0), channel_id=1, source_target_pairs={{0,1},{1,0},{2,3},{3,2},{4,5},{5,4},{6,7},{7,6},{8,9},{9,8},{10,11... | collective-permute-start | bytes 786440 | tf_op jit(solution)/shard_map/ppermute | solution.py:22
  10.2 11.7 %collective-permute-start.3 = (s32[1,64]{1,0:T(1,128)}, s32[1,64]{1,0:T(1,128)S(1)}, u32[]{:S(2)}, u32[]{:S(2)}) collective-permute-start(s32[1,64]{1,0:T(1,128)} %bitcast.22), channel_id=1, source_target_pairs={{0,4},{4,0},{8,12},{12,8},{1,5},{5,1},{9,13},{13,9},{2,6},{6,2},{1... | collective-permute-start | bytes 776 | tf_op jit(solution)/shard_map/ppermute | solution.py:22
  14.9 14.3 %collective-permute-start.2 = (bf16[512,256]{1,0:T(8,128)(2,1)S(1)}, bf16[512,256]{1,0:T(8,128)(2,1)S(1)}, u32[]{:S(2)}, u32[]{:S(2)}) collective-permute-start(bf16[512,256]{1,0:T(8,128)(2,1)S(1)} %collective-permute-done.1.s2), channel_id=1, source_target_pairs={{0,1},{1,0},{2,3},{3,2},{4,5},{5,4},{6,7},{7,6},{8,9},{9,8},{10,11... | collective-permute-start | bytes 786440 | tf_op jit(solution)/shard_map/ppermute | solution.py:22
  22.6 6.7 %collective-permute-start.4 = (s32[2,64]{1,0:T(2,128)S(1)}, s32[2,64]{1,0:T(2,128)S(1)}, u32[]{:S(2)}, u32[]{:S(2)}) collective-permute-start(s32[2,64]{1,0:T(2,128)S(1)} %pad_add_fusion.1), channel_id=1, source_target_pairs={{0,12},{4,8},{8,4},{12,0},{1,13},{5,9},{9,5},{13,1},{2,14},{6,10},... | collective-permute-start | bytes 1544 | tf_op jit(solution)/shard_map/ppermute | solution.py:22
  28.4 4.9 %copy-start = (bf16[512,2048]{1,0:T(8,128)(2,1)S(1)}, bf16[512,2048]{1,0:T(8,128)(2,1)}, u32[]{:S(2)}) copy-start(bf16[512,2048]{1,0:T(8,128)(2,1)} %cot_ref.1) | copy-start | bytes 6291460
  28.4 4.9 %copy-start.1 = (bf16[512,256]{1,0:T(8,128)(2,1)S(1)}, bf16[512,256]{1,0:T(8,128)(2,1)}, u32[]{:S(2)}) copy-start(bf16[512,256]{1,0:T(8,128)(2,1)} %s0) | copy-start | bytes 786436
  35.6 17.9 %copy-start.10 = (s32[1,1,1,64]{3,2,1,0:T(1,128)S(1)}, s32[1,1,1,64]{3,2,1,0:T(1,128)}, u32[]{:S(2)}) copy-start(s32[1,1,1,64]{3,2,1,0:T(1,128)} %param.8) | copy-start | bytes 772
  35.6 36.3 %collective-permute-start.5 = (bf16[64,4096]{1,0:T(8,128)(2,1)S(1)}, bf16[64,4096]{1,0:T(8,128)(2,1)S(1)}, u32[]{:S(2)}, u32[]{:S(2)}) collective-permute-start(bf16[64,4096]{1,0:T(8,128)(2,1)S(1)} %shard_map.77), channel_id=1, source_target_pairs={{0,4},{4,0},{8,12},{12,8},{1,5},{5,1},{9,13},{13,9},{2,6},{6,2},{1... | collective-permute-start | bytes 1572872 | tf_op jit(solution)/shard_map/ppermute | solution.py:22
  37.6 34.3 %collective-permute-start.6 = (bf16[64,4096]{1,0:T(8,128)(2,1)S(1)}, bf16[64,4096]{1,0:T(8,128)(2,1)S(1)}, u32[]{:S(2)}, u32[]{:S(2)}) collective-permute-start(bf16[64,4096]{1,0:T(8,128)(2,1)S(1)} %shard_map.76), channel_id=1, source_target_pairs={{0,8},{4,12},{8,0},{12,4},{1,9},{5,13},{9,1},{13,5},{2,10},{6,14},... | collective-permute-start | bytes 1572872 | tf_op jit(solution)/shard_map/ppermute | solution.py:22
  44.3 27.6 %copy-start.2 = (bf16[1,256,2048]{2,1,0:T(8,128)(2,1)S(1)}, bf16[1,256,2048]{2,1,0:T(8,128)(2,1)}, u32[]{:S(2)}) copy-start(bf16[1,256,2048]{2,1,0:T(8,128)(2,1)} %param.7) | copy-start | bytes 3145732
  45.8 26.1 %collective-permute-start.7 = (bf16[64,4096]{1,0:T(8,128)(2,1)S(1)}, bf16[64,4096]{1,0:T(8,128)(2,1)S(1)}, u32[]{:S(2)}, u32[]{:S(2)}) collective-permute-start(bf16[64,4096]{1,0:T(8,128)(2,1)S(1)} %shard_map.78), channel_id=1, source_target_pairs={{0,12},{4,8},{8,4},{12,0},{1,13},{5,9},{9,5},{13,1},{2,14},{6,10},... | collective-permute-start | bytes 1572872 | tf_op jit(solution)/shard_map/ppermute | solution.py:22
  48.4 12.2 %collective-permute-start.8 = (f32[64,256]{1,0:T(8,128)S(1)}, f32[64,256]{1,0:T(8,128)S(1)}, u32[]{:S(2)}, u32[]{:S(2)}) collective-permute-start(f32[64,256]{1,0:T(8,128)S(1)} %reshape.122), channel_id=1, source_target_pairs={{0,32},{32,0},{1,33},{33,1},{2,34},{34,2},{3,35},{35,3},{4,36},{36... | collective-permute-start | bytes 196616 | tf_op jit(solution)/shard_map/ppermute | solution.py:22
  60.5 13.4 %copy-start.6 = (bf16[64,2048]{1,0:T(8,128)(2,1)}, bf16[64,2048]{1,0:T(8,128)(2,1)S(1)}, u32[]{:S(2)}) copy-start(bf16[64,2048]{1,0:T(8,128)(2,1)S(1)} %get-tuple-element.93) | copy-start | bytes 786436
  60.5 13.4 %copy-start.7 = (bf16[64,2048]{1,0:T(8,128)(2,1)}, bf16[64,2048]{1,0:T(8,128)(2,1)S(1)}, u32[]{:S(2)}) copy-start(bf16[64,2048]{1,0:T(8,128)(2,1)S(1)} %get-tuple-element.94) | copy-start | bytes 786436
  60.5 15.3 %copy-start.11 = (bf16[2,64,2048]{2,1,0:T(8,128)(2,1)}, bf16[2,64,2048]{2,1,0:T(8,128)(2,1)S(1)}, u32[]{:S(2)}) copy-start(bf16[2,64,2048]{2,1,0:T(8,128)(2,1)S(1)} %get-tuple-element.85) | copy-start | bytes 1572868
  60.6 17.2 %copy-start.12 = (f32[64,256]{1,0:T(8,128)}, f32[64,256]{1,0:T(8,128)S(1)}, u32[]{:S(2)}) copy-start(f32[64,256]{1,0:T(8,128)S(1)} %collective-permute-done.8) | copy-start | bytes 196612
  74.0 3.8 %collective-permute-start.9 = (bf16[8,64,512]{2,1,0:T(8,128)(2,1)S(1)}, bf16[8,64,512]{2,1,0:T(8,128)(2,1)S(1)}, u32[]{:S(2)}, u32[]{:S(2)}) collective-permute-start(bf16[8,64,512]{2,1,0:T(8,128)(2,1)S(1)} %get-tuple-element.80), channel_id=1, source_target_pairs={{0,16},{16,0},{1,17},{17,1},{2,18},{18,2},{3,19},{19,3},{4,20},{20... | collective-permute-start | bytes 1572872 | tf_op jit(solution)/shard_map/ppermute | solution.py:22
  78.8 28.2 %all-to-all-start = ((bf16[8,64,512]{2,1,0:T(8,128)(2,1)}), bf16[8,64,512]{2,1,0:T(8,128)(2,1)}, u32[]{:S(2)}, u32[]{:S(2)}) async-start(bf16[8,64,512]{2,1,0:T(8,128)(2,1)} %add_convert_fusion), calls=%async_computation | async-start | bytes 1048576 | tf_op jit(solution)/shard_map/all_to_all | solution.py:357
  89.1 23.9 %collective-permute-start.11 = (bf16[2,64,2048]{2,1,0:T(8,128)(2,1)}, bf16[2,64,2048]{2,1,0:T(8,128)(2,1)S(1)}, u32[]{:S(2)}, u32[]{:S(2)}) collective-permute-start(bf16[2,64,2048]{2,1,0:T(8,128)(2,1)} %get-tuple-element.84), channel_id=1, source_target_pairs={{0,4},{4,0},{8,12},{12,8},{1,5},{5,1},{9,13},{13,9},{2,6},{6,2},{1... | collective-permute-start | bytes 1572872 | tf_op jit(solution)/shard_map/ppermute | solution.py:22
  91.0 22.0 %collective-permute-start.12 = (bf16[2,64,2048]{2,1,0:T(8,128)(2,1)}, bf16[2,64,2048]{2,1,0:T(8,128)(2,1)S(1)}, u32[]{:S(2)}, u32[]{:S(2)}) collective-permute-start(bf16[2,64,2048]{2,1,0:T(8,128)(2,1)} %copy-done.11), channel_id=1, source_target_pairs={{0,12},{4,8},{8,4},{12,0},{1,13},{5,9},{9,5},{13,1},{2,14},{6,10},... | collective-permute-start | bytes 1572872 | tf_op jit(solution)/shard_map/ppermute | solution.py:22
  108.1 13.3 %collective-permute-start.10 = (f32[64,512]{1,0:T(8,128)S(1)}, f32[64,512]{1,0:T(8,128)}, u32[]{:S(2)}, u32[]{:S(2)}) collective-permute-start(f32[64,512]{1,0:T(8,128)S(1)} %convert_reduce_fusion.mine_ref), channel_id=1, source_target_pairs={{0,32},{32,0},{1,33},{33,1},{2,34},{34,2},{3,35},{35,3},{4,36},{36... | collective-permute-start | bytes 393224 | tf_op jit(solution)/shard_map/ppermute | solution.py:22
  113.0 10.8 %copy-start.3 = (bf16[2,64,2048]{2,1,0:T(8,128)(2,1)}, bf16[2,64,2048]{2,1,0:T(8,128)(2,1)S(1)}, u32[]{:S(2)}) copy-start(bf16[2,64,2048]{2,1,0:T(8,128)(2,1)S(1)} %collective-permute-done.12.got_b) | copy-start | bytes 1572868
  123.1 0.8 copy-start.5
  123.9 21.3 %all-to-all-start.1 = ((bf16[8,64,512]{2,1,0:T(8,128)(2,1)}), bf16[8,64,512]{2,1,0:T(8,128)(2,1)S(1)}, u32[]{:S(2)}, u32[]{:S(2)}) async-start(bf16[8,64,512]{2,1,0:T(8,128)(2,1)} %copy-done.5), calls=%async_computation.1 | async-start | bytes 1048576 | tf_op jit(solution)/shard_map/all_to_all | solution.py:368
  129.2 21.7 %collective-permute-start.14 = (bf16[64,2048]{1,0:T(8,128)(2,1)}, bf16[64,2048]{1,0:T(8,128)(2,1)S(1)}, u32[]{:S(2)}, u32[]{:S(2)}) collective-permute-start(bf16[64,2048]{1,0:T(8,128)(2,1)} %fusion), channel_id=1, source_target_pairs={{0,4},{4,0},{8,12},{12,8},{1,5},{5,1},{9,13},{13,9},{2,6},{6,2},{1... | collective-permute-start | bytes 786440 | tf_op jit(solution)/shard_map/ppermute | solution.py:22
  145.2 20.0 %collective-permute-start.15 = (bf16[8,64,512]{2,1,0:T(8,128)(2,1)S(1)}, bf16[8,64,512]{2,1,0:T(8,128)(2,1)S(1)}, u32[]{:S(2)}, u32[]{:S(2)}) collective-permute-start(bf16[8,64,512]{2,1,0:T(8,128)(2,1)S(1)} %all-to-all-done.1.mine_ref), channel_id=1, source_target_pairs={{0,16},{16,0},{1,17},{17,1},{2,18},{18,2},{3,19},{19,3},{4,20},{20... | collective-permute-start | bytes 1572872 | tf_op jit(solution)/shard_map/ppermute | solution.py:22
  148.1 11.8 %collective-permute-start.13 = (bf16[64,2048]{1,0:T(8,128)(2,1)S(1)}, bf16[64,2048]{1,0:T(8,128)(2,1)S(1)}, u32[]{:S(2)}, u32[]{:S(2)}) collective-permute-start(bf16[64,2048]{1,0:T(8,128)(2,1)S(1)} %fusion.1), channel_id=1, source_target_pairs={{0,12},{4,8},{8,4},{12,0},{1,13},{5,9},{9,5},{13,1},{2,14},{6,10},... | collective-permute-start | bytes 786440 | tf_op jit(solution)/shard_map/ppermute | solution.py:22
  150.8 0.7 copy-start.8
  160.0 1.0 copy-start.4
  161.0 0.9 copy-start.9

commit v9 on v8

--- a/solution.py
+++ b/solution.py
@@ -83,25 +83,21 @@
     lax.fori_loop(0, count // 2, tile, 0, unroll=True)
 
 
-def first_kernel(row, list_ref, part_ref, out_ref):
-    pack(list_ref, row, 0, HALF, part_ref, out_ref)
+def first_kernel(rows, *refs):
+    n = len(rows)
+    for row, list_ref, part_ref, out_ref in zip(rows, refs[:n], refs[n : 2 * n], refs[2 * n :]):
+        pack(list_ref, row, 0, HALF, part_ref, out_ref)
 
 
 def rest_kernel(
-    list_ref, at_ref, s0, s1, s2, s3, cot_ref,
-    give_a, give_b, keep_a, keep_b, own_ref, left_ref, part_ref,
+    list_ref, at_ref, s0, s1, s2, s3, cot_ref, give_ref, keep_ref, own_ref, left_ref, part_ref
 ):
-    shards, half = (s0, s1, s2, s3), HALF // 2
-    low, high = 0, half
-    product(at_ref, 1, shards, cot_ref, left_ref, part_ref)
-    pack(list_ref, 1, low, half, part_ref, give_a, 0)
-    pack(list_ref, 1, high, half, part_ref, keep_b)
-    product(at_ref, 2, shards, cot_ref, left_ref, part_ref)
-    pack(list_ref, 2, low, half, part_ref, give_a, 1)
-    pack(list_ref, 2, high, half, part_ref, give_b, 1)
+    shards = (s0, s1, s2, s3)
+    for lead, k in enumerate((1, 2)):
+        product(at_ref, k, shards, cot_ref, left_ref, part_ref)
+        pack(list_ref, k, 0, HALF, part_ref, give_ref, lead)
     product(at_ref, 3, shards, cot_ref, left_ref, part_ref)
-    pack(list_ref, 3, high, half, part_ref, give_b, 0)
-    pack(list_ref, 3, low, half, part_ref, keep_a)
+    pack(list_ref, 3, 0, HALF, part_ref, keep_ref)
     product(at_ref, 0, shards, cot_ref, left_ref, own_ref)
 
 
@@ -124,16 +120,21 @@
     return jax.ShapeDtypeStruct((*lead, BLK, blocks * BLK), BF16)
 
 
-def chosen_part(row, lists, part):
-    whole = pl.BlockSpec(memory_space=pltpu.VMEM)
-    body = functools.partial(first_kernel, row)
-    return kernel_call(body, (), [SMEM, whole], whole, packed(), 1 << 20)(lists, part)
+def chosen_parts(rows, lists, parts):
+    whole, n = pl.BlockSpec(memory_space=pltpu.VMEM), len(rows)
+    return kernel_call(
+        functools.partial(first_kernel, rows),
+        (),
+        [SMEM] * n + [whole] * n,
+        [whole] * n,
+        [packed()] * n,
+        1 << 20,
+    )(*lists, *parts)
 
 
 def rest_parts(lists, at, shards, cotangent):
-    half = HALF // 2
     own = jax.ShapeDtypeStruct((shards[0].shape[1], cotangent.shape[1]), BF16)
-    shapes = [packed(2, blocks=half)] * 2 + [packed(blocks=half)] * 2 + [own]
+    shapes = [packed(2), packed(), own]
     return products_call(rest_kernel, lists, at, shards, cotangent, shapes)
 
 
@@ -182,17 +183,13 @@
             other_ref[h, :, place] = jnp.where(first, sent[1], sent[0]).astype(BF16)
 
 
-def residual_kernel(
-    list_ref, mask_ref, fb_ref, own_ref, got_a, got_b, next_a, next_b, new_ref, grad_ref
-):
+def residual_kernel(list_ref, mask_ref, fb_ref, own_ref, got, nxt, new_ref, grad_ref):
     row = pl.program_id(0)
 
     @pl.when(row == 0)
     def _():
-        half = HALF // 2
-        for base, got, nxt in ((0, got_a, next_a), (half, got_b, next_b)):
-            terms = [lambda at, ref=got: ref[0, :, at], lambda at, ref=nxt: ref[:, at]]
-            unpack(list_ref, base, half, terms, grad_ref)
+        terms = [lambda at: got[0, :, at], lambda at: nxt[:, at]]
+        unpack(list_ref, 0, HALF, terms, grad_ref)
 
     rows = pl.ds(pl.multiple_of(row * BLK, BLK), BLK)
     for at in range(0, fb_ref.shape[1], 256):
@@ -329,44 +326,46 @@
         (*gather_hidden(hidden), near_picks, far_picks)
     )
     at = (lax.axis_index("dp") ^ lax.axis_index("t")).astype(jnp.int32).reshape(1)
-    got = {}
-    for k, row, lists in ((2, 1, far_picks), (1, 0, near_picks), (3, 0, far_picks)):
-        part = lax.dot_general(
+
+    def part(k, shards):
+        return lax.dot_general(
             lax.select_n(at[0] ^ k, *shards),
             cotangent,
             (((0,), (0,)), ((), ())),
             preferred_element_type=F32,
         ).astype(BF16)
-        given = chosen_part(row, lists, part)
-        if k == 3:
-            *shards, given, moment = lax.optimization_barrier((*shards, given, moment))
-        else:
-            *shards, _ = lax.optimization_barrier((*shards, given))
-        got[k] = swap(given, "dp", k, 4)
+
+    (give_2,) = chosen_parts((1,), (far_picks,), (part(2, shards),))
+    got_2 = swap(give_2, "dp", 2, 4)
+    *shards, _ = lax.optimization_barrier((*shards, give_2))
+    give_1, give_3 = chosen_parts(
+        (0, 0), (near_picks, far_picks), (part(1, shards), part(3, shards))
+    )
+    got_1 = swap(give_1, "dp", 1, 4)
+    *shards, give_3, moment = lax.optimization_barrier((*shards, give_3, moment))
+    got_3 = swap(give_3, "dp", 3, 4)
     far_moment = swap(moment, "yh", 1, 2)
     others = jnp.concatenate([picks, near_picks, far_picks[1:], far_picks[:1]])
     others = others_of(others, rows_blk * cols_blk)
     rest = rest_parts(others, at, shards, cotangent)
-    got_1, got_2, got_3, far_moment, give_a, give_b, keep_a, keep_b, own = (
-        lax.optimization_barrier((got[1], got[2], got[3], far_moment, *rest))
+    got_1, got_2, got_3, far_moment, give, keep, own = lax.optimization_barrier(
+        (got_1, got_2, got_3, far_moment, *rest)
     )
     mine, other = chosen_sums(picks, at_c, mask, feedback[0], own, got_1, got_2, got_3)
     pair = (mine + swap(other, "c", 1, 2).astype(F32)).astype(BF16)
-    pair, give_a, give_b = lax.optimization_barrier((pair, give_a, give_b))
-    got_a, got_b = swap(give_a, "dp", 1, 4), swap(give_b, "dp", 3, 4)
+    pair, give = lax.optimization_barrier((pair, give))
+    got_rest = swap(give, "dp", 1, 4)
     across = lax.all_to_all(pair, "z", 0, 0, tiled=True)
     near = jnp.sum(across.astype(F32), axis=0)
     far = swap(near, "yh", 1, 2)
-    far, got_a, got_b = lax.optimization_barrier((far, got_a, got_b))
+    far, give_rest = lax.optimization_barrier((far, plus(keep, got_rest[1])))
     moment = jnp.where(
         yh == 0, jnp.concatenate([moment, far_moment], 1), jnp.concatenate([far_moment, moment], 1)
     )
     momentum_new, copies = owner_update(at_yh, near, far, moment)
-    copies, got_a, got_b = lax.optimization_barrier((copies, got_a, got_b))
-    next_a = swap(plus(keep_a, got_a[1]), "dp", 3, 4)
-    next_b = swap(plus(keep_b, got_b[1]), "dp", 1, 4)
+    next_rest = swap(give_rest, "dp", 3, 4)
     every = lax.all_to_all(copies, "z", 0, 0, tiled=True)
-    feedback_new = residual(others, mask, feedback[0], own, got_a, got_b, next_a, next_b)
+    feedback_new = residual(others, mask, feedback[0], own, got_rest, next_rest)
     step = assemble(at_c, every, swap(every, "c", 1, 2), rows, cols)
     return feedback_new[None], momentum_new[None, None], step
 

time: 168 us -> 142 us (0.85)
  the two profiles are of different devices: /device:TPU:16 before, /device:TPU:1 now
where the time goes in v9:
time: 142 us; the launch traced here: 141 us
  starting transfers between devices  71.5 us (50%)
  waiting for transfers between devices  39.1 us (28%)
  Pallas kernels  19 us (13%)
  other arithmetic  5.2 us (4%)
  matrix products  4.04 us (3%)
    ppermute x14, starting transfers between devices, swap(): return lax.ppermute(value, axis, [(i, i ^ flip) for i in range(size)])  56.6 us
    all_to_all x1, waiting for transfers between devices, local(): across = lax.all_to_all(pair, 'z', 0, 0, tiled=True)  14.3 us
    all_to_all x1, waiting for transfers between devices, local(): every = lax.all_to_all(copies, 'z', 0, 0, tiled=True)  12.5 us
    ppermute x14, waiting for transfers between devices, swap(): return lax.ppermute(value, axis, [(i, i ^ flip) for i in range(size)])  12.4 us
    all_to_all x1, starting transfers between devices, local(): across = lax.all_to_all(pair, 'z', 0, 0, tiled=True)  10 us
    pallas_call x1, Pallas kernels, products_call(): pl.pallas_call(body, in_specs=[SMEM, SMEM] + [whole] * 5, out_specs=jax.t...  6.58 us
    pallas_call x2, Pallas kernels, state_call(): pl.pallas_call(body, grid=(rows // BLK,), in_specs=[SMEM] * len(scalars)...  5.93 us
    all_to_all x1, starting transfers between devices, local(): every = lax.all_to_all(copies, 'z', 0, 0, tiled=True)  4.84 us
  transfers between devices with their start and end apart: 16, of which 7 were waited for; matrix products, arithmetic and copies ran while one was open for 5% of the time, Pallas kernels for 9%

profile of v9, /device:TPU:1, one launch (start us, length us, event | category | flops | bytes accessed | tf_op | source)
XLA Modules:
  0.0 141.1 jit_solution(867144926777917612)
XLA Ops:
  0.6 5.0 %collective-permute-start.1 = (bf16[512,256]{1,0:T(8,128)(2,1)}, bf16[512,256]{1,0:T(8,128)(2,1)S(1)}, u32[]{:S(2)}, u32[]{:S(2)}) collective-permute-start(bf16[512,256]{1,0:T(8,128)(2,1)} %s0), channel_id=1, source_target_pairs={{0,2},{1,3},{2,0},{3,1},{4,6},{5,7},{6,4},{7,5},{8,10},{9,11},{10,... | collective-permute-start | bytes 786440 | tf_op jit(solution)/shard_map/ppermute | solution.py:22
  5.7 3.2 %collective-permute-start = (bf16[512,256]{1,0:T(8,128)(2,1)}, bf16[512,256]{1,0:T(8,128)(2,1)S(1)}, u32[]{:S(2)}, u32[]{:S(2)}) collective-permute-start(bf16[512,256]{1,0:T(8,128)(2,1)} %s0), channel_id=1, source_target_pairs={{0,1},{1,0},{2,3},{3,2},{4,5},{5,4},{6,7},{7,6},{8,9},{9,8},{10,11... | collective-permute-start | bytes 786440 | tf_op jit(solution)/shard_map/ppermute | solution.py:22
  8.9 3.1 %collective-permute-start.3 = (s32[1,64]{1,0:T(1,128)}, s32[1,64]{1,0:T(1,128)S(1)}, u32[]{:S(2)}, u32[]{:S(2)}) collective-permute-start(s32[1,64]{1,0:T(1,128)} %bitcast.21), channel_id=1, source_target_pairs={{0,4},{4,0},{8,12},{12,8},{1,5},{5,1},{9,13},{13,9},{2,6},{6,2},{1... | collective-permute-start | bytes 776 | tf_op jit(solution)/shard_map/ppermute | solution.py:22
  12.1 4.6 %collective-permute-done.1.s2 = bf16[512,256]{1,0:T(8,128)(2,1)S(1)} collective-permute-done((bf16[512,256]{1,0:T(8,128)(2,1)}, bf16[512,256]{1,0:T(8,128)(2,1)S(1)}, u32[]{:S(2)}, u32[]{:S(2)}) %collective-permute-start.1) | collective-permute-done | bytes 262176 | tf_op jit(solution)/shard_map/ppermute | solution.py:22
  16.8 4.0 %collective-permute-start.2 = (bf16[512,256]{1,0:T(8,128)(2,1)S(1)}, bf16[512,256]{1,0:T(8,128)(2,1)S(1)}, u32[]{:S(2)}, u32[]{:S(2)}) collective-permute-start(bf16[512,256]{1,0:T(8,128)(2,1)S(1)} %collective-permute-done.1.s2), channel_id=1, source_target_pairs={{0,1},{1,0},{2,3},{3,2},{4,5},{5,4},{6,7},{7,6},{8,9},{9,8},{10,11... | collective-permute-start | bytes 786440 | tf_op jit(solution)/shard_map/ppermute | solution.py:22
  20.8 1.0 compare_reduce_fusion
  22.5 4.3 %collective-permute-start.4 = (s32[2,64]{1,0:T(2,128)S(1)}, s32[2,64]{1,0:T(2,128)S(1)}, u32[]{:S(2)}, u32[]{:S(2)}) collective-permute-start(s32[2,64]{1,0:T(2,128)S(1)} %pad_add_fusion.1), channel_id=1, source_target_pairs={{0,12},{4,8},{8,4},{12,0},{1,13},{5,9},{9,5},{13,1},{2,14},{6,10},... | collective-permute-start | bytes 1544 | tf_op jit(solution)/shard_map/ppermute | solution.py:22
  28.1 2.5 %convolution_convert_fusion.2.refs_1_ = bf16[256,2048]{1,0:T(8,128)(2,1)S(1)} fusion(bf16[512,2048]{1,0:T(8,128)(2,1)} %cot_ref.1, bf16[512,256]{1,0:T(8,128)(2,1)S(1)} %collective-permute-done.1.s2, bf16[512,256]{1,0:T(8,128)(2,1)S(1)} %collective-permute-done.2.s3, bf16[512,256]{1,0:T(8,128)(2,1)} %s0, bf16[512,256]{1,0:T(8,128)(2,1)S(1)} %collective-permute-done.s1, ...), kind=kOutput, calls=%fused_computation.2 | convolution fusion | flops 537788416 | bytes 4194307 | tf_op jit(solution)/shard_map/dot_general | solution.py:331
  30.6 1.5 %shard_map.76 = bf16[64,4096]{1,0:T(8,128)(2,1)S(1)} custom-call(s32[2,64]{1,0:T(2,128)S(1)} %collective-permute-done.4.refs_0_.refs_1_, bf16[256,2048]{1,0:T(8,128)(2,1)S(1)} %convolution_convert_fusion.2.refs_1_), custom_call_target="tpu_custom_call" | custom-call | flops 1048576 | bytes 1048576 | tf_op jit(solution)/shard_map/pallas_call | solution.py:125
  32.2 3.6 %collective-permute-start.6 = (bf16[64,4096]{1,0:T(8,128)(2,1)S(1)}, bf16[64,4096]{1,0:T(8,128)(2,1)S(1)}, u32[]{:S(2)}, u32[]{:S(2)}) collective-permute-start(bf16[64,4096]{1,0:T(8,128)(2,1)S(1)} %shard_map.76), channel_id=1, source_target_pairs={{0,8},{4,12},{8,0},{12,4},{1,9},{5,13},{9,1},{13,5},{2,10},{6,14},... | collective-permute-start | bytes 1572872 | tf_op jit(solution)/shard_map/ppermute | solution.py:22
  37.3 2.5 %shard_map.77 = (bf16[64,4096]{1,0:T(8,128)(2,1)S(1)}, bf16[64,4096]{1,0:T(8,128)(2,1)S(1)}) custom-call(s32[1,64]{1,0:T(1,128)S(1)} %collective-permute-done.3.refs_0_, s32[2,64]{1,0:T(2,128)S(1)} %collective-permute-done.4.refs_0_.refs_1_, bf16[256,2048]{1,0:T(8,128)(2,1)S(1)} %convolution_convert_fusion.1.refs_2_, ...), custom_call_target="tpu_custom_call" | custom-call | flops 1048576 | bytes 1048576 | tf_op jit(solution)/shard_map/pallas_call | solution.py:125
  39.9 3.0 %collective-permute-start.7 = (bf16[64,4096]{1,0:T(8,128)(2,1)S(1)}, bf16[64,4096]{1,0:T(8,128)(2,1)S(1)}, u32[]{:S(2)}, u32[]{:S(2)}) collective-permute-start(bf16[64,4096]{1,0:T(8,128)(2,1)S(1)} %get-tuple-element.51), channel_id=1, source_target_pairs={{0,12},{4,8},{8,4},{12,0},{1,13},{5,9},{9,5},{13,1},{2,14},{6,10},... | collective-permute-start | bytes 1572872 | tf_op jit(solution)/shard_map/ppermute | solution.py:22
  42.9 2.1 %collective-permute-start.5 = (bf16[64,4096]{1,0:T(8,128)(2,1)S(1)}, bf16[64,4096]{1,0:T(8,128)(2,1)S(1)}, u32[]{:S(2)}, u32[]{:S(2)}) collective-permute-start(bf16[64,4096]{1,0:T(8,128)(2,1)S(1)} %get-tuple-element.49), channel_id=1, source_target_pairs={{0,4},{4,0},{8,12},{12,8},{1,5},{5,1},{9,13},{13,9},{2,6},{6,2},{1... | collective-permute-start | bytes 1572872 | tf_op jit(solution)/shard_map/ppermute | solution.py:22
  45.0 7.3 %collective-permute-start.8 = (f32[64,256]{1,0:T(8,128)S(1)}, f32[64,256]{1,0:T(8,128)S(1)}, u32[]{:S(2)}, u32[]{:S(2)}) collective-permute-start(f32[64,256]{1,0:T(8,128)S(1)} %reshape.120), channel_id=1, source_target_pairs={{0,32},{32,0},{1,33},{33,1},{2,34},{34,2},{3,35},{35,3},{4,36},{36... | collective-permute-start | bytes 196616 | tf_op jit(solution)/shard_map/ppermute | solution.py:22
  52.8 6.6 %shard_map.78 = (bf16[2,64,4096]{2,1,0:T(8,128)(2,1)S(1)}, bf16[64,4096]{1,0:T(8,128)(2,1)S(1)}, bf16[256,2048]{1,0:T(8,128)(2,1)S(1)}) custom-call(s32[4,64]{1,0:T(4,128)S(1)} %select_reduce_fusion.1.list_ref, s32[1]{0:T(128)} %bitcast.5.at_ref, bf16[512,256]{1,0:T(8,128)(2,1)S(1)} %copy-done.1, bf16[512,256]{1,0:T(8,128)(2,1)S(1)} %collective-permute-done.s1, ...), custom_call_target="tpu_custom_call" | custom-call | flops 1048576 | bytes 1048576 | tf_op jit(solution)/shard_map/pallas_call | solution.py:108
  59.4 1.3 collective-permute-done.7.got_3
  60.7 2.0 %shard_map.79 = (f32[8,64,512]{2,1,0:T(8,128)S(1)}, bf16[8,64,512]{2,1,0:T(8,128)(2,1)S(1)}) custom-call(s32[1,64]{1,0:T(1,128)S(1)} %bitcast.25, s32[1]{0:T(128)} %bitcast.6.c_ref, f32[4,1,2048]{2,1,0:T(1,128)S(1)} %reshape.124.mask_ref, bf16[256,2048]{1,0:T(8,128)(2,1)S(1)} %bitcast.19, bf16[256,2048]{1,0:T(8,128)(2,1)S(1)} %get-tuple-element.60.own_ref, ...), custom_call_target="tpu_custom_call" | custom-call | flops 4194304 | bytes 4194304 | tf_op jit(solution)/shard_map/pallas_call | solution.py:208
  62.7 4.1 %collective-permute-start.9 = (bf16[8,64,512]{2,1,0:T(8,128)(2,1)S(1)}, bf16[8,64,512]{2,1,0:T(8,128)(2,1)S(1)}, u32[]{:S(2)}, u32[]{:S(2)}) collective-permute-start(bf16[8,64,512]{2,1,0:T(8,128)(2,1)S(1)} %get-tuple-element.65), channel_id=1, source_target_pairs={{0,16},{16,0},{1,17},{17,1},{2,18},{18,2},{3,19},{19,3},{4,20},{20... | collective-permute-start | bytes 1572872 | tf_op jit(solution)/shard_map/ppermute | solution.py:22
  66.8 1.5 %collective-permute-done.9 = bf16[8,64,512]{2,1,0:T(8,128)(2,1)S(1)} collective-permute-done((bf16[8,64,512]{2,1,0:T(8,128)(2,1)S(1)}, bf16[8,64,512]{2,1,0:T(8,128)(2,1)S(1)}, u32[]{:S(2)}, u32[]{:S(2)}) %collective-permute-start.9) | collective-permute-done | bytes 524320 | tf_op jit(solution)/shard_map/ppermute | solution.py:22
  69.3 10.0 %all-to-all-start = ((bf16[8,64,512]{2,1,0:T(8,128)(2,1)}), bf16[8,64,512]{2,1,0:T(8,128)(2,1)S(1)}, u32[]{:S(2)}, u32[]{:S(2)}) async-start(bf16[8,64,512]{2,1,0:T(8,128)(2,1)} %add_convert_fusion), calls=%async_computation | async-start | bytes 1048576 | tf_op jit(solution)/shard_map/all_to_all | solution.py:358
  79.3 3.6 %collective-permute-start.10 = (bf16[2,64,4096]{2,1,0:T(8,128)(2,1)}, bf16[2,64,4096]{2,1,0:T(8,128)(2,1)}, u32[]{:S(2)}, u32[]{:S(2)}) collective-permute-start(bf16[2,64,4096]{2,1,0:T(8,128)(2,1)} %copy-done.4), channel_id=1, source_target_pairs={{0,4},{4,0},{8,12},{12,8},{1,5},{5,1},{9,13},{13,9},{2,6},{6,2},{1... | collective-permute-start | bytes 3145736 | tf_op jit(solution)/shard_map/ppermute | solution.py:22
  83.0 14.3 %all-to-all-done = bf16[8,64,512]{2,1,0:T(8,128)(2,1)S(1)} async-done(((bf16[8,64,512]{2,1,0:T(8,128)(2,1)}), bf16[8,64,512]{2,1,0:T(8,128)(2,1)S(1)}, u32[]{:S(2)}, u32[]{:S(2)}) %all-to-all-start) | async-done | bytes 524320 | tf_op jit(solution)/shard_map/all_to_all | solution.py:358
  97.3 5.3 %collective-permute-start.11 = (f32[64,512]{1,0:T(8,128)S(1)}, f32[64,512]{1,0:T(8,128)S(1)}, u32[]{:S(2)}, u32[]{:S(2)}) collective-permute-start(f32[64,512]{1,0:T(8,128)S(1)} %convert_reduce_fusion.mine_ref), channel_id=1, source_target_pairs={{0,32},{32,0},{1,33},{33,1},{2,34},{34,2},{3,35},{35,3},{4,36},{36... | collective-permute-start | bytes 393224 | tf_op jit(solution)/shard_map/ppermute | solution.py:22
  102.7 3.5 %collective-permute-done.10.got = bf16[2,64,4096]{2,1,0:T(8,128)(2,1)} collective-permute-done((bf16[2,64,4096]{2,1,0:T(8,128)(2,1)}, bf16[2,64,4096]{2,1,0:T(8,128)(2,1)}, u32[]{:S(2)}, u32[]{:S(2)}) %collective-permute-start.10) | collective-permute-done | bytes 1048608 | tf_op jit(solution)/shard_map/ppermute | solution.py:22
  106.2 2.0 %fusion = bf16[64,4096]{1,0:T(8,128)(2,1)} fusion(bf16[64,4096]{1,0:T(8,128)(2,1)S(1)} %get-tuple-element.69, bf16[2,64,4096]{2,1,0:T(8,128)(2,1)} %collective-permute-done.10.got), kind=kLoop, calls=%fused_computation.5 | loop fusion | flops 1048576 | bytes 1572864 | tf_op jit(solution)/shard_map/convert_element_type | solution.py:303
  108.1 1.5 %collective-permute-done.11.peer_ref = f32[64,512]{1,0:T(8,128)S(1)} collective-permute-done((f32[64,512]{1,0:T(8,128)S(1)}, f32[64,512]{1,0:T(8,128)S(1)}, u32[]{:S(2)}, u32[]{:S(2)}) %collective-permute-start.11) | collective-permute-done | bytes 131104 | tf_op jit(solution)/shard_map/ppermute | solution.py:22
  110.5 4.8 %all-to-all-start.1 = ((bf16[8,64,512]{2,1,0:T(8,128)(2,1)}), bf16[8,64,512]{2,1,0:T(8,128)(2,1)S(1)}, u32[]{:S(2)}, u32[]{:S(2)}) async-start(bf16[8,64,512]{2,1,0:T(8,128)(2,1)} %get-tuple-element.74), calls=%async_computation.1 | async-start | bytes 1048576 | tf_op jit(solution)/shard_map/all_to_all | solution.py:367
  115.3 3.5 %collective-permute-start.12 = (bf16[64,4096]{1,0:T(8,128)(2,1)}, bf16[64,4096]{1,0:T(8,128)(2,1)S(1)}, u32[]{:S(2)}, u32[]{:S(2)}) collective-permute-start(bf16[64,4096]{1,0:T(8,128)(2,1)} %fusion), channel_id=1, source_target_pairs={{0,12},{4,8},{8,4},{12,0},{1,13},{5,9},{9,5},{13,1},{2,14},{6,10},... | collective-permute-start | bytes 1572872 | tf_op jit(solution)/shard_map/ppermute | solution.py:22
  118.8 12.5 %all-to-all-done.1.mine_ref = bf16[8,64,512]{2,1,0:T(8,128)(2,1)S(1)} async-done(((bf16[8,64,512]{2,1,0:T(8,128)(2,1)}), bf16[8,64,512]{2,1,0:T(8,128)(2,1)S(1)}, u32[]{:S(2)}, u32[]{:S(2)}) %all-to-all-start.1) | async-done | bytes 524320 | tf_op jit(solution)/shard_map/all_to_all | solution.py:367
  131.3 4.4 %collective-permute-start.13 = (bf16[8,64,512]{2,1,0:T(8,128)(2,1)S(1)}, bf16[8,64,512]{2,1,0:T(8,128)(2,1)S(1)}, u32[]{:S(2)}, u32[]{:S(2)}) collective-permute-start(bf16[8,64,512]{2,1,0:T(8,128)(2,1)S(1)} %all-to-all-done.1.mine_ref), channel_id=1, source_target_pairs={{0,16},{16,0},{1,17},{17,1},{2,18},{18,2},{3,19},{19,3},{4,20},{20... | collective-permute-start | bytes 1572872 | tf_op jit(solution)/shard_map/ppermute | solution.py:22
  135.7 3.9 %shard_map.80 = bf16[256,2048]{1,0:T(8,128)(2,1)} custom-call(s32[4,64]{1,0:T(4,128)S(1)} %select_reduce_fusion.1.list_ref, f32[4,1,2048]{2,1,0:T(1,128)S(1)} %reshape.124.mask_ref, bf16[256,2048]{1,0:T(8,128)(2,1)S(1)} %bitcast.20, bf16[256,2048]{1,0:T(8,128)(2,1)S(1)} %get-tuple-element.60.own_ref, bf16[2,64,4096]{2,1,0:T(8,128)(2,1)} %collective-permute-done.10.got, ...), custom_call_target="tpu_custom_call" | custom-call | flops 4194304 | bytes 4194304 | tf_op jit(solution)/shard_map/pallas_call | solution.py:208
  139.6 1.5 %shard_map.82 = bf16[256,2048]{1,0:T(8,128)(2,1)} custom-call(s32[1]{0:T(128)} %bitcast.6.c_ref, bf16[8,64,512]{2,1,0:T(8,128)(2,1)S(1)} %all-to-all-done.1.mine_ref, bf16[8,64,512]{2,1,0:T(8,128)(2,1)S(1)} %collective-permute-done.13.other_ref), custom_call_target="tpu_custom_call" | custom-call | flops 2097152 | bytes 2097152 | tf_op jit(solution)/shard_map/pallas_call | solution.py:276
  (43 shorter events, 5.9 us)
Async XLA Ops:
  0.6 16.1 %collective-permute-start.1 = (bf16[512,256]{1,0:T(8,128)(2,1)}, bf16[512,256]{1,0:T(8,128)(2,1)S(1)}, u32[]{:S(2)}, u32[]{:S(2)}) collective-permute-start(bf16[512,256]{1,0:T(8,128)(2,1)} %s0), channel_id=1, source_target_pairs={{0,2},{1,3},{2,0},{3,1},{4,6},{5,7},{6,4},{7,5},{8,10},{9,11},{10,... | collective-permute-start | bytes 786440 | tf_op jit(solution)/shard_map/ppermute | solution.py:22
  5.7 22.4 %collective-permute-start = (bf16[512,256]{1,0:T(8,128)(2,1)}, bf16[512,256]{1,0:T(8,128)(2,1)S(1)}, u32[]{:S(2)}, u32[]{:S(2)}) collective-permute-start(bf16[512,256]{1,0:T(8,128)(2,1)} %s0), channel_id=1, source_target_pairs={{0,1},{1,0},{2,3},{3,2},{4,5},{5,4},{6,7},{7,6},{8,9},{9,8},{10,11... | collective-permute-start | bytes 786440 | tf_op jit(solution)/shard_map/ppermute | solution.py:22
  8.9 13.0 %collective-permute-start.3 = (s32[1,64]{1,0:T(1,128)}, s32[1,64]{1,0:T(1,128)S(1)}, u32[]{:S(2)}, u32[]{:S(2)}) collective-permute-start(s32[1,64]{1,0:T(1,128)} %bitcast.21), channel_id=1, source_target_pairs={{0,4},{4,0},{8,12},{12,8},{1,5},{5,1},{9,13},{13,9},{2,6},{6,2},{1... | collective-permute-start | bytes 776 | tf_op jit(solution)/shard_map/ppermute | solution.py:22
  16.8 11.3 %collective-permute-start.2 = (bf16[512,256]{1,0:T(8,128)(2,1)S(1)}, bf16[512,256]{1,0:T(8,128)(2,1)S(1)}, u32[]{:S(2)}, u32[]{:S(2)}) collective-permute-start(bf16[512,256]{1,0:T(8,128)(2,1)S(1)} %collective-permute-done.1.s2), channel_id=1, source_target_pairs={{0,1},{1,0},{2,3},{3,2},{4,5},{5,4},{6,7},{7,6},{8,9},{9,8},{10,11... | collective-permute-start | bytes 786440 | tf_op jit(solution)/shard_map/ppermute | solution.py:22
  22.5 5.5 %collective-permute-start.4 = (s32[2,64]{1,0:T(2,128)S(1)}, s32[2,64]{1,0:T(2,128)S(1)}, u32[]{:S(2)}, u32[]{:S(2)}) collective-permute-start(s32[2,64]{1,0:T(2,128)S(1)} %pad_add_fusion.1), channel_id=1, source_target_pairs={{0,12},{4,8},{8,4},{12,0},{1,13},{5,9},{9,5},{13,1},{2,14},{6,10},... | collective-permute-start | bytes 1544 | tf_op jit(solution)/shard_map/ppermute | solution.py:22
  28.1 7.7 %copy-start = (bf16[512,2048]{1,0:T(8,128)(2,1)S(1)}, bf16[512,2048]{1,0:T(8,128)(2,1)}, u32[]{:S(2)}) copy-start(bf16[512,2048]{1,0:T(8,128)(2,1)} %cot_ref.1) | copy-start | bytes 6291460
  28.1 7.7 %copy-start.1 = (bf16[512,256]{1,0:T(8,128)(2,1)S(1)}, bf16[512,256]{1,0:T(8,128)(2,1)}, u32[]{:S(2)}) copy-start(bf16[512,256]{1,0:T(8,128)(2,1)} %s0) | copy-start | bytes 786436
  32.2 28.5 %collective-permute-start.6 = (bf16[64,4096]{1,0:T(8,128)(2,1)S(1)}, bf16[64,4096]{1,0:T(8,128)(2,1)S(1)}, u32[]{:S(2)}, u32[]{:S(2)}) collective-permute-start(bf16[64,4096]{1,0:T(8,128)(2,1)S(1)} %shard_map.76), channel_id=1, source_target_pairs={{0,8},{4,12},{8,0},{12,4},{1,9},{5,13},{9,1},{13,5},{2,10},{6,14},... | collective-permute-start | bytes 1572872 | tf_op jit(solution)/shard_map/ppermute | solution.py:22
  37.3 15.0 %copy-start.3 = (s32[1,1,1,64]{3,2,1,0:T(1,128)S(1)}, s32[1,1,1,64]{3,2,1,0:T(1,128)}, u32[]{:S(2)}) copy-start(s32[1,1,1,64]{3,2,1,0:T(1,128)} %param.8) | copy-start | bytes 772
  39.9 20.8 %copy-start.2 = (bf16[1,256,2048]{2,1,0:T(8,128)(2,1)S(1)}, bf16[1,256,2048]{2,1,0:T(8,128)(2,1)}, u32[]{:S(2)}) copy-start(bf16[1,256,2048]{2,1,0:T(8,128)(2,1)} %param.7) | copy-start | bytes 3145732
  39.9 20.7 %collective-permute-start.7 = (bf16[64,4096]{1,0:T(8,128)(2,1)S(1)}, bf16[64,4096]{1,0:T(8,128)(2,1)S(1)}, u32[]{:S(2)}, u32[]{:S(2)}) collective-permute-start(bf16[64,4096]{1,0:T(8,128)(2,1)S(1)} %get-tuple-element.51), channel_id=1, source_target_pairs={{0,12},{4,8},{8,4},{12,0},{1,13},{5,9},{9,5},{13,1},{2,14},{6,10},... | collective-permute-start | bytes 1572872 | tf_op jit(solution)/shard_map/ppermute | solution.py:22
  42.9 17.8 %collective-permute-start.5 = (bf16[64,4096]{1,0:T(8,128)(2,1)S(1)}, bf16[64,4096]{1,0:T(8,128)(2,1)S(1)}, u32[]{:S(2)}, u32[]{:S(2)}) collective-permute-start(bf16[64,4096]{1,0:T(8,128)(2,1)S(1)} %get-tuple-element.49), channel_id=1, source_target_pairs={{0,4},{4,0},{8,12},{12,8},{1,5},{5,1},{9,13},{13,9},{2,6},{6,2},{1... | collective-permute-start | bytes 1572872 | tf_op jit(solution)/shard_map/ppermute | solution.py:22
  45.0 14.4 %collective-permute-start.8 = (f32[64,256]{1,0:T(8,128)S(1)}, f32[64,256]{1,0:T(8,128)S(1)}, u32[]{:S(2)}, u32[]{:S(2)}) collective-permute-start(f32[64,256]{1,0:T(8,128)S(1)} %reshape.120), channel_id=1, source_target_pairs={{0,32},{32,0},{1,33},{33,1},{2,34},{34,2},{3,35},{35,3},{4,36},{36... | collective-permute-start | bytes 196616 | tf_op jit(solution)/shard_map/ppermute | solution.py:22
  59.4 1.3 copy-start.4
  59.4 1.3 copy-start.5
  62.7 20.2 %copy-start.6 = (f32[64,256]{1,0:T(8,128)S(1)}, f32[64,256]{1,0:T(8,128)}, u32[]{:S(2)}) copy-start(f32[64,256]{1,0:T(8,128)} %copy-done.5) | copy-start | bytes 196612
  62.7 5.6 %collective-permute-start.9 = (bf16[8,64,512]{2,1,0:T(8,128)(2,1)S(1)}, bf16[8,64,512]{2,1,0:T(8,128)(2,1)S(1)}, u32[]{:S(2)}, u32[]{:S(2)}) collective-permute-start(bf16[8,64,512]{2,1,0:T(8,128)(2,1)S(1)} %get-tuple-element.65), channel_id=1, source_target_pairs={{0,16},{16,0},{1,17},{17,1},{2,18},{18,2},{3,19},{19,3},{4,20},{20... | collective-permute-start | bytes 1572872 | tf_op jit(solution)/shard_map/ppermute | solution.py:22
  69.3 28.0 %all-to-all-start = ((bf16[8,64,512]{2,1,0:T(8,128)(2,1)}), bf16[8,64,512]{2,1,0:T(8,128)(2,1)S(1)}, u32[]{:S(2)}, u32[]{:S(2)}) async-start(bf16[8,64,512]{2,1,0:T(8,128)(2,1)} %add_convert_fusion), calls=%async_computation | async-start | bytes 1048576 | tf_op jit(solution)/shard_map/all_to_all | solution.py:358
  79.3 26.9 %collective-permute-start.10 = (bf16[2,64,4096]{2,1,0:T(8,128)(2,1)}, bf16[2,64,4096]{2,1,0:T(8,128)(2,1)}, u32[]{:S(2)}, u32[]{:S(2)}) collective-permute-start(bf16[2,64,4096]{2,1,0:T(8,128)(2,1)} %copy-done.4), channel_id=1, source_target_pairs={{0,4},{4,0},{8,12},{12,8},{1,5},{5,1},{9,13},{13,9},{2,6},{6,2},{1... | collective-permute-start | bytes 3145736 | tf_op jit(solution)/shard_map/ppermute | solution.py:22
  97.3 12.3 %collective-permute-start.11 = (f32[64,512]{1,0:T(8,128)S(1)}, f32[64,512]{1,0:T(8,128)S(1)}, u32[]{:S(2)}, u32[]{:S(2)}) collective-permute-start(f32[64,512]{1,0:T(8,128)S(1)} %convert_reduce_fusion.mine_ref), channel_id=1, source_target_pairs={{0,32},{32,0},{1,33},{33,1},{2,34},{34,2},{3,35},{35,3},{4,36},{36... | collective-permute-start | bytes 393224 | tf_op jit(solution)/shard_map/ppermute | solution.py:22
  110.5 20.8 %all-to-all-start.1 = ((bf16[8,64,512]{2,1,0:T(8,128)(2,1)}), bf16[8,64,512]{2,1,0:T(8,128)(2,1)S(1)}, u32[]{:S(2)}, u32[]{:S(2)}) async-start(bf16[8,64,512]{2,1,0:T(8,128)(2,1)} %get-tuple-element.74), calls=%async_computation.1 | async-start | bytes 1048576 | tf_op jit(solution)/shard_map/all_to_all | solution.py:367
  115.3 20.4 %collective-permute-start.12 = (bf16[64,4096]{1,0:T(8,128)(2,1)}, bf16[64,4096]{1,0:T(8,128)(2,1)S(1)}, u32[]{:S(2)}, u32[]{:S(2)}) collective-permute-start(bf16[64,4096]{1,0:T(8,128)(2,1)} %fusion), channel_id=1, source_target_pairs={{0,12},{4,8},{8,4},{12,0},{1,13},{5,9},{9,5},{13,1},{2,14},{6,10},... | collective-permute-start | bytes 1572872 | tf_op jit(solution)/shard_map/ppermute | solution.py:22
  131.3 8.3 %collective-permute-start.13 = (bf16[8,64,512]{2,1,0:T(8,128)(2,1)S(1)}, bf16[8,64,512]{2,1,0:T(8,128)(2,1)S(1)}, u32[]{:S(2)}, u32[]{:S(2)}) collective-permute-start(bf16[8,64,512]{2,1,0:T(8,128)(2,1)S(1)} %all-to-all-done.1.mine_ref), channel_id=1, source_target_pairs={{0,16},{16,0},{1,17},{17,1},{2,18},{18,2},{3,19},{19,3},{4,20},{20... | collective-permute-start | bytes 1572872 | tf_op jit(solution)/shard_map/ppermute | solution.py:22

commit v10 on v9

--- a/solution.py
+++ b/solution.py
@@ -90,14 +90,19 @@
 
 
 def rest_kernel(
-    list_ref, at_ref, s0, s1, s2, s3, cot_ref, give_ref, keep_ref, own_ref, left_ref, part_ref
+    list_ref, at_ref, s0, s1, s2, s3, cot_ref,
+    give_a, give_b, keep_a, keep_b, own_ref, left_ref, part_ref,
 ):
-    shards = (s0, s1, s2, s3)
-    for lead, k in enumerate((1, 2)):
-        product(at_ref, k, shards, cot_ref, left_ref, part_ref)
-        pack(list_ref, k, 0, HALF, part_ref, give_ref, lead)
+    shards, half = (s0, s1, s2, s3), HALF // 2
+    product(at_ref, 1, shards, cot_ref, left_ref, part_ref)
+    pack(list_ref, 1, 0, half, part_ref, give_a, 0)
+    pack(list_ref, 1, half, half, part_ref, keep_b)
+    product(at_ref, 2, shards, cot_ref, left_ref, part_ref)
+    pack(list_ref, 2, 0, half, part_ref, give_a, 1)
+    pack(list_ref, 2, half, half, part_ref, give_b, 1)
     product(at_ref, 3, shards, cot_ref, left_ref, part_ref)
-    pack(list_ref, 3, 0, HALF, part_ref, keep_ref)
+    pack(list_ref, 3, half, half, part_ref, give_b, 0)
+    pack(list_ref, 3, 0, half, part_ref, keep_a)
     product(at_ref, 0, shards, cot_ref, left_ref, own_ref)
 
 
@@ -134,7 +139,8 @@
 
 def rest_parts(lists, at, shards, cotangent):
     own = jax.ShapeDtypeStruct((shards[0].shape[1], cotangent.shape[1]), BF16)
-    shapes = [packed(2), packed(), own]
+    half = HALF // 2
+    shapes = [packed(2, blocks=half)] * 2 + [packed(blocks=half)] * 2 + [own]
     return products_call(rest_kernel, lists, at, shards, cotangent, shapes)
 
 
@@ -183,13 +189,17 @@
             other_ref[h, :, place] = jnp.where(first, sent[1], sent[0]).astype(BF16)
 
 
-def residual_kernel(list_ref, mask_ref, fb_ref, own_ref, got, nxt, new_ref, grad_ref):
+def residual_kernel(
+    list_ref, mask_ref, fb_ref, own_ref, got_a, got_b, next_a, next_b, new_ref, grad_ref
+):
     row = pl.program_id(0)
 
     @pl.when(row == 0)
     def _():
-        terms = [lambda at: got[0, :, at], lambda at: nxt[:, at]]
-        unpack(list_ref, 0, HALF, terms, grad_ref)
+        half = HALF // 2
+        for base, got, nxt in ((0, got_a, next_a), (half, got_b, next_b)):
+            terms = [lambda at, ref=got: ref[0, :, at], lambda at, ref=nxt: ref[:, at]]
+            unpack(list_ref, base, half, terms, grad_ref)
 
     rows = pl.ds(pl.multiple_of(row * BLK, BLK), BLK)
     for at in range(0, fb_ref.shape[1], 256):
@@ -348,24 +358,28 @@
     others = jnp.concatenate([picks, near_picks, far_picks[1:], far_picks[:1]])
     others = others_of(others, rows_blk * cols_blk)
     rest = rest_parts(others, at, shards, cotangent)
-    got_1, got_2, got_3, far_moment, give, keep, own = lax.optimization_barrier(
-        (got_1, got_2, got_3, far_moment, *rest)
+    got_1, got_2, got_3, far_moment, give_a, give_b, keep_a, keep_b, own = (
+        lax.optimization_barrier((got_1, got_2, got_3, far_moment, *rest))
     )
     mine, other = chosen_sums(picks, at_c, mask, feedback[0], own, got_1, got_2, got_3)
     pair = (mine + swap(other, "c", 1, 2).astype(F32)).astype(BF16)
-    pair, give = lax.optimization_barrier((pair, give))
-    got_rest = swap(give, "dp", 1, 4)
+    pair, give_a, give_b = lax.optimization_barrier((pair, give_a, give_b))
+    got_a, got_b = swap(give_a, "dp", 1, 4), swap(give_b, "dp", 3, 4)
     across = lax.all_to_all(pair, "z", 0, 0, tiled=True)
     near = jnp.sum(across.astype(F32), axis=0)
+    near, keep_a, keep_b = lax.optimization_barrier((near, keep_a, keep_b))
     far = swap(near, "yh", 1, 2)
-    far, give_rest = lax.optimization_barrier((far, plus(keep, got_rest[1])))
+    far, give_a, give_b = lax.optimization_barrier(
+        (far, plus(keep_a, got_a[1]), plus(keep_b, got_b[1]))
+    )
     moment = jnp.where(
         yh == 0, jnp.concatenate([moment, far_moment], 1), jnp.concatenate([far_moment, moment], 1)
     )
     momentum_new, copies = owner_update(at_yh, near, far, moment)
-    next_rest = swap(give_rest, "dp", 3, 4)
+    next_a, next_b = swap(give_a, "dp", 3, 4), swap(give_b, "dp", 1, 4)
     every = lax.all_to_all(copies, "z", 0, 0, tiled=True)
-    feedback_new = residual(others, mask, feedback[0], own, got_rest, next_rest)
+    every, next_a, next_b = lax.optimization_barrier((every, next_a, next_b))
+    feedback_new = residual(others, mask, feedback[0], own, got_a, got_b, next_a, next_b)
     step = assemble(at_c, every, swap(every, "c", 1, 2), rows, cols)
     return feedback_new[None], momentum_new[None, None], step
 

time: 142 us -> 145 us (1.021)
  the two profiles are of different devices: /device:TPU:1 before, /device:TPU:5 now
where the time goes in v10:
time: 145 us; the launch traced here: 144 us
  starting transfers between devices  67.1 us (46%)
  waiting for transfers between devices  40 us (28%)
  Pallas kernels  18.3 us (13%)
  other arithmetic  7.94 us (5%)
  local copies, waits for them, and re-layouts  5.45 us (4%)
  matrix products  3.98 us (3%)
    ppermute x16, starting transfers between devices, swap(): return lax.ppermute(value, axis, [(i, i ^ flip) for i in range(size)])  53.6 us
    ppermute x16, waiting for transfers between devices, swap(): return lax.ppermute(value, axis, [(i, i ^ flip) for i in range(size)])  19.6 us
    all_to_all x1, waiting for transfers between devices, local(): across = lax.all_to_all(pair, 'z', 0, 0, tiled=True)  13.7 us
    all_to_all x1, starting transfers between devices, local(): across = lax.all_to_all(pair, 'z', 0, 0, tiled=True)  10 us
    all_to_all x1, waiting for transfers between devices, local(): every = lax.all_to_all(copies, 'z', 0, 0, tiled=True)  6.62 us
    pallas_call x1, Pallas kernels, products_call(): pl.pallas_call(body, in_specs=[SMEM, SMEM] + [whole] * 5, out_specs=jax.t...  6.61 us
    pallas_call x2, Pallas kernels, state_call(): pl.pallas_call(body, grid=(rows // BLK,), in_specs=[SMEM] * len(scalars)...  5.27 us
    unnamed x28, local copies, waits for them, and re-layouts  4.29 us
  transfers between devices with their start and end apart: 18, of which 8 were waited for; matrix products, arithmetic and copies ran while one was open for 7% of the time, Pallas kernels for 9%

profile of v10, /device:TPU:5, one launch (start us, length us, event | category | flops | bytes accessed | tf_op | source)
XLA Modules:
  0.0 143.8 jit_solution(10677824650242760518)
XLA Ops:
  0.6 4.2 %collective-permute-start.1 = (bf16[512,256]{1,0:T(8,128)(2,1)}, bf16[512,256]{1,0:T(8,128)(2,1)S(1)}, u32[]{:S(2)}, u32[]{:S(2)}) collective-permute-start(bf16[512,256]{1,0:T(8,128)(2,1)} %s0), channel_id=1, source_target_pairs={{0,2},{1,3},{2,0},{3,1},{4,6},{5,7},{6,4},{7,5},{8,10},{9,11},{10,... | collective-permute-start | bytes 786440 | tf_op jit(solution)/shard_map/ppermute | solution.py:22
  4.9 3.2 %collective-permute-start = (bf16[512,256]{1,0:T(8,128)(2,1)}, bf16[512,256]{1,0:T(8,128)(2,1)S(1)}, u32[]{:S(2)}, u32[]{:S(2)}) collective-permute-start(bf16[512,256]{1,0:T(8,128)(2,1)} %s0), channel_id=1, source_target_pairs={{0,1},{1,0},{2,3},{3,2},{4,5},{5,4},{6,7},{7,6},{8,9},{9,8},{10,11... | collective-permute-start | bytes 786440 | tf_op jit(solution)/shard_map/ppermute | solution.py:22
  8.1 2.8 %collective-permute-start.3 = (s32[1,64]{1,0:T(1,128)}, s32[1,64]{1,0:T(1,128)S(1)}, u32[]{:S(2)}, u32[]{:S(2)}) collective-permute-start(s32[1,64]{1,0:T(1,128)} %bitcast.26), channel_id=1, source_target_pairs={{0,4},{4,0},{8,12},{12,8},{1,5},{5,1},{9,13},{13,9},{2,6},{6,2},{1... | collective-permute-start | bytes 776 | tf_op jit(solution)/shard_map/ppermute | solution.py:22
  11.0 5.5 %collective-permute-done.1.s2 = bf16[512,256]{1,0:T(8,128)(2,1)S(1)} collective-permute-done((bf16[512,256]{1,0:T(8,128)(2,1)}, bf16[512,256]{1,0:T(8,128)(2,1)S(1)}, u32[]{:S(2)}, u32[]{:S(2)}) %collective-permute-start.1) | collective-permute-done | bytes 262176 | tf_op jit(solution)/shard_map/ppermute | solution.py:22
  16.5 3.4 %collective-permute-start.2 = (bf16[512,256]{1,0:T(8,128)(2,1)S(1)}, bf16[512,256]{1,0:T(8,128)(2,1)S(1)}, u32[]{:S(2)}, u32[]{:S(2)}) collective-permute-start(bf16[512,256]{1,0:T(8,128)(2,1)S(1)} %collective-permute-done.1.s2), channel_id=1, source_target_pairs={{0,1},{1,0},{2,3},{3,2},{4,5},{5,4},{6,7},{7,6},{8,9},{9,8},{10,11... | collective-permute-start | bytes 786440 | tf_op jit(solution)/shard_map/ppermute | solution.py:22
  21.7 2.2 %collective-permute-start.4 = (s32[2,64]{1,0:T(2,128)S(1)}, s32[2,64]{1,0:T(2,128)S(1)}, u32[]{:S(2)}, u32[]{:S(2)}) collective-permute-start(s32[2,64]{1,0:T(2,128)S(1)} %pad_add_fusion.1), channel_id=1, source_target_pairs={{0,12},{4,8},{8,4},{12,0},{1,13},{5,9},{9,5},{13,1},{2,14},{6,10},... | collective-permute-start | bytes 1544 | tf_op jit(solution)/shard_map/ppermute | solution.py:22
  26.3 2.4 %convolution_convert_fusion.2.refs_1_ = bf16[256,2048]{1,0:T(8,128)(2,1)S(1)} fusion(bf16[512,2048]{1,0:T(8,128)(2,1)} %cot_ref.1, bf16[512,256]{1,0:T(8,128)(2,1)S(1)} %collective-permute-done.1.s2, bf16[512,256]{1,0:T(8,128)(2,1)S(1)} %collective-permute-done.2.s3, bf16[512,256]{1,0:T(8,128)(2,1)} %s0, bf16[512,256]{1,0:T(8,128)(2,1)S(1)} %collective-permute-done.s1, ...), kind=kOutput, calls=%fused_computation.2 | convolution fusion | flops 537788416 | bytes 4194307 | tf_op jit(solution)/shard_map/dot_general | solution.py:341
  28.7 1.5 %shard_map.76 = bf16[64,4096]{1,0:T(8,128)(2,1)S(1)} custom-call(s32[2,64]{1,0:T(2,128)S(1)} %collective-permute-done.4.refs_0_.refs_1_, bf16[256,2048]{1,0:T(8,128)(2,1)S(1)} %convolution_convert_fusion.2.refs_1_), custom_call_target="tpu_custom_call" | custom-call | flops 1048576 | bytes 1048576 | tf_op jit(solution)/shard_map/pallas_call | solution.py:130
  30.3 3.2 %collective-permute-start.6 = (bf16[64,4096]{1,0:T(8,128)(2,1)S(1)}, bf16[64,4096]{1,0:T(8,128)(2,1)S(1)}, u32[]{:S(2)}, u32[]{:S(2)}) collective-permute-start(bf16[64,4096]{1,0:T(8,128)(2,1)S(1)} %shard_map.76), channel_id=1, source_target_pairs={{0,8},{4,12},{8,0},{12,4},{1,9},{5,13},{9,1},{13,5},{2,10},{6,14},... | collective-permute-start | bytes 1572872 | tf_op jit(solution)/shard_map/ppermute | solution.py:22
  35.1 2.5 %shard_map.77 = (bf16[64,4096]{1,0:T(8,128)(2,1)S(1)}, bf16[64,4096]{1,0:T(8,128)(2,1)S(1)}) custom-call(s32[1,64]{1,0:T(1,128)S(1)} %collective-permute-done.3.refs_0_, s32[2,64]{1,0:T(2,128)S(1)} %collective-permute-done.4.refs_0_.refs_1_, bf16[256,2048]{1,0:T(8,128)(2,1)S(1)} %convolution_convert_fusion.1.refs_2_, ...), custom_call_target="tpu_custom_call" | custom-call | flops 1048576 | bytes 1048576 | tf_op jit(solution)/shard_map/pallas_call | solution.py:130
  37.6 3.6 %collective-permute-start.7 = (bf16[64,4096]{1,0:T(8,128)(2,1)S(1)}, bf16[64,4096]{1,0:T(8,128)(2,1)S(1)}, u32[]{:S(2)}, u32[]{:S(2)}) collective-permute-start(bf16[64,4096]{1,0:T(8,128)(2,1)S(1)} %get-tuple-element.63), channel_id=1, source_target_pairs={{0,12},{4,8},{8,4},{12,0},{1,13},{5,9},{9,5},{13,1},{2,14},{6,10},... | collective-permute-start | bytes 1572872 | tf_op jit(solution)/shard_map/ppermute | solution.py:22
  41.3 2.9 %collective-permute-start.5 = (bf16[64,4096]{1,0:T(8,128)(2,1)S(1)}, bf16[64,4096]{1,0:T(8,128)(2,1)S(1)}, u32[]{:S(2)}, u32[]{:S(2)}) collective-permute-start(bf16[64,4096]{1,0:T(8,128)(2,1)S(1)} %get-tuple-element.61), channel_id=1, source_target_pairs={{0,4},{4,0},{8,12},{12,8},{1,5},{5,1},{9,13},{13,9},{2,6},{6,2},{1... | collective-permute-start | bytes 1572872 | tf_op jit(solution)/shard_map/ppermute | solution.py:22
  44.2 7.7 %collective-permute-start.8 = (f32[64,256]{1,0:T(8,128)S(1)}, f32[64,256]{1,0:T(8,128)S(1)}, u32[]{:S(2)}, u32[]{:S(2)}) collective-permute-start(f32[64,256]{1,0:T(8,128)S(1)} %reshape.122), channel_id=1, source_target_pairs={{0,32},{32,0},{1,33},{33,1},{2,34},{34,2},{3,35},{35,3},{4,36},{36... | collective-permute-start | bytes 196616 | tf_op jit(solution)/shard_map/ppermute | solution.py:22
  52.3 6.6 %shard_map.78 = (bf16[2,64,2048]{2,1,0:T(8,128)(2,1)S(1)}, bf16[2,64,2048]{2,1,0:T(8,128)(2,1)}, bf16[64,2048]{1,0:T(8,128)(2,1)S(1)}, bf16[64,2048]{1,0:T(8,128)(2,1)S(1)}, bf16[256,2048]{1,0:T(8,128)(2,1)S(1)}) custom-call(s32[4,64]{1,0:T(4,128)S(1)} %select_reduce_fusion.1.list_ref, s32[1]{0:T(128)} %bitcast.5.at_ref, bf16[512,256]{1,0:T(8,128)(2,1)S(1)} %copy-done.1, ...), custom_call_target="tpu_custom_call" | custom-call | flops 1048576 | bytes 1048576 | tf_op jit(solution)/shard_map/pallas_call | solution.py:113
  58.9 2.0 %shard_map.79 = (f32[8,64,512]{2,1,0:T(8,128)S(1)}, bf16[8,64,512]{2,1,0:T(8,128)(2,1)S(1)}) custom-call(s32[1,64]{1,0:T(1,128)S(1)} %bitcast.30, s32[1]{0:T(128)} %bitcast.6.c_ref, f32[4,1,2048]{2,1,0:T(1,128)S(1)} %reshape.126.mask_ref, bf16[256,2048]{1,0:T(8,128)(2,1)S(1)} %bitcast.24, bf16[256,2048]{1,0:T(8,128)(2,1)S(1)} %get-tuple-element.74.own_ref, ...), custom_call_target="tpu_custom_call" | custom-call | flops 4194304 | bytes 4194304 | tf_op jit(solution)/shard_map/pallas_call | solution.py:218
  61.0 4.6 %collective-permute-start.9 = (bf16[8,64,512]{2,1,0:T(8,128)(2,1)S(1)}, bf16[8,64,512]{2,1,0:T(8,128)(2,1)S(1)}, u32[]{:S(2)}, u32[]{:S(2)}) collective-permute-start(bf16[8,64,512]{2,1,0:T(8,128)(2,1)S(1)} %get-tuple-element.79), channel_id=1, source_target_pairs={{0,16},{16,0},{1,17},{17,1},{2,18},{18,2},{3,19},{19,3},{4,20},{20... | collective-permute-start | bytes 1572872 | tf_op jit(solution)/shard_map/ppermute | solution.py:22
  68.1 10.0 %all-to-all-start = ((bf16[8,64,512]{2,1,0:T(8,128)(2,1)}), bf16[8,64,512]{2,1,0:T(8,128)(2,1)}, u32[]{:S(2)}, u32[]{:S(2)}) async-start(bf16[8,64,512]{2,1,0:T(8,128)(2,1)} %add_convert_fusion), calls=%async_computation | async-start | bytes 1048576 | tf_op jit(solution)/shard_map/all_to_all | solution.py:368
  78.1 2.1 %collective-permute-start.11 = (bf16[2,64,2048]{2,1,0:T(8,128)(2,1)}, bf16[2,64,2048]{2,1,0:T(8,128)(2,1)S(1)}, u32[]{:S(2)}, u32[]{:S(2)}) collective-permute-start(bf16[2,64,2048]{2,1,0:T(8,128)(2,1)} %get-tuple-element.83), channel_id=1, source_target_pairs={{0,12},{4,8},{8,4},{12,0},{1,13},{5,9},{9,5},{13,1},{2,14},{6,10},... | collective-permute-start | bytes 1572872 | tf_op jit(solution)/shard_map/ppermute | solution.py:22
  80.2 2.2 %collective-permute-start.10 = (bf16[2,64,2048]{2,1,0:T(8,128)(2,1)}, bf16[2,64,2048]{2,1,0:T(8,128)(2,1)S(1)}, u32[]{:S(2)}, u32[]{:S(2)}) collective-permute-start(bf16[2,64,2048]{2,1,0:T(8,128)(2,1)} %copy-done.13), channel_id=1, source_target_pairs={{0,4},{4,0},{8,12},{12,8},{1,5},{5,1},{9,13},{13,9},{2,6},{6,2},{1... | collective-permute-start | bytes 1572872 | tf_op jit(solution)/shard_map/ppermute | solution.py:22
  82.5 13.7 %all-to-all-done = bf16[8,64,512]{2,1,0:T(8,128)(2,1)} async-done(((bf16[8,64,512]{2,1,0:T(8,128)(2,1)}), bf16[8,64,512]{2,1,0:T(8,128)(2,1)}, u32[]{:S(2)}, u32[]{:S(2)}) %all-to-all-start) | async-done | bytes 524320 | tf_op jit(solution)/shard_map/all_to_all | solution.py:368
  97.3 5.3 %collective-permute-start.12 = (f32[64,512]{1,0:T(8,128)S(1)}, f32[64,512]{1,0:T(8,128)S(1)}, u32[]{:S(2)}, u32[]{:S(2)}) collective-permute-start(f32[64,512]{1,0:T(8,128)S(1)} %convert_reduce_fusion.mine_ref), channel_id=1, source_target_pairs={{0,32},{32,0},{1,33},{33,1},{2,34},{34,2},{3,35},{35,3},{4,36},{36... | collective-permute-start | bytes 393224 | tf_op jit(solution)/shard_map/ppermute | solution.py:22
  102.6 1.7 %fusion = bf16[64,2048]{1,0:T(8,128)(2,1)} fusion(bf16[64,2048]{1,0:T(8,128)(2,1)} %copy-done.9, bf16[2,64,2048]{2,1,0:T(8,128)(2,1)S(1)} %collective-permute-done.11.got_b), kind=kLoop, calls=%fused_computation.7 | loop fusion | flops 524288 | bytes 786432 | tf_op jit(solution)/shard_map/convert_element_type | solution.py:313
  104.4 1.9 %fusion.1 = bf16[64,2048]{1,0:T(8,128)(2,1)} fusion(bf16[64,2048]{1,0:T(8,128)(2,1)} %copy-done.8, bf16[2,64,2048]{2,1,0:T(8,128)(2,1)S(1)} %collective-permute-done.10.got_a), kind=kLoop, calls=%fused_computation.9 | loop fusion | flops 524288 | bytes 786432 | tf_op jit(solution)/shard_map/convert_element_type | solution.py:313
  106.3 4.7 %collective-permute-done.12.peer_ref = f32[64,512]{1,0:T(8,128)S(1)} collective-permute-done((f32[64,512]{1,0:T(8,128)S(1)}, f32[64,512]{1,0:T(8,128)S(1)}, u32[]{:S(2)}, u32[]{:S(2)}) %collective-permute-start.12) | collective-permute-done | bytes 131104 | tf_op jit(solution)/shard_map/ppermute | solution.py:22
  112.5 3.5 %all-to-all-start.1 = ((bf16[8,64,512]{2,1,0:T(8,128)(2,1)}), bf16[8,64,512]{2,1,0:T(8,128)(2,1)S(1)}, u32[]{:S(2)}, u32[]{:S(2)}) async-start(bf16[8,64,512]{2,1,0:T(8,128)(2,1)} %copy-done.5), calls=%async_computation.1 | async-start | bytes 1048576 | tf_op jit(solution)/shard_map/all_to_all | solution.py:380
  116.0 1.9 %collective-permute-start.13 = (bf16[64,2048]{1,0:T(8,128)(2,1)}, bf16[64,2048]{1,0:T(8,128)(2,1)S(1)}, u32[]{:S(2)}, u32[]{:S(2)}) collective-permute-start(bf16[64,2048]{1,0:T(8,128)(2,1)} %fusion.1), channel_id=1, source_target_pairs={{0,12},{4,8},{8,4},{12,0},{1,13},{5,9},{9,5},{13,1},{2,14},{6,10},... | collective-permute-start | bytes 786440 | tf_op jit(solution)/shard_map/ppermute | solution.py:22
  118.0 1.9 %collective-permute-start.14 = (bf16[64,2048]{1,0:T(8,128)(2,1)}, bf16[64,2048]{1,0:T(8,128)(2,1)S(1)}, u32[]{:S(2)}, u32[]{:S(2)}) collective-permute-start(bf16[64,2048]{1,0:T(8,128)(2,1)} %fusion), channel_id=1, source_target_pairs={{0,4},{4,0},{8,12},{12,8},{1,5},{5,1},{9,13},{13,9},{2,6},{6,2},{1... | collective-permute-start | bytes 786440 | tf_op jit(solution)/shard_map/ppermute | solution.py:22
  119.9 5.2 %collective-permute-done.13.next_a = bf16[64,2048]{1,0:T(8,128)(2,1)S(1)} collective-permute-done((bf16[64,2048]{1,0:T(8,128)(2,1)}, bf16[64,2048]{1,0:T(8,128)(2,1)S(1)}, u32[]{:S(2)}, u32[]{:S(2)}) %collective-permute-start.13) | collective-permute-done | bytes 262176 | tf_op jit(solution)/shard_map/ppermute | solution.py:22
  127.3 6.6 %all-to-all-done.1.mine_ref = bf16[8,64,512]{2,1,0:T(8,128)(2,1)S(1)} async-done(((bf16[8,64,512]{2,1,0:T(8,128)(2,1)}), bf16[8,64,512]{2,1,0:T(8,128)(2,1)S(1)}, u32[]{:S(2)}, u32[]{:S(2)}) %all-to-all-start.1) | async-done | bytes 524320 | tf_op jit(solution)/shard_map/all_to_all | solution.py:380
  133.9 2.4 %collective-permute-start.15 = (bf16[8,64,512]{2,1,0:T(8,128)(2,1)S(1)}, bf16[8,64,512]{2,1,0:T(8,128)(2,1)S(1)}, u32[]{:S(2)}, u32[]{:S(2)}) collective-permute-start(bf16[8,64,512]{2,1,0:T(8,128)(2,1)S(1)} %all-to-all-done.1.mine_ref), channel_id=1, source_target_pairs={{0,16},{16,0},{1,17},{17,1},{2,18},{18,2},{3,19},{19,3},{4,20},{20... | collective-permute-start | bytes 1572872 | tf_op jit(solution)/shard_map/ppermute | solution.py:22
  139.1 3.2 %shard_map.81 = bf16[256,2048]{1,0:T(8,128)(2,1)} custom-call(s32[4,64]{1,0:T(4,128)S(1)} %select_reduce_fusion.1.list_ref, f32[4,1,2048]{2,1,0:T(1,128)S(1)} %copy-done.7, bf16[256,2048]{1,0:T(8,128)(2,1)S(1)} %bitcast.25, bf16[256,2048]{1,0:T(8,128)(2,1)S(1)} %get-tuple-element.74.own_ref, bf16[2,64,2048]{2,1,0:T(8,128)(2,1)S(1)} %copy-done.4, ...), custom_call_target="tpu_custom_call" | custom-call | flops 4194304 | bytes 4194304 | tf_op jit(solution)/shard_map/pallas_call | solution.py:218
  142.3 1.5 %shard_map.82 = bf16[256,2048]{1,0:T(8,128)(2,1)} custom-call(s32[1]{0:T(128)} %bitcast.6.c_ref, bf16[8,64,512]{2,1,0:T(8,128)(2,1)S(1)} %all-to-all-done.1.mine_ref, bf16[8,64,512]{2,1,0:T(8,128)(2,1)S(1)} %collective-permute-done.15.other_ref), custom_call_target="tpu_custom_call" | custom-call | flops 2097152 | bytes 2097152 | tf_op jit(solution)/shard_map/pallas_call | solution.py:286
  (62 shorter events, 16.3 us)
Async XLA Ops:
  0.6 15.9 %collective-permute-start.1 = (bf16[512,256]{1,0:T(8,128)(2,1)}, bf16[512,256]{1,0:T(8,128)(2,1)S(1)}, u32[]{:S(2)}, u32[]{:S(2)}) collective-permute-start(bf16[512,256]{1,0:T(8,128)(2,1)} %s0), channel_id=1, source_target_pairs={{0,2},{1,3},{2,0},{3,1},{4,6},{5,7},{6,4},{7,5},{8,10},{9,11},{10,... | collective-permute-start | bytes 786440 | tf_op jit(solution)/shard_map/ppermute | solution.py:22
  4.9 21.4 %collective-permute-start = (bf16[512,256]{1,0:T(8,128)(2,1)}, bf16[512,256]{1,0:T(8,128)(2,1)S(1)}, u32[]{:S(2)}, u32[]{:S(2)}) collective-permute-start(bf16[512,256]{1,0:T(8,128)(2,1)} %s0), channel_id=1, source_target_pairs={{0,1},{1,0},{2,3},{3,2},{4,5},{5,4},{6,7},{7,6},{8,9},{9,8},{10,11... | collective-permute-start | bytes 786440 | tf_op jit(solution)/shard_map/ppermute | solution.py:22
  8.1 12.9 %collective-permute-start.3 = (s32[1,64]{1,0:T(1,128)}, s32[1,64]{1,0:T(1,128)S(1)}, u32[]{:S(2)}, u32[]{:S(2)}) collective-permute-start(s32[1,64]{1,0:T(1,128)} %bitcast.26), channel_id=1, source_target_pairs={{0,4},{4,0},{8,12},{12,8},{1,5},{5,1},{9,13},{13,9},{2,6},{6,2},{1... | collective-permute-start | bytes 776 | tf_op jit(solution)/shard_map/ppermute | solution.py:22
  16.5 9.8 %collective-permute-start.2 = (bf16[512,256]{1,0:T(8,128)(2,1)S(1)}, bf16[512,256]{1,0:T(8,128)(2,1)S(1)}, u32[]{:S(2)}, u32[]{:S(2)}) collective-permute-start(bf16[512,256]{1,0:T(8,128)(2,1)S(1)} %collective-permute-done.1.s2), channel_id=1, source_target_pairs={{0,1},{1,0},{2,3},{3,2},{4,5},{5,4},{6,7},{7,6},{8,9},{9,8},{10,11... | collective-permute-start | bytes 786440 | tf_op jit(solution)/shard_map/ppermute | solution.py:22
  21.7 4.6 %collective-permute-start.4 = (s32[2,64]{1,0:T(2,128)S(1)}, s32[2,64]{1,0:T(2,128)S(1)}, u32[]{:S(2)}, u32[]{:S(2)}) collective-permute-start(s32[2,64]{1,0:T(2,128)S(1)} %pad_add_fusion.1), channel_id=1, source_target_pairs={{0,12},{4,8},{8,4},{12,0},{1,13},{5,9},{9,5},{13,1},{2,14},{6,10},... | collective-permute-start | bytes 1544 | tf_op jit(solution)/shard_map/ppermute | solution.py:22
  25.0 33.9 %copy-start.6 = (f32[4,1,2048]{2,1,0:T(1,128)}, f32[4,1,2048]{2,1,0:T(1,128)S(1)}, u32[]{:S(2)}) copy-start(f32[4,1,2048]{2,1,0:T(1,128)S(1)} %reshape.126.mask_ref) | copy-start | bytes 98308
  25.0 8.5 %copy-start = (bf16[512,2048]{1,0:T(8,128)(2,1)S(1)}, bf16[512,2048]{1,0:T(8,128)(2,1)}, u32[]{:S(2)}) copy-start(bf16[512,2048]{1,0:T(8,128)(2,1)} %cot_ref.1) | copy-start | bytes 6291460
  25.0 8.5 %copy-start.1 = (bf16[512,256]{1,0:T(8,128)(2,1)S(1)}, bf16[512,256]{1,0:T(8,128)(2,1)}, u32[]{:S(2)}) copy-start(bf16[512,256]{1,0:T(8,128)(2,1)} %s0) | copy-start | bytes 786436
  30.3 28.7 %collective-permute-start.6 = (bf16[64,4096]{1,0:T(8,128)(2,1)S(1)}, bf16[64,4096]{1,0:T(8,128)(2,1)S(1)}, u32[]{:S(2)}, u32[]{:S(2)}) collective-permute-start(bf16[64,4096]{1,0:T(8,128)(2,1)S(1)} %shard_map.76), channel_id=1, source_target_pairs={{0,8},{4,12},{8,0},{12,4},{1,9},{5,13},{9,1},{13,5},{2,10},{6,14},... | collective-permute-start | bytes 1572872 | tf_op jit(solution)/shard_map/ppermute | solution.py:22
  35.1 16.8 %copy-start.12 = (s32[1,1,1,64]{3,2,1,0:T(1,128)S(1)}, s32[1,1,1,64]{3,2,1,0:T(1,128)}, u32[]{:S(2)}) copy-start(s32[1,1,1,64]{3,2,1,0:T(1,128)} %param.8) | copy-start | bytes 772
  37.6 21.3 %copy-start.2 = (bf16[1,256,2048]{2,1,0:T(8,128)(2,1)S(1)}, bf16[1,256,2048]{2,1,0:T(8,128)(2,1)}, u32[]{:S(2)}) copy-start(bf16[1,256,2048]{2,1,0:T(8,128)(2,1)} %param.7) | copy-start | bytes 3145732
  37.6 21.3 %collective-permute-start.7 = (bf16[64,4096]{1,0:T(8,128)(2,1)S(1)}, bf16[64,4096]{1,0:T(8,128)(2,1)S(1)}, u32[]{:S(2)}, u32[]{:S(2)}) collective-permute-start(bf16[64,4096]{1,0:T(8,128)(2,1)S(1)} %get-tuple-element.63), channel_id=1, source_target_pairs={{0,12},{4,8},{8,4},{12,0},{1,13},{5,9},{9,5},{13,1},{2,14},{6,10},... | collective-permute-start | bytes 1572872 | tf_op jit(solution)/shard_map/ppermute | solution.py:22
  41.3 17.6 %collective-permute-start.5 = (bf16[64,4096]{1,0:T(8,128)(2,1)S(1)}, bf16[64,4096]{1,0:T(8,128)(2,1)S(1)}, u32[]{:S(2)}, u32[]{:S(2)}) collective-permute-start(bf16[64,4096]{1,0:T(8,128)(2,1)S(1)} %get-tuple-element.61), channel_id=1, source_target_pairs={{0,4},{4,0},{8,12},{12,8},{1,5},{5,1},{9,13},{13,9},{2,6},{6,2},{1... | collective-permute-start | bytes 1572872 | tf_op jit(solution)/shard_map/ppermute | solution.py:22
  44.2 14.7 %collective-permute-start.8 = (f32[64,256]{1,0:T(8,128)S(1)}, f32[64,256]{1,0:T(8,128)S(1)}, u32[]{:S(2)}, u32[]{:S(2)}) collective-permute-start(f32[64,256]{1,0:T(8,128)S(1)} %reshape.122), channel_id=1, source_target_pairs={{0,32},{32,0},{1,33},{33,1},{2,34},{34,2},{3,35},{35,3},{4,36},{36... | collective-permute-start | bytes 196616 | tf_op jit(solution)/shard_map/ppermute | solution.py:22
  58.9 2.1 %copy-start.8 = (bf16[64,2048]{1,0:T(8,128)(2,1)}, bf16[64,2048]{1,0:T(8,128)(2,1)S(1)}, u32[]{:S(2)}) copy-start(bf16[64,2048]{1,0:T(8,128)(2,1)S(1)} %get-tuple-element.88) | copy-start | bytes 786436
  58.9 2.1 %copy-start.9 = (bf16[64,2048]{1,0:T(8,128)(2,1)}, bf16[64,2048]{1,0:T(8,128)(2,1)S(1)}, u32[]{:S(2)}) copy-start(bf16[64,2048]{1,0:T(8,128)(2,1)S(1)} %get-tuple-element.89) | copy-start | bytes 786436
  58.9 6.7 %copy-start.13 = (bf16[2,64,2048]{2,1,0:T(8,128)(2,1)}, bf16[2,64,2048]{2,1,0:T(8,128)(2,1)S(1)}, u32[]{:S(2)}) copy-start(bf16[2,64,2048]{2,1,0:T(8,128)(2,1)S(1)} %get-tuple-element.82) | copy-start | bytes 1572868
  61.0 6.1 %collective-permute-start.9 = (bf16[8,64,512]{2,1,0:T(8,128)(2,1)S(1)}, bf16[8,64,512]{2,1,0:T(8,128)(2,1)S(1)}, u32[]{:S(2)}, u32[]{:S(2)}) collective-permute-start(bf16[8,64,512]{2,1,0:T(8,128)(2,1)S(1)} %get-tuple-element.79), channel_id=1, source_target_pairs={{0,16},{16,0},{1,17},{17,1},{2,18},{18,2},{3,19},{19,3},{4,20},{20... | collective-permute-start | bytes 1572872 | tf_op jit(solution)/shard_map/ppermute | solution.py:22
  68.1 28.1 %all-to-all-start = ((bf16[8,64,512]{2,1,0:T(8,128)(2,1)}), bf16[8,64,512]{2,1,0:T(8,128)(2,1)}, u32[]{:S(2)}, u32[]{:S(2)}) async-start(bf16[8,64,512]{2,1,0:T(8,128)(2,1)} %add_convert_fusion), calls=%async_computation | async-start | bytes 1048576 | tf_op jit(solution)/shard_map/all_to_all | solution.py:368
  78.1 24.5 %collective-permute-start.11 = (bf16[2,64,2048]{2,1,0:T(8,128)(2,1)}, bf16[2,64,2048]{2,1,0:T(8,128)(2,1)S(1)}, u32[]{:S(2)}, u32[]{:S(2)}) collective-permute-start(bf16[2,64,2048]{2,1,0:T(8,128)(2,1)} %get-tuple-element.83), channel_id=1, source_target_pairs={{0,12},{4,8},{8,4},{12,0},{1,13},{5,9},{9,5},{13,1},{2,14},{6,10},... | collective-permute-start | bytes 1572872 | tf_op jit(solution)/shard_map/ppermute | solution.py:22
  80.2 24.1 %collective-permute-start.10 = (bf16[2,64,2048]{2,1,0:T(8,128)(2,1)}, bf16[2,64,2048]{2,1,0:T(8,128)(2,1)S(1)}, u32[]{:S(2)}, u32[]{:S(2)}) collective-permute-start(bf16[2,64,2048]{2,1,0:T(8,128)(2,1)} %copy-done.13), channel_id=1, source_target_pairs={{0,4},{4,0},{8,12},{12,8},{1,5},{5,1},{9,13},{13,9},{2,6},{6,2},{1... | collective-permute-start | bytes 1572872 | tf_op jit(solution)/shard_map/ppermute | solution.py:22
  97.3 13.7 %collective-permute-start.12 = (f32[64,512]{1,0:T(8,128)S(1)}, f32[64,512]{1,0:T(8,128)S(1)}, u32[]{:S(2)}, u32[]{:S(2)}) collective-permute-start(f32[64,512]{1,0:T(8,128)S(1)} %convert_reduce_fusion.mine_ref), channel_id=1, source_target_pairs={{0,32},{32,0},{1,33},{33,1},{2,34},{34,2},{3,35},{35,3},{4,36},{36... | collective-permute-start | bytes 393224 | tf_op jit(solution)/shard_map/ppermute | solution.py:22
  104.4 8.2 %copy-start.3 = (bf16[2,64,2048]{2,1,0:T(8,128)(2,1)}, bf16[2,64,2048]{2,1,0:T(8,128)(2,1)S(1)}, u32[]{:S(2)}) copy-start(bf16[2,64,2048]{2,1,0:T(8,128)(2,1)S(1)} %collective-permute-done.10.got_a) | copy-start | bytes 1572868
  111.7 0.8 copy-start.5
  112.5 21.4 %all-to-all-start.1 = ((bf16[8,64,512]{2,1,0:T(8,128)(2,1)}), bf16[8,64,512]{2,1,0:T(8,128)(2,1)S(1)}, u32[]{:S(2)}, u32[]{:S(2)}) async-start(bf16[8,64,512]{2,1,0:T(8,128)(2,1)} %copy-done.5), calls=%async_computation.1 | async-start | bytes 1048576 | tf_op jit(solution)/shard_map/all_to_all | solution.py:380
  116.0 9.1 %collective-permute-start.13 = (bf16[64,2048]{1,0:T(8,128)(2,1)}, bf16[64,2048]{1,0:T(8,128)(2,1)S(1)}, u32[]{:S(2)}, u32[]{:S(2)}) collective-permute-start(bf16[64,2048]{1,0:T(8,128)(2,1)} %fusion.1), channel_id=1, source_target_pairs={{0,12},{4,8},{8,4},{12,0},{1,13},{5,9},{9,5},{13,1},{2,14},{6,10},... | collective-permute-start | bytes 786440 | tf_op jit(solution)/shard_map/ppermute | solution.py:22
  118.0 8.6 %collective-permute-start.14 = (bf16[64,2048]{1,0:T(8,128)(2,1)}, bf16[64,2048]{1,0:T(8,128)(2,1)S(1)}, u32[]{:S(2)}, u32[]{:S(2)}) collective-permute-start(bf16[64,2048]{1,0:T(8,128)(2,1)} %fusion), channel_id=1, source_target_pairs={{0,4},{4,0},{8,12},{12,8},{1,5},{5,1},{9,13},{13,9},{2,6},{6,2},{1... | collective-permute-start | bytes 786440 | tf_op jit(solution)/shard_map/ppermute | solution.py:22
  126.6 0.7 copy-start.10
  133.9 8.4 %collective-permute-start.15 = (bf16[8,64,512]{2,1,0:T(8,128)(2,1)S(1)}, bf16[8,64,512]{2,1,0:T(8,128)(2,1)S(1)}, u32[]{:S(2)}, u32[]{:S(2)}) collective-permute-start(bf16[8,64,512]{2,1,0:T(8,128)(2,1)S(1)} %all-to-all-done.1.mine_ref), channel_id=1, source_target_pairs={{0,16},{16,0},{1,17},{17,1},{2,18},{18,2},{3,19},{19,3},{4,20},{20... | collective-permute-start | bytes 1572872 | tf_op jit(solution)/shard_map/ppermute | solution.py:22
  136.3 1.0 copy-start.4
  137.3 0.8 copy-start.7
  138.1 0.9 copy-start.11

commit v11 on v9

--- a/solution.py
+++ b/solution.py
@@ -183,7 +183,10 @@
             other_ref[h, :, place] = jnp.where(first, sent[1], sent[0]).astype(BF16)
 
 
-def residual_kernel(list_ref, mask_ref, fb_ref, own_ref, got, nxt, new_ref, grad_ref):
+def finish_kernel(
+    list_ref, c_ref, mask_ref, fb_ref, own_ref, got, nxt, near_ref, far_ref,
+    new_ref, step_ref, grad_ref,
+):
     row = pl.program_id(0)
 
     @pl.when(row == 0)
@@ -198,23 +201,32 @@
         acc = fb_ref[:, at].astype(F32) + acc
         chosen = jnp.broadcast_to(mask_ref[0, :, at], acc.shape) > 0.5
         new_ref[:, at] = jnp.where(chosen, 0.0, acc).astype(BF16)
-
-
-def state_call(body, scalars, mask, feedback, own, received, outs, out_shape):
+    first = c_ref[0] == 0
+    for h in range(2):
+        for yh in range(2):
+            place = slice(yh * 256, yh * 256 + 256)
+            near, far = near_ref[h, :, place], far_ref[h, :, place]
+            at = h * 1024 + yh * 512
+            step_ref[:, at : at + 256] = jnp.where(first, near, far)
+            step_ref[:, at + 256 : at + 512] = jnp.where(first, far, near)
+
+
+def state_call(body, scalars, mask, feedback, own, received, outs, out_shape, slabs=()):
     rows, cols = feedback.shape
     wide = pl.BlockSpec((BLK, cols), lambda i: (i, 0))
     line = pl.BlockSpec((1, 1, cols), lambda i: (i, 0, 0))
+    slab = pl.BlockSpec((2, BLK, 512), lambda i: (i, 0, 0))
     given = [pl.BlockSpec(r.shape, lambda i, n=r.ndim: (0,) * n) for r in received]
     return pl.pallas_call(
         body,
         grid=(rows // BLK,),
-        in_specs=[SMEM] * len(scalars) + [line, wide, wide] + given,
+        in_specs=[SMEM] * len(scalars) + [line, wide, wide] + given + [slab] * len(slabs),
         out_specs=outs,
         out_shape=out_shape,
         scratch_shapes=[pltpu.VMEM((rows, cols), F32)],
         compiler_params=pltpu.CompilerParams(vmem_limit_bytes=VMEM_LIMIT),
         cost_estimate=pl.CostEstimate(flops=1 << 22, bytes_accessed=1 << 22, transcendentals=0),
-    )(*scalars, mask, feedback, own, *received)
+    )(*scalars, mask, feedback, own, *received, *slabs)
 
 
 def chosen_sums(lists, c, mask, feedback, own, *received):
@@ -226,16 +238,18 @@
     )
 
 
-def residual(lists, mask, feedback, own, *received):
+def finish(lists, c, mask, feedback, own, got, nxt, near, far):
     rows, cols = feedback.shape
+    wide = pl.BlockSpec((BLK, cols), lambda i: (i, 0))
+    out = jax.ShapeDtypeStruct((rows, cols), BF16)
     return state_call(
-        residual_kernel, (lists,), mask, feedback, own, received,
-        pl.BlockSpec((BLK, cols), lambda i: (i, 0)), jax.ShapeDtypeStruct((rows, cols), BF16),
+        finish_kernel, (lists, c), mask, feedback, own, (got, nxt), [wide] * 2, [out] * 2,
+        (near, far),
     )
 
 
 def owner_kernel(yh_ref, mine_ref, peer_ref, moment_ref, new_ref, step_ref):
-    mean = (mine_ref[...] + peer_ref[...]) * (1.0 / NODES)
+    mean = (mine_ref[...].astype(F32) + peer_ref[...].astype(F32)) * (1.0 / NODES)
     moment = DECAY * moment_ref[...] + mean
     step = (mean + DECAY * moment).astype(BF16)
     for z in range(8):
@@ -260,29 +274,6 @@
     )(yh, mine, peer, moment)
 
 
-def assemble_kernel(c_ref, mine_ref, other_ref, out_ref):
-    first = c_ref[0] == 0
-    for h in range(2):
-        for yh in range(2):
-            place = slice(yh * 256, yh * 256 + 256)
-            mine, other = mine_ref[h, :, place], other_ref[h, :, place]
-            at = h * 1024 + yh * 512
-            out_ref[:, at : at + 256] = jnp.where(first, mine, other)
-            out_ref[:, at + 256 : at + 512] = jnp.where(first, other, mine)
-
-
-def assemble(c, mine, other, rows, cols):
-    slab = pl.BlockSpec((2, BLK, 512), lambda i: (i, 0, 0))
-    return kernel_call(
-        assemble_kernel,
-        (rows // BLK,),
-        [SMEM, slab, slab],
-        pl.BlockSpec((BLK, cols), lambda i: (i, 0)),
-        jax.ShapeDtypeStruct((rows, cols), BF16),
-        4 * rows * cols,
-    )(c, mine, other)
-
-
 def others_of(lists, count):
     blocks = jnp.arange(count, dtype=jnp.int32)
     left = jnp.all(lists[:, :, None] != blocks, axis=1)
@@ -356,7 +347,7 @@
     pair, give = lax.optimization_barrier((pair, give))
     got_rest = swap(give, "dp", 1, 4)
     across = lax.all_to_all(pair, "z", 0, 0, tiled=True)
-    near = jnp.sum(across.astype(F32), axis=0)
+    near = jnp.sum(across.astype(F32), axis=0).astype(BF16)
     far = swap(near, "yh", 1, 2)
     far, give_rest = lax.optimization_barrier((far, plus(keep, got_rest[1])))
     moment = jnp.where(
@@ -365,8 +356,9 @@
     momentum_new, copies = owner_update(at_yh, near, far, moment)
     next_rest = swap(give_rest, "dp", 3, 4)
     every = lax.all_to_all(copies, "z", 0, 0, tiled=True)
-    feedback_new = residual(others, mask, feedback[0], own, got_rest, next_rest)
-    step = assemble(at_c, every, swap(every, "c", 1, 2), rows, cols)
+    feedback_new, step = finish(
+        others, at_c, mask, feedback[0], own, got_rest, next_rest, every, swap(every, "c", 1, 2)
+    )
     return feedback_new[None], momentum_new[None, None], step
 
 

time: 142 us -> 142 us (level)
  waiting for transfers between devices: 39.1 us -> 44.1 us
  starting transfers between devices: 71.5 us -> 66.8 us
    ppermute x14, starting transfers between devices: 56.6 us -> 53.2 us  [swap(): return lax.ppermute(value, axis, [(i, i ^ flip) for i in range(size)])]
    all_to_all x1, waiting for transfers between devices: 14.3 us -> 17 us  [local(): across = lax.all_to_all(pair, 'z', 0, 0, tiled=True)]
    all_to_all x1, waiting for transfers between devices: 12.5 us -> 14.8 us  [local(): every = lax.all_to_all(copies, 'z', 0, 0, tiled=True)]
    pallas_call x1 -> x0, Pallas kernels: 1.54 us -> none  [assemble(): kernel_call(assemble_kernel, (rows // BLK,), [SMEM, slab, slab], pl.Block...]
  transfers between devices with their start and end apart: 16 -> 16, of which waited for: 7 -> 7; matrix products, arithmetic and copies ran while one was open for 5% -> 6% of each run, Pallas kernels for 9% -> 7%
where the time goes in v11:
time: 142 us; the launch traced here: 141 us
  starting transfers between devices  66.8 us (47%)
  waiting for transfers between devices  44.1 us (31%)
  Pallas kernels  17.9 us (13%)
  other arithmetic  6.17 us (4%)
  matrix products  4.04 us (3%)
    ppermute x14, starting transfers between devices, swap(): return lax.ppermute(value, axis, [(i, i ^ flip) for i in range(size)])  53.2 us
    all_to_all x1, waiting for transfers between devices, local(): across = lax.all_to_all(pair, 'z', 0, 0, tiled=True)  17 us
    all_to_all x1, waiting for transfers between devices, local(): every = lax.all_to_all(copies, 'z', 0, 0, tiled=True)  14.8 us
    ppermute x14, waiting for transfers between devices, swap(): return lax.ppermute(value, axis, [(i, i ^ flip) for i in range(size)])  12.3 us
    all_to_all x1, starting transfers between devices, local(): across = lax.all_to_all(pair, 'z', 0, 0, tiled=True)  10.1 us
    pallas_call x1, Pallas kernels, products_call(): pl.pallas_call(body, in_specs=[SMEM, SMEM] + [whole] * 5, out_specs=jax.t...  6.78 us
    pallas_call x2, Pallas kernels, state_call(): pl.pallas_call(body, grid=(rows // BLK,), in_specs=[SMEM] * len(scalars)...  6.15 us
    pallas_call x2, Pallas kernels, chosen_parts(): kernel_call(functools.partial(first_kernel, rows), (), [SMEM] * n + [whol...  4.08 us
  transfers between devices with their start and end apart: 16, of which 7 were waited for; matrix products, arithmetic and copies ran while one was open for 6% of the time, Pallas kernels for 7%

profile of v11, /device:TPU:1, one launch (start us, length us, event | category | flops | bytes accessed | tf_op | source)
XLA Modules:
  0.0 141.2 jit_solution(12513548846695965931)
XLA Ops:
  0.6 5.0 %collective-permute-start.1 = (bf16[512,256]{1,0:T(8,128)(2,1)}, bf16[512,256]{1,0:T(8,128)(2,1)S(1)}, u32[]{:S(2)}, u32[]{:S(2)}) collective-permute-start(bf16[512,256]{1,0:T(8,128)(2,1)} %s0), channel_id=1, source_target_pairs={{0,2},{1,3},{2,0},{3,1},{4,6},{5,7},{6,4},{7,5},{8,10},{9,11},{10,... | collective-permute-start | bytes 786440 | tf_op jit(solution)/shard_map/ppermute | solution.py:22
  5.7 3.2 %collective-permute-start = (bf16[512,256]{1,0:T(8,128)(2,1)}, bf16[512,256]{1,0:T(8,128)(2,1)S(1)}, u32[]{:S(2)}, u32[]{:S(2)}) collective-permute-start(bf16[512,256]{1,0:T(8,128)(2,1)} %s0), channel_id=1, source_target_pairs={{0,1},{1,0},{2,3},{3,2},{4,5},{5,4},{6,7},{7,6},{8,9},{9,8},{10,11... | collective-permute-start | bytes 786440 | tf_op jit(solution)/shard_map/ppermute | solution.py:22
  8.9 3.1 %collective-permute-start.3 = (s32[1,64]{1,0:T(1,128)}, s32[1,64]{1,0:T(1,128)S(1)}, u32[]{:S(2)}, u32[]{:S(2)}) collective-permute-start(s32[1,64]{1,0:T(1,128)} %bitcast.21), channel_id=1, source_target_pairs={{0,4},{4,0},{8,12},{12,8},{1,5},{5,1},{9,13},{13,9},{2,6},{6,2},{1... | collective-permute-start | bytes 776 | tf_op jit(solution)/shard_map/ppermute | solution.py:22
  12.1 4.6 %collective-permute-done.1.s2 = bf16[512,256]{1,0:T(8,128)(2,1)S(1)} collective-permute-done((bf16[512,256]{1,0:T(8,128)(2,1)}, bf16[512,256]{1,0:T(8,128)(2,1)S(1)}, u32[]{:S(2)}, u32[]{:S(2)}) %collective-permute-start.1) | collective-permute-done | bytes 262176 | tf_op jit(solution)/shard_map/ppermute | solution.py:22
  16.8 4.0 %collective-permute-start.2 = (bf16[512,256]{1,0:T(8,128)(2,1)S(1)}, bf16[512,256]{1,0:T(8,128)(2,1)S(1)}, u32[]{:S(2)}, u32[]{:S(2)}) collective-permute-start(bf16[512,256]{1,0:T(8,128)(2,1)S(1)} %collective-permute-done.1.s2), channel_id=1, source_target_pairs={{0,1},{1,0},{2,3},{3,2},{4,5},{5,4},{6,7},{7,6},{8,9},{9,8},{10,11... | collective-permute-start | bytes 786440 | tf_op jit(solution)/shard_map/ppermute | solution.py:22
  20.8 1.0 compare_reduce_fusion
  22.5 4.3 %collective-permute-start.4 = (s32[2,64]{1,0:T(2,128)S(1)}, s32[2,64]{1,0:T(2,128)S(1)}, u32[]{:S(2)}, u32[]{:S(2)}) collective-permute-start(s32[2,64]{1,0:T(2,128)S(1)} %pad_add_fusion.1), channel_id=1, source_target_pairs={{0,12},{4,8},{8,4},{12,0},{1,13},{5,9},{9,5},{13,1},{2,14},{6,10},... | collective-permute-start | bytes 1544 | tf_op jit(solution)/shard_map/ppermute | solution.py:22
  28.1 2.5 %convolution_convert_fusion.2.refs_1_ = bf16[256,2048]{1,0:T(8,128)(2,1)S(1)} fusion(bf16[512,2048]{1,0:T(8,128)(2,1)} %cot_ref.1, bf16[512,256]{1,0:T(8,128)(2,1)S(1)} %collective-permute-done.1.s2, bf16[512,256]{1,0:T(8,128)(2,1)S(1)} %collective-permute-done.2.s3, bf16[512,256]{1,0:T(8,128)(2,1)} %s0, bf16[512,256]{1,0:T(8,128)(2,1)S(1)} %collective-permute-done.s1, ...), kind=kOutput, calls=%fused_computation.2 | convolution fusion | flops 537788416 | bytes 4194307 | tf_op jit(solution)/shard_map/dot_general | solution.py:322
  30.6 1.5 %shard_map.76 = bf16[64,4096]{1,0:T(8,128)(2,1)S(1)} custom-call(s32[2,64]{1,0:T(2,128)S(1)} %collective-permute-done.4.refs_0_.refs_1_, bf16[256,2048]{1,0:T(8,128)(2,1)S(1)} %convolution_convert_fusion.2.refs_1_), custom_call_target="tpu_custom_call" | custom-call | flops 1048576 | bytes 1048576 | tf_op jit(solution)/shard_map/pallas_call | solution.py:125
  32.2 3.6 %collective-permute-start.6 = (bf16[64,4096]{1,0:T(8,128)(2,1)S(1)}, bf16[64,4096]{1,0:T(8,128)(2,1)S(1)}, u32[]{:S(2)}, u32[]{:S(2)}) collective-permute-start(bf16[64,4096]{1,0:T(8,128)(2,1)S(1)} %shard_map.76), channel_id=1, source_target_pairs={{0,8},{4,12},{8,0},{12,4},{1,9},{5,13},{9,1},{13,5},{2,10},{6,14},... | collective-permute-start | bytes 1572872 | tf_op jit(solution)/shard_map/ppermute | solution.py:22
  37.4 2.5 %shard_map.77 = (bf16[64,4096]{1,0:T(8,128)(2,1)S(1)}, bf16[64,4096]{1,0:T(8,128)(2,1)S(1)}) custom-call(s32[1,64]{1,0:T(1,128)S(1)} %collective-permute-done.3.refs_0_, s32[2,64]{1,0:T(2,128)S(1)} %collective-permute-done.4.refs_0_.refs_1_, bf16[256,2048]{1,0:T(8,128)(2,1)S(1)} %convolution_convert_fusion.1.refs_2_, ...), custom_call_target="tpu_custom_call" | custom-call | flops 1048576 | bytes 1048576 | tf_op jit(solution)/shard_map/pallas_call | solution.py:125
  39.9 3.0 %collective-permute-start.7 = (bf16[64,4096]{1,0:T(8,128)(2,1)S(1)}, bf16[64,4096]{1,0:T(8,128)(2,1)S(1)}, u32[]{:S(2)}, u32[]{:S(2)}) collective-permute-start(bf16[64,4096]{1,0:T(8,128)(2,1)S(1)} %get-tuple-element.53), channel_id=1, source_target_pairs={{0,12},{4,8},{8,4},{12,0},{1,13},{5,9},{9,5},{13,1},{2,14},{6,10},... | collective-permute-start | bytes 1572872 | tf_op jit(solution)/shard_map/ppermute | solution.py:22
  42.9 2.1 %collective-permute-start.5 = (bf16[64,4096]{1,0:T(8,128)(2,1)S(1)}, bf16[64,4096]{1,0:T(8,128)(2,1)S(1)}, u32[]{:S(2)}, u32[]{:S(2)}) collective-permute-start(bf16[64,4096]{1,0:T(8,128)(2,1)S(1)} %get-tuple-element.51), channel_id=1, source_target_pairs={{0,4},{4,0},{8,12},{12,8},{1,5},{5,1},{9,13},{13,9},{2,6},{6,2},{1... | collective-permute-start | bytes 1572872 | tf_op jit(solution)/shard_map/ppermute | solution.py:22
  45.0 7.3 %collective-permute-start.8 = (f32[64,256]{1,0:T(8,128)S(1)}, f32[64,256]{1,0:T(8,128)S(1)}, u32[]{:S(2)}, u32[]{:S(2)}) collective-permute-start(f32[64,256]{1,0:T(8,128)S(1)} %reshape.121), channel_id=1, source_target_pairs={{0,32},{32,0},{1,33},{33,1},{2,34},{34,2},{3,35},{35,3},{4,36},{36... | collective-permute-start | bytes 196616 | tf_op jit(solution)/shard_map/ppermute | solution.py:22
  52.8 6.8 %shard_map.78 = (bf16[2,64,4096]{2,1,0:T(8,128)(2,1)}, bf16[64,4096]{1,0:T(8,128)(2,1)S(1)}, bf16[256,2048]{1,0:T(8,128)(2,1)S(1)}) custom-call(s32[4,64]{1,0:T(4,128)S(1)} %select_reduce_fusion.1.list_ref, s32[1]{0:T(128)} %bitcast.6.at_ref, bf16[512,256]{1,0:T(8,128)(2,1)S(1)} %copy-done.1, bf16[512,256]{1,0:T(8,128)(2,1)S(1)} %collective-permute-done.s1, ...), custom_call_target="tpu_custom_call" | custom-call | flops 1048576 | bytes 1048576 | tf_op jit(solution)/shard_map/pallas_call | solution.py:108
  59.6 1.1 collective-permute-done.7.got_3
  60.7 2.0 %shard_map.79 = (f32[8,64,512]{2,1,0:T(8,128)S(1)}, bf16[8,64,512]{2,1,0:T(8,128)(2,1)S(1)}) custom-call(s32[1,64]{1,0:T(1,128)S(1)} %bitcast.25, s32[1]{0:T(128)} %bitcast.1.c_ref, f32[4,1,2048]{2,1,0:T(1,128)S(1)} %reshape.124.mask_ref, bf16[256,2048]{1,0:T(8,128)(2,1)S(1)} %bitcast.19, bf16[256,2048]{1,0:T(8,128)(2,1)S(1)} %get-tuple-element.62.own_ref, ...), custom_call_target="tpu_custom_call" | custom-call | flops 4194304 | bytes 4194304 | tf_op jit(solution)/shard_map/pallas_call | solution.py:220
  62.7 3.2 %collective-permute-start.9 = (bf16[8,64,512]{2,1,0:T(8,128)(2,1)S(1)}, bf16[8,64,512]{2,1,0:T(8,128)(2,1)S(1)}, u32[]{:S(2)}, u32[]{:S(2)}) collective-permute-start(bf16[8,64,512]{2,1,0:T(8,128)(2,1)S(1)} %get-tuple-element.67), channel_id=1, source_target_pairs={{0,16},{16,0},{1,17},{17,1},{2,18},{18,2},{3,19},{19,3},{4,20},{20... | collective-permute-start | bytes 1572872 | tf_op jit(solution)/shard_map/ppermute | solution.py:22
  65.9 1.5 %collective-permute-done.9 = bf16[8,64,512]{2,1,0:T(8,128)(2,1)S(1)} collective-permute-done((bf16[8,64,512]{2,1,0:T(8,128)(2,1)S(1)}, bf16[8,64,512]{2,1,0:T(8,128)(2,1)S(1)}, u32[]{:S(2)}, u32[]{:S(2)}) %collective-permute-start.9) | collective-permute-done | bytes 524320 | tf_op jit(solution)/shard_map/ppermute | solution.py:22
  67.4 1.0 add_convert_fusion
  68.4 3.6 %collective-permute-start.10 = (bf16[2,64,4096]{2,1,0:T(8,128)(2,1)}, bf16[2,64,4096]{2,1,0:T(8,128)(2,1)}, u32[]{:S(2)}, u32[]{:S(2)}) collective-permute-start(bf16[2,64,4096]{2,1,0:T(8,128)(2,1)} %get-tuple-element.69), channel_id=1, source_target_pairs={{0,4},{4,0},{8,12},{12,8},{1,5},{5,1},{9,13},{13,9},{2,6},{6,2},{1... | collective-permute-start | bytes 3145736 | tf_op jit(solution)/shard_map/ppermute | solution.py:22
  72.1 10.1 %all-to-all-start = ((bf16[8,64,512]{2,1,0:T(8,128)(2,1)}), bf16[8,64,512]{2,1,0:T(8,128)(2,1)S(1)}, u32[]{:S(2)}, u32[]{:S(2)}) async-start(bf16[8,64,512]{2,1,0:T(8,128)(2,1)} %add_convert_fusion), calls=%async_computation | async-start | bytes 1048576 | tf_op jit(solution)/shard_map/all_to_all | solution.py:349
  83.1 17.0 %all-to-all-done = bf16[8,64,512]{2,1,0:T(8,128)(2,1)S(1)} async-done(((bf16[8,64,512]{2,1,0:T(8,128)(2,1)}), bf16[8,64,512]{2,1,0:T(8,128)(2,1)S(1)}, u32[]{:S(2)}, u32[]{:S(2)}) %all-to-all-start) | async-done | bytes 524320 | tf_op jit(solution)/shard_map/all_to_all | solution.py:349
  100.2 5.3 %collective-permute-start.11 = (bf16[64,512]{1,0:T(8,128)(2,1)S(1)}, bf16[64,512]{1,0:T(8,128)(2,1)S(1)}, u32[]{:S(2)}, u32[]{:S(2)}) collective-permute-start(bf16[64,512]{1,0:T(8,128)(2,1)S(1)} %reduce_sum.32.mine_ref), channel_id=1, source_target_pairs={{0,32},{32,0},{1,33},{33,1},{2,34},{34,2},{3,35},{35,3},{4,36},{36... | collective-permute-start | bytes 196616 | tf_op jit(solution)/shard_map/ppermute | solution.py:22
  105.5 2.0 %fusion = bf16[64,4096]{1,0:T(8,128)(2,1)} fusion(bf16[64,4096]{1,0:T(8,128)(2,1)S(1)} %get-tuple-element.71, bf16[2,64,4096]{2,1,0:T(8,128)(2,1)} %collective-permute-done.10.got), kind=kLoop, calls=%fused_computation.5 | loop fusion | flops 1048576 | bytes 1572864 | tf_op jit(solution)/shard_map/convert_element_type | solution.py:294
  107.4 3.5 %collective-permute-done.11.peer_ref = bf16[64,512]{1,0:T(8,128)(2,1)S(1)} collective-permute-done((bf16[64,512]{1,0:T(8,128)(2,1)S(1)}, bf16[64,512]{1,0:T(8,128)(2,1)S(1)}, u32[]{:S(2)}, u32[]{:S(2)}) %collective-permute-start.11) | collective-permute-done | bytes 65568 | tf_op jit(solution)/shard_map/ppermute | solution.py:22
  111.8 3.5 %all-to-all-start.1 = ((bf16[8,64,512]{2,1,0:T(8,128)(2,1)}), bf16[8,64,512]{2,1,0:T(8,128)(2,1)S(1)}, u32[]{:S(2)}, u32[]{:S(2)}) async-start(bf16[8,64,512]{2,1,0:T(8,128)(2,1)} %get-tuple-element.75), calls=%async_computation.1 | async-start | bytes 1048576 | tf_op jit(solution)/shard_map/all_to_all | solution.py:358
  115.3 3.0 %collective-permute-start.12 = (bf16[64,4096]{1,0:T(8,128)(2,1)}, bf16[64,4096]{1,0:T(8,128)(2,1)S(1)}, u32[]{:S(2)}, u32[]{:S(2)}) collective-permute-start(bf16[64,4096]{1,0:T(8,128)(2,1)} %fusion), channel_id=1, source_target_pairs={{0,12},{4,8},{8,4},{12,0},{1,13},{5,9},{9,5},{13,1},{2,14},{6,10},... | collective-permute-start | bytes 1572872 | tf_op jit(solution)/shard_map/ppermute | solution.py:22
  118.4 14.8 %all-to-all-done.1.near_ref = bf16[8,64,512]{2,1,0:T(8,128)(2,1)S(1)} async-done(((bf16[8,64,512]{2,1,0:T(8,128)(2,1)}), bf16[8,64,512]{2,1,0:T(8,128)(2,1)S(1)}, u32[]{:S(2)}, u32[]{:S(2)}) %all-to-all-start.1) | async-done | bytes 524320 | tf_op jit(solution)/shard_map/all_to_all | solution.py:358
  133.2 2.4 %collective-permute-start.13 = (bf16[8,64,512]{2,1,0:T(8,128)(2,1)S(1)}, bf16[8,64,512]{2,1,0:T(8,128)(2,1)S(1)}, u32[]{:S(2)}, u32[]{:S(2)}) collective-permute-start(bf16[8,64,512]{2,1,0:T(8,128)(2,1)S(1)} %all-to-all-done.1.near_ref), channel_id=1, source_target_pairs={{0,16},{16,0},{1,17},{17,1},{2,18},{18,2},{3,19},{19,3},{4,20},{20... | collective-permute-start | bytes 1572872 | tf_op jit(solution)/shard_map/ppermute | solution.py:22
  135.6 1.5 %collective-permute-done.13.far_ref = bf16[8,64,512]{2,1,0:T(8,128)(2,1)S(1)} collective-permute-done((bf16[8,64,512]{2,1,0:T(8,128)(2,1)S(1)}, bf16[8,64,512]{2,1,0:T(8,128)(2,1)S(1)}, u32[]{:S(2)}, u32[]{:S(2)}) %collective-permute-start.13) | collective-permute-done | bytes 524320 | tf_op jit(solution)/shard_map/ppermute | solution.py:22
  137.1 4.1 %shard_map.81 = (bf16[256,2048]{1,0:T(8,128)(2,1)}, bf16[256,2048]{1,0:T(8,128)(2,1)}) custom-call(s32[4,64]{1,0:T(4,128)S(1)} %select_reduce_fusion.1.list_ref, s32[1]{0:T(128)} %bitcast.1.c_ref, f32[4,1,2048]{2,1,0:T(1,128)S(1)} %reshape.124.mask_ref, bf16[256,2048]{1,0:T(8,128)(2,1)S(1)} %bitcast.20, bf16[256,2048]{1,0:T(8,128)(2,1)S(1)} %get-tuple-element.62.own_ref, ...), custom_call_target="tpu_custom_call" | custom-call | flops 4194304 | bytes 4194304 | tf_op jit(solution)/shard_map/pallas_call | solution.py:220
  (38 shorter events, 5.9 us)
Async XLA Ops:
  0.6 16.1 %collective-permute-start.1 = (bf16[512,256]{1,0:T(8,128)(2,1)}, bf16[512,256]{1,0:T(8,128)(2,1)S(1)}, u32[]{:S(2)}, u32[]{:S(2)}) collective-permute-start(bf16[512,256]{1,0:T(8,128)(2,1)} %s0), channel_id=1, source_target_pairs={{0,2},{1,3},{2,0},{3,1},{4,6},{5,7},{6,4},{7,5},{8,10},{9,11},{10,... | collective-permute-start | bytes 786440 | tf_op jit(solution)/shard_map/ppermute | solution.py:22
  5.7 22.4 %collective-permute-start = (bf16[512,256]{1,0:T(8,128)(2,1)}, bf16[512,256]{1,0:T(8,128)(2,1)S(1)}, u32[]{:S(2)}, u32[]{:S(2)}) collective-permute-start(bf16[512,256]{1,0:T(8,128)(2,1)} %s0), channel_id=1, source_target_pairs={{0,1},{1,0},{2,3},{3,2},{4,5},{5,4},{6,7},{7,6},{8,9},{9,8},{10,11... | collective-permute-start | bytes 786440 | tf_op jit(solution)/shard_map/ppermute | solution.py:22
  8.9 13.0 %collective-permute-start.3 = (s32[1,64]{1,0:T(1,128)}, s32[1,64]{1,0:T(1,128)S(1)}, u32[]{:S(2)}, u32[]{:S(2)}) collective-permute-start(s32[1,64]{1,0:T(1,128)} %bitcast.21), channel_id=1, source_target_pairs={{0,4},{4,0},{8,12},{12,8},{1,5},{5,1},{9,13},{13,9},{2,6},{6,2},{1... | collective-permute-start | bytes 776 | tf_op jit(solution)/shard_map/ppermute | solution.py:22
  16.8 11.3 %collective-permute-start.2 = (bf16[512,256]{1,0:T(8,128)(2,1)S(1)}, bf16[512,256]{1,0:T(8,128)(2,1)S(1)}, u32[]{:S(2)}, u32[]{:S(2)}) collective-permute-start(bf16[512,256]{1,0:T(8,128)(2,1)S(1)} %collective-permute-done.1.s2), channel_id=1, source_target_pairs={{0,1},{1,0},{2,3},{3,2},{4,5},{5,4},{6,7},{7,6},{8,9},{9,8},{10,11... | collective-permute-start | bytes 786440 | tf_op jit(solution)/shard_map/ppermute | solution.py:22
  22.5 5.5 %collective-permute-start.4 = (s32[2,64]{1,0:T(2,128)S(1)}, s32[2,64]{1,0:T(2,128)S(1)}, u32[]{:S(2)}, u32[]{:S(2)}) collective-permute-start(s32[2,64]{1,0:T(2,128)S(1)} %pad_add_fusion.1), channel_id=1, source_target_pairs={{0,12},{4,8},{8,4},{12,0},{1,13},{5,9},{9,5},{13,1},{2,14},{6,10},... | collective-permute-start | bytes 1544 | tf_op jit(solution)/shard_map/ppermute | solution.py:22
  28.1 7.7 %copy-start = (bf16[512,2048]{1,0:T(8,128)(2,1)S(1)}, bf16[512,2048]{1,0:T(8,128)(2,1)}, u32[]{:S(2)}) copy-start(bf16[512,2048]{1,0:T(8,128)(2,1)} %cot_ref.1) | copy-start | bytes 6291460
  28.1 7.7 %copy-start.1 = (bf16[512,256]{1,0:T(8,128)(2,1)S(1)}, bf16[512,256]{1,0:T(8,128)(2,1)}, u32[]{:S(2)}) copy-start(bf16[512,256]{1,0:T(8,128)(2,1)} %s0) | copy-start | bytes 786436
  32.2 28.5 %collective-permute-start.6 = (bf16[64,4096]{1,0:T(8,128)(2,1)S(1)}, bf16[64,4096]{1,0:T(8,128)(2,1)S(1)}, u32[]{:S(2)}, u32[]{:S(2)}) collective-permute-start(bf16[64,4096]{1,0:T(8,128)(2,1)S(1)} %shard_map.76), channel_id=1, source_target_pairs={{0,8},{4,12},{8,0},{12,4},{1,9},{5,13},{9,1},{13,5},{2,10},{6,14},... | collective-permute-start | bytes 1572872 | tf_op jit(solution)/shard_map/ppermute | solution.py:22
  37.3 15.0 %copy-start.3 = (s32[1,1,1,64]{3,2,1,0:T(1,128)S(1)}, s32[1,1,1,64]{3,2,1,0:T(1,128)}, u32[]{:S(2)}) copy-start(s32[1,1,1,64]{3,2,1,0:T(1,128)} %param.8) | copy-start | bytes 772
  39.9 20.8 %copy-start.2 = (bf16[1,256,2048]{2,1,0:T(8,128)(2,1)S(1)}, bf16[1,256,2048]{2,1,0:T(8,128)(2,1)}, u32[]{:S(2)}) copy-start(bf16[1,256,2048]{2,1,0:T(8,128)(2,1)} %param.7) | copy-start | bytes 3145732
  39.9 20.7 %collective-permute-start.7 = (bf16[64,4096]{1,0:T(8,128)(2,1)S(1)}, bf16[64,4096]{1,0:T(8,128)(2,1)S(1)}, u32[]{:S(2)}, u32[]{:S(2)}) collective-permute-start(bf16[64,4096]{1,0:T(8,128)(2,1)S(1)} %get-tuple-element.53), channel_id=1, source_target_pairs={{0,12},{4,8},{8,4},{12,0},{1,13},{5,9},{9,5},{13,1},{2,14},{6,10},... | collective-permute-start | bytes 1572872 | tf_op jit(solution)/shard_map/ppermute | solution.py:22
  42.9 17.8 %collective-permute-start.5 = (bf16[64,4096]{1,0:T(8,128)(2,1)S(1)}, bf16[64,4096]{1,0:T(8,128)(2,1)S(1)}, u32[]{:S(2)}, u32[]{:S(2)}) collective-permute-start(bf16[64,4096]{1,0:T(8,128)(2,1)S(1)} %get-tuple-element.51), channel_id=1, source_target_pairs={{0,4},{4,0},{8,12},{12,8},{1,5},{5,1},{9,13},{13,9},{2,6},{6,2},{1... | collective-permute-start | bytes 1572872 | tf_op jit(solution)/shard_map/ppermute | solution.py:22
  45.0 14.5 %collective-permute-start.8 = (f32[64,256]{1,0:T(8,128)S(1)}, f32[64,256]{1,0:T(8,128)S(1)}, u32[]{:S(2)}, u32[]{:S(2)}) collective-permute-start(f32[64,256]{1,0:T(8,128)S(1)} %reshape.121), channel_id=1, source_target_pairs={{0,32},{32,0},{1,33},{33,1},{2,34},{34,2},{3,35},{35,3},{4,36},{36... | collective-permute-start | bytes 196616 | tf_op jit(solution)/shard_map/ppermute | solution.py:22
  59.5 8.9 %copy-start.4 = (f32[64,256]{1,0:T(8,128)}, f32[64,256]{1,0:T(8,128)S(1)}, u32[]{:S(2)}) copy-start(f32[64,256]{1,0:T(8,128)S(1)} %collective-permute-done.8) | copy-start | bytes 196612
  62.7 4.7 %collective-permute-start.9 = (bf16[8,64,512]{2,1,0:T(8,128)(2,1)S(1)}, bf16[8,64,512]{2,1,0:T(8,128)(2,1)S(1)}, u32[]{:S(2)}, u32[]{:S(2)}) collective-permute-start(bf16[8,64,512]{2,1,0:T(8,128)(2,1)S(1)} %get-tuple-element.67), channel_id=1, source_target_pairs={{0,16},{16,0},{1,17},{17,1},{2,18},{18,2},{3,19},{19,3},{4,20},{20... | collective-permute-start | bytes 1572872 | tf_op jit(solution)/shard_map/ppermute | solution.py:22
  68.4 37.0 %collective-permute-start.10 = (bf16[2,64,4096]{2,1,0:T(8,128)(2,1)}, bf16[2,64,4096]{2,1,0:T(8,128)(2,1)}, u32[]{:S(2)}, u32[]{:S(2)}) collective-permute-start(bf16[2,64,4096]{2,1,0:T(8,128)(2,1)} %get-tuple-element.69), channel_id=1, source_target_pairs={{0,4},{4,0},{8,12},{12,8},{1,5},{5,1},{9,13},{13,9},{2,6},{6,2},{1... | collective-permute-start | bytes 3145736 | tf_op jit(solution)/shard_map/ppermute | solution.py:22
  72.1 28.0 %all-to-all-start = ((bf16[8,64,512]{2,1,0:T(8,128)(2,1)}), bf16[8,64,512]{2,1,0:T(8,128)(2,1)S(1)}, u32[]{:S(2)}, u32[]{:S(2)}) async-start(bf16[8,64,512]{2,1,0:T(8,128)(2,1)} %add_convert_fusion), calls=%async_computation | async-start | bytes 1048576 | tf_op jit(solution)/shard_map/all_to_all | solution.py:349
  100.2 10.8 %collective-permute-start.11 = (bf16[64,512]{1,0:T(8,128)(2,1)S(1)}, bf16[64,512]{1,0:T(8,128)(2,1)S(1)}, u32[]{:S(2)}, u32[]{:S(2)}) collective-permute-start(bf16[64,512]{1,0:T(8,128)(2,1)S(1)} %reduce_sum.32.mine_ref), channel_id=1, source_target_pairs={{0,32},{32,0},{1,33},{33,1},{2,34},{34,2},{3,35},{35,3},{4,36},{36... | collective-permute-start | bytes 196616 | tf_op jit(solution)/shard_map/ppermute | solution.py:22
  111.8 21.4 %all-to-all-start.1 = ((bf16[8,64,512]{2,1,0:T(8,128)(2,1)}), bf16[8,64,512]{2,1,0:T(8,128)(2,1)S(1)}, u32[]{:S(2)}, u32[]{:S(2)}) async-start(bf16[8,64,512]{2,1,0:T(8,128)(2,1)} %get-tuple-element.75), calls=%async_computation.1 | async-start | bytes 1048576 | tf_op jit(solution)/shard_map/all_to_all | solution.py:358
  115.3 20.3 %collective-permute-start.12 = (bf16[64,4096]{1,0:T(8,128)(2,1)}, bf16[64,4096]{1,0:T(8,128)(2,1)S(1)}, u32[]{:S(2)}, u32[]{:S(2)}) collective-permute-start(bf16[64,4096]{1,0:T(8,128)(2,1)} %fusion), channel_id=1, source_target_pairs={{0,12},{4,8},{8,4},{12,0},{1,13},{5,9},{9,5},{13,1},{2,14},{6,10},... | collective-permute-start | bytes 1572872 | tf_op jit(solution)/shard_map/ppermute | solution.py:22
  133.2 3.9 %collective-permute-start.13 = (bf16[8,64,512]{2,1,0:T(8,128)(2,1)S(1)}, bf16[8,64,512]{2,1,0:T(8,128)(2,1)S(1)}, u32[]{:S(2)}, u32[]{:S(2)}) collective-permute-start(bf16[8,64,512]{2,1,0:T(8,128)(2,1)S(1)} %all-to-all-done.1.near_ref), channel_id=1, source_target_pairs={{0,16},{16,0},{1,17},{17,1},{2,18},{18,2},{3,19},{19,3},{4,20},{20... | collective-permute-start | bytes 1572872 | tf_op jit(solution)/shard_map/ppermute | solution.py:22

commit v12 on v11

--- a/solution.py
+++ b/solution.py
@@ -90,15 +90,12 @@
 
 
 def rest_kernel(
-    list_ref, at_ref, s0, s1, s2, s3, cot_ref, give_ref, keep_ref, own_ref, left_ref, part_ref
+    list_ref, at_ref, s0, s1, s2, s3, cot_ref, give_1, give_2, keep_ref, own_ref, left_ref, part_ref
 ):
-    shards = (s0, s1, s2, s3)
-    for lead, k in enumerate((1, 2)):
-        product(at_ref, k, shards, cot_ref, left_ref, part_ref)
-        pack(list_ref, k, 0, HALF, part_ref, give_ref, lead)
-    product(at_ref, 3, shards, cot_ref, left_ref, part_ref)
-    pack(list_ref, 3, 0, HALF, part_ref, keep_ref)
-    product(at_ref, 0, shards, cot_ref, left_ref, own_ref)
+    for k, out_ref in ((1, give_1), (2, give_2), (3, keep_ref)):
+        product(at_ref, k, (s0, s1, s2, s3), cot_ref, left_ref, part_ref)
+        pack(list_ref, k, 0, HALF, part_ref, out_ref)
+    product(at_ref, 0, (s0, s1, s2, s3), cot_ref, left_ref, own_ref)
 
 
 def products_call(body, lists, at, shards, cotangent, out_shape):
@@ -134,7 +131,7 @@
 
 def rest_parts(lists, at, shards, cotangent):
     own = jax.ShapeDtypeStruct((shards[0].shape[1], cotangent.shape[1]), BF16)
-    shapes = [packed(2), packed(), own]
+    shapes = [packed(), packed(), packed(), own]
     return products_call(rest_kernel, lists, at, shards, cotangent, shapes)
 
 
@@ -191,7 +188,7 @@
 
     @pl.when(row == 0)
     def _():
-        terms = [lambda at: got[0, :, at], lambda at: nxt[:, at]]
+        terms = [lambda at: got[:, at], lambda at: nxt[:, at]]
         unpack(list_ref, 0, HALF, terms, grad_ref)
 
     rows = pl.ds(pl.multiple_of(row * BLK, BLK), BLK)
@@ -339,22 +336,22 @@
     others = jnp.concatenate([picks, near_picks, far_picks[1:], far_picks[:1]])
     others = others_of(others, rows_blk * cols_blk)
     rest = rest_parts(others, at, shards, cotangent)
-    got_1, got_2, got_3, far_moment, give, keep, own = lax.optimization_barrier(
+    got_1, got_2, got_3, far_moment, give_1, give_2, keep, own = lax.optimization_barrier(
         (got_1, got_2, got_3, far_moment, *rest)
     )
     mine, other = chosen_sums(picks, at_c, mask, feedback[0], own, got_1, got_2, got_3)
     pair = (mine + swap(other, "c", 1, 2).astype(F32)).astype(BF16)
-    pair, give = lax.optimization_barrier((pair, give))
-    got_rest = swap(give, "dp", 1, 4)
+    pair, give_1, give_2 = lax.optimization_barrier((pair, give_1, give_2))
+    via = swap(give_2, "dp", 1, 4)
     across = lax.all_to_all(pair, "z", 0, 0, tiled=True)
     near = jnp.sum(across.astype(F32), axis=0).astype(BF16)
     far = swap(near, "yh", 1, 2)
-    far, give_rest = lax.optimization_barrier((far, plus(keep, got_rest[1])))
+    far, give_3 = lax.optimization_barrier((far, plus(keep, via)))
     moment = jnp.where(
         yh == 0, jnp.concatenate([moment, far_moment], 1), jnp.concatenate([far_moment, moment], 1)
     )
     momentum_new, copies = owner_update(at_yh, near, far, moment)
-    next_rest = swap(give_rest, "dp", 3, 4)
+    got_rest, next_rest = swap(give_1, "dp", 1, 4), swap(give_3, "dp", 3, 4)
     every = lax.all_to_all(copies, "z", 0, 0, tiled=True)
     feedback_new, step = finish(
         others, at_c, mask, feedback[0], own, got_rest, next_rest, every, swap(every, "c", 1, 2)

time: 142 us -> 139 us (0.979); the launches traced: 141 us -> 137 us
  waiting for transfers between devices: 44.1 us -> 30.7 us
  starting transfers between devices: 66.8 us -> 75.8 us
    ppermute x14 -> x15, starting transfers between devices: 53.2 us -> 62.2 us  [swap(): return lax.ppermute(value, axis, [(i, i ^ flip) for i in range(size)])]
    all_to_all x1, waiting for transfers between devices: 14.8 us -> 6.59 us  [local(): every = lax.all_to_all(copies, 'z', 0, 0, tiled=True)]
    all_to_all x1, waiting for transfers between devices: 17 us -> 14.4 us  [local(): across = lax.all_to_all(pair, 'z', 0, 0, tiled=True)]
    ppermute x14 -> x15, waiting for transfers between devices: 12.3 us -> 9.71 us  [swap(): return lax.ppermute(value, axis, [(i, i ^ flip) for i in range(size)])]
  transfers between devices with their start and end apart: 16 -> 17, of which waited for: 7 -> 7; matrix products, arithmetic and copies ran while one was open for 6% -> 6% of each run, Pallas kernels for 7% -> 7%
where the time goes in v12:
time: 139 us; the launch traced here: 137 us
  starting transfers between devices  75.8 us (55%)
  waiting for transfers between devices  30.7 us (22%)
  Pallas kernels  17.5 us (13%)
  other arithmetic  6.32 us (5%)
  matrix products  4.04 us (3%)
    ppermute x15, starting transfers between devices, swap(): return lax.ppermute(value, axis, [(i, i ^ flip) for i in range(size)])  62.2 us
    all_to_all x1, waiting for transfers between devices, local(): across = lax.all_to_all(pair, 'z', 0, 0, tiled=True)  14.4 us
    all_to_all x1, starting transfers between devices, local(): across = lax.all_to_all(pair, 'z', 0, 0, tiled=True)  10.1 us
    ppermute x15, waiting for transfers between devices, swap(): return lax.ppermute(value, axis, [(i, i ^ flip) for i in range(size)])  9.71 us
    all_to_all x1, waiting for transfers between devices, local(): every = lax.all_to_all(copies, 'z', 0, 0, tiled=True)  6.59 us
    pallas_call x1, Pallas kernels, products_call(): pl.pallas_call(body, in_specs=[SMEM, SMEM] + [whole] * 5, out_specs=jax.t...  6.55 us
    pallas_call x2, Pallas kernels, state_call(): pl.pallas_call(body, grid=(rows // BLK,), in_specs=[SMEM] * len(scalars)...  5.95 us
    pallas_call x2, Pallas kernels, chosen_parts(): kernel_call(functools.partial(first_kernel, rows), (), [SMEM] * n + [whol...  4.08 us
  transfers between devices with their start and end apart: 17, of which 7 were waited for; matrix products, arithmetic and copies ran while one was open for 6% of the time, Pallas kernels for 7%

profile of v12, /device:TPU:1, one launch (start us, length us, event | category | flops | bytes accessed | tf_op | source)
XLA Modules:
  0.0 136.6 jit_solution(6787779394817562178)
XLA Ops:
  0.6 5.0 %collective-permute-start.1 = (bf16[512,256]{1,0:T(8,128)(2,1)}, bf16[512,256]{1,0:T(8,128)(2,1)S(1)}, u32[]{:S(2)}, u32[]{:S(2)}) collective-permute-start(bf16[512,256]{1,0:T(8,128)(2,1)} %s0), channel_id=1, source_target_pairs={{0,2},{1,3},{2,0},{3,1},{4,6},{5,7},{6,4},{7,5},{8,10},{9,11},{10,... | collective-permute-start | bytes 786440 | tf_op jit(solution)/shard_map/ppermute | solution.py:22
  5.7 3.2 %collective-permute-start = (bf16[512,256]{1,0:T(8,128)(2,1)}, bf16[512,256]{1,0:T(8,128)(2,1)S(1)}, u32[]{:S(2)}, u32[]{:S(2)}) collective-permute-start(bf16[512,256]{1,0:T(8,128)(2,1)} %s0), channel_id=1, source_target_pairs={{0,1},{1,0},{2,3},{3,2},{4,5},{5,4},{6,7},{7,6},{8,9},{9,8},{10,11... | collective-permute-start | bytes 786440 | tf_op jit(solution)/shard_map/ppermute | solution.py:22
  8.9 3.1 %collective-permute-start.3 = (s32[1,64]{1,0:T(1,128)}, s32[1,64]{1,0:T(1,128)S(1)}, u32[]{:S(2)}, u32[]{:S(2)}) collective-permute-start(s32[1,64]{1,0:T(1,128)} %bitcast.16), channel_id=1, source_target_pairs={{0,4},{4,0},{8,12},{12,8},{1,5},{5,1},{9,13},{13,9},{2,6},{6,2},{1... | collective-permute-start | bytes 776 | tf_op jit(solution)/shard_map/ppermute | solution.py:22
  12.1 4.6 %collective-permute-done.1.s2 = bf16[512,256]{1,0:T(8,128)(2,1)S(1)} collective-permute-done((bf16[512,256]{1,0:T(8,128)(2,1)}, bf16[512,256]{1,0:T(8,128)(2,1)S(1)}, u32[]{:S(2)}, u32[]{:S(2)}) %collective-permute-start.1) | collective-permute-done | bytes 262176 | tf_op jit(solution)/shard_map/ppermute | solution.py:22
  16.8 4.0 %collective-permute-start.2 = (bf16[512,256]{1,0:T(8,128)(2,1)S(1)}, bf16[512,256]{1,0:T(8,128)(2,1)S(1)}, u32[]{:S(2)}, u32[]{:S(2)}) collective-permute-start(bf16[512,256]{1,0:T(8,128)(2,1)S(1)} %collective-permute-done.1.s2), channel_id=1, source_target_pairs={{0,1},{1,0},{2,3},{3,2},{4,5},{5,4},{6,7},{7,6},{8,9},{9,8},{10,11... | collective-permute-start | bytes 786440 | tf_op jit(solution)/shard_map/ppermute | solution.py:22
  22.5 4.3 %collective-permute-start.4 = (s32[2,64]{1,0:T(2,128)S(1)}, s32[2,64]{1,0:T(2,128)S(1)}, u32[]{:S(2)}, u32[]{:S(2)}) collective-permute-start(s32[2,64]{1,0:T(2,128)S(1)} %pad_add_fusion.1), channel_id=1, source_target_pairs={{0,12},{4,8},{8,4},{12,0},{1,13},{5,9},{9,5},{13,1},{2,14},{6,10},... | collective-permute-start | bytes 1544 | tf_op jit(solution)/shard_map/ppermute | solution.py:22
  28.1 2.5 %convolution_convert_fusion.2.refs_1_ = bf16[256,2048]{1,0:T(8,128)(2,1)S(1)} fusion(bf16[512,2048]{1,0:T(8,128)(2,1)} %cot_ref.1, bf16[512,256]{1,0:T(8,128)(2,1)S(1)} %collective-permute-done.1.s2, bf16[512,256]{1,0:T(8,128)(2,1)S(1)} %collective-permute-done.2.s3, bf16[512,256]{1,0:T(8,128)(2,1)} %s0, bf16[512,256]{1,0:T(8,128)(2,1)S(1)} %collective-permute-done.s1, ...), kind=kOutput, calls=%fused_computation.2 | convolution fusion | flops 537788416 | bytes 4194307 | tf_op jit(solution)/shard_map/dot_general | solution.py:319
  30.6 1.5 %shard_map.76 = bf16[64,4096]{1,0:T(8,128)(2,1)S(1)} custom-call(s32[2,64]{1,0:T(2,128)S(1)} %collective-permute-done.4.refs_0_.refs_1_, bf16[256,2048]{1,0:T(8,128)(2,1)S(1)} %convolution_convert_fusion.2.refs_1_), custom_call_target="tpu_custom_call" | custom-call | flops 1048576 | bytes 1048576 | tf_op jit(solution)/shard_map/pallas_call | solution.py:122
  32.2 3.6 %collective-permute-start.6 = (bf16[64,4096]{1,0:T(8,128)(2,1)S(1)}, bf16[64,4096]{1,0:T(8,128)(2,1)S(1)}, u32[]{:S(2)}, u32[]{:S(2)}) collective-permute-start(bf16[64,4096]{1,0:T(8,128)(2,1)S(1)} %shard_map.76), channel_id=1, source_target_pairs={{0,8},{4,12},{8,0},{12,4},{1,9},{5,13},{9,1},{13,5},{2,10},{6,14},... | collective-permute-start | bytes 1572872 | tf_op jit(solution)/shard_map/ppermute | solution.py:22
  37.4 2.5 %shard_map.77 = (bf16[64,4096]{1,0:T(8,128)(2,1)S(1)}, bf16[64,4096]{1,0:T(8,128)(2,1)S(1)}) custom-call(s32[1,64]{1,0:T(1,128)S(1)} %collective-permute-done.3.refs_0_, s32[2,64]{1,0:T(2,128)S(1)} %collective-permute-done.4.refs_0_.refs_1_, bf16[256,2048]{1,0:T(8,128)(2,1)S(1)} %convolution_convert_fusion.1.refs_2_, ...), custom_call_target="tpu_custom_call" | custom-call | flops 1048576 | bytes 1048576 | tf_op jit(solution)/shard_map/pallas_call | solution.py:122
  39.9 3.0 %collective-permute-start.7 = (bf16[64,4096]{1,0:T(8,128)(2,1)S(1)}, bf16[64,4096]{1,0:T(8,128)(2,1)S(1)}, u32[]{:S(2)}, u32[]{:S(2)}) collective-permute-start(bf16[64,4096]{1,0:T(8,128)(2,1)S(1)} %get-tuple-element.56), channel_id=1, source_target_pairs={{0,12},{4,8},{8,4},{12,0},{1,13},{5,9},{9,5},{13,1},{2,14},{6,10},... | collective-permute-start | bytes 1572872 | tf_op jit(solution)/shard_map/ppermute | solution.py:22
  42.9 2.1 %collective-permute-start.5 = (bf16[64,4096]{1,0:T(8,128)(2,1)S(1)}, bf16[64,4096]{1,0:T(8,128)(2,1)S(1)}, u32[]{:S(2)}, u32[]{:S(2)}) collective-permute-start(bf16[64,4096]{1,0:T(8,128)(2,1)S(1)} %get-tuple-element.54), channel_id=1, source_target_pairs={{0,4},{4,0},{8,12},{12,8},{1,5},{5,1},{9,13},{13,9},{2,6},{6,2},{1... | collective-permute-start | bytes 1572872 | tf_op jit(solution)/shard_map/ppermute | solution.py:22
  45.0 7.3 %collective-permute-start.8 = (f32[64,256]{1,0:T(8,128)S(1)}, f32[64,256]{1,0:T(8,128)S(1)}, u32[]{:S(2)}, u32[]{:S(2)}) collective-permute-start(f32[64,256]{1,0:T(8,128)S(1)} %reshape.119), channel_id=1, source_target_pairs={{0,32},{32,0},{1,33},{33,1},{2,34},{34,2},{3,35},{35,3},{4,36},{36... | collective-permute-start | bytes 196616 | tf_op jit(solution)/shard_map/ppermute | solution.py:22
  52.8 6.6 %shard_map.78 = (bf16[64,4096]{1,0:T(8,128)(2,1)S(1)}, bf16[64,4096]{1,0:T(8,128)(2,1)S(1)}, bf16[64,4096]{1,0:T(8,128)(2,1)S(1)}, bf16[256,2048]{1,0:T(8,128)(2,1)S(1)}) custom-call(s32[4,64]{1,0:T(4,128)S(1)} %select_reduce_fusion.1.list_ref, s32[1]{0:T(128)} %bitcast.6.at_ref, bf16[512,256]{1,0:T(8,128)(2,1)S(1)} %copy-done.1, ...), custom_call_target="tpu_custom_call" | custom-call | flops 1048576 | bytes 1048576 | tf_op jit(solution)/shard_map/pallas_call | solution.py:105
  59.4 1.3 collective-permute-done.7.got_3
  60.7 2.0 %shard_map.79 = (f32[8,64,512]{2,1,0:T(8,128)S(1)}, bf16[8,64,512]{2,1,0:T(8,128)(2,1)S(1)}) custom-call(s32[1,64]{1,0:T(1,128)S(1)} %bitcast.20, s32[1]{0:T(128)} %bitcast.1.c_ref, f32[4,1,2048]{2,1,0:T(1,128)S(1)} %reshape.122.mask_ref, bf16[256,2048]{1,0:T(8,128)(2,1)S(1)} %bitcast.14, bf16[256,2048]{1,0:T(8,128)(2,1)S(1)} %get-tuple-element.66.own_ref, ...), custom_call_target="tpu_custom_call" | custom-call | flops 4194304 | bytes 4194304 | tf_op jit(solution)/shard_map/pallas_call | solution.py:217
  62.7 3.0 %collective-permute-start.9 = (bf16[8,64,512]{2,1,0:T(8,128)(2,1)S(1)}, bf16[8,64,512]{2,1,0:T(8,128)(2,1)S(1)}, u32[]{:S(2)}, u32[]{:S(2)}) collective-permute-start(bf16[8,64,512]{2,1,0:T(8,128)(2,1)S(1)} %get-tuple-element.71), channel_id=1, source_target_pairs={{0,16},{16,0},{1,17},{17,1},{2,18},{18,2},{3,19},{19,3},{4,20},{20... | collective-permute-start | bytes 1572872 | tf_op jit(solution)/shard_map/ppermute | solution.py:22
  65.8 1.5 %collective-permute-done.9 = bf16[8,64,512]{2,1,0:T(8,128)(2,1)S(1)} collective-permute-done((bf16[8,64,512]{2,1,0:T(8,128)(2,1)S(1)}, bf16[8,64,512]{2,1,0:T(8,128)(2,1)S(1)}, u32[]{:S(2)}, u32[]{:S(2)}) %collective-permute-start.9) | collective-permute-done | bytes 524320 | tf_op jit(solution)/shard_map/ppermute | solution.py:22
  67.3 1.0 add_convert_fusion.1
  68.3 10.1 %all-to-all-start = ((bf16[8,64,512]{2,1,0:T(8,128)(2,1)}), bf16[8,64,512]{2,1,0:T(8,128)(2,1)}, u32[]{:S(2)}, u32[]{:S(2)}) async-start(bf16[8,64,512]{2,1,0:T(8,128)(2,1)} %add_convert_fusion.1), calls=%async_computation | async-start | bytes 1048576 | tf_op jit(solution)/shard_map/all_to_all | solution.py:346
  78.4 3.6 %collective-permute-start.12 = (bf16[64,4096]{1,0:T(8,128)(2,1)S(1)}, bf16[64,4096]{1,0:T(8,128)(2,1)}, u32[]{:S(2)}, u32[]{:S(2)}) collective-permute-start(bf16[64,4096]{1,0:T(8,128)(2,1)S(1)} %copy-done.6), channel_id=1, source_target_pairs={{0,4},{4,0},{8,12},{12,8},{1,5},{5,1},{9,13},{13,9},{2,6},{6,2},{1... | collective-permute-start | bytes 1572872 | tf_op jit(solution)/shard_map/ppermute | solution.py:22
  82.1 14.4 %all-to-all-done = bf16[8,64,512]{2,1,0:T(8,128)(2,1)} async-done(((bf16[8,64,512]{2,1,0:T(8,128)(2,1)}), bf16[8,64,512]{2,1,0:T(8,128)(2,1)}, u32[]{:S(2)}, u32[]{:S(2)}) %all-to-all-start) | async-done | bytes 524320 | tf_op jit(solution)/shard_map/all_to_all | solution.py:346
  96.4 1.1 reduce_sum.32.mine_ref
  97.6 6.2 %collective-permute-start.11 = (bf16[64,512]{1,0:T(8,128)(2,1)S(1)}, bf16[64,512]{1,0:T(8,128)(2,1)S(1)}, u32[]{:S(2)}, u32[]{:S(2)}) collective-permute-start(bf16[64,512]{1,0:T(8,128)(2,1)S(1)} %reduce_sum.32.mine_ref), channel_id=1, source_target_pairs={{0,32},{32,0},{1,33},{33,1},{2,34},{34,2},{3,35},{35,3},{4,36},{36... | collective-permute-start | bytes 196616 | tf_op jit(solution)/shard_map/ppermute | solution.py:22
  103.8 2.0 %add_convert_fusion = bf16[64,4096]{1,0:T(8,128)(2,1)} fusion(bf16[64,4096]{1,0:T(8,128)(2,1)} %collective-permute-done.12, bf16[64,4096]{1,0:T(8,128)(2,1)S(1)} %get-tuple-element.76), kind=kLoop, calls=%fused_computation.4 | loop fusion | flops 1048576 | bytes 1572864 | tf_op jit(solution)/shard_map/convert_element_type | solution.py:291
  107.4 3.5 %all-to-all-start.1 = ((bf16[8,64,512]{2,1,0:T(8,128)(2,1)}), bf16[8,64,512]{2,1,0:T(8,128)(2,1)S(1)}, u32[]{:S(2)}, u32[]{:S(2)}) async-start(bf16[8,64,512]{2,1,0:T(8,128)(2,1)} %get-tuple-element.81), calls=%async_computation.1 | async-start | bytes 1048576 | tf_op jit(solution)/shard_map/all_to_all | solution.py:355
  110.9 3.7 %collective-permute-start.10 = (bf16[64,4096]{1,0:T(8,128)(2,1)}, bf16[64,4096]{1,0:T(8,128)(2,1)S(1)}, u32[]{:S(2)}, u32[]{:S(2)}) collective-permute-start(bf16[64,4096]{1,0:T(8,128)(2,1)} %copy-done.4), channel_id=1, source_target_pairs={{0,4},{4,0},{8,12},{12,8},{1,5},{5,1},{9,13},{13,9},{2,6},{6,2},{1... | collective-permute-start | bytes 1572872 | tf_op jit(solution)/shard_map/ppermute | solution.py:22
  114.6 5.7 %collective-permute-start.13 = (bf16[64,4096]{1,0:T(8,128)(2,1)}, bf16[64,4096]{1,0:T(8,128)(2,1)}, u32[]{:S(2)}, u32[]{:S(2)}) collective-permute-start(bf16[64,4096]{1,0:T(8,128)(2,1)} %add_convert_fusion), channel_id=1, source_target_pairs={{0,12},{4,8},{8,4},{12,0},{1,13},{5,9},{9,5},{13,1},{2,14},{6,10},... | collective-permute-start | bytes 1572872 | tf_op jit(solution)/shard_map/ppermute | solution.py:22
  120.3 6.6 %all-to-all-done.1.near_ref = bf16[8,64,512]{2,1,0:T(8,128)(2,1)S(1)} async-done(((bf16[8,64,512]{2,1,0:T(8,128)(2,1)}), bf16[8,64,512]{2,1,0:T(8,128)(2,1)S(1)}, u32[]{:S(2)}, u32[]{:S(2)}) %all-to-all-start.1) | async-done | bytes 524320 | tf_op jit(solution)/shard_map/all_to_all | solution.py:355
  126.9 4.3 %collective-permute-start.14 = (bf16[8,64,512]{2,1,0:T(8,128)(2,1)S(1)}, bf16[8,64,512]{2,1,0:T(8,128)(2,1)S(1)}, u32[]{:S(2)}, u32[]{:S(2)}) collective-permute-start(bf16[8,64,512]{2,1,0:T(8,128)(2,1)S(1)} %all-to-all-done.1.near_ref), channel_id=1, source_target_pairs={{0,16},{16,0},{1,17},{17,1},{2,18},{18,2},{3,19},{19,3},{4,20},{20... | collective-permute-start | bytes 1572872 | tf_op jit(solution)/shard_map/ppermute | solution.py:22
  131.2 1.5 %collective-permute-done.14.far_ref = bf16[8,64,512]{2,1,0:T(8,128)(2,1)S(1)} collective-permute-done((bf16[8,64,512]{2,1,0:T(8,128)(2,1)S(1)}, bf16[8,64,512]{2,1,0:T(8,128)(2,1)S(1)}, u32[]{:S(2)}, u32[]{:S(2)}) %collective-permute-start.14) | collective-permute-done | bytes 524320 | tf_op jit(solution)/shard_map/ppermute | solution.py:22
  132.7 3.9 %shard_map.81 = (bf16[256,2048]{1,0:T(8,128)(2,1)}, bf16[256,2048]{1,0:T(8,128)(2,1)}) custom-call(s32[4,64]{1,0:T(4,128)S(1)} %select_reduce_fusion.1.list_ref, s32[1]{0:T(128)} %bitcast.1.c_ref, f32[4,1,2048]{2,1,0:T(1,128)S(1)} %reshape.122.mask_ref, bf16[256,2048]{1,0:T(8,128)(2,1)S(1)} %bitcast.15, bf16[256,2048]{1,0:T(8,128)(2,1)S(1)} %get-tuple-element.66.own_ref, ...), custom_call_target="tpu_custom_call" | custom-call | flops 4194304 | bytes 4194304 | tf_op jit(solution)/shard_map/pallas_call | solution.py:217
  (48 shorter events, 6.7 us)
Async XLA Ops:
  0.6 16.1 %collective-permute-start.1 = (bf16[512,256]{1,0:T(8,128)(2,1)}, bf16[512,256]{1,0:T(8,128)(2,1)S(1)}, u32[]{:S(2)}, u32[]{:S(2)}) collective-permute-start(bf16[512,256]{1,0:T(8,128)(2,1)} %s0), channel_id=1, source_target_pairs={{0,2},{1,3},{2,0},{3,1},{4,6},{5,7},{6,4},{7,5},{8,10},{9,11},{10,... | collective-permute-start | bytes 786440 | tf_op jit(solution)/shard_map/ppermute | solution.py:22
  5.7 22.4 %collective-permute-start = (bf16[512,256]{1,0:T(8,128)(2,1)}, bf16[512,256]{1,0:T(8,128)(2,1)S(1)}, u32[]{:S(2)}, u32[]{:S(2)}) collective-permute-start(bf16[512,256]{1,0:T(8,128)(2,1)} %s0), channel_id=1, source_target_pairs={{0,1},{1,0},{2,3},{3,2},{4,5},{5,4},{6,7},{7,6},{8,9},{9,8},{10,11... | collective-permute-start | bytes 786440 | tf_op jit(solution)/shard_map/ppermute | solution.py:22
  8.9 13.0 %collective-permute-start.3 = (s32[1,64]{1,0:T(1,128)}, s32[1,64]{1,0:T(1,128)S(1)}, u32[]{:S(2)}, u32[]{:S(2)}) collective-permute-start(s32[1,64]{1,0:T(1,128)} %bitcast.16), channel_id=1, source_target_pairs={{0,4},{4,0},{8,12},{12,8},{1,5},{5,1},{9,13},{13,9},{2,6},{6,2},{1... | collective-permute-start | bytes 776 | tf_op jit(solution)/shard_map/ppermute | solution.py:22
  16.8 11.3 %collective-permute-start.2 = (bf16[512,256]{1,0:T(8,128)(2,1)S(1)}, bf16[512,256]{1,0:T(8,128)(2,1)S(1)}, u32[]{:S(2)}, u32[]{:S(2)}) collective-permute-start(bf16[512,256]{1,0:T(8,128)(2,1)S(1)} %collective-permute-done.1.s2), channel_id=1, source_target_pairs={{0,1},{1,0},{2,3},{3,2},{4,5},{5,4},{6,7},{7,6},{8,9},{9,8},{10,11... | collective-permute-start | bytes 786440 | tf_op jit(solution)/shard_map/ppermute | solution.py:22
  22.5 5.5 %collective-permute-start.4 = (s32[2,64]{1,0:T(2,128)S(1)}, s32[2,64]{1,0:T(2,128)S(1)}, u32[]{:S(2)}, u32[]{:S(2)}) collective-permute-start(s32[2,64]{1,0:T(2,128)S(1)} %pad_add_fusion.1), channel_id=1, source_target_pairs={{0,12},{4,8},{8,4},{12,0},{1,13},{5,9},{9,5},{13,1},{2,14},{6,10},... | collective-permute-start | bytes 1544 | tf_op jit(solution)/shard_map/ppermute | solution.py:22
  28.1 7.7 %copy-start = (bf16[512,2048]{1,0:T(8,128)(2,1)S(1)}, bf16[512,2048]{1,0:T(8,128)(2,1)}, u32[]{:S(2)}) copy-start(bf16[512,2048]{1,0:T(8,128)(2,1)} %cot_ref.1) | copy-start | bytes 6291460
  28.1 7.7 %copy-start.1 = (bf16[512,256]{1,0:T(8,128)(2,1)S(1)}, bf16[512,256]{1,0:T(8,128)(2,1)}, u32[]{:S(2)}) copy-start(bf16[512,256]{1,0:T(8,128)(2,1)} %s0) | copy-start | bytes 786436
  32.2 28.5 %collective-permute-start.6 = (bf16[64,4096]{1,0:T(8,128)(2,1)S(1)}, bf16[64,4096]{1,0:T(8,128)(2,1)S(1)}, u32[]{:S(2)}, u32[]{:S(2)}) collective-permute-start(bf16[64,4096]{1,0:T(8,128)(2,1)S(1)} %shard_map.76), channel_id=1, source_target_pairs={{0,8},{4,12},{8,0},{12,4},{1,9},{5,13},{9,1},{13,5},{2,10},{6,14},... | collective-permute-start | bytes 1572872 | tf_op jit(solution)/shard_map/ppermute | solution.py:22
  37.3 15.0 %copy-start.3 = (s32[1,1,1,64]{3,2,1,0:T(1,128)S(1)}, s32[1,1,1,64]{3,2,1,0:T(1,128)}, u32[]{:S(2)}) copy-start(s32[1,1,1,64]{3,2,1,0:T(1,128)} %param.8) | copy-start | bytes 772
  39.9 20.8 %copy-start.2 = (bf16[1,256,2048]{2,1,0:T(8,128)(2,1)S(1)}, bf16[1,256,2048]{2,1,0:T(8,128)(2,1)}, u32[]{:S(2)}) copy-start(bf16[1,256,2048]{2,1,0:T(8,128)(2,1)} %param.7) | copy-start | bytes 3145732
  39.9 20.7 %collective-permute-start.7 = (bf16[64,4096]{1,0:T(8,128)(2,1)S(1)}, bf16[64,4096]{1,0:T(8,128)(2,1)S(1)}, u32[]{:S(2)}, u32[]{:S(2)}) collective-permute-start(bf16[64,4096]{1,0:T(8,128)(2,1)S(1)} %get-tuple-element.56), channel_id=1, source_target_pairs={{0,12},{4,8},{8,4},{12,0},{1,13},{5,9},{9,5},{13,1},{2,14},{6,10},... | collective-permute-start | bytes 1572872 | tf_op jit(solution)/shard_map/ppermute | solution.py:22
  42.9 17.8 %collective-permute-start.5 = (bf16[64,4096]{1,0:T(8,128)(2,1)S(1)}, bf16[64,4096]{1,0:T(8,128)(2,1)S(1)}, u32[]{:S(2)}, u32[]{:S(2)}) collective-permute-start(bf16[64,4096]{1,0:T(8,128)(2,1)S(1)} %get-tuple-element.54), channel_id=1, source_target_pairs={{0,4},{4,0},{8,12},{12,8},{1,5},{5,1},{9,13},{13,9},{2,6},{6,2},{1... | collective-permute-start | bytes 1572872 | tf_op jit(solution)/shard_map/ppermute | solution.py:22
  45.0 14.3 %collective-permute-start.8 = (f32[64,256]{1,0:T(8,128)S(1)}, f32[64,256]{1,0:T(8,128)S(1)}, u32[]{:S(2)}, u32[]{:S(2)}) collective-permute-start(f32[64,256]{1,0:T(8,128)S(1)} %reshape.119), channel_id=1, source_target_pairs={{0,32},{32,0},{1,33},{33,1},{2,34},{34,2},{3,35},{35,3},{4,36},{36... | collective-permute-start | bytes 196616 | tf_op jit(solution)/shard_map/ppermute | solution.py:22
  59.3 3.4 %copy-start.4 = (bf16[64,4096]{1,0:T(8,128)(2,1)}, bf16[64,4096]{1,0:T(8,128)(2,1)S(1)}, u32[]{:S(2)}) copy-start(bf16[64,4096]{1,0:T(8,128)(2,1)S(1)} %get-tuple-element.74) | copy-start | bytes 1572868
  59.3 3.4 %copy-start.5 = (bf16[64,4096]{1,0:T(8,128)(2,1)}, bf16[64,4096]{1,0:T(8,128)(2,1)S(1)}, u32[]{:S(2)}) copy-start(bf16[64,4096]{1,0:T(8,128)(2,1)S(1)} %get-tuple-element.77) | copy-start | bytes 1572868
  59.4 7.9 %copy-start.7 = (f32[64,256]{1,0:T(8,128)}, f32[64,256]{1,0:T(8,128)S(1)}, u32[]{:S(2)}) copy-start(f32[64,256]{1,0:T(8,128)S(1)} %collective-permute-done.8) | copy-start | bytes 196612
  62.7 4.6 %collective-permute-start.9 = (bf16[8,64,512]{2,1,0:T(8,128)(2,1)S(1)}, bf16[8,64,512]{2,1,0:T(8,128)(2,1)S(1)}, u32[]{:S(2)}, u32[]{:S(2)}) collective-permute-start(bf16[8,64,512]{2,1,0:T(8,128)(2,1)S(1)} %get-tuple-element.71), channel_id=1, source_target_pairs={{0,16},{16,0},{1,17},{17,1},{2,18},{18,2},{3,19},{19,3},{4,20},{20... | collective-permute-start | bytes 1572872 | tf_op jit(solution)/shard_map/ppermute | solution.py:22
  65.8 12.6 %copy-start.6 = (bf16[64,4096]{1,0:T(8,128)(2,1)S(1)}, bf16[64,4096]{1,0:T(8,128)(2,1)}, u32[]{:S(2)}) copy-start(bf16[64,4096]{1,0:T(8,128)(2,1)} %copy-done.5) | copy-start | bytes 1572868
  67.3 14.7 %copy-start.8 = (f32[64,256]{1,0:T(8,128)S(1)}, f32[64,256]{1,0:T(8,128)}, u32[]{:S(2)}) copy-start(f32[64,256]{1,0:T(8,128)} %copy-done.7) | copy-start | bytes 196612
  68.3 28.1 %all-to-all-start = ((bf16[8,64,512]{2,1,0:T(8,128)(2,1)}), bf16[8,64,512]{2,1,0:T(8,128)(2,1)}, u32[]{:S(2)}, u32[]{:S(2)}) async-start(bf16[8,64,512]{2,1,0:T(8,128)(2,1)} %add_convert_fusion.1), calls=%async_computation | async-start | bytes 1048576 | tf_op jit(solution)/shard_map/all_to_all | solution.py:346
  78.4 25.4 %collective-permute-start.12 = (bf16[64,4096]{1,0:T(8,128)(2,1)S(1)}, bf16[64,4096]{1,0:T(8,128)(2,1)}, u32[]{:S(2)}, u32[]{:S(2)}) collective-permute-start(bf16[64,4096]{1,0:T(8,128)(2,1)S(1)} %copy-done.6), channel_id=1, source_target_pairs={{0,4},{4,0},{8,12},{12,8},{1,5},{5,1},{9,13},{13,9},{2,6},{6,2},{1... | collective-permute-start | bytes 1572872 | tf_op jit(solution)/shard_map/ppermute | solution.py:22
  97.6 9.0 %collective-permute-start.11 = (bf16[64,512]{1,0:T(8,128)(2,1)S(1)}, bf16[64,512]{1,0:T(8,128)(2,1)S(1)}, u32[]{:S(2)}, u32[]{:S(2)}) collective-permute-start(bf16[64,512]{1,0:T(8,128)(2,1)S(1)} %reduce_sum.32.mine_ref), channel_id=1, source_target_pairs={{0,32},{32,0},{1,33},{33,1},{2,34},{34,2},{3,35},{35,3},{4,36},{36... | collective-permute-start | bytes 196616 | tf_op jit(solution)/shard_map/ppermute | solution.py:22
  107.4 19.5 %all-to-all-start.1 = ((bf16[8,64,512]{2,1,0:T(8,128)(2,1)}), bf16[8,64,512]{2,1,0:T(8,128)(2,1)S(1)}, u32[]{:S(2)}, u32[]{:S(2)}) async-start(bf16[8,64,512]{2,1,0:T(8,128)(2,1)} %get-tuple-element.81), calls=%async_computation.1 | async-start | bytes 1048576 | tf_op jit(solution)/shard_map/all_to_all | solution.py:355
  110.9 20.3 %collective-permute-start.10 = (bf16[64,4096]{1,0:T(8,128)(2,1)}, bf16[64,4096]{1,0:T(8,128)(2,1)S(1)}, u32[]{:S(2)}, u32[]{:S(2)}) collective-permute-start(bf16[64,4096]{1,0:T(8,128)(2,1)} %copy-done.4), channel_id=1, source_target_pairs={{0,4},{4,0},{8,12},{12,8},{1,5},{5,1},{9,13},{13,9},{2,6},{6,2},{1... | collective-permute-start | bytes 1572872 | tf_op jit(solution)/shard_map/ppermute | solution.py:22
  114.6 16.6 %collective-permute-start.13 = (bf16[64,4096]{1,0:T(8,128)(2,1)}, bf16[64,4096]{1,0:T(8,128)(2,1)}, u32[]{:S(2)}, u32[]{:S(2)}) collective-permute-start(bf16[64,4096]{1,0:T(8,128)(2,1)} %add_convert_fusion), channel_id=1, source_target_pairs={{0,12},{4,8},{8,4},{12,0},{1,13},{5,9},{9,5},{13,1},{2,14},{6,10},... | collective-permute-start | bytes 1572872 | tf_op jit(solution)/shard_map/ppermute | solution.py:22
  126.9 5.8 %collective-permute-start.14 = (bf16[8,64,512]{2,1,0:T(8,128)(2,1)S(1)}, bf16[8,64,512]{2,1,0:T(8,128)(2,1)S(1)}, u32[]{:S(2)}, u32[]{:S(2)}) collective-permute-start(bf16[8,64,512]{2,1,0:T(8,128)(2,1)S(1)} %all-to-all-done.1.near_ref), channel_id=1, source_target_pairs={{0,16},{16,0},{1,17},{17,1},{2,18},{18,2},{3,19},{19,3},{4,20},{20... | collective-permute-start | bytes 1572872 | tf_op jit(solution)/shard_map/ppermute | solution.py:22

commit v13 on v12

--- a/solution.py
+++ b/solution.py
@@ -308,11 +308,9 @@
     moment = as_matrix(momentum[0, 0])
     mask = mask[:, None]
     picks = chosen.reshape(1, -1)
-    near_picks = swap(picks, "dp", 1, 4)
-    far_picks = swap(jnp.concatenate([picks, near_picks]), "dp", 3, 4)
-    *shards, near_picks, far_picks = lax.optimization_barrier(
-        (*gather_hidden(hidden), near_picks, far_picks)
-    )
+    far_picks = swap(picks, "dp", 2, 4)
+    near_picks = swap(jnp.concatenate([picks, far_picks]), "dp", 1, 4)
+    *shards, far_picks = lax.optimization_barrier((*gather_hidden(hidden), far_picks))
     at = (lax.axis_index("dp") ^ lax.axis_index("t")).astype(jnp.int32).reshape(1)
 
     def part(k, shards):
@@ -323,17 +321,17 @@
             preferred_element_type=F32,
         ).astype(BF16)
 
-    (give_2,) = chosen_parts((1,), (far_picks,), (part(2, shards),))
+    (give_2,) = chosen_parts((0,), (far_picks,), (part(2, shards),))
     got_2 = swap(give_2, "dp", 2, 4)
     *shards, _ = lax.optimization_barrier((*shards, give_2))
     give_1, give_3 = chosen_parts(
-        (0, 0), (near_picks, far_picks), (part(1, shards), part(3, shards))
+        (0, 1), (near_picks, near_picks), (part(1, shards), part(3, shards))
     )
     got_1 = swap(give_1, "dp", 1, 4)
     *shards, give_3, moment = lax.optimization_barrier((*shards, give_3, moment))
     got_3 = swap(give_3, "dp", 3, 4)
     far_moment = swap(moment, "yh", 1, 2)
-    others = jnp.concatenate([picks, near_picks, far_picks[1:], far_picks[:1]])
+    others = jnp.concatenate([picks, near_picks[:1], far_picks, near_picks[1:]])
     others = others_of(others, rows_blk * cols_blk)
     rest = rest_parts(others, at, shards, cotangent)
     got_1, got_2, got_3, far_moment, give_1, give_2, keep, own = lax.optimization_barrier(

time: 139 us -> 139 us (level)
  starting transfers between devices: 75.8 us -> 80 us
  waiting for transfers between devices: 30.7 us -> 26.6 us
    ppermute x15, starting transfers between devices: 62.2 us -> 66.5 us  [swap(): return lax.ppermute(value, axis, [(i, i ^ flip) for i in range(size)])]
    ppermute x15, waiting for transfers between devices: 9.71 us -> 7.22 us  [swap(): return lax.ppermute(value, axis, [(i, i ^ flip) for i in range(size)])]
    all_to_all x1, waiting for transfers between devices: 6.59 us -> 4.98 us  [local(): every = lax.all_to_all(copies, 'z', 0, 0, tiled=True)]
  transfers between devices with their start and end apart: 17 -> 17, of which waited for: 7 -> 7; matrix products, arithmetic and copies ran while one was open for 6% -> 8% of each run, Pallas kernels for 7% -> 8%
where the time goes in v13:
time: 139 us; the launch traced here: 137 us
  starting transfers between devices  80 us (58%)
  waiting for transfers between devices  26.6 us (19%)
  Pallas kernels  17.5 us (13%)
  other arithmetic  6.32 us (5%)
  matrix products  3.89 us (3%)
    ppermute x15, starting transfers between devices, swap(): return lax.ppermute(value, axis, [(i, i ^ flip) for i in range(size)])  66.5 us
    all_to_all x1, waiting for transfers between devices, local(): across = lax.all_to_all(pair, 'z', 0, 0, tiled=True)  14.4 us
    all_to_all x1, starting transfers between devices, local(): across = lax.all_to_all(pair, 'z', 0, 0, tiled=True)  10 us
    ppermute x15, waiting for transfers between devices, swap(): return lax.ppermute(value, axis, [(i, i ^ flip) for i in range(size)])  7.22 us
    pallas_call x1, Pallas kernels, products_call(): pl.pallas_call(body, in_specs=[SMEM, SMEM] + [whole] * 5, out_specs=jax.t...  6.56 us
    pallas_call x2, Pallas kernels, state_call(): pl.pallas_call(body, grid=(rows // BLK,), in_specs=[SMEM] * len(scalars)...  5.95 us
    all_to_all x1, waiting for transfers between devices, local(): every = lax.all_to_all(copies, 'z', 0, 0, tiled=True)  4.98 us
    pallas_call x2, Pallas kernels, chosen_parts(): kernel_call(functools.partial(first_kernel, rows), (), [SMEM] * n + [whol...  4.08 us
  transfers between devices with their start and end apart: 17, of which 7 were waited for; matrix products, arithmetic and copies ran while one was open for 8% of the time, Pallas kernels for 8%

profile of v13, /device:TPU:1, one launch (start us, length us, event | category | flops | bytes accessed | tf_op | source)
XLA Modules:
  0.0 136.6 jit_solution(13561576751681186072)
XLA Ops:
  0.6 5.0 %collective-permute-start.3 = (bf16[512,256]{1,0:T(8,128)(2,1)}, bf16[512,256]{1,0:T(8,128)(2,1)S(1)}, u32[]{:S(2)}, u32[]{:S(2)}) collective-permute-start(bf16[512,256]{1,0:T(8,128)(2,1)} %s0), channel_id=1, source_target_pairs={{0,2},{1,3},{2,0},{3,1},{4,6},{5,7},{6,4},{7,5},{8,10},{9,11},{10,... | collective-permute-start | bytes 786440 | tf_op jit(solution)/shard_map/ppermute | solution.py:22
  5.7 3.2 %collective-permute-start.2 = (bf16[512,256]{1,0:T(8,128)(2,1)}, bf16[512,256]{1,0:T(8,128)(2,1)S(1)}, u32[]{:S(2)}, u32[]{:S(2)}) collective-permute-start(bf16[512,256]{1,0:T(8,128)(2,1)} %s0), channel_id=1, source_target_pairs={{0,1},{1,0},{2,3},{3,2},{4,5},{5,4},{6,7},{7,6},{8,9},{9,8},{10,11... | collective-permute-start | bytes 786440 | tf_op jit(solution)/shard_map/ppermute | solution.py:22
  8.9 4.7 %collective-permute-start = (s32[1,64]{1,0:T(1,128)}, s32[1,64]{1,0:T(1,128)S(1)}, u32[]{:S(2)}, u32[]{:S(2)}) collective-permute-start(s32[1,64]{1,0:T(1,128)} %bitcast.16), channel_id=1, source_target_pairs={{0,8},{4,12},{8,0},{12,4},{1,9},{5,13},{9,1},{13,5},{2,10},{6,14},... | collective-permute-start | bytes 776 | tf_op jit(solution)/shard_map/ppermute | solution.py:22
  13.7 3.1 %collective-permute-done.3.s2 = bf16[512,256]{1,0:T(8,128)(2,1)S(1)} collective-permute-done((bf16[512,256]{1,0:T(8,128)(2,1)}, bf16[512,256]{1,0:T(8,128)(2,1)S(1)}, u32[]{:S(2)}, u32[]{:S(2)}) %collective-permute-start.3) | collective-permute-done | bytes 262176 | tf_op jit(solution)/shard_map/ppermute | solution.py:22
  16.8 4.0 %collective-permute-start.4 = (bf16[512,256]{1,0:T(8,128)(2,1)S(1)}, bf16[512,256]{1,0:T(8,128)(2,1)S(1)}, u32[]{:S(2)}, u32[]{:S(2)}) collective-permute-start(bf16[512,256]{1,0:T(8,128)(2,1)S(1)} %collective-permute-done.3.s2), channel_id=1, source_target_pairs={{0,1},{1,0},{2,3},{3,2},{4,5},{5,4},{6,7},{7,6},{8,9},{9,8},{10,11... | collective-permute-start | bytes 786440 | tf_op jit(solution)/shard_map/ppermute | solution.py:22
  22.0 1.0 compare_reduce_fusion
  23.7 3.2 %collective-permute-start.1 = (s32[2,64]{1,0:T(2,128)S(1)}, s32[2,64]{1,0:T(2,128)S(1)}, u32[]{:S(2)}, u32[]{:S(2)}) collective-permute-start(s32[2,64]{1,0:T(2,128)S(1)} %pad_add_fusion.1), channel_id=1, source_target_pairs={{0,4},{4,0},{8,12},{12,8},{1,5},{5,1},{9,13},{13,9},{2,6},{6,2},{1... | collective-permute-start | bytes 1544 | tf_op jit(solution)/shard_map/ppermute | solution.py:22
  27.0 2.3 %convolution_convert_fusion.2.refs_1_ = bf16[256,2048]{1,0:T(8,128)(2,1)S(1)} fusion(bf16[512,2048]{1,0:T(8,128)(2,1)} %cot_ref.1, bf16[512,256]{1,0:T(8,128)(2,1)S(1)} %collective-permute-done.3.s2, bf16[512,256]{1,0:T(8,128)(2,1)S(1)} %collective-permute-done.4.s3, bf16[512,256]{1,0:T(8,128)(2,1)} %s0, bf16[512,256]{1,0:T(8,128)(2,1)S(1)} %collective-permute-done.2.s1, ...), kind=kOutput, calls=%fused_computation.2 | convolution fusion | flops 537788416 | bytes 4194307 | tf_op jit(solution)/shard_map/dot_general | solution.py:317
  29.3 1.5 %shard_map.76 = bf16[64,4096]{1,0:T(8,128)(2,1)S(1)} custom-call(s32[1,64]{1,0:T(1,128)S(1)} %collective-permute-done.refs_0_, bf16[256,2048]{1,0:T(8,128)(2,1)S(1)} %convolution_convert_fusion.2.refs_1_), custom_call_target="tpu_custom_call" | custom-call | flops 1048576 | bytes 1048576 | tf_op jit(solution)/shard_map/pallas_call | solution.py:122
  30.9 4.5 %collective-permute-start.6 = (bf16[64,4096]{1,0:T(8,128)(2,1)S(1)}, bf16[64,4096]{1,0:T(8,128)(2,1)S(1)}, u32[]{:S(2)}, u32[]{:S(2)}) collective-permute-start(bf16[64,4096]{1,0:T(8,128)(2,1)S(1)} %shard_map.76), channel_id=1, source_target_pairs={{0,8},{4,12},{8,0},{12,4},{1,9},{5,13},{9,1},{13,5},{2,10},{6,14},... | collective-permute-start | bytes 1572872 | tf_op jit(solution)/shard_map/ppermute | solution.py:22
  36.9 2.5 %shard_map.77 = (bf16[64,4096]{1,0:T(8,128)(2,1)S(1)}, bf16[64,4096]{1,0:T(8,128)(2,1)S(1)}) custom-call(s32[2,64]{1,0:T(2,128)S(1)} %collective-permute-done.1.refs_0_.refs_1_, s32[2,64]{1,0:T(2,128)S(1)} %collective-permute-done.1.refs_0_.refs_1_, bf16[256,2048]{1,0:T(8,128)(2,1)S(1)} %convolution_convert_fusion.1.refs_2_, ...), custom_call_target="tpu_custom_call" | custom-call | flops 1048576 | bytes 1048576 | tf_op jit(solution)/shard_map/pallas_call | solution.py:122
  39.5 2.2 %collective-permute-start.7 = (bf16[64,4096]{1,0:T(8,128)(2,1)S(1)}, bf16[64,4096]{1,0:T(8,128)(2,1)S(1)}, u32[]{:S(2)}, u32[]{:S(2)}) collective-permute-start(bf16[64,4096]{1,0:T(8,128)(2,1)S(1)} %get-tuple-element.54), channel_id=1, source_target_pairs={{0,12},{4,8},{8,4},{12,0},{1,13},{5,9},{9,5},{13,1},{2,14},{6,10},... | collective-permute-start | bytes 1572872 | tf_op jit(solution)/shard_map/ppermute | solution.py:22
  41.7 1.9 %collective-permute-start.5 = (bf16[64,4096]{1,0:T(8,128)(2,1)S(1)}, bf16[64,4096]{1,0:T(8,128)(2,1)S(1)}, u32[]{:S(2)}, u32[]{:S(2)}) collective-permute-start(bf16[64,4096]{1,0:T(8,128)(2,1)S(1)} %get-tuple-element.52), channel_id=1, source_target_pairs={{0,4},{4,0},{8,12},{12,8},{1,5},{5,1},{9,13},{13,9},{2,6},{6,2},{1... | collective-permute-start | bytes 1572872 | tf_op jit(solution)/shard_map/ppermute | solution.py:22
  43.6 8.7 %collective-permute-start.8 = (f32[64,256]{1,0:T(8,128)S(1)}, f32[64,256]{1,0:T(8,128)S(1)}, u32[]{:S(2)}, u32[]{:S(2)}) collective-permute-start(f32[64,256]{1,0:T(8,128)S(1)} %reshape.119), channel_id=1, source_target_pairs={{0,32},{32,0},{1,33},{33,1},{2,34},{34,2},{3,35},{35,3},{4,36},{36... | collective-permute-start | bytes 196616 | tf_op jit(solution)/shard_map/ppermute | solution.py:22
  52.8 6.6 %shard_map.78 = (bf16[64,4096]{1,0:T(8,128)(2,1)S(1)}, bf16[64,4096]{1,0:T(8,128)(2,1)S(1)}, bf16[64,4096]{1,0:T(8,128)(2,1)S(1)}, bf16[256,2048]{1,0:T(8,128)(2,1)S(1)}) custom-call(s32[4,64]{1,0:T(4,128)S(1)} %select_reduce_fusion.1.list_ref, s32[1]{0:T(128)} %bitcast.6.at_ref, bf16[512,256]{1,0:T(8,128)(2,1)S(1)} %copy-done.1, ...), custom_call_target="tpu_custom_call" | custom-call | flops 1048576 | bytes 1048576 | tf_op jit(solution)/shard_map/pallas_call | solution.py:105
  59.4 2.0 %shard_map.79 = (f32[8,64,512]{2,1,0:T(8,128)S(1)}, bf16[8,64,512]{2,1,0:T(8,128)(2,1)S(1)}) custom-call(s32[1,64]{1,0:T(1,128)S(1)} %bitcast.20, s32[1]{0:T(128)} %bitcast.1.c_ref, f32[4,1,2048]{2,1,0:T(1,128)S(1)} %reshape.122.mask_ref, bf16[256,2048]{1,0:T(8,128)(2,1)S(1)} %bitcast.14, bf16[256,2048]{1,0:T(8,128)(2,1)S(1)} %get-tuple-element.64.own_ref, ...), custom_call_target="tpu_custom_call" | custom-call | flops 4194304 | bytes 4194304 | tf_op jit(solution)/shard_map/pallas_call | solution.py:217
  61.5 4.3 %collective-permute-start.9 = (bf16[8,64,512]{2,1,0:T(8,128)(2,1)S(1)}, bf16[8,64,512]{2,1,0:T(8,128)(2,1)S(1)}, u32[]{:S(2)}, u32[]{:S(2)}) collective-permute-start(bf16[8,64,512]{2,1,0:T(8,128)(2,1)S(1)} %get-tuple-element.69), channel_id=1, source_target_pairs={{0,16},{16,0},{1,17},{17,1},{2,18},{18,2},{3,19},{19,3},{4,20},{20... | collective-permute-start | bytes 1572872 | tf_op jit(solution)/shard_map/ppermute | solution.py:22
  65.8 1.5 %collective-permute-done.9 = bf16[8,64,512]{2,1,0:T(8,128)(2,1)S(1)} collective-permute-done((bf16[8,64,512]{2,1,0:T(8,128)(2,1)S(1)}, bf16[8,64,512]{2,1,0:T(8,128)(2,1)S(1)}, u32[]{:S(2)}, u32[]{:S(2)}) %collective-permute-start.9) | collective-permute-done | bytes 524320 | tf_op jit(solution)/shard_map/ppermute | solution.py:22
  67.3 1.0 add_convert_fusion.1
  68.3 10.0 %all-to-all-start = ((bf16[8,64,512]{2,1,0:T(8,128)(2,1)}), bf16[8,64,512]{2,1,0:T(8,128)(2,1)}, u32[]{:S(2)}, u32[]{:S(2)}) async-start(bf16[8,64,512]{2,1,0:T(8,128)(2,1)} %add_convert_fusion.1), calls=%async_computation | async-start | bytes 1048576 | tf_op jit(solution)/shard_map/all_to_all | solution.py:344
  78.4 3.6 %collective-permute-start.12 = (bf16[64,4096]{1,0:T(8,128)(2,1)S(1)}, bf16[64,4096]{1,0:T(8,128)(2,1)}, u32[]{:S(2)}, u32[]{:S(2)}) collective-permute-start(bf16[64,4096]{1,0:T(8,128)(2,1)S(1)} %copy-done.6), channel_id=1, source_target_pairs={{0,4},{4,0},{8,12},{12,8},{1,5},{5,1},{9,13},{13,9},{2,6},{6,2},{1... | collective-permute-start | bytes 1572872 | tf_op jit(solution)/shard_map/ppermute | solution.py:22
  82.1 14.4 %all-to-all-done = bf16[8,64,512]{2,1,0:T(8,128)(2,1)} async-done(((bf16[8,64,512]{2,1,0:T(8,128)(2,1)}), bf16[8,64,512]{2,1,0:T(8,128)(2,1)}, u32[]{:S(2)}, u32[]{:S(2)}) %all-to-all-start) | async-done | bytes 524320 | tf_op jit(solution)/shard_map/all_to_all | solution.py:344
  96.4 1.1 reduce_sum.32.mine_ref
  97.5 5.9 %collective-permute-start.11 = (bf16[64,512]{1,0:T(8,128)(2,1)S(1)}, bf16[64,512]{1,0:T(8,128)(2,1)S(1)}, u32[]{:S(2)}, u32[]{:S(2)}) collective-permute-start(bf16[64,512]{1,0:T(8,128)(2,1)S(1)} %reduce_sum.32.mine_ref), channel_id=1, source_target_pairs={{0,32},{32,0},{1,33},{33,1},{2,34},{34,2},{3,35},{35,3},{4,36},{36... | collective-permute-start | bytes 196616 | tf_op jit(solution)/shard_map/ppermute | solution.py:22
  103.5 2.0 %add_convert_fusion = bf16[64,4096]{1,0:T(8,128)(2,1)} fusion(bf16[64,4096]{1,0:T(8,128)(2,1)} %collective-permute-done.12, bf16[64,4096]{1,0:T(8,128)(2,1)S(1)} %get-tuple-element.74), kind=kLoop, calls=%fused_computation.4 | loop fusion | flops 1048576 | bytes 1572864 | tf_op jit(solution)/shard_map/convert_element_type | solution.py:291
  105.4 1.1 collective-permute-done.11.peer_ref
  107.4 3.5 %all-to-all-start.1 = ((bf16[8,64,512]{2,1,0:T(8,128)(2,1)}), bf16[8,64,512]{2,1,0:T(8,128)(2,1)S(1)}, u32[]{:S(2)}, u32[]{:S(2)}) async-start(bf16[8,64,512]{2,1,0:T(8,128)(2,1)} %get-tuple-element.79), calls=%async_computation.1 | async-start | bytes 1048576 | tf_op jit(solution)/shard_map/all_to_all | solution.py:353
  110.9 5.4 %collective-permute-start.10 = (bf16[64,4096]{1,0:T(8,128)(2,1)}, bf16[64,4096]{1,0:T(8,128)(2,1)S(1)}, u32[]{:S(2)}, u32[]{:S(2)}) collective-permute-start(bf16[64,4096]{1,0:T(8,128)(2,1)} %copy-done.4), channel_id=1, source_target_pairs={{0,4},{4,0},{8,12},{12,8},{1,5},{5,1},{9,13},{13,9},{2,6},{6,2},{1... | collective-permute-start | bytes 1572872 | tf_op jit(solution)/shard_map/ppermute | solution.py:22
  116.3 4.0 %collective-permute-start.13 = (bf16[64,4096]{1,0:T(8,128)(2,1)}, bf16[64,4096]{1,0:T(8,128)(2,1)}, u32[]{:S(2)}, u32[]{:S(2)}) collective-permute-start(bf16[64,4096]{1,0:T(8,128)(2,1)} %add_convert_fusion), channel_id=1, source_target_pairs={{0,12},{4,8},{8,4},{12,0},{1,13},{5,9},{9,5},{13,1},{2,14},{6,10},... | collective-permute-start | bytes 1572872 | tf_op jit(solution)/shard_map/ppermute | solution.py:22
  120.3 5.0 %all-to-all-done.1.near_ref = bf16[8,64,512]{2,1,0:T(8,128)(2,1)S(1)} async-done(((bf16[8,64,512]{2,1,0:T(8,128)(2,1)}), bf16[8,64,512]{2,1,0:T(8,128)(2,1)S(1)}, u32[]{:S(2)}, u32[]{:S(2)}) %all-to-all-start.1) | async-done | bytes 524320 | tf_op jit(solution)/shard_map/all_to_all | solution.py:353
  125.3 5.9 %collective-permute-start.14 = (bf16[8,64,512]{2,1,0:T(8,128)(2,1)S(1)}, bf16[8,64,512]{2,1,0:T(8,128)(2,1)S(1)}, u32[]{:S(2)}, u32[]{:S(2)}) collective-permute-start(bf16[8,64,512]{2,1,0:T(8,128)(2,1)S(1)} %all-to-all-done.1.near_ref), channel_id=1, source_target_pairs={{0,16},{16,0},{1,17},{17,1},{2,18},{18,2},{3,19},{19,3},{4,20},{20... | collective-permute-start | bytes 1572872 | tf_op jit(solution)/shard_map/ppermute | solution.py:22
  132.7 3.9 %shard_map.81 = (bf16[256,2048]{1,0:T(8,128)(2,1)}, bf16[256,2048]{1,0:T(8,128)(2,1)}) custom-call(s32[4,64]{1,0:T(4,128)S(1)} %select_reduce_fusion.1.list_ref, s32[1]{0:T(128)} %bitcast.1.c_ref, f32[4,1,2048]{2,1,0:T(1,128)S(1)} %reshape.122.mask_ref, bf16[256,2048]{1,0:T(8,128)(2,1)S(1)} %bitcast.15, bf16[256,2048]{1,0:T(8,128)(2,1)S(1)} %get-tuple-element.64.own_ref, ...), custom_call_target="tpu_custom_call" | custom-call | flops 4194304 | bytes 4194304 | tf_op jit(solution)/shard_map/pallas_call | solution.py:217
  (48 shorter events, 6.4 us)
Async XLA Ops:
  0.6 16.1 %collective-permute-start.3 = (bf16[512,256]{1,0:T(8,128)(2,1)}, bf16[512,256]{1,0:T(8,128)(2,1)S(1)}, u32[]{:S(2)}, u32[]{:S(2)}) collective-permute-start(bf16[512,256]{1,0:T(8,128)(2,1)} %s0), channel_id=1, source_target_pairs={{0,2},{1,3},{2,0},{3,1},{4,6},{5,7},{6,4},{7,5},{8,10},{9,11},{10,... | collective-permute-start | bytes 786440 | tf_op jit(solution)/shard_map/ppermute | solution.py:22
  5.7 21.3 %collective-permute-start.2 = (bf16[512,256]{1,0:T(8,128)(2,1)}, bf16[512,256]{1,0:T(8,128)(2,1)S(1)}, u32[]{:S(2)}, u32[]{:S(2)}) collective-permute-start(bf16[512,256]{1,0:T(8,128)(2,1)} %s0), channel_id=1, source_target_pairs={{0,1},{1,0},{2,3},{3,2},{4,5},{5,4},{6,7},{7,6},{8,9},{9,8},{10,11... | collective-permute-start | bytes 786440 | tf_op jit(solution)/shard_map/ppermute | solution.py:22
  8.9 14.1 %collective-permute-start = (s32[1,64]{1,0:T(1,128)}, s32[1,64]{1,0:T(1,128)S(1)}, u32[]{:S(2)}, u32[]{:S(2)}) collective-permute-start(s32[1,64]{1,0:T(1,128)} %bitcast.16), channel_id=1, source_target_pairs={{0,8},{4,12},{8,0},{12,4},{1,9},{5,13},{9,1},{13,5},{2,10},{6,14},... | collective-permute-start | bytes 776 | tf_op jit(solution)/shard_map/ppermute | solution.py:22
  16.8 10.2 %collective-permute-start.4 = (bf16[512,256]{1,0:T(8,128)(2,1)S(1)}, bf16[512,256]{1,0:T(8,128)(2,1)S(1)}, u32[]{:S(2)}, u32[]{:S(2)}) collective-permute-start(bf16[512,256]{1,0:T(8,128)(2,1)S(1)} %collective-permute-done.3.s2), channel_id=1, source_target_pairs={{0,1},{1,0},{2,3},{3,2},{4,5},{5,4},{6,7},{7,6},{8,9},{9,8},{10,11... | collective-permute-start | bytes 786440 | tf_op jit(solution)/shard_map/ppermute | solution.py:22
  23.7 11.6 %copy-start = (bf16[512,2048]{1,0:T(8,128)(2,1)S(1)}, bf16[512,2048]{1,0:T(8,128)(2,1)}, u32[]{:S(2)}) copy-start(bf16[512,2048]{1,0:T(8,128)(2,1)} %cot_ref.1) | copy-start | bytes 6291460
  23.7 11.6 %copy-start.1 = (bf16[512,256]{1,0:T(8,128)(2,1)S(1)}, bf16[512,256]{1,0:T(8,128)(2,1)}, u32[]{:S(2)}) copy-start(bf16[512,256]{1,0:T(8,128)(2,1)} %s0) | copy-start | bytes 786436
  23.7 13.2 %collective-permute-start.1 = (s32[2,64]{1,0:T(2,128)S(1)}, s32[2,64]{1,0:T(2,128)S(1)}, u32[]{:S(2)}, u32[]{:S(2)}) collective-permute-start(s32[2,64]{1,0:T(2,128)S(1)} %pad_add_fusion.1), channel_id=1, source_target_pairs={{0,4},{4,0},{8,12},{12,8},{1,5},{5,1},{9,13},{13,9},{2,6},{6,2},{1... | collective-permute-start | bytes 1544 | tf_op jit(solution)/shard_map/ppermute | solution.py:22
  30.9 28.6 %collective-permute-start.6 = (bf16[64,4096]{1,0:T(8,128)(2,1)S(1)}, bf16[64,4096]{1,0:T(8,128)(2,1)S(1)}, u32[]{:S(2)}, u32[]{:S(2)}) collective-permute-start(bf16[64,4096]{1,0:T(8,128)(2,1)S(1)} %shard_map.76), channel_id=1, source_target_pairs={{0,8},{4,12},{8,0},{12,4},{1,9},{5,13},{9,1},{13,5},{2,10},{6,14},... | collective-permute-start | bytes 1572872 | tf_op jit(solution)/shard_map/ppermute | solution.py:22
  36.9 15.4 %copy-start.3 = (s32[1,1,1,64]{3,2,1,0:T(1,128)S(1)}, s32[1,1,1,64]{3,2,1,0:T(1,128)}, u32[]{:S(2)}) copy-start(s32[1,1,1,64]{3,2,1,0:T(1,128)} %param.8) | copy-start | bytes 772
  39.5 19.9 %copy-start.2 = (bf16[1,256,2048]{2,1,0:T(8,128)(2,1)S(1)}, bf16[1,256,2048]{2,1,0:T(8,128)(2,1)}, u32[]{:S(2)}) copy-start(bf16[1,256,2048]{2,1,0:T(8,128)(2,1)} %param.7) | copy-start | bytes 3145732
  39.5 19.9 %collective-permute-start.7 = (bf16[64,4096]{1,0:T(8,128)(2,1)S(1)}, bf16[64,4096]{1,0:T(8,128)(2,1)S(1)}, u32[]{:S(2)}, u32[]{:S(2)}) collective-permute-start(bf16[64,4096]{1,0:T(8,128)(2,1)S(1)} %get-tuple-element.54), channel_id=1, source_target_pairs={{0,12},{4,8},{8,4},{12,0},{1,13},{5,9},{9,5},{13,1},{2,14},{6,10},... | collective-permute-start | bytes 1572872 | tf_op jit(solution)/shard_map/ppermute | solution.py:22
  41.7 17.7 %collective-permute-start.5 = (bf16[64,4096]{1,0:T(8,128)(2,1)S(1)}, bf16[64,4096]{1,0:T(8,128)(2,1)S(1)}, u32[]{:S(2)}, u32[]{:S(2)}) collective-permute-start(bf16[64,4096]{1,0:T(8,128)(2,1)S(1)} %get-tuple-element.52), channel_id=1, source_target_pairs={{0,4},{4,0},{8,12},{12,8},{1,5},{5,1},{9,13},{13,9},{2,6},{6,2},{1... | collective-permute-start | bytes 1572872 | tf_op jit(solution)/shard_map/ppermute | solution.py:22
  43.6 15.7 %collective-permute-start.8 = (f32[64,256]{1,0:T(8,128)S(1)}, f32[64,256]{1,0:T(8,128)S(1)}, u32[]{:S(2)}, u32[]{:S(2)}) collective-permute-start(f32[64,256]{1,0:T(8,128)S(1)} %reshape.119), channel_id=1, source_target_pairs={{0,32},{32,0},{1,33},{33,1},{2,34},{34,2},{3,35},{35,3},{4,36},{36... | collective-permute-start | bytes 196616 | tf_op jit(solution)/shard_map/ppermute | solution.py:22
  59.3 2.1 %copy-start.4 = (bf16[64,4096]{1,0:T(8,128)(2,1)}, bf16[64,4096]{1,0:T(8,128)(2,1)S(1)}, u32[]{:S(2)}) copy-start(bf16[64,4096]{1,0:T(8,128)(2,1)S(1)} %get-tuple-element.72) | copy-start | bytes 1572868
  59.4 2.1 %copy-start.5 = (bf16[64,4096]{1,0:T(8,128)(2,1)}, bf16[64,4096]{1,0:T(8,128)(2,1)S(1)}, u32[]{:S(2)}) copy-start(bf16[64,4096]{1,0:T(8,128)(2,1)S(1)} %get-tuple-element.75) | copy-start | bytes 1572868
  59.4 7.9 %copy-start.7 = (f32[64,256]{1,0:T(8,128)}, f32[64,256]{1,0:T(8,128)S(1)}, u32[]{:S(2)}) copy-start(f32[64,256]{1,0:T(8,128)S(1)} %collective-permute-done.8) | copy-start | bytes 196612
  61.5 5.8 %collective-permute-start.9 = (bf16[8,64,512]{2,1,0:T(8,128)(2,1)S(1)}, bf16[8,64,512]{2,1,0:T(8,128)(2,1)S(1)}, u32[]{:S(2)}, u32[]{:S(2)}) collective-permute-start(bf16[8,64,512]{2,1,0:T(8,128)(2,1)S(1)} %get-tuple-element.69), channel_id=1, source_target_pairs={{0,16},{16,0},{1,17},{17,1},{2,18},{18,2},{3,19},{19,3},{4,20},{20... | collective-permute-start | bytes 1572872 | tf_op jit(solution)/shard_map/ppermute | solution.py:22
  65.8 12.6 %copy-start.6 = (bf16[64,4096]{1,0:T(8,128)(2,1)S(1)}, bf16[64,4096]{1,0:T(8,128)(2,1)}, u32[]{:S(2)}) copy-start(bf16[64,4096]{1,0:T(8,128)(2,1)} %copy-done.5) | copy-start | bytes 1572868
  67.3 14.7 %copy-start.8 = (f32[64,256]{1,0:T(8,128)S(1)}, f32[64,256]{1,0:T(8,128)}, u32[]{:S(2)}) copy-start(f32[64,256]{1,0:T(8,128)} %copy-done.7) | copy-start | bytes 196612
  68.3 28.1 %all-to-all-start = ((bf16[8,64,512]{2,1,0:T(8,128)(2,1)}), bf16[8,64,512]{2,1,0:T(8,128)(2,1)}, u32[]{:S(2)}, u32[]{:S(2)}) async-start(bf16[8,64,512]{2,1,0:T(8,128)(2,1)} %add_convert_fusion.1), calls=%async_computation | async-start | bytes 1048576 | tf_op jit(solution)/shard_map/all_to_all | solution.py:344
  78.4 25.1 %collective-permute-start.12 = (bf16[64,4096]{1,0:T(8,128)(2,1)S(1)}, bf16[64,4096]{1,0:T(8,128)(2,1)}, u32[]{:S(2)}, u32[]{:S(2)}) collective-permute-start(bf16[64,4096]{1,0:T(8,128)(2,1)S(1)} %copy-done.6), channel_id=1, source_target_pairs={{0,4},{4,0},{8,12},{12,8},{1,5},{5,1},{9,13},{13,9},{2,6},{6,2},{1... | collective-permute-start | bytes 1572872 | tf_op jit(solution)/shard_map/ppermute | solution.py:22
  97.5 9.0 %collective-permute-start.11 = (bf16[64,512]{1,0:T(8,128)(2,1)S(1)}, bf16[64,512]{1,0:T(8,128)(2,1)S(1)}, u32[]{:S(2)}, u32[]{:S(2)}) collective-permute-start(bf16[64,512]{1,0:T(8,128)(2,1)S(1)} %reduce_sum.32.mine_ref), channel_id=1, source_target_pairs={{0,32},{32,0},{1,33},{33,1},{2,34},{34,2},{3,35},{35,3},{4,36},{36... | collective-permute-start | bytes 196616 | tf_op jit(solution)/shard_map/ppermute | solution.py:22
  107.4 17.8 %all-to-all-start.1 = ((bf16[8,64,512]{2,1,0:T(8,128)(2,1)}), bf16[8,64,512]{2,1,0:T(8,128)(2,1)S(1)}, u32[]{:S(2)}, u32[]{:S(2)}) async-start(bf16[8,64,512]{2,1,0:T(8,128)(2,1)} %get-tuple-element.79), calls=%async_computation.1 | async-start | bytes 1048576 | tf_op jit(solution)/shard_map/all_to_all | solution.py:353
  110.9 20.3 %collective-permute-start.10 = (bf16[64,4096]{1,0:T(8,128)(2,1)}, bf16[64,4096]{1,0:T(8,128)(2,1)S(1)}, u32[]{:S(2)}, u32[]{:S(2)}) collective-permute-start(bf16[64,4096]{1,0:T(8,128)(2,1)} %copy-done.4), channel_id=1, source_target_pairs={{0,4},{4,0},{8,12},{12,8},{1,5},{5,1},{9,13},{13,9},{2,6},{6,2},{1... | collective-permute-start | bytes 1572872 | tf_op jit(solution)/shard_map/ppermute | solution.py:22
  116.3 15.6 %collective-permute-start.13 = (bf16[64,4096]{1,0:T(8,128)(2,1)}, bf16[64,4096]{1,0:T(8,128)(2,1)}, u32[]{:S(2)}, u32[]{:S(2)}) collective-permute-start(bf16[64,4096]{1,0:T(8,128)(2,1)} %add_convert_fusion), channel_id=1, source_target_pairs={{0,12},{4,8},{8,4},{12,0},{1,13},{5,9},{9,5},{13,1},{2,14},{6,10},... | collective-permute-start | bytes 1572872 | tf_op jit(solution)/shard_map/ppermute | solution.py:22
  125.3 7.4 %collective-permute-start.14 = (bf16[8,64,512]{2,1,0:T(8,128)(2,1)S(1)}, bf16[8,64,512]{2,1,0:T(8,128)(2,1)S(1)}, u32[]{:S(2)}, u32[]{:S(2)}) collective-permute-start(bf16[8,64,512]{2,1,0:T(8,128)(2,1)S(1)} %all-to-all-done.1.near_ref), channel_id=1, source_target_pairs={{0,16},{16,0},{1,17},{17,1},{2,18},{18,2},{3,19},{19,3},{4,20},{20... | collective-permute-start | bytes 1572872 | tf_op jit(solution)/shard_map/ppermute | solution.py:22

commit v14 on v13

--- a/solution.py
+++ b/solution.py
@@ -330,16 +330,16 @@
     got_1 = swap(give_1, "dp", 1, 4)
     *shards, give_3, moment = lax.optimization_barrier((*shards, give_3, moment))
     got_3 = swap(give_3, "dp", 3, 4)
-    far_moment = swap(moment, "yh", 1, 2)
     others = jnp.concatenate([picks, near_picks[:1], far_picks, near_picks[1:]])
     others = others_of(others, rows_blk * cols_blk)
     rest = rest_parts(others, at, shards, cotangent)
-    got_1, got_2, got_3, far_moment, give_1, give_2, keep, own = lax.optimization_barrier(
-        (got_1, got_2, got_3, far_moment, *rest)
+    got_1, got_2, got_3, give_1, give_2, keep, own = lax.optimization_barrier(
+        (got_1, got_2, got_3, *rest)
     )
     mine, other = chosen_sums(picks, at_c, mask, feedback[0], own, got_1, got_2, got_3)
     pair = (mine + swap(other, "c", 1, 2).astype(F32)).astype(BF16)
-    pair, give_1, give_2 = lax.optimization_barrier((pair, give_1, give_2))
+    pair, give_1, give_2, moment = lax.optimization_barrier((pair, give_1, give_2, moment))
+    far_moment = swap(moment, "yh", 1, 2)
     via = swap(give_2, "dp", 1, 4)
     across = lax.all_to_all(pair, "z", 0, 0, tiled=True)
     near = jnp.sum(across.astype(F32), axis=0).astype(BF16)

time: 139 us -> 137 us (0.986)
  starting transfers between devices: 80 us -> 74.9 us
  waiting for transfers between devices: 26.6 us -> 30.8 us
    ppermute x15, waiting for transfers between devices: 7.22 us -> 16.5 us  [swap(): return lax.ppermute(value, axis, [(i, i ^ flip) for i in range(size)])]
    all_to_all x1, waiting for transfers between devices: 14.4 us -> 5.29 us  [local(): across = lax.all_to_all(pair, 'z', 0, 0, tiled=True)]
    ppermute x15, starting transfers between devices: 66.5 us -> 61.3 us  [swap(): return lax.ppermute(value, axis, [(i, i ^ flip) for i in range(size)])]
    all_to_all x1, waiting for transfers between devices: 4.98 us -> 8.94 us  [local(): every = lax.all_to_all(copies, 'z', 0, 0, tiled=True)]
where the time goes in v14:
time: 137 us; the launch traced here: 136 us
  starting transfers between devices  74.9 us (55%)
  waiting for transfers between devices  30.8 us (22%)
  Pallas kernels  17.5 us (13%)
  other arithmetic  6.32 us (5%)
  matrix products  3.89 us (3%)
    ppermute x15, starting transfers between devices, swap(): return lax.ppermute(value, axis, [(i, i ^ flip) for i in range(size)])  61.3 us
    ppermute x15, waiting for transfers between devices, swap(): return lax.ppermute(value, axis, [(i, i ^ flip) for i in range(size)])  16.5 us
    all_to_all x1, starting transfers between devices, local(): across = lax.all_to_all(pair, 'z', 0, 0, tiled=True)  10 us
    all_to_all x1, waiting for transfers between devices, local(): every = lax.all_to_all(copies, 'z', 0, 0, tiled=True)  8.94 us
    pallas_call x1, Pallas kernels, products_call(): pl.pallas_call(body, in_specs=[SMEM, SMEM] + [whole] * 5, out_specs=jax.t...  6.54 us
    pallas_call x2, Pallas kernels, state_call(): pl.pallas_call(body, grid=(rows // BLK,), in_specs=[SMEM] * len(scalars)...  5.95 us
    all_to_all x1, waiting for transfers between devices, local(): across = lax.all_to_all(pair, 'z', 0, 0, tiled=True)  5.29 us
    pallas_call x2, Pallas kernels, chosen_parts(): kernel_call(functools.partial(first_kernel, rows), (), [SMEM] * n + [whol...  4.08 us
  transfers between devices with their start and end apart: 17, of which 7 were waited for; matrix products, arithmetic and copies ran while one was open for 8% of the time, Pallas kernels for 8%

profile of v14, /device:TPU:1, one launch (start us, length us, event | category | flops | bytes accessed | tf_op | source)
XLA Modules:
  0.0 135.6 jit_solution(11904575874192133579)
XLA Ops:
  0.6 5.0 %collective-permute-start.3 = (bf16[512,256]{1,0:T(8,128)(2,1)}, bf16[512,256]{1,0:T(8,128)(2,1)S(1)}, u32[]{:S(2)}, u32[]{:S(2)}) collective-permute-start(bf16[512,256]{1,0:T(8,128)(2,1)} %s0), channel_id=1, source_target_pairs={{0,2},{1,3},{2,0},{3,1},{4,6},{5,7},{6,4},{7,5},{8,10},{9,11},{10,... | collective-permute-start | bytes 786440 | tf_op jit(solution)/shard_map/ppermute | solution.py:22
  5.7 3.2 %collective-permute-start.2 = (bf16[512,256]{1,0:T(8,128)(2,1)}, bf16[512,256]{1,0:T(8,128)(2,1)S(1)}, u32[]{:S(2)}, u32[]{:S(2)}) collective-permute-start(bf16[512,256]{1,0:T(8,128)(2,1)} %s0), channel_id=1, source_target_pairs={{0,1},{1,0},{2,3},{3,2},{4,5},{5,4},{6,7},{7,6},{8,9},{9,8},{10,11... | collective-permute-start | bytes 786440 | tf_op jit(solution)/shard_map/ppermute | solution.py:22
  8.9 4.7 %collective-permute-start = (s32[1,64]{1,0:T(1,128)}, s32[1,64]{1,0:T(1,128)S(1)}, u32[]{:S(2)}, u32[]{:S(2)}) collective-permute-start(s32[1,64]{1,0:T(1,128)} %bitcast.16), channel_id=1, source_target_pairs={{0,8},{4,12},{8,0},{12,4},{1,9},{5,13},{9,1},{13,5},{2,10},{6,14},... | collective-permute-start | bytes 776 | tf_op jit(solution)/shard_map/ppermute | solution.py:22
  13.7 3.1 %collective-permute-done.3.s2 = bf16[512,256]{1,0:T(8,128)(2,1)S(1)} collective-permute-done((bf16[512,256]{1,0:T(8,128)(2,1)}, bf16[512,256]{1,0:T(8,128)(2,1)S(1)}, u32[]{:S(2)}, u32[]{:S(2)}) %collective-permute-start.3) | collective-permute-done | bytes 262176 | tf_op jit(solution)/shard_map/ppermute | solution.py:22
  16.8 4.0 %collective-permute-start.4 = (bf16[512,256]{1,0:T(8,128)(2,1)S(1)}, bf16[512,256]{1,0:T(8,128)(2,1)S(1)}, u32[]{:S(2)}, u32[]{:S(2)}) collective-permute-start(bf16[512,256]{1,0:T(8,128)(2,1)S(1)} %collective-permute-done.3.s2), channel_id=1, source_target_pairs={{0,1},{1,0},{2,3},{3,2},{4,5},{5,4},{6,7},{7,6},{8,9},{9,8},{10,11... | collective-permute-start | bytes 786440 | tf_op jit(solution)/shard_map/ppermute | solution.py:22
  23.7 3.2 %collective-permute-start.1 = (s32[2,64]{1,0:T(2,128)S(1)}, s32[2,64]{1,0:T(2,128)S(1)}, u32[]{:S(2)}, u32[]{:S(2)}) collective-permute-start(s32[2,64]{1,0:T(2,128)S(1)} %pad_add_fusion.1), channel_id=1, source_target_pairs={{0,4},{4,0},{8,12},{12,8},{1,5},{5,1},{9,13},{13,9},{2,6},{6,2},{1... | collective-permute-start | bytes 1544 | tf_op jit(solution)/shard_map/ppermute | solution.py:22
  27.0 2.3 %convolution_convert_fusion.2.refs_1_ = bf16[256,2048]{1,0:T(8,128)(2,1)S(1)} fusion(bf16[512,2048]{1,0:T(8,128)(2,1)} %cot_ref.1, bf16[512,256]{1,0:T(8,128)(2,1)S(1)} %collective-permute-done.3.s2, bf16[512,256]{1,0:T(8,128)(2,1)S(1)} %collective-permute-done.4.s3, bf16[512,256]{1,0:T(8,128)(2,1)} %s0, bf16[512,256]{1,0:T(8,128)(2,1)S(1)} %collective-permute-done.2.s1, ...), kind=kOutput, calls=%fused_computation.2 | convolution fusion | flops 537788416 | bytes 4194307 | tf_op jit(solution)/shard_map/dot_general | solution.py:317
  29.3 1.5 %shard_map.76 = bf16[64,4096]{1,0:T(8,128)(2,1)S(1)} custom-call(s32[1,64]{1,0:T(1,128)S(1)} %collective-permute-done.refs_0_, bf16[256,2048]{1,0:T(8,128)(2,1)S(1)} %convolution_convert_fusion.2.refs_1_), custom_call_target="tpu_custom_call" | custom-call | flops 1048576 | bytes 1048576 | tf_op jit(solution)/shard_map/pallas_call | solution.py:122
  30.9 4.5 %collective-permute-start.6 = (bf16[64,4096]{1,0:T(8,128)(2,1)S(1)}, bf16[64,4096]{1,0:T(8,128)(2,1)S(1)}, u32[]{:S(2)}, u32[]{:S(2)}) collective-permute-start(bf16[64,4096]{1,0:T(8,128)(2,1)S(1)} %shard_map.76), channel_id=1, source_target_pairs={{0,8},{4,12},{8,0},{12,4},{1,9},{5,13},{9,1},{13,5},{2,10},{6,14},... | collective-permute-start | bytes 1572872 | tf_op jit(solution)/shard_map/ppermute | solution.py:22
  36.9 2.5 %shard_map.77 = (bf16[64,4096]{1,0:T(8,128)(2,1)S(1)}, bf16[64,4096]{1,0:T(8,128)(2,1)S(1)}) custom-call(s32[2,64]{1,0:T(2,128)S(1)} %collective-permute-done.1.refs_0_.refs_1_, s32[2,64]{1,0:T(2,128)S(1)} %collective-permute-done.1.refs_0_.refs_1_, bf16[256,2048]{1,0:T(8,128)(2,1)S(1)} %convolution_convert_fusion.1.refs_2_, ...), custom_call_target="tpu_custom_call" | custom-call | flops 1048576 | bytes 1048576 | tf_op jit(solution)/shard_map/pallas_call | solution.py:122
  39.5 2.2 %collective-permute-start.7 = (bf16[64,4096]{1,0:T(8,128)(2,1)S(1)}, bf16[64,4096]{1,0:T(8,128)(2,1)S(1)}, u32[]{:S(2)}, u32[]{:S(2)}) collective-permute-start(bf16[64,4096]{1,0:T(8,128)(2,1)S(1)} %get-tuple-element.54), channel_id=1, source_target_pairs={{0,12},{4,8},{8,4},{12,0},{1,13},{5,9},{9,5},{13,1},{2,14},{6,10},... | collective-permute-start | bytes 1572872 | tf_op jit(solution)/shard_map/ppermute | solution.py:22
  41.7 1.9 %collective-permute-start.5 = (bf16[64,4096]{1,0:T(8,128)(2,1)S(1)}, bf16[64,4096]{1,0:T(8,128)(2,1)S(1)}, u32[]{:S(2)}, u32[]{:S(2)}) collective-permute-start(bf16[64,4096]{1,0:T(8,128)(2,1)S(1)} %get-tuple-element.52), channel_id=1, source_target_pairs={{0,4},{4,0},{8,12},{12,8},{1,5},{5,1},{9,13},{13,9},{2,6},{6,2},{1... | collective-permute-start | bytes 1572872 | tf_op jit(solution)/shard_map/ppermute | solution.py:22
  44.1 6.5 %shard_map.78 = (bf16[64,4096]{1,0:T(8,128)(2,1)S(1)}, bf16[64,4096]{1,0:T(8,128)(2,1)S(1)}, bf16[64,4096]{1,0:T(8,128)(2,1)S(1)}, bf16[256,2048]{1,0:T(8,128)(2,1)S(1)}) custom-call(s32[4,64]{1,0:T(4,128)S(1)} %select_reduce_fusion.1.list_ref, s32[1]{0:T(128)} %bitcast.6.at_ref, bf16[512,256]{1,0:T(8,128)(2,1)S(1)} %copy-done.1, ...), custom_call_target="tpu_custom_call" | custom-call | flops 1048576 | bytes 1048576 | tf_op jit(solution)/shard_map/pallas_call | solution.py:105
  50.6 8.7 %collective-permute-done.7.got_3 = bf16[64,4096]{1,0:T(8,128)(2,1)S(1)} collective-permute-done((bf16[64,4096]{1,0:T(8,128)(2,1)S(1)}, bf16[64,4096]{1,0:T(8,128)(2,1)S(1)}, u32[]{:S(2)}, u32[]{:S(2)}) %collective-permute-start.7) | collective-permute-done | bytes 524320 | tf_op jit(solution)/shard_map/ppermute | solution.py:22
  59.3 2.0 %shard_map.79 = (f32[8,64,512]{2,1,0:T(8,128)S(1)}, bf16[8,64,512]{2,1,0:T(8,128)(2,1)S(1)}) custom-call(s32[1,64]{1,0:T(1,128)S(1)} %bitcast.20, s32[1]{0:T(128)} %bitcast.1.c_ref, f32[4,1,2048]{2,1,0:T(1,128)S(1)} %reshape.122.mask_ref, bf16[256,2048]{1,0:T(8,128)(2,1)S(1)} %bitcast.14, bf16[256,2048]{1,0:T(8,128)(2,1)S(1)} %get-tuple-element.63.own_ref, ...), custom_call_target="tpu_custom_call" | custom-call | flops 4194304 | bytes 4194304 | tf_op jit(solution)/shard_map/pallas_call | solution.py:217
  61.4 2.4 %collective-permute-start.8 = (bf16[8,64,512]{2,1,0:T(8,128)(2,1)S(1)}, bf16[8,64,512]{2,1,0:T(8,128)(2,1)S(1)}, u32[]{:S(2)}, u32[]{:S(2)}) collective-permute-start(bf16[8,64,512]{2,1,0:T(8,128)(2,1)S(1)} %get-tuple-element.68), channel_id=1, source_target_pairs={{0,16},{16,0},{1,17},{17,1},{2,18},{18,2},{3,19},{19,3},{4,20},{20... | collective-permute-start | bytes 1572872 | tf_op jit(solution)/shard_map/ppermute | solution.py:22
  63.8 1.5 %collective-permute-done.8 = bf16[8,64,512]{2,1,0:T(8,128)(2,1)S(1)} collective-permute-done((bf16[8,64,512]{2,1,0:T(8,128)(2,1)S(1)}, bf16[8,64,512]{2,1,0:T(8,128)(2,1)S(1)}, u32[]{:S(2)}, u32[]{:S(2)}) %collective-permute-start.8) | collective-permute-done | bytes 524320 | tf_op jit(solution)/shard_map/ppermute | solution.py:22
  66.4 10.0 %all-to-all-start = ((bf16[8,64,512]{2,1,0:T(8,128)(2,1)}), bf16[8,64,512]{2,1,0:T(8,128)(2,1)}, u32[]{:S(2)}, u32[]{:S(2)}) async-start(bf16[8,64,512]{2,1,0:T(8,128)(2,1)} %add_convert_fusion.1), calls=%async_computation | async-start | bytes 1048576 | tf_op jit(solution)/shard_map/all_to_all | solution.py:344
  76.4 3.0 %collective-permute-start.11 = (bf16[64,4096]{1,0:T(8,128)(2,1)S(1)}, bf16[64,4096]{1,0:T(8,128)(2,1)}, u32[]{:S(2)}, u32[]{:S(2)}) collective-permute-start(bf16[64,4096]{1,0:T(8,128)(2,1)S(1)} %copy-done.6), channel_id=1, source_target_pairs={{0,4},{4,0},{8,12},{12,8},{1,5},{5,1},{9,13},{13,9},{2,6},{6,2},{1... | collective-permute-start | bytes 1572872 | tf_op jit(solution)/shard_map/ppermute | solution.py:22
  79.4 8.1 %collective-permute-start.13 = (f32[64,256]{1,0:T(8,128)S(1)}, f32[64,256]{1,0:T(8,128)S(1)}, u32[]{:S(2)}, u32[]{:S(2)}) collective-permute-start(f32[64,256]{1,0:T(8,128)S(1)} %reshape.119), channel_id=1, source_target_pairs={{0,32},{32,0},{1,33},{33,1},{2,34},{34,2},{3,35},{35,3},{4,36},{36... | collective-permute-start | bytes 196616 | tf_op jit(solution)/shard_map/ppermute | solution.py:22
  87.5 1.7 %collective-permute-done.13 = f32[64,256]{1,0:T(8,128)S(1)} collective-permute-done((f32[64,256]{1,0:T(8,128)S(1)}, f32[64,256]{1,0:T(8,128)S(1)}, u32[]{:S(2)}, u32[]{:S(2)}) %collective-permute-start.13) | collective-permute-done | bytes 65568 | tf_op jit(solution)/shard_map/ppermute | solution.py:22
  89.2 5.3 %all-to-all-done = bf16[8,64,512]{2,1,0:T(8,128)(2,1)} async-done(((bf16[8,64,512]{2,1,0:T(8,128)(2,1)}), bf16[8,64,512]{2,1,0:T(8,128)(2,1)}, u32[]{:S(2)}, u32[]{:S(2)}) %all-to-all-start) | async-done | bytes 524320 | tf_op jit(solution)/shard_map/all_to_all | solution.py:344
  94.5 1.1 reduce_sum.32.mine_ref
  95.6 7.9 %collective-permute-start.10 = (bf16[64,512]{1,0:T(8,128)(2,1)S(1)}, bf16[64,512]{1,0:T(8,128)(2,1)S(1)}, u32[]{:S(2)}, u32[]{:S(2)}) collective-permute-start(bf16[64,512]{1,0:T(8,128)(2,1)S(1)} %reduce_sum.32.mine_ref), channel_id=1, source_target_pairs={{0,32},{32,0},{1,33},{33,1},{2,34},{34,2},{3,35},{35,3},{4,36},{36... | collective-permute-start | bytes 196616 | tf_op jit(solution)/shard_map/ppermute | solution.py:22
  103.5 2.0 %add_convert_fusion = bf16[64,4096]{1,0:T(8,128)(2,1)} fusion(bf16[64,4096]{1,0:T(8,128)(2,1)} %collective-permute-done.11, bf16[64,4096]{1,0:T(8,128)(2,1)S(1)} %get-tuple-element.74), kind=kLoop, calls=%fused_computation.4 | loop fusion | flops 1048576 | bytes 1572864 | tf_op jit(solution)/shard_map/convert_element_type | solution.py:291
  106.4 3.5 %all-to-all-start.1 = ((bf16[8,64,512]{2,1,0:T(8,128)(2,1)}), bf16[8,64,512]{2,1,0:T(8,128)(2,1)S(1)}, u32[]{:S(2)}, u32[]{:S(2)}) async-start(bf16[8,64,512]{2,1,0:T(8,128)(2,1)} %get-tuple-element.79), calls=%async_computation.1 | async-start | bytes 1048576 | tf_op jit(solution)/shard_map/all_to_all | solution.py:353
  109.9 3.2 %collective-permute-start.9 = (bf16[64,4096]{1,0:T(8,128)(2,1)}, bf16[64,4096]{1,0:T(8,128)(2,1)S(1)}, u32[]{:S(2)}, u32[]{:S(2)}) collective-permute-start(bf16[64,4096]{1,0:T(8,128)(2,1)} %copy-done.4), channel_id=1, source_target_pairs={{0,4},{4,0},{8,12},{12,8},{1,5},{5,1},{9,13},{13,9},{2,6},{6,2},{1... | collective-permute-start | bytes 1572872 | tf_op jit(solution)/shard_map/ppermute | solution.py:22
  113.0 3.7 %collective-permute-start.12 = (bf16[64,4096]{1,0:T(8,128)(2,1)}, bf16[64,4096]{1,0:T(8,128)(2,1)}, u32[]{:S(2)}, u32[]{:S(2)}) collective-permute-start(bf16[64,4096]{1,0:T(8,128)(2,1)} %add_convert_fusion), channel_id=1, source_target_pairs={{0,12},{4,8},{8,4},{12,0},{1,13},{5,9},{9,5},{13,1},{2,14},{6,10},... | collective-permute-start | bytes 1572872 | tf_op jit(solution)/shard_map/ppermute | solution.py:22
  116.7 8.9 %all-to-all-done.1.near_ref = bf16[8,64,512]{2,1,0:T(8,128)(2,1)S(1)} async-done(((bf16[8,64,512]{2,1,0:T(8,128)(2,1)}), bf16[8,64,512]{2,1,0:T(8,128)(2,1)S(1)}, u32[]{:S(2)}, u32[]{:S(2)}) %all-to-all-start.1) | async-done | bytes 524320 | tf_op jit(solution)/shard_map/all_to_all | solution.py:353
  125.7 4.5 %collective-permute-start.14 = (bf16[8,64,512]{2,1,0:T(8,128)(2,1)S(1)}, bf16[8,64,512]{2,1,0:T(8,128)(2,1)S(1)}, u32[]{:S(2)}, u32[]{:S(2)}) collective-permute-start(bf16[8,64,512]{2,1,0:T(8,128)(2,1)S(1)} %all-to-all-done.1.near_ref), channel_id=1, source_target_pairs={{0,16},{16,0},{1,17},{17,1},{2,18},{18,2},{3,19},{19,3},{4,20},{20... | collective-permute-start | bytes 1572872 | tf_op jit(solution)/shard_map/ppermute | solution.py:22
  130.2 1.5 %collective-permute-done.14.far_ref = bf16[8,64,512]{2,1,0:T(8,128)(2,1)S(1)} collective-permute-done((bf16[8,64,512]{2,1,0:T(8,128)(2,1)S(1)}, bf16[8,64,512]{2,1,0:T(8,128)(2,1)S(1)}, u32[]{:S(2)}, u32[]{:S(2)}) %collective-permute-start.14) | collective-permute-done | bytes 524320 | tf_op jit(solution)/shard_map/ppermute | solution.py:22
  131.7 3.9 %shard_map.81 = (bf16[256,2048]{1,0:T(8,128)(2,1)}, bf16[256,2048]{1,0:T(8,128)(2,1)}) custom-call(s32[4,64]{1,0:T(4,128)S(1)} %select_reduce_fusion.1.list_ref, s32[1]{0:T(128)} %bitcast.1.c_ref, f32[4,1,2048]{2,1,0:T(1,128)S(1)} %reshape.122.mask_ref, bf16[256,2048]{1,0:T(8,128)(2,1)S(1)} %bitcast.15, bf16[256,2048]{1,0:T(8,128)(2,1)S(1)} %get-tuple-element.63.own_ref, ...), custom_call_target="tpu_custom_call" | custom-call | flops 4194304 | bytes 4194304 | tf_op jit(solution)/shard_map/pallas_call | solution.py:217
  (44 shorter events, 6.9 us)
Async XLA Ops:
  0.6 16.1 %collective-permute-start.3 = (bf16[512,256]{1,0:T(8,128)(2,1)}, bf16[512,256]{1,0:T(8,128)(2,1)S(1)}, u32[]{:S(2)}, u32[]{:S(2)}) collective-permute-start(bf16[512,256]{1,0:T(8,128)(2,1)} %s0), channel_id=1, source_target_pairs={{0,2},{1,3},{2,0},{3,1},{4,6},{5,7},{6,4},{7,5},{8,10},{9,11},{10,... | collective-permute-start | bytes 786440 | tf_op jit(solution)/shard_map/ppermute | solution.py:22
  5.7 21.3 %collective-permute-start.2 = (bf16[512,256]{1,0:T(8,128)(2,1)}, bf16[512,256]{1,0:T(8,128)(2,1)S(1)}, u32[]{:S(2)}, u32[]{:S(2)}) collective-permute-start(bf16[512,256]{1,0:T(8,128)(2,1)} %s0), channel_id=1, source_target_pairs={{0,1},{1,0},{2,3},{3,2},{4,5},{5,4},{6,7},{7,6},{8,9},{9,8},{10,11... | collective-permute-start | bytes 786440 | tf_op jit(solution)/shard_map/ppermute | solution.py:22
  8.9 14.1 %collective-permute-start = (s32[1,64]{1,0:T(1,128)}, s32[1,64]{1,0:T(1,128)S(1)}, u32[]{:S(2)}, u32[]{:S(2)}) collective-permute-start(s32[1,64]{1,0:T(1,128)} %bitcast.16), channel_id=1, source_target_pairs={{0,8},{4,12},{8,0},{12,4},{1,9},{5,13},{9,1},{13,5},{2,10},{6,14},... | collective-permute-start | bytes 776 | tf_op jit(solution)/shard_map/ppermute | solution.py:22
  16.8 10.2 %collective-permute-start.4 = (bf16[512,256]{1,0:T(8,128)(2,1)S(1)}, bf16[512,256]{1,0:T(8,128)(2,1)S(1)}, u32[]{:S(2)}, u32[]{:S(2)}) collective-permute-start(bf16[512,256]{1,0:T(8,128)(2,1)S(1)} %collective-permute-done.3.s2), channel_id=1, source_target_pairs={{0,1},{1,0},{2,3},{3,2},{4,5},{5,4},{6,7},{7,6},{8,9},{9,8},{10,11... | collective-permute-start | bytes 786440 | tf_op jit(solution)/shard_map/ppermute | solution.py:22
  23.7 11.6 %copy-start = (bf16[512,2048]{1,0:T(8,128)(2,1)S(1)}, bf16[512,2048]{1,0:T(8,128)(2,1)}, u32[]{:S(2)}) copy-start(bf16[512,2048]{1,0:T(8,128)(2,1)} %cot_ref.1) | copy-start | bytes 6291460
  23.7 11.6 %copy-start.1 = (bf16[512,256]{1,0:T(8,128)(2,1)S(1)}, bf16[512,256]{1,0:T(8,128)(2,1)}, u32[]{:S(2)}) copy-start(bf16[512,256]{1,0:T(8,128)(2,1)} %s0) | copy-start | bytes 786436
  23.7 13.2 %collective-permute-start.1 = (s32[2,64]{1,0:T(2,128)S(1)}, s32[2,64]{1,0:T(2,128)S(1)}, u32[]{:S(2)}, u32[]{:S(2)}) collective-permute-start(s32[2,64]{1,0:T(2,128)S(1)} %pad_add_fusion.1), channel_id=1, source_target_pairs={{0,4},{4,0},{8,12},{12,8},{1,5},{5,1},{9,13},{13,9},{2,6},{6,2},{1... | collective-permute-start | bytes 1544 | tf_op jit(solution)/shard_map/ppermute | solution.py:22
  30.9 28.5 %collective-permute-start.6 = (bf16[64,4096]{1,0:T(8,128)(2,1)S(1)}, bf16[64,4096]{1,0:T(8,128)(2,1)S(1)}, u32[]{:S(2)}, u32[]{:S(2)}) collective-permute-start(bf16[64,4096]{1,0:T(8,128)(2,1)S(1)} %shard_map.76), channel_id=1, source_target_pairs={{0,8},{4,12},{8,0},{12,4},{1,9},{5,13},{9,1},{13,5},{2,10},{6,14},... | collective-permute-start | bytes 1572872 | tf_op jit(solution)/shard_map/ppermute | solution.py:22
  36.9 6.7 %copy-start.3 = (s32[1,1,1,64]{3,2,1,0:T(1,128)S(1)}, s32[1,1,1,64]{3,2,1,0:T(1,128)}, u32[]{:S(2)}) copy-start(s32[1,1,1,64]{3,2,1,0:T(1,128)} %param.8) | copy-start | bytes 772
  39.5 19.9 %copy-start.2 = (bf16[1,256,2048]{2,1,0:T(8,128)(2,1)S(1)}, bf16[1,256,2048]{2,1,0:T(8,128)(2,1)}, u32[]{:S(2)}) copy-start(bf16[1,256,2048]{2,1,0:T(8,128)(2,1)} %param.7) | copy-start | bytes 3145732
  39.5 19.8 %collective-permute-start.7 = (bf16[64,4096]{1,0:T(8,128)(2,1)S(1)}, bf16[64,4096]{1,0:T(8,128)(2,1)S(1)}, u32[]{:S(2)}, u32[]{:S(2)}) collective-permute-start(bf16[64,4096]{1,0:T(8,128)(2,1)S(1)} %get-tuple-element.54), channel_id=1, source_target_pairs={{0,12},{4,8},{8,4},{12,0},{1,13},{5,9},{9,5},{13,1},{2,14},{6,10},... | collective-permute-start | bytes 1572872 | tf_op jit(solution)/shard_map/ppermute | solution.py:22
  41.7 17.7 %collective-permute-start.5 = (bf16[64,4096]{1,0:T(8,128)(2,1)S(1)}, bf16[64,4096]{1,0:T(8,128)(2,1)S(1)}, u32[]{:S(2)}, u32[]{:S(2)}) collective-permute-start(bf16[64,4096]{1,0:T(8,128)(2,1)S(1)} %get-tuple-element.52), channel_id=1, source_target_pairs={{0,4},{4,0},{8,12},{12,8},{1,5},{5,1},{9,13},{13,9},{2,6},{6,2},{1... | collective-permute-start | bytes 1572872 | tf_op jit(solution)/shard_map/ppermute | solution.py:22
  50.6 10.8 %copy-start.4 = (bf16[64,4096]{1,0:T(8,128)(2,1)}, bf16[64,4096]{1,0:T(8,128)(2,1)S(1)}, u32[]{:S(2)}) copy-start(bf16[64,4096]{1,0:T(8,128)(2,1)S(1)} %get-tuple-element.72) | copy-start | bytes 1572868
  50.6 10.8 %copy-start.5 = (bf16[64,4096]{1,0:T(8,128)(2,1)}, bf16[64,4096]{1,0:T(8,128)(2,1)S(1)}, u32[]{:S(2)}) copy-start(bf16[64,4096]{1,0:T(8,128)(2,1)S(1)} %get-tuple-element.75) | copy-start | bytes 1572868
  61.4 3.9 %collective-permute-start.8 = (bf16[8,64,512]{2,1,0:T(8,128)(2,1)S(1)}, bf16[8,64,512]{2,1,0:T(8,128)(2,1)S(1)}, u32[]{:S(2)}, u32[]{:S(2)}) collective-permute-start(bf16[8,64,512]{2,1,0:T(8,128)(2,1)S(1)} %get-tuple-element.68), channel_id=1, source_target_pairs={{0,16},{16,0},{1,17},{17,1},{2,18},{18,2},{3,19},{19,3},{4,20},{20... | collective-permute-start | bytes 1572872 | tf_op jit(solution)/shard_map/ppermute | solution.py:22
  63.8 12.6 %copy-start.6 = (bf16[64,4096]{1,0:T(8,128)(2,1)S(1)}, bf16[64,4096]{1,0:T(8,128)(2,1)}, u32[]{:S(2)}) copy-start(bf16[64,4096]{1,0:T(8,128)(2,1)} %copy-done.5) | copy-start | bytes 1572868
  66.4 28.1 %all-to-all-start = ((bf16[8,64,512]{2,1,0:T(8,128)(2,1)}), bf16[8,64,512]{2,1,0:T(8,128)(2,1)}, u32[]{:S(2)}, u32[]{:S(2)}) async-start(bf16[8,64,512]{2,1,0:T(8,128)(2,1)} %add_convert_fusion.1), calls=%async_computation | async-start | bytes 1048576 | tf_op jit(solution)/shard_map/all_to_all | solution.py:344
  76.4 27.1 %collective-permute-start.11 = (bf16[64,4096]{1,0:T(8,128)(2,1)S(1)}, bf16[64,4096]{1,0:T(8,128)(2,1)}, u32[]{:S(2)}, u32[]{:S(2)}) collective-permute-start(bf16[64,4096]{1,0:T(8,128)(2,1)S(1)} %copy-done.6), channel_id=1, source_target_pairs={{0,4},{4,0},{8,12},{12,8},{1,5},{5,1},{9,13},{13,9},{2,6},{6,2},{1... | collective-permute-start | bytes 1572872 | tf_op jit(solution)/shard_map/ppermute | solution.py:22
  79.4 9.8 %collective-permute-start.13 = (f32[64,256]{1,0:T(8,128)S(1)}, f32[64,256]{1,0:T(8,128)S(1)}, u32[]{:S(2)}, u32[]{:S(2)}) collective-permute-start(f32[64,256]{1,0:T(8,128)S(1)} %reshape.119), channel_id=1, source_target_pairs={{0,32},{32,0},{1,33},{33,1},{2,34},{34,2},{3,35},{35,3},{4,36},{36... | collective-permute-start | bytes 196616 | tf_op jit(solution)/shard_map/ppermute | solution.py:22
  95.6 9.9 %collective-permute-start.10 = (bf16[64,512]{1,0:T(8,128)(2,1)S(1)}, bf16[64,512]{1,0:T(8,128)(2,1)S(1)}, u32[]{:S(2)}, u32[]{:S(2)}) collective-permute-start(bf16[64,512]{1,0:T(8,128)(2,1)S(1)} %reduce_sum.32.mine_ref), channel_id=1, source_target_pairs={{0,32},{32,0},{1,33},{33,1},{2,34},{34,2},{3,35},{35,3},{4,36},{36... | collective-permute-start | bytes 196616 | tf_op jit(solution)/shard_map/ppermute | solution.py:22
  106.4 19.3 %all-to-all-start.1 = ((bf16[8,64,512]{2,1,0:T(8,128)(2,1)}), bf16[8,64,512]{2,1,0:T(8,128)(2,1)S(1)}, u32[]{:S(2)}, u32[]{:S(2)}) async-start(bf16[8,64,512]{2,1,0:T(8,128)(2,1)} %get-tuple-element.79), calls=%async_computation.1 | async-start | bytes 1048576 | tf_op jit(solution)/shard_map/all_to_all | solution.py:353
  109.9 20.3 %collective-permute-start.9 = (bf16[64,4096]{1,0:T(8,128)(2,1)}, bf16[64,4096]{1,0:T(8,128)(2,1)S(1)}, u32[]{:S(2)}, u32[]{:S(2)}) collective-permute-start(bf16[64,4096]{1,0:T(8,128)(2,1)} %copy-done.4), channel_id=1, source_target_pairs={{0,4},{4,0},{8,12},{12,8},{1,5},{5,1},{9,13},{13,9},{2,6},{6,2},{1... | collective-permute-start | bytes 1572872 | tf_op jit(solution)/shard_map/ppermute | solution.py:22
  113.0 17.1 %collective-permute-start.12 = (bf16[64,4096]{1,0:T(8,128)(2,1)}, bf16[64,4096]{1,0:T(8,128)(2,1)}, u32[]{:S(2)}, u32[]{:S(2)}) collective-permute-start(bf16[64,4096]{1,0:T(8,128)(2,1)} %add_convert_fusion), channel_id=1, source_target_pairs={{0,12},{4,8},{8,4},{12,0},{1,13},{5,9},{9,5},{13,1},{2,14},{6,10},... | collective-permute-start | bytes 1572872 | tf_op jit(solution)/shard_map/ppermute | solution.py:22
  125.7 6.0 %collective-permute-start.14 = (bf16[8,64,512]{2,1,0:T(8,128)(2,1)S(1)}, bf16[8,64,512]{2,1,0:T(8,128)(2,1)S(1)}, u32[]{:S(2)}, u32[]{:S(2)}) collective-permute-start(bf16[8,64,512]{2,1,0:T(8,128)(2,1)S(1)} %all-to-all-done.1.near_ref), channel_id=1, source_target_pairs={{0,16},{16,0},{1,17},{17,1},{2,18},{18,2},{3,19},{19,3},{4,20},{20... | collective-permute-start | bytes 1572872 | tf_op jit(solution)/shard_map/ppermute | solution.py:22
